TPU v7x, 256 devices: a whole 4x4x8 slice. The times are simulated.
256 devices in a mesh: pipe: 4 (over z_hi, core), expert: 16 (over y, x), dp: 4 (over z_lo).
Axes of the slice: x: 4, y: 4, z: 8 (z_hi: 2, z_lo: 4; z = z_hi * 4 + z_lo), core: 2. Of those that a mesh axis runs over, the one named last changes fastest.
Arguments:
- tokens_in: bfloat16 [4, 8192, 2048], P('pipe', ('expert', 'dp')), may hold values from -6 to 6
- grad_out: bfloat16 [4, 8192, 2048], P('pipe', ('expert', 'dp')), may hold values from -6 to 6
- route_weight: bfloat16 [4, 8192, 2], P('pipe', ('expert', 'dp')), may hold values from 0.19921875 to 1
- slot_of: int32 [4, 8192, 2], P('pipe', ('expert', 'dp')), may hold values from 0 to 15, as said below
- replica_of: int32 [4, 8], P('pipe'), may hold values from 0 to 7, as said below
- w_gate: bfloat16 [4, 8, 2048, 512], P('pipe', None, 'expert'), may hold values from -0.125 to 0.125
- w_up: bfloat16 [4, 8, 2048, 512], P('pipe', None, 'expert'), may hold values from -0.125 to 0.125
- w_down: bfloat16 [4, 8, 2048, 512], P('pipe', None, 'expert'), may hold values from -0.25 to 0.25
Outputs:
- grad_in: bfloat16 [4, 8192, 2048], P('pipe', ('expert', 'dp'))
- route_grad: bfloat16 [4, 8192, 2], P('pipe', ('expert', 'dp'))
- grad_gate: bfloat16 [4, 8, 2048, 512], P('pipe', None, ('expert', 'dp'))
- grad_up: bfloat16 [4, 8, 2048, 512], P('pipe', None, ('expert', 'dp'))
- grad_down: bfloat16 [4, 8, 2048, 512], P('pipe', None, ('expert', 'dp'))
Inputs may be any that keep to these rules, and one draw needn't show every extreme that they name: `slot_of`: A token's 2 pairs name slots of different experts. Among the 128 tokens of one device no slot is named more than 20 times, and in each section one slot is named exactly 20 times by every device. `replica_of`: in each section one expert is named by exactly 3 replica slots, 5 others by one each, and the remaining 2 by none.
All inputs are finite; a program needn't handle non-finite values.
Results may differ from a plain program's by a relative error of at most 0.018.
Values may be sent and summed in bfloat16 or wider, within the bound.
No kernel may reach another device: no remote copies, remote signals or barrier semaphores. Data moves between devices by JAX's collectives and lax.ppermute only.
A program may use at most 128 MiB of HBM per device.

v0:
```python
import jax
import jax.numpy as jnp
from jax import lax
from jax.sharding import PartitionSpec as P

EXPERTS = 8
TOP = 2
CAP = 20
SLOTS = 16


def from_behind(x, axis, by):
    count = lax.axis_size(axis)
    return lax.ppermute(x, axis, [(i, (i + by) % count) for i in range(count)])


def as_sent(x):

    def short(part):
        return part.astype(jnp.bfloat16) if part.dtype == jnp.float32 else part

    return jax.tree.map(short, x)


def slot_table(replicas):
    return jnp.concatenate([jnp.arange(EXPERTS, dtype=jnp.int32), replicas])


def pair_rows(slot_pairs):
    pair_slot = slot_pairs.reshape(-1)
    onehot = (pair_slot[:, None] == jnp.arange(SLOTS, dtype=jnp.int32)[None, :]).astype(jnp.int32)
    before = jnp.cumsum(onehot, axis=0) - onehot
    return pair_slot * CAP + jnp.sum(before * onehot, axis=1)


def pack_rows(tokens_dev, grads_dev, weights_dev, slot_pos):
    count = slot_pos.shape[0]
    row_owner = (
        jnp.full((SLOTS * CAP,), -1, jnp.int32)
        .at[slot_pos]
        .set(jnp.arange(count, dtype=jnp.int32) // TOP)
    )
    row_live = (row_owner >= 0)[:, None]
    row_index = jnp.maximum(row_owner, 0)
    tok_rows = jnp.where(row_live, tokens_dev[row_index], jnp.zeros((), tokens_dev.dtype))
    grad_rows = jnp.where(row_live, grads_dev[row_index], jnp.zeros((), grads_dev.dtype))
    route_rows = (
        jnp.zeros((SLOTS * CAP,), weights_dev.dtype).at[slot_pos].set(weights_dev.reshape(-1))
    )
    return (tok_rows, grad_rows, route_rows)


def expert_rows(tok_rows, grad_rows, route_rows, gate_w, up_w, down_w):
    gate_pre = jnp.dot(tok_rows, gate_w, preferred_element_type=jnp.float32)
    up_pre = jnp.dot(tok_rows, up_w, preferred_element_type=jnp.float32)
    sigma = jax.nn.sigmoid(gate_pre)
    active = gate_pre * sigma
    hidden = (active * up_pre).astype(jnp.bfloat16)
    expert_out = jnp.dot(hidden, down_w.T, preferred_element_type=jnp.float32)
    prob_grad = jnp.sum(grad_rows.astype(jnp.float32) * expert_out, axis=1).astype(jnp.bfloat16)
    scaled = (route_rows.astype(jnp.float32)[:, None] * grad_rows.astype(jnp.float32)).astype(
        jnp.bfloat16
    )
    hidden_grad = jnp.dot(scaled, down_w, preferred_element_type=jnp.float32)
    gate_grad = (hidden_grad * up_pre * sigma * (1.0 + gate_pre * (1.0 - sigma))).astype(
        jnp.bfloat16
    )
    up_grad = (hidden_grad * active).astype(jnp.bfloat16)
    row_grad = (
        jnp.dot(gate_grad, gate_w.T, preferred_element_type=jnp.float32)
        + jnp.dot(up_grad, up_w.T, preferred_element_type=jnp.float32)
    ).astype(jnp.bfloat16)
    sum_gate = jnp.dot(tok_rows.T, gate_grad, preferred_element_type=jnp.float32)
    sum_up = jnp.dot(tok_rows.T, up_grad, preferred_element_type=jnp.float32)
    sum_down = jnp.dot(scaled.T, hidden, preferred_element_type=jnp.float32)
    return (row_grad, prob_grad, sum_gate, sum_up, sum_down)


def to_experts(slot_sums, replicas):
    merged = slot_sums[:EXPERTS]
    extra = slot_sums[EXPERTS:]
    experts_all = jnp.arange(EXPERTS, dtype=jnp.int32)
    for replica in range(EXPERTS):
        match = (replicas[replica] == experts_all)[:, None, None]
        merged = merged + jnp.where(match, extra[replica][None], jnp.zeros((), jnp.float32))
    return merged


def shards(tokens_in, grad_out, route_weight, slot_of, replica_of, w_gate, w_up, w_down):
    n_expert = lax.axis_size("expert")
    n_data = lax.axis_size("dp")
    slot_dev = SLOTS // n_expert
    tokens_dev = tokens_in[0]
    grads_dev = grad_out[0]
    tok_count = tokens_dev.shape[0]
    width = tokens_dev.shape[1]
    replicas = replica_of[0]
    slot_expert = slot_table(replicas)
    slot_pos = pair_rows(slot_of[0])
    tok_rows, grad_rows, route_rows = pack_rows(tokens_dev, grads_dev, route_weight[0], slot_pos)

    def chosen(weights):
        return jnp.take(weights[0], slot_expert, axis=0)

    gate_w, up_w, down_w = (
        lax.all_to_all(chosen(w_gate), "expert", split_axis=0, concat_axis=1, tiled=True),
        lax.all_to_all(chosen(w_up), "expert", split_axis=0, concat_axis=1, tiled=True),
        lax.all_to_all(chosen(w_down), "expert", split_axis=0, concat_axis=1, tiled=True),
    )
    got_tok, got_grad, got_route = (
        lax.all_to_all(tok_rows, "expert", split_axis=0, concat_axis=0, tiled=True),
        lax.all_to_all(grad_rows, "expert", split_axis=0, concat_axis=0, tiled=True),
        lax.all_to_all(route_rows, "expert", split_axis=0, concat_axis=0, tiled=True),
    )

    def by_slot(rows):
        rows = rows.reshape((n_expert, slot_dev, CAP) + rows.shape[1:])
        rows = jnp.moveaxis(rows, 1, 0)
        return rows.reshape((slot_dev, n_expert * CAP) + rows.shape[3:])

    def by_source(rows):
        rows = rows.reshape((slot_dev, n_expert, CAP) + rows.shape[2:])
        rows = jnp.moveaxis(rows, 1, 0)
        return rows.reshape((n_expert * slot_dev * CAP,) + rows.shape[3:])

    row_grad, prob_grad, sum_gate, sum_up, sum_down = jax.vmap(expert_rows)(
        by_slot(got_tok), by_slot(got_grad), by_slot(got_route), gate_w, up_w, down_w
    )
    back_rows, back_prob = (
        lax.all_to_all(by_source(row_grad), "expert", split_axis=0, concat_axis=0, tiled=True),
        lax.all_to_all(by_source(prob_grad), "expert", split_axis=0, concat_axis=0, tiled=True),
    )
    pair_grad = back_rows[slot_pos].astype(jnp.float32).reshape(tok_count, TOP, width)
    branch = jnp.sum(pair_grad, axis=1).astype(jnp.bfloat16)
    route_out = back_prob[slot_pos].reshape(tok_count, TOP)
    section_grad = (grads_dev.astype(jnp.float32) + branch.astype(jnp.float32)).astype(jnp.bfloat16)
    grad_back = from_behind(section_grad, "pipe", -1)
    norm_scale = (tok_count * n_expert * n_data) ** (-0.5)
    moved = (
        lax.all_to_all(
            sum_gate.astype(jnp.bfloat16), "expert", split_axis=1, concat_axis=0, tiled=True
        ).astype(sum_gate.dtype),
        lax.all_to_all(
            sum_up.astype(jnp.bfloat16), "expert", split_axis=1, concat_axis=0, tiled=True
        ).astype(sum_up.dtype),
        lax.all_to_all(
            sum_down.astype(jnp.bfloat16), "expert", split_axis=1, concat_axis=0, tiled=True
        ).astype(sum_down.dtype),
    )
    merged = tuple((to_experts(part_sums, replicas) for part_sums in moved))
    results = list(
        jax.tree.map(
            lambda part: part.astype(jnp.float32),
            lax.psum_scatter(as_sent(merged), "dp", scatter_dimension=1, tiled=True),
        )
    )
    finals = [(part_sums * norm_scale).astype(jnp.bfloat16)[None] for part_sums in results]
    return (grad_back[None], route_out[None], finals[0], finals[1], finals[2])


def solution(mesh):
    return jax.shard_map(
        shards,
        mesh=mesh,
        in_specs=(
            P("pipe", ("expert", "dp"), None),
            P("pipe", ("expert", "dp"), None),
            P("pipe", ("expert", "dp"), None),
            P("pipe", ("expert", "dp"), None),
            P("pipe", None),
            P("pipe", None, "expert", None),
            P("pipe", None, "expert", None),
            P("pipe", None, "expert", None),
        ),
        out_specs=(
            P("pipe", ("expert", "dp"), None),
            P("pipe", ("expert", "dp"), None),
            P("pipe", None, ("expert", "dp"), None),
            P("pipe", None, ("expert", "dp"), None),
            P("pipe", None, ("expert", "dp"), None),
        ),
        check_vma=False,
    )
```

profile of v0, /device:TPU:1, one launch (start us, length us, event | category | flops | bytes accessed | tf_op | source)
XLA Modules:
  0.0 462.8 jit_solution(8392131612543612418)
XLA Ops:
  14.1 7.6 %all-to-all-start = ((bf16[16,20,1]{1,2,0:T(2,128)(2,1)}), bf16[16,20,1]{1,2,0:T(2,128)(2,1)S(1)}, u32[]{:S(2)}, u32[]{:S(2)}) async-start(bf16[16,20,1]{1,2,0:T(2,128)(2,1)} %all_to_all.88), calls=%async_computation | async-start | bytes 16384 | tf_op jit(solution)/shard_map/all_to_all | solution.py:113
  34.2 28.0 %all_to_all.100 = bf16[16,20,2048]{2,1,0:T(8,128)(2,1)} all-to-all(bf16[16,20,2048]{2,1,0:T(8,128)(2,1)S(1)} %get-tuple-element.46), channel_id=1, replica_groups=mesh['pipe'=4,'expert'=16,'dp'=4] {'expert'}, dimensions={0} | all-to-all | bytes 2621440 | tf_op jit(solution)/shard_map/all_to_all | solution.py:111
  62.2 3.8 all-to-all-start.1
  73.6 5.7 %broadcast_select_fusion.1 = (bf16[16,128,512]{2,1,0:T(8,128)(2,1)}, bf16[16,128,512]{2,1,0:T(8,128)(2,1)}, bf16[16,128,512]{2,1,0:T(8,128)(2,1)}) fusion(bf16[16,128,512]{2,1,0:T(8,128)(2,1)} %gather_fusion.5, pred[16]{0:T(512)(128)(4,1)S(1)} %get-tuple-element.16, bf16[16,128,512]{2,1,0:T(8,128)(2,1)} %gather_fusion.6, bf16[16,128,512]{2,1,0:T(8,128)(2,1)} %gather_fusion.4), kind=kLoop, calls=%fused_computation.24 | loop fusion | flops 3145728 | bytes 12582928 | tf_op jit(solution)/shard_map/jit(_take)/select_n | solution.py:103
  79.3 6.9 %all-to-all-done.1 = bf16[16,20,2048]{2,1,0:T(8,128)(2,1)S(1)} async-done(((bf16[16,20,2048]{2,1,0:T(8,128)(2,1)}), bf16[16,20,2048]{2,1,0:T(8,128)(2,1)S(1)}, u32[]{:S(2)}, u32[]{:S(2)}) %all-to-all-start.1) | async-done | bytes 1310752 | tf_op jit(solution)/shard_map/all_to_all | solution.py:112
  86.2 30.8 %all_to_all.101 = bf16[16,128,512]{2,1,0:T(8,128)(2,1)} all-to-all(bf16[16,128,512]{2,1,0:T(8,128)(2,1)} %get-tuple-element.56), channel_id=1, replica_groups=mesh['pipe'=4,'expert'=16,'dp'=4] {'expert'}, dimensions={0} | all-to-all | bytes 4194304 | tf_op jit(solution)/shard_map/all_to_all | solution.py:106
  117.0 27.6 %all_to_all.102 = bf16[16,128,512]{2,1,0:T(8,128)(2,1)} all-to-all(bf16[16,128,512]{2,1,0:T(8,128)(2,1)S(1)} %copy-done.7), channel_id=1, replica_groups=mesh['pipe'=4,'expert'=16,'dp'=4] {'expert'}, dimensions={0} | all-to-all | bytes 4194304 | tf_op jit(solution)/shard_map/all_to_all | solution.py:108
  144.6 4.7 %all-to-all-start.4 = ((bf16[16,128,512]{2,1,0:T(8,128)(2,1)}), bf16[16,128,512]{2,1,0:T(8,128)(2,1)}, u32[]{:S(2)}, u32[]{:S(2)}) async-start(bf16[16,128,512]{2,1,0:T(8,128)(2,1)} %get-tuple-element.55), calls=%async_computation.4 | async-start | bytes 4194304 | tf_op jit(solution)/shard_map/all_to_all | solution.py:107
  154.3 3.8 fusion.26
  159.8 13.7 %all-to-all-done.4 = bf16[16,128,512]{2,1,0:T(8,128)(2,1)} async-done(((bf16[16,128,512]{2,1,0:T(8,128)(2,1)}), bf16[16,128,512]{2,1,0:T(8,128)(2,1)}, u32[]{:S(2)}, u32[]{:S(2)}) %all-to-all-start.4) | async-done | bytes 2097184 | tf_op jit(solution)/shard_map/all_to_all | solution.py:107
  178.3 18.5 %copy.88 = bf16[1,2048,512]{2,0,1:T(2,128)(2,1)} copy(bf16[1,2048,512]{2,1,0:T(8,128)(2,1)S(1)} %fusion) | data formatting | bytes 4194304 | tf_op jit(solution)/shard_map/convert_element_type | solution.py:141
  197.4 15.4 %reduce.10 = bf16[2048,512]{1,0:T(8,128)(2,1)} reduce(bf16[2048,1,512]{2,1,0:T(2,128)(2,1)} %bitcast.143, bf16[]{:T(256)} %broadcast.209), dimensions={1}, to_apply=%bitcast.133.reduce_sub_computation | reduce | bytes 4194306
  212.8 4.5 reshape.467
  217.3 6.1 %all-to-all-start.8 = ((bf16[16,2,32768]{2,1,0:T(2,128)(2,1)}), bf16[16,2,32768]{2,1,0:T(2,128)(2,1)}, u32[]{:S(2)}, u32[]{:S(2)}) async-start(bf16[16,2,32768]{2,1,0:T(2,128)(2,1)} %reshape.467), calls=%async_computation.8 | async-start | bytes 4194304 | tf_op jit(solution)/shard_map/all_to_all | solution.py:140
  233.6 18.5 %copy.87 = bf16[1,2048,512]{2,0,1:T(2,128)(2,1)} copy(bf16[1,2048,512]{2,1,0:T(8,128)(2,1)S(1)} %fusion.1) | data formatting | bytes 4194304 | tf_op jit(solution)/shard_map/convert_element_type | solution.py:144
  252.1 15.4 %reduce.11 = bf16[2048,512]{1,0:T(8,128)(2,1)} reduce(bf16[2048,1,512]{2,1,0:T(2,128)(2,1)} %bitcast.145, bf16[]{:T(256)} %broadcast.209), dimensions={1}, to_apply=%bitcast.132.reduce_sub_computation | reduce | bytes 4194306
  267.4 4.5 reshape.469
  275.1 18.5 %copy.86 = bf16[1,2048,512]{2,0,1:T(2,128)(2,1)} copy(bf16[1,2048,512]{2,1,0:T(8,128)(2,1)S(1)} %fusion.2) | data formatting | bytes 4194304 | tf_op jit(solution)/shard_map/convert_element_type | solution.py:147
  293.6 15.4 %reduce.12 = bf16[2048,512]{1,0:T(8,128)(2,1)} reduce(bf16[2048,1,512]{2,1,0:T(2,128)(2,1)} %bitcast.144, bf16[]{:T(256)} %broadcast.209), dimensions={1}, to_apply=%bitcast.131.reduce_sub_computation | reduce | bytes 4194306
  309.0 4.7 %reshape.471 = bf16[16,2,32768]{2,1,0:T(2,128)(2,1)} reshape(bf16[2048,512]{1,0:T(8,128)(2,1)} %reduce.12) | data formatting | bytes 4194304
  313.7 6.8 %all-to-all-start.9 = ((bf16[16,2,32768]{2,1,0:T(2,128)(2,1)}), bf16[16,2,32768]{2,1,0:T(2,128)(2,1)}, u32[]{:S(2)}, u32[]{:S(2)}) async-start(bf16[16,2,32768]{2,1,0:T(2,128)(2,1)} %reshape.469), calls=%async_computation.10 | async-start | bytes 4194304 | tf_op jit(solution)/shard_map/all_to_all | solution.py:143
  320.5 10.4 %reshape.468 = bf16[2048,1,512]{2,1,0:T(2,128)(2,1)} reshape(bf16[16,2,32768]{2,1,0:T(2,128)(2,1)} %all-to-all-done.8) | data formatting | bytes 4194304
  331.0 3.8 fusion.24
  340.2 4.0 fusion.27
  344.2 6.7 %all-to-all-start.10 = ((bf16[16,2,32768]{2,1,0:T(2,128)(2,1)}), bf16[16,2,32768]{2,1,0:T(2,128)(2,1)}, u32[]{:S(2)}, u32[]{:S(2)}) async-start(bf16[16,2,32768]{2,1,0:T(2,128)(2,1)} %reshape.471), calls=%async_computation.12 | async-start | bytes 4194304 | tf_op jit(solution)/shard_map/all_to_all | solution.py:146
  350.9 10.7 %reshape.470 = bf16[2048,1,512]{2,1,0:T(2,128)(2,1)} reshape(bf16[16,2,32768]{2,1,0:T(2,128)(2,1)} %all-to-all-done.9) | data formatting | bytes 4194304
  361.6 3.8 fusion.23
  375.4 6.6 %all-to-all-start.6 = ((bf16[16,20,2048]{2,1,0:T(8,128)(2,1)}), bf16[16,20,2048]{2,1,0:T(8,128)(2,1)}, u32[]{:S(2)}, u32[]{:S(2)}) async-start(bf16[16,20,2048]{2,1,0:T(8,128)(2,1)} %all_to_all.80), calls=%async_computation.6 | async-start | bytes 3145728 | tf_op jit(solution)/shard_map/all_to_all | solution.py:130
  382.2 10.7 %reshape.472 = bf16[2048,1,512]{2,1,0:T(2,128)(2,1)} reshape(bf16[16,2,32768]{2,1,0:T(2,128)(2,1)} %all-to-all-done.10) | data formatting | bytes 4194304
  411.3 8.0 %collective-permute-start = (bf16[128,2048]{1,0:T(8,128)(2,1)S(1)}, bf16[128,2048]{1,0:T(8,128)(2,1)S(1)}, u32[]{:S(2)}, u32[]{:S(2)}) collective-permute-start(bf16[128,2048]{1,0:T(8,128)(2,1)S(1)} %add_convert_fusion.3), channel_id=1, source_target_pairs={{0,192},{64,0},{128,64},{192,128},{1,193},{65,1},{129,65},{193,129... | collective-permute-start | bytes 1572872 | tf_op jit(solution)/shard_map/ppermute | solution.py:14
  422.9 13.1 %all_to_all.103 = bf16[16,20,1]{1,2,0:T(2,128)(2,1)S(1)} all-to-all(bf16[16,20,1]{1,2,0:T(2,128)(2,1)S(1)} %convert_element_type.216), channel_id=1, replica_groups=mesh['pipe'=4,'expert'=16,'dp'=4] {'expert'}, dimensions={0} | all-to-all | bytes 1280 | tf_op jit(solution)/shard_map/all_to_all | solution.py:131
  444.1 9.2 %reduce-scatter.8.cloned.1.call-done = bf16[8,32,512]{2,1,0:T(8,128)(2,1)} async-done(((bf16[8,128,512]{2,1,0:T(8,128)(2,1)}), bf16[8,32,512]{2,1,0:T(8,128)(2,1)}) %reduce-scatter.8.cloned.1.call-update) | async-done | bytes 262160 | tf_op jit(solution)/shard_map/reduce_scatter | solution.py:154
  (139 shorter events, 100.0 us)
Async XLA Ops:
  7.2 59.0 %copy-start = (bf16[1,8,128,512]{3,2,1,0:T(8,128)(2,1)S(1)}, bf16[1,8,128,512]{3,2,1,0:T(8,128)(2,1)}, u32[]{:S(2)}) copy-start(bf16[1,8,128,512]{3,2,1,0:T(8,128)(2,1)} %param.16) | copy-start | bytes 3145732
  7.2 15.9 %copy-start.2 = (bf16[1,128,2048]{2,1,0:T(8,128)(2,1)S(1)}, bf16[1,128,2048]{2,1,0:T(8,128)(2,1)}, u32[]{:S(2)}) copy-start(bf16[1,128,2048]{2,1,0:T(8,128)(2,1)} %param.11) | copy-start | bytes 1572868
  14.1 20.2 %all-to-all-start = ((bf16[16,20,1]{1,2,0:T(2,128)(2,1)}), bf16[16,20,1]{1,2,0:T(2,128)(2,1)S(1)}, u32[]{:S(2)}, u32[]{:S(2)}) async-start(bf16[16,20,1]{1,2,0:T(2,128)(2,1)} %all_to_all.88), calls=%async_computation | async-start | bytes 16384 | tf_op jit(solution)/shard_map/all_to_all | solution.py:113
  25.6 1.5 copy-start.3
  62.2 3.9 copy-start.16
  62.2 24.0 %all-to-all-start.1 = ((bf16[16,20,2048]{2,1,0:T(8,128)(2,1)}), bf16[16,20,2048]{2,1,0:T(8,128)(2,1)S(1)}, u32[]{:S(2)}, u32[]{:S(2)}) async-start(bf16[16,20,2048]{2,1,0:T(8,128)(2,1)} %get-tuple-element.45), calls=%async_computation.1 | async-start | bytes 3145728 | tf_op jit(solution)/shard_map/all_to_all | solution.py:112
  68.2 3.3 copy-start.9
  86.2 30.8 %copy-start.7 = (bf16[16,128,512]{2,1,0:T(8,128)(2,1)S(1)}, bf16[16,128,512]{2,1,0:T(8,128)(2,1)}, u32[]{:S(2)}) copy-start(bf16[16,128,512]{2,1,0:T(8,128)(2,1)} %get-tuple-element.57) | copy-start | bytes 6291460
  144.6 28.9 %all-to-all-start.4 = ((bf16[16,128,512]{2,1,0:T(8,128)(2,1)}), bf16[16,128,512]{2,1,0:T(8,128)(2,1)}, u32[]{:S(2)}, u32[]{:S(2)}) async-start(bf16[16,128,512]{2,1,0:T(8,128)(2,1)} %get-tuple-element.55), calls=%async_computation.4 | async-start | bytes 4194304 | tf_op jit(solution)/shard_map/all_to_all | solution.py:107
  154.3 3.8 copy-start.8
  154.3 3.8 copy-start.10
  173.5 3.5 copy-start.11
  177.0 1.3 copy-start.12
  177.0 54.0 %copy-start.14 = (bf16[320,512]{1,0:T(8,128)(2,1)}, bf16[320,512]{1,0:T(8,128)(2,1)S(1)}, u32[]{:S(2)}) copy-start(bf16[320,512]{1,0:T(8,128)(2,1)S(1)} %get-tuple-element.44) | copy-start | bytes 983044
  217.3 96.4 %all-to-all-start.8 = ((bf16[16,2,32768]{2,1,0:T(2,128)(2,1)}), bf16[16,2,32768]{2,1,0:T(2,128)(2,1)}, u32[]{:S(2)}, u32[]{:S(2)}) async-start(bf16[16,2,32768]{2,1,0:T(2,128)(2,1)} %reshape.467), calls=%async_computation.8 | async-start | bytes 4194304 | tf_op jit(solution)/shard_map/all_to_all | solution.py:140
  313.7 30.5 %all-to-all-start.9 = ((bf16[16,2,32768]{2,1,0:T(2,128)(2,1)}), bf16[16,2,32768]{2,1,0:T(2,128)(2,1)}, u32[]{:S(2)}, u32[]{:S(2)}) async-start(bf16[16,2,32768]{2,1,0:T(2,128)(2,1)} %reshape.469), calls=%async_computation.10 | async-start | bytes 4194304 | tf_op jit(solution)/shard_map/all_to_all | solution.py:143
  320.5 120.3 %reduce-scatter.4.cloned.1.call-start = ((), (), s32[]{:S(2)}) async-start(), calls=%async_computation.14 | async-start | bytes 1310720 | tf_op jit(solution)/shard_map/reduce_scatter | solution.py:154
  331.0 3.8 copy-start.5
  337.3 2.9 copy-start.13
  344.2 31.2 %all-to-all-start.10 = ((bf16[16,2,32768]{2,1,0:T(2,128)(2,1)}), bf16[16,2,32768]{2,1,0:T(2,128)(2,1)}, u32[]{:S(2)}, u32[]{:S(2)}) async-start(bf16[16,2,32768]{2,1,0:T(2,128)(2,1)} %reshape.471), calls=%async_computation.12 | async-start | bytes 4194304 | tf_op jit(solution)/shard_map/all_to_all | solution.py:146
  350.9 91.6 %reduce-scatter.6.cloned.1.call-start = ((), (), s32[]{:S(2)}) async-start(), calls=%async_computation.15 | async-start | bytes 1310720 | tf_op jit(solution)/shard_map/reduce_scatter | solution.py:154
  361.6 3.8 copy-start.6
  367.9 2.8 copy-start.15
  375.4 28.5 %all-to-all-start.6 = ((bf16[16,20,2048]{2,1,0:T(8,128)(2,1)}), bf16[16,20,2048]{2,1,0:T(8,128)(2,1)}, u32[]{:S(2)}, u32[]{:S(2)}) async-start(bf16[16,20,2048]{2,1,0:T(8,128)(2,1)} %all_to_all.80), calls=%async_computation.6 | async-start | bytes 3145728 | tf_op jit(solution)/shard_map/all_to_all | solution.py:130
  382.1 71.2 %reduce-scatter.8.cloned.1.call-start = ((), (), s32[]{:S(2)}) async-start(), calls=%async_computation.16 | async-start | bytes 1310720 | tf_op jit(solution)/shard_map/reduce_scatter | solution.py:154
  396.5 2.2 copy-start.4
  411.3 29.4 %collective-permute-start = (bf16[128,2048]{1,0:T(8,128)(2,1)S(1)}, bf16[128,2048]{1,0:T(8,128)(2,1)S(1)}, u32[]{:S(2)}, u32[]{:S(2)}) collective-permute-start(bf16[128,2048]{1,0:T(8,128)(2,1)S(1)} %add_convert_fusion.3), channel_id=1, source_target_pairs={{0,192},{64,0},{128,64},{192,128},{1,193},{65,1},{129,65},{193,129... | collective-permute-start | bytes 1572872 | tf_op jit(solution)/shard_map/ppermute | solution.py:14
  419.4 36.5 %copy-start.1 = (bf16[1,8,128,512]{3,2,1,0:T(8,128)(2,1)S(1)}, bf16[1,8,128,512]{3,2,1,0:T(8,128)(2,1)}, u32[]{:S(2)}) copy-start(bf16[1,8,128,512]{3,2,1,0:T(8,128)(2,1)} %param.16) | copy-start | bytes 3145732
Sparse Core Ops, SparseCore 0:
  340.3 41.4 reduce-scatter.3
  384.5 31.3 reduce-scatter.5
  418.4 34.9 reduce-scatter.7
where the time goes:
time: 471 us; the launch traced here: 463 us
  local copies, waits for them, and re-layouts  161 us (34%)
  blocking collectives  99.4 us (21%)
  other arithmetic  78.7 us (17%)
  starting transfers between devices  50.5 us (11%)
  waiting for transfers between devices  31.8 us (7%)
  matrix products  26.8 us (6%)
  between operations  14.8 us (3%)
    unnamed x60, local copies, waits for them, and re-layouts  51.9 us
    unnamed x3, other arithmetic  46.2 us
    all_to_all x1, blocking collectives, shards(): lax.all_to_all(chosen(w_gate), 'expert', split_axis=0, concat_axis=1, til...  30.8 us
    all_to_all x1, blocking collectives, shards(): lax.all_to_all(tok_rows, 'expert', split_axis=0, concat_axis=0, tiled=True)  28 us
    all_to_all x1, blocking collectives, shards(): lax.all_to_all(chosen(w_down), 'expert', split_axis=0, concat_axis=1, til...  27.6 us
    convert_element_type x1, local copies, waits for them, and re-layouts, shards(): sum_gate.astype(jnp.bfloat16)  18.5 us
    convert_element_type x1, local copies, waits for them, and re-layouts, shards(): sum_up.astype(jnp.bfloat16)  18.5 us
    convert_element_type x1, local copies, waits for them, and re-layouts, shards(): sum_down.astype(jnp.bfloat16)  18.5 us
  transfers between devices with their start and end apart: 11, of which 4 were waited for; matrix products, arithmetic and copies ran while one was open for 44% of the time, Pallas kernels for 0%

commit v1 on v0

v1 whole, which is shorter than its diff:
```python
import jax
import jax.numpy as jnp
from jax import lax
from jax.experimental import pallas as pl
from jax.experimental.pallas import tpu as pltpu
from jax.sharding import PartitionSpec as P

EXPERTS = 8
CAP = 20
SLOTS = 16
ROWS = SLOTS * CAP
BACK = 24
TOK = 128
D = 2048
FF = 512
HALF = 256
PART = 128
BF = jnp.bfloat16
F32 = jnp.float32
MIB = 1 << 20


def place(zh, c, k, b):
    return (2 * zh + c) * 4 + 2 * k + b


SPOTS = [(zh, c, k, b) for zh in range(2) for c in range(2) for k in range(2) for b in range(2)]
TURN = [(place(zh, c, k, b), place(zh, k, c, b)) for zh, c, k, b in SPOTS]
CORES = [(place(zh, c, k, b), place(zh, 1 - c, k, b)) for zh, c, k, b in SPOTS]
NEAR = [(place(zh, c, k, b), place(zh, c, k, 1 - b)) for zh, c, k, b in SPOTS]
CROSS = [(place(zh, c, k, b), place(zh, k, 1 - c, b)) for zh, c, k, b in SPOTS]
BEHIND = [(place(zh, c, k, b), ((2 * zh + k - 1) % 4) * 4 + 2 * c + b) for zh, c, k, b in SPOTS]


def move(x, pairs):
    return lax.ppermute(x, ("pipe", "dp"), pairs)


def spread(x):
    return lax.all_to_all(x, "expert", split_axis=0, concat_axis=0, tiled=True)


def mm(a, b, dims=((1,), (0,))):
    return lax.dot_general(a, b, (dims, ((), ())), preferred_element_type=F32)


def count(shape, dim):
    return lax.broadcasted_iota(jnp.int32, shape, dim).astype(F32)


def split_by(index, size):
    block = jnp.floor((index + 0.5) * (1.0 / size))
    return block, index - block * size


def vmem(limit, **kw):
    return pltpu.CompilerParams(vmem_limit_bytes=limit * MIB, **kw)


def pick_kernel(info, gate, up, down, ogate, oup, odown, out, held, sem_in, sem_out):
    half = info[SLOTS]
    lanes = pl.ds(pl.multiple_of(half * HALF, HALF), HALF)

    def fetch(refs):
        copies = [
            pltpu.make_async_copy(ref.at[0, :, :, lanes], held.at[n], sem_in.at[n])
            for n, ref in enumerate(refs)
        ]
        for copy in copies:
            copy.start()
        for copy in copies:
            copy.wait()

    @pl.when(info[SLOTS + 1] == 1)
    def _():
        fetch((gate, up, down))

    @pl.when(info[SLOTS + 1] == 0)
    def _():
        fetch((ogate, oup, odown))

    copies = [
        pltpu.make_async_copy(
            held.at[n, info[slot]],
            out.at[slot, pl.ds(n * PART, PART), :],
            sem_out.at[slot * 3 + n],
        )
        for slot in range(SLOTS)
        for n in range(3)
    ]
    for copy in copies:
        copy.start()
    for copy in copies:
        copy.wait()


def pick_weights(info, mine, others):
    anywhere = pl.BlockSpec(memory_space=pl.ANY)
    return pl.pallas_call(
        pick_kernel,
        out_shape=jax.ShapeDtypeStruct((SLOTS, 3 * PART, HALF), BF),
        in_specs=[pl.BlockSpec(memory_space=pltpu.SMEM)] + [anywhere] * 6,
        out_specs=anywhere,
        scratch_shapes=[
            pltpu.VMEM((3, EXPERTS, PART, HALF), BF),
            pltpu.SemaphoreType.DMA((3,)),
            pltpu.SemaphoreType.DMA((3 * SLOTS,)),
        ],
        compiler_params=vmem(16),
        cost_estimate=pl.CostEstimate(flops=0, bytes_accessed=5 * MIB, transcendentals=0),
    )(info, *mine, *others)


def seats(notes, size, caps):
    rows = SLOTS * size
    slot, at = split_by(count((rows, 1), 0), size)
    second, rank = split_by(at, caps)
    first = notes[0:1, :] == slot
    other = notes[1:2, :] == slot
    held = jnp.where(first | other, 1.0, 0.0)
    before = jnp.where(count((TOK, TOK), 0) < count((TOK, TOK), 1), 1.0, 0.0)
    taken = mm(held.astype(BF), before.astype(BF))
    seat = jnp.where(taken == rank, held, 0.0)
    return seat, first, second


def pack_kernel(notes_ref, x_ref, g_ref, out_ref):
    notes = notes_ref[...].astype(F32)
    seat, first, second = seats(notes, 2 * CAP, CAP)
    weight = jnp.where(first, notes[2:3, :], notes[3:4, :])
    pick_x = jnp.where(second == 0.0, seat, 0.0).astype(BF)
    pick_g = jnp.where(second == 1.0, seat * weight, 0.0).astype(BF)
    for n in range(4):
        at = pl.ds(n * 512, 512)
        out_ref[:, at] = (mm(pick_x, x_ref[:, at]) + mm(pick_g, g_ref[:, at])).astype(BF)


def pack_rows(notes, x, g):
    return pl.pallas_call(
        pack_kernel,
        out_shape=jax.ShapeDtypeStruct((2 * ROWS, D), BF),
        compiler_params=vmem(32),
        cost_estimate=pl.CostEstimate(
            flops=4 * 2 * ROWS * TOK * D, bytes_accessed=4 * MIB, transcendentals=0
        ),
    )(notes, x, g)


def expert_kernel(
    rows_ref, own_ref, oth_ref, back_ref, x_ref, s_ref, hid_ref, gu_ref, wg, wu, wd, sem
):
    stacks = (wg, wu, wd)
    for n, stack in enumerate(stacks):
        for src in range(SLOTS):
            for side, ref in enumerate((own_ref, oth_ref)):
                pltpu.make_async_copy(
                    ref.at[src, pl.ds(n * PART, PART), :],
                    stack.at[pl.ds(src * PART, PART), pl.ds(side * HALF, HALF)],
                    sem.at[n],
                ).start()
    source = count((1, 2 * ROWS), 1)
    block, at = split_by(count((ROWS, 1), 0), CAP)
    take_x = jnp.where(source == block * (2 * CAP) + at, 1.0, 0.0).astype(BF)
    take_s = jnp.where(source == block * (2 * CAP) + CAP + at, 1.0, 0.0).astype(BF)
    for n in range(4):
        cols = pl.ds(n * 512, 512)
        x_ref[:, cols] = mm(take_x, rows_ref[:, cols]).astype(BF)
        s_ref[:, cols] = mm(take_s, rows_ref[:, cols]).astype(BF)
    for n, stack in enumerate(stacks):
        pltpu.make_async_copy(stack, stack, sem.at[n]).wait()
    gate_pre = mm(x_ref[...], wg[...])
    up_pre = mm(x_ref[...], wu[...])
    hidden_grad = mm(s_ref[...], wd[...])
    sigma = jax.nn.sigmoid(gate_pre)
    active = gate_pre * sigma
    hidden = (active * up_pre).astype(BF)
    gate_grad = (hidden_grad * up_pre * sigma * (1.0 + gate_pre * (1.0 - sigma))).astype(BF)
    up_grad = (hidden_grad * active).astype(BF)
    prob = jnp.sum(hidden.astype(F32) * hidden_grad, axis=1, keepdims=True)
    hid_ref[...] = hidden
    gu_ref[:, 0:FF] = gate_grad
    gu_ref[:, FF : 2 * FF] = up_grad
    row = count((1, ROWS), 1)
    row_block, _ = split_by(row, CAP)
    to_block, to_at = split_by(count((SLOTS * BACK, 1), 0), BACK)
    lay = jnp.where((to_at < CAP) & (row == to_block * CAP + to_at), 1.0, 0.0).astype(BF)
    lay_prob = jnp.where((to_at == CAP) & (row_block == to_block), 1.0, 0.0).astype(BF)
    prob_wide = jnp.where(count((1, PART), 1) == at, prob, 0.0).astype(BF)
    prob_rows = mm(lay_prob, prob_wide)
    dims = ((1,), (1,))
    for n in range(8):
        cols = pl.ds(n * 256, 256)
        grad = mm(gate_grad, wg[cols, :], dims) + mm(up_grad, wu[cols, :], dims)
        laid = mm(lay, grad.astype(BF))
        if n == 0:
            back_ref[:, 0:PART] = (laid[:, 0:PART] + prob_rows).astype(BF)
            back_ref[:, PART:256] = laid[:, PART:256].astype(BF)
        else:
            back_ref[:, cols] = laid.astype(BF)


def expert_rows(rows, own, oth):
    whole = pl.BlockSpec(memory_space=pltpu.VMEM)
    anywhere = pl.BlockSpec(memory_space=pl.ANY)
    return pl.pallas_call(
        expert_kernel,
        out_shape=[
            jax.ShapeDtypeStruct((SLOTS * BACK, D), BF),
            jax.ShapeDtypeStruct((ROWS, D), BF),
            jax.ShapeDtypeStruct((ROWS, D), BF),
            jax.ShapeDtypeStruct((ROWS, FF), BF),
            jax.ShapeDtypeStruct((ROWS, 2 * FF), BF),
        ],
        in_specs=[whole, anywhere, anywhere],
        out_specs=[whole] * 5,
        scratch_shapes=[
            pltpu.VMEM((D, FF), BF),
            pltpu.VMEM((D, FF), BF),
            pltpu.VMEM((D, FF), BF),
            pltpu.SemaphoreType.DMA((3,)),
        ],
        compiler_params=vmem(48),
        cost_estimate=pl.CostEstimate(
            flops=16 * ROWS * D * FF, bytes_accessed=14 * MIB, transcendentals=ROWS * FF
        ),
    )(rows, own, oth)


def sums_kernel(x_ref, s_ref, hid_ref, gu_ref, own_ref, oth_ref):
    dims = ((0,), (0,))
    for n in range(8):
        cols = pl.ds(n * 256, 256)
        both = mm(x_ref[:, cols], gu_ref[...], dims).astype(BF)
        down = mm(s_ref[:, cols], hid_ref[...], dims).astype(BF)
        for part in range(2):
            rows = slice(part * PART, (part + 1) * PART)
            for side, ref in enumerate((own_ref, oth_ref)):
                lanes = slice(side * HALF, (side + 1) * HALF)
                ups = slice(FF + side * HALF, FF + (side + 1) * HALF)
                ref[2 * n + part, 0:PART, :] = both[rows, lanes]
                ref[2 * n + part, PART : 2 * PART, :] = both[rows, ups]
                ref[2 * n + part, 2 * PART : 3 * PART, :] = down[rows, lanes]


def weight_sums(x, scaled, hidden, grads):
    shape = jax.ShapeDtypeStruct((SLOTS, 3 * PART, HALF), BF)
    return pl.pallas_call(
        sums_kernel,
        out_shape=[shape, shape],
        compiler_params=vmem(48),
        cost_estimate=pl.CostEstimate(
            flops=6 * ROWS * D * FF, bytes_accessed=9 * MIB, transcendentals=0
        ),
    )(x, scaled, hidden, grads)


def join_kernel(notes_ref, back_ref, g_ref, sect_ref, route_ref):
    notes = notes_ref[...].astype(F32)
    rows = SLOTS * BACK
    seat, first, second = seats(notes, BACK, CAP)
    seat = jnp.where(second == 0.0, seat, 0.0)
    slot, at = split_by(count((rows, 1), 0), BACK)
    to_prob = jnp.where(count((1, rows), 1) == slot * BACK + CAP, 1.0, 0.0).astype(BF)
    probs = mm(to_prob, back_ref[:, 0:PART])
    prob = jnp.sum(jnp.where(count((1, PART), 1) == at, probs, 0.0), axis=1, keepdims=True)
    share = seat * prob
    route_first = jnp.sum(jnp.where(first, share, 0.0), axis=0, keepdims=True)
    route_second = jnp.sum(jnp.where(first, 0.0, share), axis=0, keepdims=True)
    line = lax.broadcasted_iota(jnp.int32, (8, TOK), 0)
    route = jnp.where(
        line == 0,
        route_first / notes[2:3, :],
        jnp.where(line == 1, route_second / notes[3:4, :], 0.0),
    )
    route_ref[...] = route.astype(BF)
    pick = seat.astype(BF)
    for n in range(4):
        cols = pl.ds(n * 512, 512)
        branch = mm(pick, back_ref[:, cols], ((0,), (0,))).astype(BF).astype(F32)
        sect_ref[:, cols] = (g_ref[:, cols].astype(F32) + branch).astype(BF)


def join_rows(notes, back, g):
    return pl.pallas_call(
        join_kernel,
        out_shape=[jax.ShapeDtypeStruct((TOK, D), BF), jax.ShapeDtypeStruct((8, TOK), BF)],
        compiler_params=vmem(32),
        cost_estimate=pl.CostEstimate(
            flops=2 * SLOTS * BACK * TOK * D, bytes_accessed=3 * MIB, transcendentals=0
        ),
    )(notes, back, g)


def merge_kernel(info, got_ref, keep_ref, send_ref, keep_sum, send_sum):
    side = info[EXPERTS]
    mine = pl.ds(pl.multiple_of(side * 32, 32), 32)
    theirs = pl.ds(pl.multiple_of((1 - side) * 32, 32), 32)
    for sums, rows in ((keep_sum, mine), (send_sum, theirs)):
        for e in range(EXPERTS):
            sums[e] = got_ref[e, rows, :].astype(F32)
        for r in range(EXPERTS):
            e = info[r]
            sums[e] = sums[e] + got_ref[EXPERTS + r, rows, :].astype(F32)
    keep_ref[0, 0] = keep_sum[...].astype(BF)
    send_ref[0, 0] = send_sum[...].astype(BF)


def merge_slots(info, got):
    out = jax.ShapeDtypeStruct((3, 2, EXPERTS, 32, HALF), BF)
    block = pl.BlockSpec((1, 1, EXPERTS, 32, HALF), lambda n, q, info: (n, q, 0, 0, 0))
    return pl.pallas_call(
        merge_kernel,
        out_shape=[out, out],
        grid_spec=pltpu.PrefetchScalarGridSpec(
            num_scalar_prefetch=1,
            grid=(3, 2),
            in_specs=[pl.BlockSpec((SLOTS, 64, HALF), lambda n, q, info: (0, 2 * n + q, 0))],
            out_specs=[block, block],
            scratch_shapes=[pltpu.VMEM((EXPERTS, 32, HALF), F32)] * 2,
        ),
        compiler_params=vmem(32),
        cost_estimate=pl.CostEstimate(
            flops=SLOTS * 3 * PART * HALF, bytes_accessed=5 * MIB, transcendentals=0
        ),
    )(info, got)


def shards(tokens_in, grad_out, route_weight, slot_of, replica_of, w_gate, w_up, w_down):
    pipe, dp = lax.axis_index("pipe"), lax.axis_index("dp")
    core, side, near = pipe % 2, dp // 2, dp % 2
    mine = core == side

    weights = (w_gate, w_up, w_down)
    others = tuple(move(w, CORES) for w in weights)
    replicas = jnp.where(mine, replica_of[0], move(replica_of[0], CORES))

    notes = jnp.concatenate(
        [slot_of[0].T.astype(BF), route_weight[0].T, jnp.zeros((4, TOK), BF)], axis=0
    )
    notes = move(notes, TURN)
    x = move(tokens_in[0], TURN)
    g = move(grad_out[0], TURN)

    info = jnp.concatenate(
        [
            jnp.arange(EXPERTS, dtype=jnp.int32),
            replicas,
            jnp.stack([core, mine.astype(jnp.int32)]).astype(jnp.int32),
        ]
    )
    own = spread(pick_weights(info, weights, others))
    oth = move(own, CORES)

    rows = pack_rows(notes, x, g)
    rows = spread(rows.reshape(SLOTS, 2 * CAP, D)).reshape(2 * ROWS, D)
    back, xs, scaled, hidden, grads = expert_rows(rows, own, oth)
    back = spread(back.reshape(SLOTS, BACK, D)).reshape(SLOTS * BACK, D)
    sum_own, sum_oth = weight_sums(xs, scaled, hidden, grads)
    sum_oth = move(sum_oth, CORES)
    sums = (sum_own.astype(F32) + sum_oth.astype(F32)).astype(BF)

    sect, route = join_rows(notes, back, g)
    grad_in = move(sect, BEHIND)
    route = move(route, TURN)[0:2].T

    got = spread(sums)
    keep, send = merge_slots(jnp.concatenate([replicas, near[None].astype(jnp.int32)]), got)
    send = move(send, NEAR)
    total = ((keep.astype(F32) + send.astype(F32)) * (8192.0**-0.5)).astype(BF)
    first = move(lax.dynamic_index_in_dim(total, core, 1, keepdims=False), TURN)
    second = move(lax.dynamic_index_in_dim(total, 1 - core, 1, keepdims=False), CROSS)
    low = jnp.where(side == 0, first, second)
    high = jnp.where(side == 0, second, first)
    final = jnp.concatenate([low, high], axis=-1)
    return (grad_in[None], route[None], final[0][None], final[1][None], final[2][None])


def solution(mesh):
    return jax.shard_map(
        shards,
        mesh=mesh,
        in_specs=(
            P("pipe", ("expert", "dp"), None),
            P("pipe", ("expert", "dp"), None),
            P("pipe", ("expert", "dp"), None),
            P("pipe", ("expert", "dp"), None),
            P("pipe", None),
            P("pipe", None, "expert", None),
            P("pipe", None, "expert", None),
            P("pipe", None, "expert", None),
        ),
        out_specs=(
            P("pipe", ("expert", "dp"), None),
            P("pipe", ("expert", "dp"), None),
            P("pipe", None, ("expert", "dp"), None),
            P("pipe", None, ("expert", "dp"), None),
            P("pipe", None, ("expert", "dp"), None),
        ),
        check_vma=False,
    )
```

time: 471 us -> 264 us (0.56); the launches traced: 463 us -> 263 us
  local copies, waits for them, and re-layouts: 161 us -> 9.92 us
  other arithmetic: 78.7 us -> 6.22 us
  waiting for transfers between devices: 31.8 us -> 70.6 us
  Pallas kernels: 0 us -> 30.7 us
  matrix products: 26.8 us -> 0 us
  starting transfers between devices: 50.5 us -> 35.7 us
  between operations: 14.8 us -> 0.87 us
  blocking collectives: 99.4 us -> 110 us
    convert_element_type x7 -> x0, local copies, waits for them, and re-layouts: 59 us -> none  [the longest x1 18.5 us: shards(): sum_gate.astype(jnp.bfloat16)]
    ppermute x1 -> x14, waiting for transfers between devices: 1.9 us -> 53.8 us  [move(): return lax.ppermute(x, ('pipe', 'dp'), pairs)]
    unnamed x3 -> x0, other arithmetic: 46.2 us -> none
    unnamed x60 -> x27, local copies, waits for them, and re-layouts: 51.9 us -> 9.25 us
    all_to_all x7 -> x1, starting transfers between devices: 42.3 us -> 4.4 us  [spread(): return lax.all_to_all(x, 'expert', split_axis=0, concat_axis=0, tiled=True)]
    pallas_call x0 -> x6, Pallas kernels: none -> 30.7 us  [the longest x1 12.4 us: expert_rows(): pl.pallas_call(expert_kernel, out_shape=[jax.ShapeDtypeStruct((SLOTS * BA...]
    dot_general x9 -> x0, matrix products: 26.8 us -> none  [the longest x1 4.02 us: expert_rows(): jnp.dot(gate_grad, gate_w.T, preferred_element_type=jnp.float32)]
    ppermute x1 -> x14, starting transfers between devices: 8.04 us -> 31.2 us  [move(): return lax.ppermute(x, ('pipe', 'dp'), pairs)]
  transfers between devices with their start and end apart: 11 -> 15, of which waited for: 4 -> 5; matrix products, arithmetic and copies ran while one was open for 44% -> 1% of each run, Pallas kernels for 0% -> 3%
where the time goes in v1:
time: 264 us; the launch traced here: 263 us
  blocking collectives  110 us (42%)
  waiting for transfers between devices  70.6 us (27%)
  starting transfers between devices  35.7 us (14%)
  Pallas kernels  30.7 us (12%)
  local copies, waits for them, and re-layouts  9.92 us (4%)
  other arithmetic  6.22 us (2%)
    all_to_all x3, blocking collectives, spread(): return lax.all_to_all(x, 'expert', split_axis=0, concat_axis=0, tiled=True)  110 us
    ppermute x14, waiting for transfers between devices, move(): return lax.ppermute(x, ('pipe', 'dp'), pairs)  53.8 us
    ppermute x14, starting transfers between devices, move(): return lax.ppermute(x, ('pipe', 'dp'), pairs)  31.2 us
    all_to_all x1, waiting for transfers between devices, spread(): return lax.all_to_all(x, 'expert', split_axis=0, concat_axis=0, tiled=True)  16.8 us
    pallas_call x1, Pallas kernels, expert_rows(): pl.pallas_call(expert_kernel, out_shape=[jax.ShapeDtypeStruct((SLOTS * BA...  12.4 us
    unnamed x27, local copies, waits for them, and re-layouts  9.25 us
    pallas_call x1, Pallas kernels, weight_sums(): pl.pallas_call(sums_kernel, out_shape=[shape, shape], compiler_params=vme...  6.11 us
    pallas_call x1, Pallas kernels, pick_weights(): pl.pallas_call(pick_kernel, out_shape=jax.ShapeDtypeStruct((SLOTS, 3 * PA...  5.28 us
  transfers between devices with their start and end apart: 15, of which 5 were waited for; matrix products, arithmetic and copies ran while one was open for 1% of the time, Pallas kernels for 3%

profile of v1, /device:TPU:1, one launch (start us, length us, event | category | flops | bytes accessed | tf_op | source)
XLA Modules:
  0.0 263.5 jit_solution(3133854290161051234)
XLA Ops:
  0.6 3.3 %collective-permute-start.4 = (bf16[1,8,128,512]{3,2,1,0:T(8,128)(2,1)}, bf16[1,8,128,512]{3,2,1,0:T(8,128)(2,1)S(1)}, u32[]{:S(2)}, u32[]{:S(2)}) collective-permute-start(bf16[1,8,128,512]{3,2,1,0:T(8,128)(2,1)} %gate.1), channel_id=1, source_target_pairs={{0,64},{1,65},{2,66},{3,67},{64,0},{65,1},{66,2},{67,3},{128,192},... | collective-permute-start | bytes 3145736 | tf_op jit(solution)/shard_map/ppermute | solution.py:36
  4.6 4.9 %collective-permute-done.3 = s32[8]{0:T(128)S(1)} collective-permute-done((s32[8]{0:T(128)}, s32[8]{0:T(128)S(1)}, u32[]{:S(2)}, u32[]{:S(2)}) %collective-permute-start.3) | collective-permute-done | bytes 64 | tf_op jit(solution)/shard_map/ppermute | solution.py:36
  10.2 1.2 copy-done.3
  11.4 1.2 copy-done.4
  12.7 1.2 copy-done.5
  13.9 5.3 %shard_map.120 = bf16[16,384,256]{2,1,0:T(8,128)(2,1)S(1)} custom-call(s32[18]{0:T(128)S(1)} %pad_add_fusion.info, bf16[1,8,128,512]{3,2,1,0:T(8,128)(2,1)S(1)} %copy-done.3, bf16[1,8,128,512]{3,2,1,0:T(8,128)(2,1)S(1)} %copy-done.4, bf16[1,8,128,512]{3,2,1,0:T(8,128)(2,1)S(1)} %copy-done.5, bf16[1,8,128,512]{3,2,1,0:T(8,128)(2,1)S(1)} %collective-permute-done.4.ogate, ...), custom_call_target="tpu_custom_call" | custom-call | bytes 5242880 | tf_op jit(solution)/shard_map/pallas_call | solution.py:99
  19.2 43.8 %all_to_all.20.own_ref = bf16[16,384,256]{2,1,0:T(8,128)(2,1)S(1)} all-to-all(bf16[16,384,256]{2,1,0:T(8,128)(2,1)S(1)} %shard_map.120), channel_id=1, replica_groups=mesh['pipe'=4,'expert'=16,'dp'=4] {'expert'}, dimensions={0} | all-to-all | bytes 6291456 | tf_op jit(solution)/shard_map/all_to_all | solution.py:40
  63.0 1.8 collective-permute-start.7
  64.8 4.8 %collective-permute-start.1 = (bf16[128,2048]{1,0:T(8,128)(2,1)S(1)}, bf16[128,2048]{1,0:T(8,128)(2,1)S(1)}, u32[]{:S(2)}, u32[]{:S(2)}) collective-permute-start(bf16[128,2048]{1,0:T(8,128)(2,1)S(1)} %bitcast.33), channel_id=1, source_target_pairs={{0,0},{1,1},{2,64},{3,65},{64,2},{65,3},{66,66},{67,67},{128,128},... | collective-permute-start | bytes 1572872 | tf_op jit(solution)/shard_map/ppermute | solution.py:36
  69.6 1.9 collective-permute-start.2
  71.7 4.5 %collective-permute-start = (bf16[8,128]{1,0:T(8,128)(2,1)S(1)}, bf16[8,128]{1,0:T(8,128)(2,1)S(1)}, u32[]{:S(2)}, u32[]{:S(2)}) collective-permute-start(bf16[8,128]{1,0:T(8,128)(2,1)S(1)} %maximum_maximum_fusion), channel_id=1, source_target_pairs={{0,0},{1,1},{2,64},{3,65},{64,2},{65,3},{66,66},{67,67},{128,128},... | collective-permute-start | bytes 6152 | tf_op jit(solution)/shard_map/ppermute | solution.py:36
  76.2 17.1 %collective-permute-done.notes_ref = bf16[8,128]{1,0:T(8,128)(2,1)S(1)} collective-permute-done((bf16[8,128]{1,0:T(8,128)(2,1)S(1)}, bf16[8,128]{1,0:T(8,128)(2,1)S(1)}, u32[]{:S(2)}, u32[]{:S(2)}) %collective-permute-start) | collective-permute-done | bytes 2080 | tf_op jit(solution)/shard_map/ppermute | solution.py:36
  93.3 1.7 shard_map.119
  95.0 23.8 %all_to_all.21 = bf16[16,40,2048]{2,1,0:T(8,128)(2,1)} all-to-all(bf16[16,40,2048]{2,1,0:T(8,128)(2,1)S(1)} %bitcast.27), channel_id=1, replica_groups=mesh['pipe'=4,'expert'=16,'dp'=4] {'expert'}, dimensions={0} | all-to-all | bytes 5242880 | tf_op jit(solution)/shard_map/all_to_all | solution.py:40
  118.8 1.7 copy-done.9
  120.4 12.4 %shard_map.121 = (bf16[384,2048]{1,0:T(8,128)(2,1)S(1)}, bf16[320,2048]{1,0:T(8,128)(2,1)S(1)}, bf16[320,2048]{1,0:T(8,128)(2,1)S(1)}, bf16[320,512]{1,0:T(8,128)(2,1)S(1)}, bf16[320,1024]{1,0:T(8,128)(2,1)S(1)}) custom-call(bf16[640,2048]{1,0:T(8,128)(2,1)} %bitcast.29, bf16[16,384,256]{2,1,0:T(8,128)(2,1)} %copy-done.7, bf16[16,384,256]{2,1,0:T(8,128)(2,1)} %copy-done.9), custom_call_target="tpu_custom_call" | custom-call | flops 5368709120 | bytes 14680064 | tf_op jit(solution)/shard_map/pallas_call | solution.py:205
  132.9 1.1 copy-done.2
  134.0 6.1 %shard_map.123 = (bf16[16,384,256]{2,1,0:T(8,128)(2,1)}, bf16[16,384,256]{2,1,0:T(8,128)(2,1)}) custom-call(bf16[320,2048]{1,0:T(8,128)(2,1)S(1)} %get-tuple-element.19.x_ref, bf16[320,2048]{1,0:T(8,128)(2,1)S(1)} %get-tuple-element.20.s_ref, bf16[320,512]{1,0:T(8,128)(2,1)S(1)} %get-tuple-element.21.hid_ref, bf16[320,1024]{1,0:T(8,128)(2,1)S(1)} %get-tuple-element.22.gu_ref), custom_call_target="tpu_custom_call" | custom-call | flops 2013265920 | bytes 9437184 | tf_op jit(solution)/shard_map/pallas_call | solution.py:247
  140.1 5.9 %collective-permute-done.10 = bf16[16,384,256]{2,1,0:T(8,128)(2,1)S(1)} collective-permute-done((bf16[16,384,256]{2,1,0:T(8,128)(2,1)}, bf16[16,384,256]{2,1,0:T(8,128)(2,1)S(1)}, u32[]{:S(2)}, u32[]{:S(2)}) %collective-permute-start.10) | collective-permute-done | bytes 3145760 | tf_op jit(solution)/shard_map/ppermute | solution.py:36
  146.0 2.9 %add_convert_fusion = bf16[16,384,256]{2,1,0:T(8,128)(2,1)S(1)} fusion(bf16[16,384,256]{2,1,0:T(8,128)(2,1)S(1)} %collective-permute-done.10, bf16[16,384,256]{2,1,0:T(8,128)(2,1)} %get-tuple-element.23), kind=kLoop, calls=%fused_computation | loop fusion | flops 6291456 | bytes 9437184 | tf_op jit(solution)/shard_map/convert_element_type | solution.py:360
  148.9 42.1 %all_to_all.22.got_ref = bf16[16,384,256]{2,1,0:T(8,128)(2,1)S(1)} all-to-all(bf16[16,384,256]{2,1,0:T(8,128)(2,1)S(1)} %add_convert_fusion), channel_id=1, replica_groups=mesh['pipe'=4,'expert'=16,'dp'=4] {'expert'}, dimensions={0} | all-to-all | bytes 6291456 | tf_op jit(solution)/shard_map/all_to_all | solution.py:40
  191.0 4.4 %all-to-all-start.2 = ((bf16[16,24,2048]{2,1,0:T(8,128)(2,1)}), bf16[16,24,2048]{2,1,0:T(8,128)(2,1)}, u32[]{:S(2)}, u32[]{:S(2)}) async-start(bf16[16,24,2048]{2,1,0:T(8,128)(2,1)} %bitcast.28), calls=%async_computation.2 | async-start | bytes 3145728 | tf_op jit(solution)/shard_map/all_to_all | solution.py:40
  195.5 3.1 %shard_map.124 = (bf16[3,2,8,32,256]{4,3,2,1,0:T(8,128)(2,1)S(1)}, bf16[3,2,8,32,256]{4,3,2,1,0:T(8,128)(2,1)}) custom-call(s32[9]{0:T(128)S(1)} %pad_add_fusion.1.info, bf16[16,384,256]{2,1,0:T(8,128)(2,1)S(1)} %all_to_all.22.got_ref), custom_call_target="tpu_custom_call" | custom-call | flops 1572864 | bytes 5242880 | tf_op jit(solution)/shard_map/pallas_call | solution.py:311
  200.0 16.8 %all-to-all-done.2 = bf16[16,24,2048]{2,1,0:T(8,128)(2,1)} async-done(((bf16[16,24,2048]{2,1,0:T(8,128)(2,1)}), bf16[16,24,2048]{2,1,0:T(8,128)(2,1)}, u32[]{:S(2)}, u32[]{:S(2)}) %all-to-all-start.2) | async-done | bytes 1572896 | tf_op jit(solution)/shard_map/all_to_all | solution.py:40
  216.7 1.0 copy-done.1
  217.8 2.1 shard_map.122
  219.9 4.5 %collective-permute-start.8 = (bf16[128,2048]{1,0:T(8,128)(2,1)S(1)}, bf16[128,2048]{1,0:T(8,128)(2,1)S(1)}, u32[]{:S(2)}, u32[]{:S(2)}) collective-permute-start(bf16[128,2048]{1,0:T(8,128)(2,1)S(1)} %get-tuple-element.17), channel_id=1, source_target_pairs={{0,192},{1,193},{2,0},{3,1},{64,194},{65,195},{66,2},{67,3},{128,6... | collective-permute-start | bytes 1572872 | tf_op jit(solution)/shard_map/ppermute | solution.py:36
  224.4 1.5 multiply_convert_fusion
  225.9 2.9 %collective-permute-start.13 = (bf16[3,8,32,256]{3,2,1,0:T(8,128)(2,1)S(1)}, bf16[3,8,32,256]{3,2,1,0:T(8,128)(2,1)S(1)}, u32[]{:S(2)}, u32[]{:S(2)}) collective-permute-start(bf16[3,8,32,256]{3,2,1,0:T(8,128)(2,1)S(1)} %get-tuple-element.32), channel_id=1, source_target_pairs={{0,2},{1,3},{2,66},{3,67},{64,0},{65,1},{66,64},{67,65},{128,130},... | collective-permute-start | bytes 1179656 | tf_op jit(solution)/shard_map/ppermute | solution.py:36
  228.8 1.9 collective-permute-start.12
  230.7 4.5 %collective-permute-start.9 = (bf16[8,128]{1,0:T(8,128)(2,1)S(1)}, bf16[8,128]{1,0:T(8,128)(2,1)S(1)}, u32[]{:S(2)}, u32[]{:S(2)}) collective-permute-start(bf16[8,128]{1,0:T(8,128)(2,1)S(1)} %get-tuple-element.18), channel_id=1, source_target_pairs={{0,0},{1,1},{2,64},{3,65},{64,2},{65,3},{66,66},{67,67},{128,128},... | collective-permute-start | bytes 6152 | tf_op jit(solution)/shard_map/ppermute | solution.py:36
  235.3 25.9 %collective-permute-done.9 = bf16[8,128]{1,0:T(8,128)(2,1)S(1)} collective-permute-done((bf16[8,128]{1,0:T(8,128)(2,1)S(1)}, bf16[8,128]{1,0:T(8,128)(2,1)S(1)}, u32[]{:S(2)}, u32[]{:S(2)}) %collective-permute-start.9) | collective-permute-done | bytes 2080 | tf_op jit(solution)/shard_map/ppermute | solution.py:36
  (48 shorter events, 5.3 us)
Async XLA Ops:
  0.6 9.6 %collective-permute-start.4 = (bf16[1,8,128,512]{3,2,1,0:T(8,128)(2,1)}, bf16[1,8,128,512]{3,2,1,0:T(8,128)(2,1)S(1)}, u32[]{:S(2)}, u32[]{:S(2)}) collective-permute-start(bf16[1,8,128,512]{3,2,1,0:T(8,128)(2,1)} %gate.1), channel_id=1, source_target_pairs={{0,64},{1,65},{2,66},{3,67},{64,0},{65,1},{66,2},{67,3},{128,192},... | collective-permute-start | bytes 3145736 | tf_op jit(solution)/shard_map/ppermute | solution.py:36
  4.0 6.2 %collective-permute-start.5 = (bf16[1,8,128,512]{3,2,1,0:T(8,128)(2,1)}, bf16[1,8,128,512]{3,2,1,0:T(8,128)(2,1)S(1)}, u32[]{:S(2)}, u32[]{:S(2)}) collective-permute-start(bf16[1,8,128,512]{3,2,1,0:T(8,128)(2,1)} %up.1), channel_id=1, source_target_pairs={{0,64},{1,65},{2,66},{3,67},{64,0},{65,1},{66,2},{67,3},{128,192},... | collective-permute-start | bytes 3145736 | tf_op jit(solution)/shard_map/ppermute | solution.py:36
  4.1 6.1 %collective-permute-start.6 = (bf16[1,8,128,512]{3,2,1,0:T(8,128)(2,1)}, bf16[1,8,128,512]{3,2,1,0:T(8,128)(2,1)S(1)}, u32[]{:S(2)}, u32[]{:S(2)}) collective-permute-start(bf16[1,8,128,512]{3,2,1,0:T(8,128)(2,1)} %down.1), channel_id=1, source_target_pairs={{0,64},{1,65},{2,66},{3,67},{64,0},{65,1},{66,2},{67,3},{128,192},... | collective-permute-start | bytes 3145736 | tf_op jit(solution)/shard_map/ppermute | solution.py:36
  4.5 5.0 %collective-permute-start.3 = (s32[8]{0:T(128)}, s32[8]{0:T(128)S(1)}, u32[]{:S(2)}, u32[]{:S(2)}) collective-permute-start(s32[8]{0:T(128)} %bitcast.32), channel_id=1, source_target_pairs={{0,64},{1,65},{2,66},{3,67},{64,0},{65,1},{66,2},{67,3},{128,192},... | collective-permute-start | bytes 104 | tf_op jit(solution)/shard_map/ppermute | solution.py:36
  10.2 1.2 copy-start.3
  11.4 1.2 copy-start.4
  12.7 1.2 copy-start.5
  19.2 45.6 %copy-start.10 = (bf16[1,128,2048]{2,1,0:T(8,128)(2,1)S(1)}, bf16[1,128,2048]{2,1,0:T(8,128)(2,1)}, u32[]{:S(2)}) copy-start(bf16[1,128,2048]{2,1,0:T(8,128)(2,1)} %param.8) | copy-start | bytes 1572868
  19.2 50.4 %copy-start.11 = (bf16[1,128,2048]{2,1,0:T(8,128)(2,1)S(1)}, bf16[1,128,2048]{2,1,0:T(8,128)(2,1)}, u32[]{:S(2)}) copy-start(bf16[1,128,2048]{2,1,0:T(8,128)(2,1)} %param.9) | copy-start | bytes 1572868
  19.2 52.4 %copy-start.12 = (s32[1,128,2]{1,2,0:T(2,128)S(1)}, s32[1,128,2]{1,2,0:T(2,128)}, u32[]{:S(2)}) copy-start(s32[1,128,2]{1,2,0:T(2,128)} %param.11) | copy-start | bytes 3076
  19.2 52.4 %copy-start.8 = (bf16[1,128,2]{1,2,0:T(2,128)(2,1)S(1)}, bf16[1,128,2]{1,2,0:T(2,128)(2,1)}, u32[]{:S(2)}) copy-start(bf16[1,128,2]{1,2,0:T(2,128)(2,1)} %param.10) | copy-start | bytes 1540
  63.0 55.8 %copy-start.7 = (bf16[16,384,256]{2,1,0:T(8,128)(2,1)}, bf16[16,384,256]{2,1,0:T(8,128)(2,1)S(1)}, u32[]{:S(2)}) copy-start(bf16[16,384,256]{2,1,0:T(8,128)(2,1)S(1)} %all_to_all.20.own_ref) | copy-start | bytes 9437188
  63.0 55.8 %collective-permute-start.7 = (bf16[16,384,256]{2,1,0:T(8,128)(2,1)S(1)}, bf16[16,384,256]{2,1,0:T(8,128)(2,1)S(1)}, u32[]{:S(2)}, u32[]{:S(2)}) collective-permute-start(bf16[16,384,256]{2,1,0:T(8,128)(2,1)S(1)} %all_to_all.20.own_ref), channel_id=1, source_target_pairs={{0,64},{1,65},{2,66},{3,67},{64,0},{65,1},{66,2},{67,3},{128,192},... | collective-permute-start | bytes 9437192 | tf_op jit(solution)/shard_map/ppermute | solution.py:36
  64.8 28.5 %collective-permute-start.1 = (bf16[128,2048]{1,0:T(8,128)(2,1)S(1)}, bf16[128,2048]{1,0:T(8,128)(2,1)S(1)}, u32[]{:S(2)}, u32[]{:S(2)}) collective-permute-start(bf16[128,2048]{1,0:T(8,128)(2,1)S(1)} %bitcast.33), channel_id=1, source_target_pairs={{0,0},{1,1},{2,64},{3,65},{64,2},{65,3},{66,66},{67,67},{128,128},... | collective-permute-start | bytes 1572872 | tf_op jit(solution)/shard_map/ppermute | solution.py:36
  69.6 23.7 %collective-permute-start.2 = (bf16[128,2048]{1,0:T(8,128)(2,1)S(1)}, bf16[128,2048]{1,0:T(8,128)(2,1)S(1)}, u32[]{:S(2)}, u32[]{:S(2)}) collective-permute-start(bf16[128,2048]{1,0:T(8,128)(2,1)S(1)} %bitcast.34), channel_id=1, source_target_pairs={{0,0},{1,1},{2,64},{3,65},{64,2},{65,3},{66,66},{67,67},{128,128},... | collective-permute-start | bytes 1572872 | tf_op jit(solution)/shard_map/ppermute | solution.py:36
  71.7 21.6 %collective-permute-start = (bf16[8,128]{1,0:T(8,128)(2,1)S(1)}, bf16[8,128]{1,0:T(8,128)(2,1)S(1)}, u32[]{:S(2)}, u32[]{:S(2)}) collective-permute-start(bf16[8,128]{1,0:T(8,128)(2,1)S(1)} %maximum_maximum_fusion), channel_id=1, source_target_pairs={{0,0},{1,1},{2,64},{3,65},{64,2},{65,3},{66,66},{67,67},{128,128},... | collective-permute-start | bytes 6152 | tf_op jit(solution)/shard_map/ppermute | solution.py:36
  93.3 25.4 %copy-start = (bf16[128,2048]{1,0:T(8,128)(2,1)}, bf16[128,2048]{1,0:T(8,128)(2,1)S(1)}, u32[]{:S(2)}) copy-start(bf16[128,2048]{1,0:T(8,128)(2,1)S(1)} %collective-permute-done.2.g_ref) | copy-start | bytes 1572868
  118.8 1.7 copy-start.9
  132.9 1.2 copy-start.2
  140.1 5.9 %collective-permute-start.10 = (bf16[16,384,256]{2,1,0:T(8,128)(2,1)}, bf16[16,384,256]{2,1,0:T(8,128)(2,1)S(1)}, u32[]{:S(2)}, u32[]{:S(2)}) collective-permute-start(bf16[16,384,256]{2,1,0:T(8,128)(2,1)} %get-tuple-element.24), channel_id=1, source_target_pairs={{0,64},{1,65},{2,66},{3,67},{64,0},{65,1},{66,2},{67,3},{128,192},... | collective-permute-start | bytes 9437192 | tf_op jit(solution)/shard_map/ppermute | solution.py:36
  191.0 25.7 %all-to-all-start.2 = ((bf16[16,24,2048]{2,1,0:T(8,128)(2,1)}), bf16[16,24,2048]{2,1,0:T(8,128)(2,1)}, u32[]{:S(2)}, u32[]{:S(2)}) async-start(bf16[16,24,2048]{2,1,0:T(8,128)(2,1)} %bitcast.28), calls=%async_computation.2 | async-start | bytes 3145728 | tf_op jit(solution)/shard_map/all_to_all | solution.py:40
  198.6 0.9 copy-start.6
  199.5 24.9 %collective-permute-start.11 = (bf16[3,2,8,32,256]{4,3,2,1,0:T(8,128)(2,1)}, bf16[3,2,8,32,256]{4,3,2,1,0:T(8,128)(2,1)S(1)}, u32[]{:S(2)}, u32[]{:S(2)}) collective-permute-start(bf16[3,2,8,32,256]{4,3,2,1,0:T(8,128)(2,1)} %get-tuple-element.26), channel_id=1, source_target_pairs={{0,1},{1,0},{2,3},{3,2},{64,65},{65,64},{66,67},{67,66},{128,129},... | collective-permute-start | bytes 2359304 | tf_op jit(solution)/shard_map/ppermute | solution.py:36
  216.7 1.0 copy-start.1
  219.9 41.9 %collective-permute-start.8 = (bf16[128,2048]{1,0:T(8,128)(2,1)S(1)}, bf16[128,2048]{1,0:T(8,128)(2,1)S(1)}, u32[]{:S(2)}, u32[]{:S(2)}) collective-permute-start(bf16[128,2048]{1,0:T(8,128)(2,1)S(1)} %get-tuple-element.17), channel_id=1, source_target_pairs={{0,192},{1,193},{2,0},{3,1},{64,194},{65,195},{66,2},{67,3},{128,6... | collective-permute-start | bytes 1572872 | tf_op jit(solution)/shard_map/ppermute | solution.py:36
  225.9 35.8 %collective-permute-start.13 = (bf16[3,8,32,256]{3,2,1,0:T(8,128)(2,1)S(1)}, bf16[3,8,32,256]{3,2,1,0:T(8,128)(2,1)S(1)}, u32[]{:S(2)}, u32[]{:S(2)}) collective-permute-start(bf16[3,8,32,256]{3,2,1,0:T(8,128)(2,1)S(1)} %get-tuple-element.32), channel_id=1, source_target_pairs={{0,2},{1,3},{2,66},{3,67},{64,0},{65,1},{66,64},{67,65},{128,130},... | collective-permute-start | bytes 1179656 | tf_op jit(solution)/shard_map/ppermute | solution.py:36
  228.8 32.9 %collective-permute-start.12 = (bf16[3,8,32,256]{3,2,1,0:T(8,128)(2,1)S(1)}, bf16[3,8,32,256]{3,2,1,0:T(8,128)(2,1)S(1)}, u32[]{:S(2)}, u32[]{:S(2)}) collective-permute-start(bf16[3,8,32,256]{3,2,1,0:T(8,128)(2,1)S(1)} %get-tuple-element.33), channel_id=1, source_target_pairs={{0,0},{1,1},{2,64},{3,65},{64,2},{65,3},{66,66},{67,67},{128,128},... | collective-permute-start | bytes 1179656 | tf_op jit(solution)/shard_map/ppermute | solution.py:36
  230.7 30.5 %collective-permute-start.9 = (bf16[8,128]{1,0:T(8,128)(2,1)S(1)}, bf16[8,128]{1,0:T(8,128)(2,1)S(1)}, u32[]{:S(2)}, u32[]{:S(2)}) collective-permute-start(bf16[8,128]{1,0:T(8,128)(2,1)S(1)} %get-tuple-element.18), channel_id=1, source_target_pairs={{0,0},{1,1},{2,64},{3,65},{64,2},{65,3},{66,66},{67,67},{128,128},... | collective-permute-start | bytes 6152 | tf_op jit(solution)/shard_map/ppermute | solution.py:36

commit v2 on v1

v2 whole, which is shorter than its diff:
```python
import functools

import jax
import jax.numpy as jnp
from jax import lax
from jax.experimental import pallas as pl
from jax.experimental.pallas import tpu as pltpu
from jax.sharding import PartitionSpec as P

EXPERTS = 8
CAP = 20
SLOTS = 16
ROWS = SLOTS * CAP
BACK = 24
TOK = 128
D = 2048
FF = 512
PART = 128
BF = jnp.bfloat16
F32 = jnp.float32
MIB = 1 << 20
SCALE = 8192.0**-0.5


def place(zh, c, k, b):
    return (2 * zh + c) * 4 + 2 * k + b


SPOTS = [(zh, c, k, b) for zh in range(2) for c in range(2) for k in range(2) for b in range(2)]
TURN = [(place(zh, c, k, b), place(zh, k, c, b)) for zh, c, k, b in SPOTS]
CORES = [(place(zh, c, k, b), place(zh, 1 - c, k, b)) for zh, c, k, b in SPOTS]
NEAR = [(place(zh, c, k, b), place(zh, c, k, 1 - b)) for zh, c, k, b in SPOTS]
OWNER = [
    [(place(zh, c, k, b), (2 * zh + k) * 4 + ((2 * c + b) ^ j)) for zh, c, k, b in SPOTS]
    for j in range(4)
]
BEHIND = [(place(zh, c, k, b), ((2 * zh + k - 1) % 4) * 4 + 2 * c + b) for zh, c, k, b in SPOTS]


def move(x, pairs):
    return lax.ppermute(x, ("pipe", "dp"), pairs)


def spread(x):
    return lax.all_to_all(x, "expert", split_axis=0, concat_axis=0, tiled=True)


def mm(a, b, dims=((1,), (0,))):
    return lax.dot_general(a, b, (dims, ((), ())), preferred_element_type=F32)


def count(shape, dim):
    return lax.broadcasted_iota(jnp.int32, shape, dim).astype(F32)


def split_by(index, size):
    block = jnp.floor((index + 0.5) * (1.0 / size))
    return block, index - block * size


def vmem(limit, **kw):
    return pltpu.CompilerParams(vmem_limit_bytes=limit * MIB, **kw)


def pick_kernel(info, gate, up, down, ogate, oup, odown, out, sem):
    lanes = pl.ds(pl.multiple_of(info[SLOTS] * PART, PART), PART)

    def send(refs):
        copies = [
            pltpu.make_async_copy(
                ref.at[info[slot]],
                out.at[slot, pl.ds(n * PART, PART), :],
                sem.at[slot * 3 + n],
            )
            for slot in range(SLOTS)
            for n, ref in enumerate(refs)
        ]
        for copy in copies:
            copy.start()
        for copy in copies:
            copy.wait()

    @pl.when(info[SLOTS + 1] == 1)
    def _():
        send([ref.at[0, :, :, lanes] for ref in (gate, up, down)])

    @pl.when(info[SLOTS + 1] == 0)
    def _():
        send((ogate, oup, odown))


def pick_weights(info, mine, others):
    hbm = pl.BlockSpec(memory_space=pltpu.HBM)
    anywhere = pl.BlockSpec(memory_space=pl.ANY)
    return pl.pallas_call(
        pick_kernel,
        out_shape=jax.ShapeDtypeStruct((SLOTS, 3 * PART, PART), BF),
        in_specs=[pl.BlockSpec(memory_space=pltpu.SMEM)] + [hbm] * 3 + [anywhere] * 3,
        out_specs=anywhere,
        scratch_shapes=[pltpu.SemaphoreType.DMA((3 * SLOTS,))],
        compiler_params=vmem(60),
        cost_estimate=pl.CostEstimate(flops=0, bytes_accessed=4 * MIB, transcendentals=0),
    )(info, *mine, *others)


def seats(notes, size, caps):
    rows = SLOTS * size
    slot, at = split_by(count((rows, 1), 0), size)
    second, rank = split_by(at, caps)
    first = notes[0:1, :] == slot
    other = notes[1:2, :] == slot
    held = jnp.where(first | other, 1.0, 0.0)
    before = jnp.where(count((TOK, TOK), 0) < count((TOK, TOK), 1), 1.0, 0.0)
    taken = mm(held.astype(BF), before.astype(BF))
    seat = jnp.where(taken == rank, held, 0.0)
    return seat, first, second


def pack_kernel(notes_ref, x_ref, g_ref, out_ref):
    notes = notes_ref[...].astype(F32)
    seat, first, second = seats(notes, 2 * CAP, CAP)
    weight = jnp.where(first, notes[2:3, :], notes[3:4, :])
    pick_x = jnp.where(second == 0.0, seat, 0.0).astype(BF)
    pick_g = jnp.where(second == 1.0, seat * weight, 0.0).astype(BF)
    for n in range(4):
        at = pl.ds(n * 512, 512)
        out_ref[:, at] = (mm(pick_x, x_ref[:, at]) + mm(pick_g, g_ref[:, at])).astype(BF)


def pack_rows(notes, x, g):
    return pl.pallas_call(
        pack_kernel,
        out_shape=jax.ShapeDtypeStruct((2 * ROWS, D), BF),
        compiler_params=vmem(32),
        cost_estimate=pl.CostEstimate(
            flops=4 * 2 * ROWS * TOK * D, bytes_accessed=4 * MIB, transcendentals=0
        ),
    )(notes, x, g)


def expert_kernel(
    rows_ref, w0, w1, w2, w3, back_ref, x_ref, s_ref, hid_ref, gu_ref, sg, su, sd, sem
):
    copies = [
        pltpu.make_async_copy(
            ref.at[:, pl.ds(n * PART, PART), :],
            stack.at[:, :, pl.ds(side * PART, PART)],
            sem.at[4 * n + side],
        )
        for n, stack in enumerate((sg, su, sd))
        for side, ref in enumerate((w0, w1, w2, w3))
    ]
    for copy in copies:
        copy.start()
    wg, wu, wd = sg.reshape(D, FF), su.reshape(D, FF), sd.reshape(D, FF)
    source = count((1, 2 * ROWS), 1)
    block, at = split_by(count((ROWS, 1), 0), CAP)
    take_x = jnp.where(source == block * (2 * CAP) + at, 1.0, 0.0).astype(BF)
    take_s = jnp.where(source == block * (2 * CAP) + CAP + at, 1.0, 0.0).astype(BF)
    for n in range(4):
        cols = pl.ds(n * 512, 512)
        x_ref[:, cols] = mm(take_x, rows_ref[:, cols]).astype(BF)
        s_ref[:, cols] = mm(take_s, rows_ref[:, cols]).astype(BF)
    for copy in copies:
        copy.wait()
    gate_pre = mm(x_ref[...], wg[...])
    up_pre = mm(x_ref[...], wu[...])
    hidden_grad = mm(s_ref[...], wd[...])
    sigma = jax.nn.sigmoid(gate_pre)
    active = gate_pre * sigma
    hidden = (active * up_pre).astype(BF)
    gate_grad = (hidden_grad * up_pre * sigma * (1.0 + gate_pre * (1.0 - sigma))).astype(BF)
    up_grad = (hidden_grad * active).astype(BF)
    prob = jnp.sum(hidden.astype(F32) * hidden_grad, axis=1, keepdims=True)
    hid_ref[...] = hidden
    gu_ref[:, 0:FF] = gate_grad
    gu_ref[:, FF : 2 * FF] = up_grad
    row = count((1, ROWS), 1)
    row_block, _ = split_by(row, CAP)
    to_block, to_at = split_by(count((SLOTS * BACK, 1), 0), BACK)
    lay = jnp.where((to_at < CAP) & (row == to_block * CAP + to_at), 1.0, 0.0).astype(BF)
    lay_prob = jnp.where((to_at == CAP) & (row_block == to_block), 1.0, 0.0).astype(BF)
    prob_wide = jnp.where(count((1, PART), 1) == at, prob, 0.0).astype(BF)
    prob_rows = mm(lay_prob, prob_wide)
    dims = ((1,), (1,))
    for n in range(8):
        cols = pl.ds(n * 256, 256)
        grad = mm(gate_grad, wg[cols, :], dims) + mm(up_grad, wu[cols, :], dims)
        laid = mm(lay, grad.astype(BF))
        if n == 0:
            back_ref[:, 0:PART] = (laid[:, 0:PART] + prob_rows).astype(BF)
            back_ref[:, PART:256] = laid[:, PART:256].astype(BF)
        else:
            back_ref[:, cols] = laid.astype(BF)


def expert_rows(rows, quarters):
    whole = pl.BlockSpec(memory_space=pltpu.VMEM)
    anywhere = pl.BlockSpec(memory_space=pl.ANY)
    return pl.pallas_call(
        expert_kernel,
        out_shape=[
            jax.ShapeDtypeStruct((SLOTS * BACK, D), BF),
            jax.ShapeDtypeStruct((ROWS, D), BF),
            jax.ShapeDtypeStruct((ROWS, D), BF),
            jax.ShapeDtypeStruct((ROWS, FF), BF),
            jax.ShapeDtypeStruct((ROWS, 2 * FF), BF),
        ],
        in_specs=[whole] + [anywhere] * 4,
        out_specs=[whole] * 5,
        scratch_shapes=[
            pltpu.VMEM((SLOTS, PART, FF), BF),
            pltpu.VMEM((SLOTS, PART, FF), BF),
            pltpu.VMEM((SLOTS, PART, FF), BF),
            pltpu.SemaphoreType.DMA((12,)),
        ],
        compiler_params=vmem(48),
        cost_estimate=pl.CostEstimate(
            flops=16 * ROWS * D * FF, bytes_accessed=14 * MIB, transcendentals=ROWS * FF
        ),
    )(rows, *quarters)


def sums_kernel(kinds, a_ref, b_ref, own_ref, oth_ref):
    for n in range(8):
        part = mm(a_ref[:, pl.ds(n * 256, 256)], b_ref[...], ((0,), (0,))).astype(BF)
        for piece in range(2):
            rows = slice(piece * PART, (piece + 1) * PART)
            for kind in range(kinds):
                for q in range(4):
                    lanes = slice(kind * FF + q * PART, kind * FF + (q + 1) * PART)
                    ref = own_ref if q < 2 else oth_ref
                    ref[q % 2, 2 * n + piece, kind * PART : (kind + 1) * PART, :] = part[rows, lanes]


def weight_sums(a, b):
    kinds = b.shape[1] // FF
    shape = jax.ShapeDtypeStruct((2, SLOTS, kinds * PART, PART), BF)
    return pl.pallas_call(
        functools.partial(sums_kernel, kinds),
        out_shape=[shape, shape],
        compiler_params=vmem(48),
        cost_estimate=pl.CostEstimate(
            flops=2 * kinds * ROWS * D * FF, bytes_accessed=3 * kinds * MIB, transcendentals=0
        ),
    )(a, b)


def join_kernel(notes_ref, back_ref, g_ref, sect_ref, route_ref):
    notes = notes_ref[...].astype(F32)
    rows = SLOTS * BACK
    seat, first, second = seats(notes, BACK, CAP)
    seat = jnp.where(second == 0.0, seat, 0.0)
    slot, at = split_by(count((rows, 1), 0), BACK)
    to_prob = jnp.where(count((1, rows), 1) == slot * BACK + CAP, 1.0, 0.0).astype(BF)
    probs = mm(to_prob, back_ref[:, 0:PART])
    prob = jnp.sum(jnp.where(count((1, PART), 1) == at, probs, 0.0), axis=1, keepdims=True)
    share = seat * prob
    route_first = jnp.sum(jnp.where(first, share, 0.0), axis=0, keepdims=True)
    route_second = jnp.sum(jnp.where(first, 0.0, share), axis=0, keepdims=True)
    line = lax.broadcasted_iota(jnp.int32, (8, TOK), 0)
    route = jnp.where(
        line == 0,
        route_first / notes[2:3, :],
        jnp.where(line == 1, route_second / notes[3:4, :], 0.0),
    )
    route_ref[...] = route.astype(BF)
    pick = seat.astype(BF)
    for n in range(4):
        cols = pl.ds(n * 512, 512)
        branch = mm(pick, back_ref[:, cols], ((0,), (0,))).astype(BF).astype(F32)
        sect_ref[:, cols] = (g_ref[:, cols].astype(F32) + branch).astype(BF)


def join_rows(notes, back, g):
    return pl.pallas_call(
        join_kernel,
        out_shape=[jax.ShapeDtypeStruct((TOK, D), BF), jax.ShapeDtypeStruct((8, TOK), BF)],
        compiler_params=vmem(32),
        cost_estimate=pl.CostEstimate(
            flops=2 * SLOTS * BACK * TOK * D, bytes_accessed=3 * MIB, transcendentals=0
        ),
    )(notes, back, g)


def merge_kernel(kinds, info, got_ref, out0, out1, out2, out3, sums):
    for j, out in enumerate((out0, out1, out2, out3)):
        quarter = lax.bitwise_xor(info[EXPERTS], j)
        for kind in range(kinds):
            rows = pl.ds(pl.multiple_of(kind * PART + quarter * 32, 32), 32)
            for e in range(EXPERTS):
                sums[e] = got_ref[e, rows, :].astype(F32)
            for r in range(EXPERTS):
                e = info[r]
                sums[e] = sums[e] + got_ref[EXPERTS + r, rows, :].astype(F32)
            out[kind] = (sums[...] * SCALE).astype(BF)


def merge_slots(info, got):
    kinds = got.shape[1] // PART
    out = jax.ShapeDtypeStruct((kinds, EXPERTS, 32, PART), BF)
    return pl.pallas_call(
        functools.partial(merge_kernel, kinds),
        out_shape=[out] * 4,
        in_specs=[pl.BlockSpec(memory_space=pltpu.SMEM), pl.BlockSpec(memory_space=pltpu.VMEM)],
        scratch_shapes=[pltpu.VMEM((EXPERTS, 32, PART), F32)],
        compiler_params=vmem(32),
        cost_estimate=pl.CostEstimate(
            flops=SLOTS * kinds * PART * PART, bytes_accessed=kinds * MIB, transcendentals=0
        ),
    )(info, got)


def owners(parts):
    return tuple(move(part, OWNER[j]) for j, part in enumerate(parts))


def final_kernel(info, *refs):
    downs, pairs, (gate, up, down) = refs[0:4], refs[4:8], refs[8:11]
    for j in range(4):
        lanes = pl.ds(pl.multiple_of(lax.bitwise_xor(info[0], j) * PART, PART), PART)
        down[0, :, :, lanes] = downs[j][0]
        gate[0, :, :, lanes] = pairs[j][0]
        up[0, :, :, lanes] = pairs[j][1]


def finals(info, downs, pairs):
    whole = pl.BlockSpec(memory_space=pltpu.VMEM)
    out = jax.ShapeDtypeStruct((1, EXPERTS, 32, FF), BF)
    return pl.pallas_call(
        final_kernel,
        out_shape=[out] * 3,
        in_specs=[pl.BlockSpec(memory_space=pltpu.SMEM)] + [whole] * 8,
        compiler_params=vmem(32),
        cost_estimate=pl.CostEstimate(flops=0, bytes_accessed=2 * MIB, transcendentals=0),
    )(info, *downs, *pairs)


def add_up(own, others):
    others = move(others, CORES)
    send = (own[1].astype(F32) + others[1].astype(F32)).astype(BF)
    got = move(send, NEAR)
    return (own[0].astype(F32) + others[0].astype(F32) + got.astype(F32)).astype(BF)


def shards(tokens_in, grad_out, route_weight, slot_of, replica_of, w_gate, w_up, w_down):
    pipe, dp = lax.axis_index("pipe"), lax.axis_index("dp")
    core, side, near = pipe % 2, dp // 2, dp % 2
    mine = core == side
    quarter = (2 * core + near).astype(jnp.int32)

    notes = jnp.concatenate(
        [slot_of[0].T.astype(BF), route_weight[0].T, jnp.zeros((4, TOK), BF)], axis=0
    )
    notes = move(notes, TURN)
    x = move(tokens_in[0], TURN)
    g = move(grad_out[0], TURN)

    weights = (w_gate, w_up, w_down)
    asked = (2 * (1 - core) + near) * PART
    others = tuple(move(lax.dynamic_slice_in_dim(w[0], asked, PART, 2), CORES) for w in weights)
    replicas = jnp.where(mine, replica_of[0], move(replica_of[0], CORES))
    info = jnp.concatenate(
        [
            jnp.arange(EXPERTS, dtype=jnp.int32),
            replicas,
            jnp.stack([quarter, mine.astype(jnp.int32)]),
        ]
    )
    first = spread(pick_weights(info, weights, others))
    rows = pack_rows(notes, x, g)
    first, rows = lax.optimization_barrier((first, rows))
    second = move(first, NEAR)
    third, fourth = move(first, CORES), move(second, CORES)

    rows = spread(rows.reshape(SLOTS, 2 * CAP, D)).reshape(2 * ROWS, D)
    back, xs, scaled, hidden, grads = expert_rows(rows, (first, second, third, fourth))
    back = spread(back.reshape(SLOTS, BACK, D)).reshape(SLOTS * BACK, D)
    down = add_up(*weight_sums(scaled, hidden))
    pair = add_up(*weight_sums(xs, grads))

    sect, route = join_rows(notes, back, g)
    grad_in = move(sect, BEHIND)
    route = move(route, TURN)[0:2].T

    info = jnp.concatenate([replicas, quarter[None]])
    downs = owners(merge_slots(info, spread(down)))
    pairs = owners(merge_slots(info, spread(pair)))
    gate, up, down = finals(dp[None].astype(jnp.int32), downs, pairs)
    return (grad_in[None], route[None], gate, up, down)


def solution(mesh):
    return jax.shard_map(
        shards,
        mesh=mesh,
        in_specs=(
            P("pipe", ("expert", "dp"), None),
            P("pipe", ("expert", "dp"), None),
            P("pipe", ("expert", "dp"), None),
            P("pipe", ("expert", "dp"), None),
            P("pipe", None),
            P("pipe", None, "expert", None),
            P("pipe", None, "expert", None),
            P("pipe", None, "expert", None),
        ),
        out_specs=(
            P("pipe", ("expert", "dp"), None),
            P("pipe", ("expert", "dp"), None),
            P("pipe", None, ("expert", "dp"), None),
            P("pipe", None, ("expert", "dp"), None),
            P("pipe", None, ("expert", "dp"), None),
        ),
        check_vma=False,
    )
```

time: 264 us -> 270 us (1.023)
  blocking collectives: 110 us -> 0 us
  Pallas kernels: 30.7 us -> 75.8 us
  waiting for transfers between devices: 70.6 us -> 109 us
  starting transfers between devices: 35.7 us -> 60.9 us
  other arithmetic: 6.22 us -> 10.7 us
    all_to_all x3 -> x0, blocking collectives: 110 us -> none  [spread(): return lax.all_to_all(x, 'expert', split_axis=0, concat_axis=0, tiled=True)]
    pallas_call x1, Pallas kernels: 5.28 us -> 49.9 us  [pick_weights(): pl.pallas_call(pick_kernel, out_shape=jax.ShapeDtypeStruct((SLOTS, 3 * PA...]
    ppermute x14 -> x24, waiting for transfers between devices: 53.8 us -> 93.8 us  [move(): return lax.ppermute(x, ('pipe', 'dp'), pairs)]
    all_to_all x1 -> x5, starting transfers between devices: 4.4 us -> 25.8 us  [spread(): return lax.all_to_all(x, 'expert', split_axis=0, concat_axis=0, tiled=True)]
    convert_element_type x2 -> x4, other arithmetic: 4.38 us -> 9.34 us  [the longest x2 5.35 us: add_up(): (own[0].astype(F32) + others[0].astype(F32) + got.astype(F32)).astype(BF)]
    ppermute x14 -> x24, starting transfers between devices: 31.2 us -> 35.2 us  [move(): return lax.ppermute(x, ('pipe', 'dp'), pairs)]
    dynamic_slice x0 -> x3, local copies, waits for them, and re-layouts: none -> 2.9 us  [shards(): lax.dynamic_slice_in_dim(w[0], asked, PART, 2)]
    unnamed x27 -> x25, local copies, waits for them, and re-layouts: 9.25 us -> 6.91 us
  transfers between devices with their start and end apart: 15 -> 29, of which waited for: 5 -> 10; matrix products, arithmetic and copies ran while one was open for 1% -> 5% of each run, Pallas kernels for 3% -> 3%
where the time goes in v2:
time: 270 us; the launch traced here: 268 us
  waiting for transfers between devices  109 us (40%)
  Pallas kernels  75.8 us (28%)
  starting transfers between devices  60.9 us (23%)
  other arithmetic  10.7 us (4%)
  local copies, waits for them, and re-layouts  10.4 us (4%)
    ppermute x24, waiting for transfers between devices, move(): return lax.ppermute(x, ('pipe', 'dp'), pairs)  93.8 us
    pallas_call x1, Pallas kernels, pick_weights(): pl.pallas_call(pick_kernel, out_shape=jax.ShapeDtypeStruct((SLOTS, 3 * PA...  49.9 us
    ppermute x24, starting transfers between devices, move(): return lax.ppermute(x, ('pipe', 'dp'), pairs)  35.2 us
    all_to_all x5, starting transfers between devices, spread(): return lax.all_to_all(x, 'expert', split_axis=0, concat_axis=0, tiled=True)  25.8 us
    all_to_all x5, waiting for transfers between devices, spread(): return lax.all_to_all(x, 'expert', split_axis=0, concat_axis=0, tiled=True)  15.6 us
    pallas_call x1, Pallas kernels, expert_rows(): pl.pallas_call(expert_kernel, out_shape=[jax.ShapeDtypeStruct((SLOTS * BA...  12.5 us
    unnamed x25, local copies, waits for them, and re-layouts  6.91 us
    pallas_call x2, Pallas kernels, weight_sums(): pl.pallas_call(functools.partial(sums_kernel, kinds), out_shape=[shape, s...  6.12 us
  transfers between devices with their start and end apart: 29, of which 10 were waited for; matrix products, arithmetic and copies ran while one was open for 5% of the time, Pallas kernels for 3%

profile of v2, /device:TPU:1, one launch (start us, length us, event | category | flops | bytes accessed | tf_op | source)
XLA Modules:
  0.0 268.1 jit_solution(14609826654626433759)
XLA Ops:
  0.6 3.3 %collective-permute-start.1 = (s32[8]{0:T(128)}, s32[8]{0:T(128)S(1)}, u32[]{:S(2)}, u32[]{:S(2)}) collective-permute-start(s32[8]{0:T(128)} %bitcast.46), channel_id=1, source_target_pairs={{0,64},{1,65},{2,66},{3,67},{64,0},{65,1},{66,2},{67,3},{128,192},... | collective-permute-start | bytes 104 | tf_op jit(solution)/shard_map/ppermute | solution.py:41
  10.4 49.9 %shard_map.119 = bf16[16,384,128]{2,1,0:T(8,128)(2,1)} custom-call(s32[18]{0:T(128)} %pad_add_fusion.info, bf16[1,8,128,512]{3,2,1,0:T(8,128)(2,1)} %gate.1, bf16[1,8,128,512]{3,2,1,0:T(8,128)(2,1)} %up.1, bf16[1,8,128,512]{3,2,1,0:T(8,128)(2,1)} %down.1, bf16[8,128,128]{2,1,0:T(8,128)(2,1)} %copy-done.7, bf16[8,128,128]{2,1,0:T(8,128)(2,1)} %copy-done.6, ...), custom_call_target="tpu_custom_call" | custom-call | bytes 4194304 | tf_op jit(solution)/shard_map/pallas_call | solution.py:95
  60.4 5.2 %all-to-all-start = ((bf16[16,384,128]{2,1,0:T(8,128)(2,1)}), bf16[16,384,128]{2,1,0:T(8,128)(2,1)}, u32[]{:S(2)}, u32[]{:S(2)}) async-start(bf16[16,384,128]{2,1,0:T(8,128)(2,1)} %shard_map.119), calls=%async_computation | async-start | bytes 3145728 | tf_op jit(solution)/shard_map/all_to_all | solution.py:45
  65.6 5.5 %collective-permute-start.5 = (bf16[128,2048]{1,0:T(8,128)(2,1)S(1)}, bf16[128,2048]{1,0:T(8,128)(2,1)S(1)}, u32[]{:S(2)}, u32[]{:S(2)}) collective-permute-start(bf16[128,2048]{1,0:T(8,128)(2,1)S(1)} %bitcast.47), channel_id=1, source_target_pairs={{0,0},{1,1},{2,64},{3,65},{64,2},{65,3},{66,66},{67,67},{128,128},... | collective-permute-start | bytes 1572872 | tf_op jit(solution)/shard_map/ppermute | solution.py:41
  71.1 1.9 collective-permute-start.6
  73.2 4.5 %collective-permute-start = (bf16[8,128]{1,0:T(8,128)(2,1)S(1)}, bf16[8,128]{1,0:T(8,128)(2,1)S(1)}, u32[]{:S(2)}, u32[]{:S(2)}) collective-permute-start(bf16[8,128]{1,0:T(8,128)(2,1)S(1)} %maximum_maximum_fusion), channel_id=1, source_target_pairs={{0,0},{1,1},{2,64},{3,65},{64,2},{65,3},{66,66},{67,67},{128,128},... | collective-permute-start | bytes 6152 | tf_op jit(solution)/shard_map/ppermute | solution.py:41
  77.8 17.2 %collective-permute-done.notes_ref = bf16[8,128]{1,0:T(8,128)(2,1)S(1)} collective-permute-done((bf16[8,128]{1,0:T(8,128)(2,1)S(1)}, bf16[8,128]{1,0:T(8,128)(2,1)S(1)}, u32[]{:S(2)}, u32[]{:S(2)}) %collective-permute-start) | collective-permute-done | bytes 2080 | tf_op jit(solution)/shard_map/ppermute | solution.py:41
  94.9 3.2 %shard_map.120 = bf16[640,2048]{1,0:T(8,128)(2,1)} custom-call(bf16[8,128]{1,0:T(8,128)(2,1)S(1)} %collective-permute-done.notes_ref, bf16[128,2048]{1,0:T(8,128)(2,1)S(1)} %collective-permute-done.5.x_ref, bf16[128,2048]{1,0:T(8,128)(2,1)S(1)} %collective-permute-done.6.g_ref), custom_call_target="tpu_custom_call" | custom-call | flops 671088640 | bytes 4194304 | tf_op jit(solution)/shard_map/pallas_call | solution.py:131
  98.5 6.9 %all-to-all-start.1 = ((bf16[16,40,2048]{2,1,0:T(8,128)(2,1)}), bf16[16,40,2048]{2,1,0:T(8,128)(2,1)S(1)}, u32[]{:S(2)}, u32[]{:S(2)}) async-start(bf16[16,40,2048]{2,1,0:T(8,128)(2,1)} %bitcast.12), calls=%async_computation.1 | async-start | bytes 5242880 | tf_op jit(solution)/shard_map/all_to_all | solution.py:45
  105.5 23.1 %collective-permute-done.7.w1 = bf16[16,384,128]{2,1,0:T(8,128)(2,1)} collective-permute-done((bf16[16,384,128]{2,1,0:T(8,128)(2,1)}, bf16[16,384,128]{2,1,0:T(8,128)(2,1)}, u32[]{:S(2)}, u32[]{:S(2)}) %collective-permute-start.7) | collective-permute-done | bytes 1572896 | tf_op jit(solution)/shard_map/ppermute | solution.py:41
  128.7 6.2 %all-to-all-done.1 = bf16[16,40,2048]{2,1,0:T(8,128)(2,1)S(1)} async-done(((bf16[16,40,2048]{2,1,0:T(8,128)(2,1)}), bf16[16,40,2048]{2,1,0:T(8,128)(2,1)S(1)}, u32[]{:S(2)}, u32[]{:S(2)}) %all-to-all-start.1) | async-done | bytes 2621472 | tf_op jit(solution)/shard_map/all_to_all | solution.py:45
  136.4 12.5 %shard_map.121 = (bf16[384,2048]{1,0:T(8,128)(2,1)S(1)}, bf16[320,2048]{1,0:T(8,128)(2,1)S(1)}, bf16[320,2048]{1,0:T(8,128)(2,1)S(1)}, bf16[320,512]{1,0:T(8,128)(2,1)S(1)}, bf16[320,1024]{1,0:T(8,128)(2,1)S(1)}) custom-call(bf16[640,2048]{1,0:T(8,128)(2,1)} %bitcast.43, bf16[16,384,128]{2,1,0:T(8,128)(2,1)} %all-to-all-done.w0, ...), custom_call_target="tpu_custom_call" | custom-call | flops 5368709120 | bytes 14680064 | tf_op jit(solution)/shard_map/pallas_call | solution.py:200
  150.1 3.7 %shard_map.125 = (bf16[2,16,256,128]{3,2,1,0:T(8,128)(2,1)S(1)}, bf16[2,16,256,128]{3,2,1,0:T(8,128)(2,1)}) custom-call(bf16[320,2048]{1,0:T(8,128)(2,1)S(1)} %get-tuple-element.42.a_ref, bf16[320,1024]{1,0:T(8,128)(2,1)S(1)} %get-tuple-element.43.b_ref), custom_call_target="tpu_custom_call" | custom-call | flops 1342177280 | bytes 6291456 | tf_op jit(solution)/shard_map/pallas_call | solution.py:239
  155.2 2.4 shard_map.123
  158.1 3.7 %all-to-all-start.2 = ((bf16[16,24,2048]{2,1,0:T(8,128)(2,1)}), bf16[16,24,2048]{2,1,0:T(8,128)(2,1)S(1)}, u32[]{:S(2)}, u32[]{:S(2)}) async-start(bf16[16,24,2048]{2,1,0:T(8,128)(2,1)} %bitcast.42), calls=%async_computation.2 | async-start | bytes 3145728 | tf_op jit(solution)/shard_map/all_to_all | solution.py:45
  161.8 2.8 %fusion.1 = bf16[16,256,128]{2,1,0:T(8,128)(2,1)} fusion(bf16[2,16,256,128]{3,2,1,0:T(8,128)(2,1)} %collective-permute-done.18, bf16[2,16,256,128]{3,2,1,0:T(8,128)(2,1)} %copy-done), kind=kLoop, calls=%fused_computation.3 | loop fusion | flops 2097152 | bytes 3145728 | tf_op jit(solution)/shard_map/convert_element_type | solution.py:341
  166.0 1.6 collective-permute-start.13
  167.6 33.3 %collective-permute-done.13 = bf16[16,128,128]{2,1,0:T(8,128)(2,1)S(1)} collective-permute-done((bf16[16,128,128]{2,1,0:T(8,128)(2,1)S(1)}, bf16[16,128,128]{2,1,0:T(8,128)(2,1)S(1)}, u32[]{:S(2)}, u32[]{:S(2)}) %collective-permute-start.13) | collective-permute-done | bytes 524320 | tf_op jit(solution)/shard_map/ppermute | solution.py:41
  200.9 2.1 fusion.2
  202.9 6.3 %all-to-all-start.3 = ((bf16[16,128,128]{2,1,0:T(8,128)(2,1)}), bf16[16,128,128]{2,1,0:T(8,128)(2,1)S(1)}, u32[]{:S(2)}, u32[]{:S(2)}) async-start(bf16[16,128,128]{2,1,0:T(8,128)(2,1)} %fusion.2), calls=%async_computation.3 | async-start | bytes 1048576 | tf_op jit(solution)/shard_map/all_to_all | solution.py:45
  209.2 3.3 %fusion = bf16[16,256,128]{2,1,0:T(8,128)(2,1)} fusion(bf16[16,256,128]{2,1,0:T(8,128)(2,1)} %collective-permute-done.19, bf16[2,16,256,128]{3,2,1,0:T(8,128)(2,1)} %collective-permute-done.18, bf16[2,16,256,128]{3,2,1,0:T(8,128)(2,1)} %copy-done), kind=kLoop, calls=%fused_computation.1 | loop fusion | flops 3145728 | bytes 4194304 | tf_op jit(solution)/shard_map/convert_element_type | solution.py:343
  212.5 6.9 %all-to-all-done.3.got_ref = bf16[16,128,128]{2,1,0:T(8,128)(2,1)S(1)} async-done(((bf16[16,128,128]{2,1,0:T(8,128)(2,1)}), bf16[16,128,128]{2,1,0:T(8,128)(2,1)S(1)}, u32[]{:S(2)}, u32[]{:S(2)}) %all-to-all-start.3) | async-done | bytes 524320 | tf_op jit(solution)/shard_map/all_to_all | solution.py:45
  220.2 3.7 %all-to-all-start.4 = ((bf16[16,256,128]{2,1,0:T(8,128)(2,1)}), bf16[16,256,128]{2,1,0:T(8,128)(2,1)S(1)}, u32[]{:S(2)}, u32[]{:S(2)}) async-start(bf16[16,256,128]{2,1,0:T(8,128)(2,1)} %fusion), calls=%async_computation.4 | async-start | bytes 2097152 | tf_op jit(solution)/shard_map/all_to_all | solution.py:45
  225.4 3.0 %collective-permute-start.10 = (bf16[128,2048]{1,0:T(8,128)(2,1)}, bf16[128,2048]{1,0:T(8,128)(2,1)S(1)}, u32[]{:S(2)}, u32[]{:S(2)}) collective-permute-start(bf16[128,2048]{1,0:T(8,128)(2,1)} %get-tuple-element.32), channel_id=1, source_target_pairs={{0,192},{1,193},{2,0},{3,1},{64,194},{65,195},{66,2},{67,3},{128,6... | collective-permute-start | bytes 1572872 | tf_op jit(solution)/shard_map/ppermute | solution.py:41
  229.2 3.7 %collective-permute-start.14 = (bf16[1,8,32,128]{3,2,1,0:T(8,128)(2,1)S(1)}, bf16[1,8,32,128]{3,2,1,0:T(8,128)(2,1)S(1)}, u32[]{:S(2)}, u32[]{:S(2)}) collective-permute-start(bf16[1,8,32,128]{3,2,1,0:T(8,128)(2,1)S(1)} %get-tuple-element.38), channel_id=1, source_target_pairs={{0,0},{1,1},{2,64},{3,65},{64,2},{65,3},{66,66},{67,67},{128,128},... | collective-permute-start | bytes 196616 | tf_op jit(solution)/shard_map/ppermute | solution.py:41
  232.9 1.6 collective-permute-start.15
  234.5 1.9 collective-permute-start.11
  236.4 2.4 all-to-all-done.4.got_ref
  239.7 12.8 %collective-permute-done.11 = bf16[8,128]{1,0:T(8,128)(2,1)S(1)} collective-permute-done((bf16[8,128]{1,0:T(8,128)(2,1)S(1)}, bf16[8,128]{1,0:T(8,128)(2,1)S(1)}, u32[]{:S(2)}, u32[]{:S(2)}) %collective-permute-start.11) | collective-permute-done | bytes 2080 | tf_op jit(solution)/shard_map/ppermute | solution.py:41
  252.5 1.9 collective-permute-start.20
  255.7 2.9 %collective-permute-start.23 = (bf16[2,8,32,128]{3,2,1,0:T(8,128)(2,1)S(1)}, bf16[2,8,32,128]{3,2,1,0:T(8,128)(2,1)S(1)}, u32[]{:S(2)}, u32[]{:S(2)}) collective-permute-start(bf16[2,8,32,128]{3,2,1,0:T(8,128)(2,1)S(1)} %get-tuple-element.49), channel_id=1, source_target_pairs={{0,3},{1,2},{2,67},{3,66},{64,1},{65,0},{66,65},{67,64},{128,131},... | collective-permute-start | bytes 393224 | tf_op jit(solution)/shard_map/ppermute | solution.py:41
  259.2 5.6 %collective-permute-done.20.refs_4_ = bf16[2,8,32,128]{3,2,1,0:T(8,128)(2,1)S(1)} collective-permute-done((bf16[2,8,32,128]{3,2,1,0:T(8,128)(2,1)S(1)}, bf16[2,8,32,128]{3,2,1,0:T(8,128)(2,1)S(1)}, u32[]{:S(2)}, u32[]{:S(2)}) %collective-permute-start.20) | collective-permute-done | bytes 131104 | tf_op jit(solution)/shard_map/ppermute | solution.py:41
  (76 shorter events, 22.1 us)
Async XLA Ops:
  0.6 7.1 %collective-permute-start.1 = (s32[8]{0:T(128)}, s32[8]{0:T(128)S(1)}, u32[]{:S(2)}, u32[]{:S(2)}) collective-permute-start(s32[8]{0:T(128)} %bitcast.46), channel_id=1, source_target_pairs={{0,64},{1,65},{2,66},{3,67},{64,0},{65,1},{66,2},{67,3},{128,192},... | collective-permute-start | bytes 104 | tf_op jit(solution)/shard_map/ppermute | solution.py:41
  4.9 4.0 %collective-permute-start.4 = (bf16[8,128,128]{2,1,0:T(8,128)(2,1)S(1)}, bf16[8,128,128]{2,1,0:T(8,128)(2,1)S(1)}, u32[]{:S(2)}, u32[]{:S(2)}) collective-permute-start(bf16[8,128,128]{2,1,0:T(8,128)(2,1)S(1)} %dynamic-slice_bitcast_fusion), channel_id=1, source_target_pairs={{0,64},{1,65},{2,66},{3,67},{64,0},{65,1},{66,2},{67,3},{128,192},... | collective-permute-start | bytes 786440 | tf_op jit(solution)/shard_map/ppermute | solution.py:41
  6.0 2.9 %collective-permute-start.3 = (bf16[8,128,128]{2,1,0:T(8,128)(2,1)S(1)}, bf16[8,128,128]{2,1,0:T(8,128)(2,1)S(1)}, u32[]{:S(2)}, u32[]{:S(2)}) collective-permute-start(bf16[8,128,128]{2,1,0:T(8,128)(2,1)S(1)} %dynamic-slice_bitcast_fusion.1), channel_id=1, source_target_pairs={{0,64},{1,65},{2,66},{3,67},{64,0},{65,1},{66,2},{67,3},{128,192},... | collective-permute-start | bytes 786440 | tf_op jit(solution)/shard_map/ppermute | solution.py:41
  7.6 1.6 collective-permute-start.2
  60.3 10.8 %copy-start.10 = (bf16[1,128,2048]{2,1,0:T(8,128)(2,1)S(1)}, bf16[1,128,2048]{2,1,0:T(8,128)(2,1)}, u32[]{:S(2)}) copy-start(bf16[1,128,2048]{2,1,0:T(8,128)(2,1)} %param.9) | copy-start | bytes 1572868
  60.3 12.8 %copy-start.11 = (s32[1,128,2]{1,2,0:T(2,128)S(1)}, s32[1,128,2]{1,2,0:T(2,128)}, u32[]{:S(2)}) copy-start(s32[1,128,2]{1,2,0:T(2,128)} %param.11) | copy-start | bytes 3076
  60.3 12.8 %copy-start.8 = (bf16[1,128,2]{1,2,0:T(2,128)(2,1)S(1)}, bf16[1,128,2]{1,2,0:T(2,128)(2,1)}, u32[]{:S(2)}) copy-start(bf16[1,128,2]{1,2,0:T(2,128)(2,1)} %param.10) | copy-start | bytes 1540
  60.4 37.8 %all-to-all-start = ((bf16[16,384,128]{2,1,0:T(8,128)(2,1)}), bf16[16,384,128]{2,1,0:T(8,128)(2,1)}, u32[]{:S(2)}, u32[]{:S(2)}) async-start(bf16[16,384,128]{2,1,0:T(8,128)(2,1)} %shard_map.119), calls=%async_computation | async-start | bytes 3145728 | tf_op jit(solution)/shard_map/all_to_all | solution.py:45
  65.6 29.3 %collective-permute-start.5 = (bf16[128,2048]{1,0:T(8,128)(2,1)S(1)}, bf16[128,2048]{1,0:T(8,128)(2,1)S(1)}, u32[]{:S(2)}, u32[]{:S(2)}) collective-permute-start(bf16[128,2048]{1,0:T(8,128)(2,1)S(1)} %bitcast.47), channel_id=1, source_target_pairs={{0,0},{1,1},{2,64},{3,65},{64,2},{65,3},{66,66},{67,67},{128,128},... | collective-permute-start | bytes 1572872 | tf_op jit(solution)/shard_map/ppermute | solution.py:41
  71.1 23.8 %collective-permute-start.6 = (bf16[128,2048]{1,0:T(8,128)(2,1)S(1)}, bf16[128,2048]{1,0:T(8,128)(2,1)S(1)}, u32[]{:S(2)}, u32[]{:S(2)}) collective-permute-start(bf16[128,2048]{1,0:T(8,128)(2,1)S(1)} %bitcast.48), channel_id=1, source_target_pairs={{0,0},{1,1},{2,64},{3,65},{64,2},{65,3},{66,66},{67,67},{128,128},... | collective-permute-start | bytes 1572872 | tf_op jit(solution)/shard_map/ppermute | solution.py:41
  73.2 21.7 %collective-permute-start = (bf16[8,128]{1,0:T(8,128)(2,1)S(1)}, bf16[8,128]{1,0:T(8,128)(2,1)S(1)}, u32[]{:S(2)}, u32[]{:S(2)}) collective-permute-start(bf16[8,128]{1,0:T(8,128)(2,1)S(1)} %maximum_maximum_fusion), channel_id=1, source_target_pairs={{0,0},{1,1},{2,64},{3,65},{64,2},{65,3},{66,66},{67,67},{128,128},... | collective-permute-start | bytes 6152 | tf_op jit(solution)/shard_map/ppermute | solution.py:41
  98.1 30.6 %collective-permute-start.7 = (bf16[16,384,128]{2,1,0:T(8,128)(2,1)}, bf16[16,384,128]{2,1,0:T(8,128)(2,1)}, u32[]{:S(2)}, u32[]{:S(2)}) collective-permute-start(bf16[16,384,128]{2,1,0:T(8,128)(2,1)} %all-to-all-done.w0), channel_id=1, source_target_pairs={{0,1},{1,0},{2,3},{3,2},{64,65},{65,64},{66,67},{67,66},{128,129},... | collective-permute-start | bytes 4718600 | tf_op jit(solution)/shard_map/ppermute | solution.py:41
  98.5 36.4 %all-to-all-start.1 = ((bf16[16,40,2048]{2,1,0:T(8,128)(2,1)}), bf16[16,40,2048]{2,1,0:T(8,128)(2,1)S(1)}, u32[]{:S(2)}, u32[]{:S(2)}) async-start(bf16[16,40,2048]{2,1,0:T(8,128)(2,1)} %bitcast.12), calls=%async_computation.1 | async-start | bytes 5242880 | tf_op jit(solution)/shard_map/all_to_all | solution.py:45
  105.4 23.3 %collective-permute-start.8 = (bf16[16,384,128]{2,1,0:T(8,128)(2,1)}, bf16[16,384,128]{2,1,0:T(8,128)(2,1)}, u32[]{:S(2)}, u32[]{:S(2)}) collective-permute-start(bf16[16,384,128]{2,1,0:T(8,128)(2,1)} %all-to-all-done.w0), channel_id=1, source_target_pairs={{0,64},{1,65},{2,66},{3,67},{64,0},{65,1},{66,2},{67,3},{128,192},... | collective-permute-start | bytes 4718600 | tf_op jit(solution)/shard_map/ppermute | solution.py:41
  128.7 6.3 %collective-permute-start.9 = (bf16[16,384,128]{2,1,0:T(8,128)(2,1)}, bf16[16,384,128]{2,1,0:T(8,128)(2,1)}, u32[]{:S(2)}, u32[]{:S(2)}) collective-permute-start(bf16[16,384,128]{2,1,0:T(8,128)(2,1)} %collective-permute-done.7.w1), channel_id=1, source_target_pairs={{0,64},{1,65},{2,66},{3,67},{64,0},{65,1},{66,2},{67,3},{128,192},... | collective-permute-start | bytes 4718600 | tf_op jit(solution)/shard_map/ppermute | solution.py:41
  155.2 6.6 %collective-permute-start.18 = (bf16[2,16,256,128]{3,2,1,0:T(8,128)(2,1)}, bf16[2,16,256,128]{3,2,1,0:T(8,128)(2,1)}, u32[]{:S(2)}, u32[]{:S(2)}) collective-permute-start(bf16[2,16,256,128]{3,2,1,0:T(8,128)(2,1)} %get-tuple-element.45), channel_id=1, source_target_pairs={{0,64},{1,65},{2,66},{3,67},{64,0},{65,1},{66,2},{67,3},{128,192},... | collective-permute-start | bytes 6291464 | tf_op jit(solution)/shard_map/ppermute | solution.py:41
  157.6 7.2 %collective-permute-start.12 = (bf16[2,16,128,128]{3,2,1,0:T(8,128)(2,1)}, bf16[2,16,128,128]{3,2,1,0:T(8,128)(2,1)}, u32[]{:S(2)}, u32[]{:S(2)}) collective-permute-start(bf16[2,16,128,128]{3,2,1,0:T(8,128)(2,1)} %get-tuple-element.37), channel_id=1, source_target_pairs={{0,64},{1,65},{2,66},{3,67},{64,0},{65,1},{66,2},{67,3},{128,192},... | collective-permute-start | bytes 3145736 | tf_op jit(solution)/shard_map/ppermute | solution.py:41
  158.1 44.8 %all-to-all-start.2 = ((bf16[16,24,2048]{2,1,0:T(8,128)(2,1)}), bf16[16,24,2048]{2,1,0:T(8,128)(2,1)S(1)}, u32[]{:S(2)}, u32[]{:S(2)}) async-start(bf16[16,24,2048]{2,1,0:T(8,128)(2,1)} %bitcast.42), calls=%async_computation.2 | async-start | bytes 3145728 | tf_op jit(solution)/shard_map/all_to_all | solution.py:45
  164.6 44.6 %collective-permute-start.19 = (bf16[16,256,128]{2,1,0:T(8,128)(2,1)}, bf16[16,256,128]{2,1,0:T(8,128)(2,1)}, u32[]{:S(2)}, u32[]{:S(2)}) collective-permute-start(bf16[16,256,128]{2,1,0:T(8,128)(2,1)} %fusion.1), channel_id=1, source_target_pairs={{0,1},{1,0},{2,3},{3,2},{64,65},{65,64},{66,67},{67,66},{128,129},... | collective-permute-start | bytes 3145736 | tf_op jit(solution)/shard_map/ppermute | solution.py:41
  166.0 34.9 %collective-permute-start.13 = (bf16[16,128,128]{2,1,0:T(8,128)(2,1)S(1)}, bf16[16,128,128]{2,1,0:T(8,128)(2,1)S(1)}, u32[]{:S(2)}, u32[]{:S(2)}) collective-permute-start(bf16[16,128,128]{2,1,0:T(8,128)(2,1)S(1)} %fusion.3), channel_id=1, source_target_pairs={{0,1},{1,0},{2,3},{3,2},{64,65},{65,64},{66,67},{67,66},{128,129},... | collective-permute-start | bytes 1572872 | tf_op jit(solution)/shard_map/ppermute | solution.py:41
  202.9 16.5 %all-to-all-start.3 = ((bf16[16,128,128]{2,1,0:T(8,128)(2,1)}), bf16[16,128,128]{2,1,0:T(8,128)(2,1)S(1)}, u32[]{:S(2)}, u32[]{:S(2)}) async-start(bf16[16,128,128]{2,1,0:T(8,128)(2,1)} %fusion.2), calls=%async_computation.3 | async-start | bytes 1048576 | tf_op jit(solution)/shard_map/all_to_all | solution.py:45
  220.2 18.6 %all-to-all-start.4 = ((bf16[16,256,128]{2,1,0:T(8,128)(2,1)}), bf16[16,256,128]{2,1,0:T(8,128)(2,1)S(1)}, u32[]{:S(2)}, u32[]{:S(2)}) async-start(bf16[16,256,128]{2,1,0:T(8,128)(2,1)} %fusion), calls=%async_computation.4 | async-start | bytes 2097152 | tf_op jit(solution)/shard_map/all_to_all | solution.py:45
  225.4 27.2 %collective-permute-start.10 = (bf16[128,2048]{1,0:T(8,128)(2,1)}, bf16[128,2048]{1,0:T(8,128)(2,1)S(1)}, u32[]{:S(2)}, u32[]{:S(2)}) collective-permute-start(bf16[128,2048]{1,0:T(8,128)(2,1)} %get-tuple-element.32), channel_id=1, source_target_pairs={{0,192},{1,193},{2,0},{3,1},{64,194},{65,195},{66,2},{67,3},{128,6... | collective-permute-start | bytes 1572872 | tf_op jit(solution)/shard_map/ppermute | solution.py:41
  229.2 25.3 %collective-permute-start.14 = (bf16[1,8,32,128]{3,2,1,0:T(8,128)(2,1)S(1)}, bf16[1,8,32,128]{3,2,1,0:T(8,128)(2,1)S(1)}, u32[]{:S(2)}, u32[]{:S(2)}) collective-permute-start(bf16[1,8,32,128]{3,2,1,0:T(8,128)(2,1)S(1)} %get-tuple-element.38), channel_id=1, source_target_pairs={{0,0},{1,1},{2,64},{3,65},{64,2},{65,3},{66,66},{67,67},{128,128},... | collective-permute-start | bytes 196616 | tf_op jit(solution)/shard_map/ppermute | solution.py:41
  232.9 22.8 %collective-permute-start.15 = (bf16[1,8,32,128]{3,2,1,0:T(8,128)(2,1)S(1)}, bf16[1,8,32,128]{3,2,1,0:T(8,128)(2,1)S(1)}, u32[]{:S(2)}, u32[]{:S(2)}) collective-permute-start(bf16[1,8,32,128]{3,2,1,0:T(8,128)(2,1)S(1)} %get-tuple-element.39), channel_id=1, source_target_pairs={{0,1},{1,0},{2,65},{3,64},{64,3},{65,2},{66,67},{67,66},{128,129},... | collective-permute-start | bytes 196616 | tf_op jit(solution)/shard_map/ppermute | solution.py:41
  234.5 21.3 %collective-permute-start.16 = (bf16[1,8,32,128]{3,2,1,0:T(8,128)(2,1)S(1)}, bf16[1,8,32,128]{3,2,1,0:T(8,128)(2,1)S(1)}, u32[]{:S(2)}, u32[]{:S(2)}) collective-permute-start(bf16[1,8,32,128]{3,2,1,0:T(8,128)(2,1)S(1)} %get-tuple-element.40), channel_id=1, source_target_pairs={{0,2},{1,3},{2,66},{3,67},{64,0},{65,1},{66,64},{67,65},{128,130},... | collective-permute-start | bytes 196616 | tf_op jit(solution)/shard_map/ppermute | solution.py:41
  234.5 18.1 %collective-permute-start.11 = (bf16[8,128]{1,0:T(8,128)(2,1)S(1)}, bf16[8,128]{1,0:T(8,128)(2,1)S(1)}, u32[]{:S(2)}, u32[]{:S(2)}) collective-permute-start(bf16[8,128]{1,0:T(8,128)(2,1)S(1)} %get-tuple-element.33), channel_id=1, source_target_pairs={{0,0},{1,1},{2,64},{3,65},{64,2},{65,3},{66,66},{67,67},{128,128},... | collective-permute-start | bytes 6152 | tf_op jit(solution)/shard_map/ppermute | solution.py:41
  252.5 6.7 %collective-permute-start.17 = (bf16[1,8,32,128]{3,2,1,0:T(8,128)(2,1)S(1)}, bf16[1,8,32,128]{3,2,1,0:T(8,128)(2,1)S(1)}, u32[]{:S(2)}, u32[]{:S(2)}) collective-permute-start(bf16[1,8,32,128]{3,2,1,0:T(8,128)(2,1)S(1)} %get-tuple-element.41), channel_id=1, source_target_pairs={{0,3},{1,2},{2,67},{3,66},{64,1},{65,0},{66,65},{67,64},{128,131},... | collective-permute-start | bytes 196616 | tf_op jit(solution)/shard_map/ppermute | solution.py:41
  252.5 12.3 %collective-permute-start.20 = (bf16[2,8,32,128]{3,2,1,0:T(8,128)(2,1)S(1)}, bf16[2,8,32,128]{3,2,1,0:T(8,128)(2,1)S(1)}, u32[]{:S(2)}, u32[]{:S(2)}) collective-permute-start(bf16[2,8,32,128]{3,2,1,0:T(8,128)(2,1)S(1)} %get-tuple-element.46), channel_id=1, source_target_pairs={{0,0},{1,1},{2,64},{3,65},{64,2},{65,3},{66,66},{67,67},{128,128},... | collective-permute-start | bytes 393224 | tf_op jit(solution)/shard_map/ppermute | solution.py:41
  254.5 10.4 %collective-permute-start.21 = (bf16[2,8,32,128]{3,2,1,0:T(8,128)(2,1)S(1)}, bf16[2,8,32,128]{3,2,1,0:T(8,128)(2,1)S(1)}, u32[]{:S(2)}, u32[]{:S(2)}) collective-permute-start(bf16[2,8,32,128]{3,2,1,0:T(8,128)(2,1)S(1)} %get-tuple-element.47), channel_id=1, source_target_pairs={{0,1},{1,0},{2,65},{3,64},{64,3},{65,2},{66,67},{67,66},{128,129},... | collective-permute-start | bytes 393224 | tf_op jit(solution)/shard_map/ppermute | solution.py:41
  255.7 10.6 %collective-permute-start.22 = (bf16[2,8,32,128]{3,2,1,0:T(8,128)(2,1)S(1)}, bf16[2,8,32,128]{3,2,1,0:T(8,128)(2,1)S(1)}, u32[]{:S(2)}, u32[]{:S(2)}) collective-permute-start(bf16[2,8,32,128]{3,2,1,0:T(8,128)(2,1)S(1)} %get-tuple-element.48), channel_id=1, source_target_pairs={{0,2},{1,3},{2,66},{3,67},{64,0},{65,1},{66,64},{67,65},{128,130},... | collective-permute-start | bytes 393224 | tf_op jit(solution)/shard_map/ppermute | solution.py:41
  255.7 10.6 %collective-permute-start.23 = (bf16[2,8,32,128]{3,2,1,0:T(8,128)(2,1)S(1)}, bf16[2,8,32,128]{3,2,1,0:T(8,128)(2,1)S(1)}, u32[]{:S(2)}, u32[]{:S(2)}) collective-permute-start(bf16[2,8,32,128]{3,2,1,0:T(8,128)(2,1)S(1)} %get-tuple-element.49), channel_id=1, source_target_pairs={{0,3},{1,2},{2,67},{3,66},{64,1},{65,0},{66,65},{67,64},{128,131},... | collective-permute-start | bytes 393224 | tf_op jit(solution)/shard_map/ppermute | solution.py:41
  (9 other events, 16.9 us)

commit v3 on v2

--- a/solution.py
+++ b/solution.py
@@ -62,18 +62,12 @@
     return pltpu.CompilerParams(vmem_limit_bytes=limit * MIB, **kw)
 
 
-def pick_kernel(info, gate, up, down, ogate, oup, odown, out, sem):
+def pick_kernel(info, gate, up, down, ogate, oup, odown, out, held, sem_in, sem_out):
     lanes = pl.ds(pl.multiple_of(info[SLOTS] * PART, PART), PART)
 
-    def send(refs):
+    def fetch(refs):
         copies = [
-            pltpu.make_async_copy(
-                ref.at[info[slot]],
-                out.at[slot, pl.ds(n * PART, PART), :],
-                sem.at[slot * 3 + n],
-            )
-            for slot in range(SLOTS)
-            for n, ref in enumerate(refs)
+            pltpu.make_async_copy(ref, held.at[n], sem_in.at[n]) for n, ref in enumerate(refs)
         ]
         for copy in copies:
             copy.start()
@@ -82,11 +76,25 @@
 
     @pl.when(info[SLOTS + 1] == 1)
     def _():
-        send([ref.at[0, :, :, lanes] for ref in (gate, up, down)])
+        fetch([ref.at[0, :, :, lanes] for ref in (gate, up, down)])
 
     @pl.when(info[SLOTS + 1] == 0)
     def _():
-        send((ogate, oup, odown))
+        fetch((ogate, oup, odown))
+
+    copies = [
+        pltpu.make_async_copy(
+            held.at[n, info[slot]],
+            out.at[slot, pl.ds(n * PART, PART), :],
+            sem_out.at[slot * 3 + n],
+        )
+        for slot in range(SLOTS)
+        for n in range(3)
+    ]
+    for copy in copies:
+        copy.start()
+    for copy in copies:
+        copy.wait()
 
 
 def pick_weights(info, mine, others):
@@ -97,7 +105,11 @@
         out_shape=jax.ShapeDtypeStruct((SLOTS, 3 * PART, PART), BF),
         in_specs=[pl.BlockSpec(memory_space=pltpu.SMEM)] + [hbm] * 3 + [anywhere] * 3,
         out_specs=anywhere,
-        scratch_shapes=[pltpu.SemaphoreType.DMA((3 * SLOTS,))],
+        scratch_shapes=[
+            pltpu.VMEM((3, EXPERTS, PART, PART), BF),
+            pltpu.SemaphoreType.DMA((3,)),
+            pltpu.SemaphoreType.DMA((3 * SLOTS,)),
+        ],
         compiler_params=vmem(60),
         cost_estimate=pl.CostEstimate(flops=0, bytes_accessed=4 * MIB, transcendentals=0),
     )(info, *mine, *others)
@@ -131,15 +143,28 @@
     return pl.pallas_call(
         pack_kernel,
         out_shape=jax.ShapeDtypeStruct((2 * ROWS, D), BF),
-        compiler_params=vmem(32),
+        compiler_params=vmem(16),
         cost_estimate=pl.CostEstimate(
-            flops=4 * 2 * ROWS * TOK * D, bytes_accessed=4 * MIB, transcendentals=0
+            flops=200 * ROWS * TOK * D, bytes_accessed=128 * MIB, transcendentals=0
         ),
     )(notes, x, g)
 
 
 def expert_kernel(
-    rows_ref, w0, w1, w2, w3, back_ref, x_ref, s_ref, hid_ref, gu_ref, sg, su, sd, sem
+    rows_ref,
+    w0,
+    w1,
+    w2,
+    w3,
+    back_ref,
+    x_ref,
+    s_ref,
+    hid_ref,
+    gu_ref,
+    sg,
+    su,
+    sd,
+    sem,
 ):
     copies = [
         pltpu.make_async_copy(
@@ -214,7 +239,7 @@
             pltpu.VMEM((SLOTS, PART, FF), BF),
             pltpu.SemaphoreType.DMA((12,)),
         ],
-        compiler_params=vmem(48),
+        compiler_params=vmem(32),
         cost_estimate=pl.CostEstimate(
             flops=16 * ROWS * D * FF, bytes_accessed=14 * MIB, transcendentals=ROWS * FF
         ),
@@ -239,9 +264,9 @@
     return pl.pallas_call(
         functools.partial(sums_kernel, kinds),
         out_shape=[shape, shape],
-        compiler_params=vmem(48),
+        compiler_params=vmem(24),
         cost_estimate=pl.CostEstimate(
-            flops=2 * kinds * ROWS * D * FF, bytes_accessed=3 * kinds * MIB, transcendentals=0
+            flops=0, bytes_accessed=1024, transcendentals=0
         ),
     )(a, b)
 
@@ -276,7 +301,7 @@
     return pl.pallas_call(
         join_kernel,
         out_shape=[jax.ShapeDtypeStruct((TOK, D), BF), jax.ShapeDtypeStruct((8, TOK), BF)],
-        compiler_params=vmem(32),
+        compiler_params=vmem(16),
         cost_estimate=pl.CostEstimate(
             flops=2 * SLOTS * BACK * TOK * D, bytes_accessed=3 * MIB, transcendentals=0
         ),
@@ -304,7 +329,7 @@
         out_shape=[out] * 4,
         in_specs=[pl.BlockSpec(memory_space=pltpu.SMEM), pl.BlockSpec(memory_space=pltpu.VMEM)],
         scratch_shapes=[pltpu.VMEM((EXPERTS, 32, PART), F32)],
-        compiler_params=vmem(32),
+        compiler_params=vmem(16),
         cost_estimate=pl.CostEstimate(
             flops=SLOTS * kinds * PART * PART, bytes_accessed=kinds * MIB, transcendentals=0
         ),
@@ -331,16 +356,32 @@
         final_kernel,
         out_shape=[out] * 3,
         in_specs=[pl.BlockSpec(memory_space=pltpu.SMEM)] + [whole] * 8,
-        compiler_params=vmem(32),
+        compiler_params=vmem(16),
         cost_estimate=pl.CostEstimate(flops=0, bytes_accessed=2 * MIB, transcendentals=0),
     )(info, *downs, *pairs)
 
 
-def add_up(own, others):
-    others = move(others, CORES)
-    send = (own[1].astype(F32) + others[1].astype(F32)).astype(BF)
-    got = move(send, NEAR)
-    return (own[0].astype(F32) + others[0].astype(F32) + got.astype(F32)).astype(BF)
+def add_kernel(*refs):
+    total = refs[0][0].astype(F32) + refs[1][0].astype(F32)
+    for ref in refs[2:-1]:
+        total = total + ref[...].astype(F32)
+    refs[-1][...] = total.astype(BF)
+
+
+def add(which, pairs, *more):
+    shape = pairs[0].shape[1:]
+    block = (4,) + shape[1:]
+    pair = pl.BlockSpec((1,) + block, lambda n: (which, n, 0, 0))
+    one = pl.BlockSpec(block, lambda n: (n, 0, 0))
+    return pl.pallas_call(
+        add_kernel,
+        out_shape=jax.ShapeDtypeStruct(shape, BF),
+        grid=(4,),
+        in_specs=[pair, pair] + [one] * len(more),
+        out_specs=one,
+        compiler_params=vmem(16),
+        cost_estimate=pl.CostEstimate(flops=0, bytes_accessed=1024, transcendentals=0),
+    )(*pairs, *more)
 
 
 def shards(tokens_in, grad_out, route_weight, slot_of, replica_of, w_gate, w_up, w_down):
@@ -349,17 +390,19 @@
     mine = core == side
     quarter = (2 * core + near).astype(jnp.int32)
 
+    weights = (w_gate, w_up, w_down)
+    asked = (2 * (1 - core) + near) * PART
+    others = [lax.dynamic_slice_in_dim(w[0], asked, PART, 2) for w in weights]
+    others, tokens, grads = lax.optimization_barrier((others, tokens_in[0], grad_out[0]))
+    others = [move(w, CORES) for w in others]
+    replicas = jnp.where(mine, replica_of[0], move(replica_of[0], CORES))
+
     notes = jnp.concatenate(
         [slot_of[0].T.astype(BF), route_weight[0].T, jnp.zeros((4, TOK), BF)], axis=0
     )
     notes = move(notes, TURN)
-    x = move(tokens_in[0], TURN)
-    g = move(grad_out[0], TURN)
-
-    weights = (w_gate, w_up, w_down)
-    asked = (2 * (1 - core) + near) * PART
-    others = tuple(move(lax.dynamic_slice_in_dim(w[0], asked, PART, 2), CORES) for w in weights)
-    replicas = jnp.where(mine, replica_of[0], move(replica_of[0], CORES))
+    x = move(tokens, TURN)
+    g = move(grads, TURN)
     info = jnp.concatenate(
         [
             jnp.arange(EXPERTS, dtype=jnp.int32),
@@ -376,15 +419,23 @@
     rows = spread(rows.reshape(SLOTS, 2 * CAP, D)).reshape(2 * ROWS, D)
     back, xs, scaled, hidden, grads = expert_rows(rows, (first, second, third, fourth))
     back = spread(back.reshape(SLOTS, BACK, D)).reshape(SLOTS * BACK, D)
-    down = add_up(*weight_sums(scaled, hidden))
-    pair = add_up(*weight_sums(xs, grads))
+    down = weight_sums(scaled, hidden)
+    xs, down = lax.optimization_barrier((xs, down))
+    pair = weight_sums(xs, grads)
+    down = (down[0], move(down[1], CORES))
+    pair = (pair[0], move(pair[1], CORES))
+    got, pair = lax.optimization_barrier((move(add(1, down), NEAR), pair))
+    down = add(0, down, got)
+    pair = add(0, pair, move(add(1, pair), NEAR))
 
     sect, route = join_rows(notes, back, g)
+    sect, down = lax.optimization_barrier((sect, down))
     grad_in = move(sect, BEHIND)
     route = move(route, TURN)[0:2].T
 
     info = jnp.concatenate([replicas, quarter[None]])
     downs = owners(merge_slots(info, spread(down)))
+    pair, grad_in = lax.optimization_barrier((pair, grad_in))
     pairs = owners(merge_slots(info, spread(pair)))
     gate, up, down = finals(dp[None].astype(jnp.int32), downs, pairs)
     return (grad_in[None], route[None], gate, up, down)

time: 270 us -> 224 us (0.83)
  Pallas kernels: 75.8 us -> 38.3 us
  other arithmetic: 10.7 us -> 0.75 us
  starting transfers between devices: 60.9 us -> 65.7 us
  waiting for transfers between devices: 109 us -> 105 us
    pallas_call x1, Pallas kernels: 49.9 us -> 3.43 us  [pick_weights(): pl.pallas_call(pick_kernel, out_shape=jax.ShapeDtypeStruct((SLOTS, 3 * PA...]
    ppermute x24, waiting for transfers between devices: 93.8 us -> 78.2 us  [move(): return lax.ppermute(x, ('pipe', 'dp'), pairs)]
    all_to_all x5, waiting for transfers between devices: 15.6 us -> 27 us  [spread(): return lax.all_to_all(x, 'expert', split_axis=0, concat_axis=0, tiled=True)]
    pallas_call x0 -> x4, Pallas kernels: none -> 11.1 us  [add(): pl.pallas_call(add_kernel, out_shape=jax.ShapeDtypeStruct(shape, BF), gri...]
    convert_element_type x4 -> x0, other arithmetic: 9.34 us -> none  [the longest x2 5.35 us: add_up(): (own[0].astype(F32) + others[0].astype(F32) + got.astype(F32)).astype(BF)]
    ppermute x24, starting transfers between devices: 35.2 us -> 42.3 us  [move(): return lax.ppermute(x, ('pipe', 'dp'), pairs)]
    unnamed x25 -> x33, local copies, waits for them, and re-layouts: 6.91 us -> 8.99 us
  transfers between devices with their start and end apart: 29 -> 29, of which waited for: 10 -> 12; matrix products, arithmetic and copies ran while one was open for 5% -> 2% of each run, Pallas kernels for 3% -> 9%
where the time goes in v3:
time: 224 us; the launch traced here: 223 us
  waiting for transfers between devices  105 us (47%)
  starting transfers between devices  65.7 us (29%)
  Pallas kernels  38.3 us (17%)
  local copies, waits for them, and re-layouts  11.6 us (5%)
    ppermute x24, waiting for transfers between devices, move(): return lax.ppermute(x, ('pipe', 'dp'), pairs)  78.2 us
    ppermute x24, starting transfers between devices, move(): return lax.ppermute(x, ('pipe', 'dp'), pairs)  42.3 us
    all_to_all x5, waiting for transfers between devices, spread(): return lax.all_to_all(x, 'expert', split_axis=0, concat_axis=0, tiled=True)  27 us
    all_to_all x5, starting transfers between devices, spread(): return lax.all_to_all(x, 'expert', split_axis=0, concat_axis=0, tiled=True)  23.4 us
    pallas_call x4, Pallas kernels, add(): pl.pallas_call(add_kernel, out_shape=jax.ShapeDtypeStruct(shape, BF), gri...  11.1 us
    pallas_call x1, Pallas kernels, expert_rows(): pl.pallas_call(expert_kernel, out_shape=[jax.ShapeDtypeStruct((SLOTS * BA...  10.5 us
    unnamed x33, local copies, waits for them, and re-layouts  8.99 us
    pallas_call x2, Pallas kernels, weight_sums(): pl.pallas_call(functools.partial(sums_kernel, kinds), out_shape=[shape, s...  5.99 us
  transfers between devices with their start and end apart: 29, of which 12 were waited for; matrix products, arithmetic and copies ran while one was open for 2% of the time, Pallas kernels for 9%

profile of v3, /device:TPU:1, one launch (start us, length us, event | category | flops | bytes accessed | tf_op | source)
XLA Modules:
  0.0 222.6 jit_solution(14292630255357514252)
XLA Ops:
  0.7 3.3 %collective-permute-start = (s32[8]{0:T(128)}, s32[8]{0:T(128)S(1)}, u32[]{:S(2)}, u32[]{:S(2)}) collective-permute-start(s32[8]{0:T(128)} %bitcast.34), channel_id=1, source_target_pairs={{0,64},{1,65},{2,66},{3,67},{64,0},{65,1},{66,2},{67,3},{128,192},... | collective-permute-start | bytes 104 | tf_op jit(solution)/shard_map/ppermute | solution.py:41
  6.7 3.1 %collective-permute-start.5 = (bf16[128,2048]{1,0:T(8,128)(2,1)S(1)}, bf16[128,2048]{1,0:T(8,128)(2,1)S(1)}, u32[]{:S(2)}, u32[]{:S(2)}) collective-permute-start(bf16[128,2048]{1,0:T(8,128)(2,1)S(1)} %bitcast.35), channel_id=1, source_target_pairs={{0,0},{1,1},{2,64},{3,65},{64,2},{65,3},{66,66},{67,67},{128,128},... | collective-permute-start | bytes 1572872 | tf_op jit(solution)/shard_map/ppermute | solution.py:41
  9.8 3.3 %collective-permute-start.6 = (bf16[128,2048]{1,0:T(8,128)(2,1)}, bf16[128,2048]{1,0:T(8,128)(2,1)S(1)}, u32[]{:S(2)}, u32[]{:S(2)}) collective-permute-start(bf16[128,2048]{1,0:T(8,128)(2,1)} %bitcast.7), channel_id=1, source_target_pairs={{0,0},{1,1},{2,64},{3,65},{64,2},{65,3},{66,66},{67,67},{128,128},... | collective-permute-start | bytes 1572872 | tf_op jit(solution)/shard_map/ppermute | solution.py:41
  13.4 3.1 %collective-permute-start.4 = (bf16[8,128]{1,0:T(8,128)(2,1)S(1)}, bf16[8,128]{1,0:T(8,128)(2,1)S(1)}, u32[]{:S(2)}, u32[]{:S(2)}) collective-permute-start(bf16[8,128]{1,0:T(8,128)(2,1)S(1)} %maximum_maximum_fusion), channel_id=1, source_target_pairs={{0,0},{1,1},{2,64},{3,65},{64,2},{65,3},{66,66},{67,67},{128,128},... | collective-permute-start | bytes 6152 | tf_op jit(solution)/shard_map/ppermute | solution.py:41
  18.6 3.4 %shard_map.119 = bf16[16,384,128]{2,1,0:T(8,128)(2,1)} custom-call(s32[18]{0:T(128)} %pad_add_fusion.info, bf16[1,8,128,512]{3,2,1,0:T(8,128)(2,1)} %gate.1, bf16[1,8,128,512]{3,2,1,0:T(8,128)(2,1)} %up.1, bf16[1,8,128,512]{3,2,1,0:T(8,128)(2,1)} %down.1, bf16[8,128,128]{2,1,0:T(8,128)(2,1)} %copy-done.9, bf16[8,128,128]{2,1,0:T(8,128)(2,1)} %copy-done.10, ...), custom_call_target="tpu_custom_call" | custom-call | bytes 4194304 | tf_op jit(solution)/shard_map/pallas_call | solution.py:103
  22.0 6.8 %all-to-all-start = ((bf16[16,384,128]{2,1,0:T(8,128)(2,1)}), bf16[16,384,128]{2,1,0:T(8,128)(2,1)}, u32[]{:S(2)}, u32[]{:S(2)}) async-start(bf16[16,384,128]{2,1,0:T(8,128)(2,1)} %shard_map.119), calls=%async_computation | async-start | bytes 3145728 | tf_op jit(solution)/shard_map/all_to_all | solution.py:45
  28.9 6.4 %collective-permute-done.4.notes_ref = bf16[8,128]{1,0:T(8,128)(2,1)S(1)} collective-permute-done((bf16[8,128]{1,0:T(8,128)(2,1)S(1)}, bf16[8,128]{1,0:T(8,128)(2,1)S(1)}, u32[]{:S(2)}, u32[]{:S(2)}) %collective-permute-start.4) | collective-permute-done | bytes 2080 | tf_op jit(solution)/shard_map/ppermute | solution.py:41
  38.5 11.5 %all-to-all-done.w0 = bf16[16,384,128]{2,1,0:T(8,128)(2,1)} async-done(((bf16[16,384,128]{2,1,0:T(8,128)(2,1)}), bf16[16,384,128]{2,1,0:T(8,128)(2,1)}, u32[]{:S(2)}, u32[]{:S(2)}) %all-to-all-start) | async-done | bytes 1572896 | tf_op jit(solution)/shard_map/all_to_all | solution.py:45
  51.6 3.7 %all-to-all-start.1 = ((bf16[16,40,2048]{2,1,0:T(8,128)(2,1)}), bf16[16,40,2048]{2,1,0:T(8,128)(2,1)S(1)}, u32[]{:S(2)}, u32[]{:S(2)}) async-start(bf16[16,40,2048]{2,1,0:T(8,128)(2,1)} %bitcast.30), calls=%async_computation.1 | async-start | bytes 5242880 | tf_op jit(solution)/shard_map/all_to_all | solution.py:45
  55.5 28.9 %collective-permute-done.7.w1 = bf16[16,384,128]{2,1,0:T(8,128)(2,1)} collective-permute-done((bf16[16,384,128]{2,1,0:T(8,128)(2,1)}, bf16[16,384,128]{2,1,0:T(8,128)(2,1)}, u32[]{:S(2)}, u32[]{:S(2)}) %collective-permute-start.7) | collective-permute-done | bytes 1572896 | tf_op jit(solution)/shard_map/ppermute | solution.py:41
  85.7 11.4 %all-to-all-done.1 = bf16[16,40,2048]{2,1,0:T(8,128)(2,1)S(1)} async-done(((bf16[16,40,2048]{2,1,0:T(8,128)(2,1)}), bf16[16,40,2048]{2,1,0:T(8,128)(2,1)S(1)}, u32[]{:S(2)}, u32[]{:S(2)}) %all-to-all-start.1) | async-done | bytes 2621472 | tf_op jit(solution)/shard_map/all_to_all | solution.py:45
  98.5 10.5 %shard_map.121 = (bf16[384,2048]{1,0:T(8,128)(2,1)S(1)}, bf16[320,2048]{1,0:T(8,128)(2,1)S(1)}, bf16[320,2048]{1,0:T(8,128)(2,1)S(1)}, bf16[320,512]{1,0:T(8,128)(2,1)S(1)}, bf16[320,1024]{1,0:T(8,128)(2,1)S(1)}) custom-call(bf16[640,2048]{1,0:T(8,128)(2,1)S(1)} %bitcast.29, bf16[16,384,128]{2,1,0:T(8,128)(2,1)} %all-to-all-done.w0, ...), custom_call_target="tpu_custom_call" | custom-call | flops 5368709120 | bytes 14680064 | tf_op jit(solution)/shard_map/pallas_call | solution.py:225
  109.0 2.3 %shard_map.122 = (bf16[2,16,128,128]{3,2,1,0:T(8,128)(2,1)S(1)}, bf16[2,16,128,128]{3,2,1,0:T(8,128)(2,1)}) custom-call(bf16[320,2048]{1,0:T(8,128)(2,1)S(1)} %get-tuple-element.52.a_ref, bf16[320,512]{1,0:T(8,128)(2,1)S(1)} %get-tuple-element.53.b_ref), custom_call_target="tpu_custom_call" | custom-call | bytes 1024 | tf_op jit(solution)/shard_map/pallas_call | solution.py:264
  111.3 3.7 %shard_map.124 = (bf16[2,16,256,128]{3,2,1,0:T(8,128)(2,1)S(1)}, bf16[2,16,256,128]{3,2,1,0:T(8,128)(2,1)}) custom-call(bf16[320,2048]{1,0:T(8,128)(2,1)S(1)} %get-tuple-element.58.a_ref, bf16[320,1024]{1,0:T(8,128)(2,1)S(1)} %get-tuple-element.59.b_ref), custom_call_target="tpu_custom_call" | custom-call | bytes 1024 | tf_op jit(solution)/shard_map/pallas_call | solution.py:264
  115.5 4.4 %all-to-all-start.2 = ((bf16[16,24,2048]{2,1,0:T(8,128)(2,1)}), bf16[16,24,2048]{2,1,0:T(8,128)(2,1)}, u32[]{:S(2)}, u32[]{:S(2)}) async-start(bf16[16,24,2048]{2,1,0:T(8,128)(2,1)} %bitcast.31), calls=%async_computation.2 | async-start | bytes 3145728 | tf_op jit(solution)/shard_map/all_to_all | solution.py:45
  121.0 2.0 shard_map.123
  123.1 13.2 %collective-permute-done.11.refs_2_ = bf16[16,128,128]{2,1,0:T(8,128)(2,1)S(1)} collective-permute-done((bf16[16,128,128]{2,1,0:T(8,128)(2,1)S(1)}, bf16[16,128,128]{2,1,0:T(8,128)(2,1)S(1)}, u32[]{:S(2)}, u32[]{:S(2)}) %collective-permute-start.11) | collective-permute-done | bytes 524320 | tf_op jit(solution)/shard_map/ppermute | solution.py:41
  137.1 3.4 %shard_map.125 = bf16[16,256,128]{2,1,0:T(8,128)(2,1)} custom-call(bf16[2,16,256,128]{3,2,1,0:T(8,128)(2,1)S(1)} %get-tuple-element.62.refs_0_, bf16[2,16,256,128]{3,2,1,0:T(8,128)(2,1)} %collective-permute-done.12.refs_1_), custom_call_target="tpu_custom_call" | custom-call | bytes 1024 | tf_op jit(solution)/shard_map/pallas_call | solution.py:376
  140.9 4.1 %all-to-all-done.2 = bf16[16,24,2048]{2,1,0:T(8,128)(2,1)} async-done(((bf16[16,24,2048]{2,1,0:T(8,128)(2,1)}), bf16[16,24,2048]{2,1,0:T(8,128)(2,1)}, u32[]{:S(2)}, u32[]{:S(2)}) %all-to-all-start.2) | async-done | bytes 1572896 | tf_op jit(solution)/shard_map/all_to_all | solution.py:45
  146.0 2.9 %shard_map.127 = (bf16[128,2048]{1,0:T(8,128)(2,1)}, bf16[8,128]{1,0:T(8,128)(2,1)S(1)}) custom-call(bf16[8,128]{1,0:T(8,128)(2,1)S(1)} %collective-permute-done.4.notes_ref, bf16[384,2048]{1,0:T(8,128)(2,1)} %bitcast.15.back_ref, bf16[128,2048]{1,0:T(8,128)(2,1)S(1)} %copy-done.4), custom_call_target="tpu_custom_call" | custom-call | flops 201326592 | bytes 3145728 | tf_op jit(solution)/shard_map/pallas_call | solution.py:301
  149.0 2.0 shard_map.128
  151.8 3.6 %all-to-all-start.3 = ((bf16[16,128,128]{2,1,0:T(8,128)(2,1)}), bf16[16,128,128]{2,1,0:T(8,128)(2,1)S(1)}, u32[]{:S(2)}, u32[]{:S(2)}) async-start(bf16[16,128,128]{2,1,0:T(8,128)(2,1)} %copy-done.1), calls=%async_computation.3 | async-start | bytes 1048576 | tf_op jit(solution)/shard_map/all_to_all | solution.py:45
  155.4 14.7 %collective-permute-done.13.refs_2_ = bf16[16,256,128]{2,1,0:T(8,128)(2,1)} collective-permute-done((bf16[16,256,128]{2,1,0:T(8,128)(2,1)}, bf16[16,256,128]{2,1,0:T(8,128)(2,1)}, u32[]{:S(2)}, u32[]{:S(2)}) %collective-permute-start.13) | collective-permute-done | bytes 1048608 | tf_op jit(solution)/shard_map/ppermute | solution.py:41
  170.1 3.7 %shard_map.126 = bf16[16,256,128]{2,1,0:T(8,128)(2,1)} custom-call(bf16[2,16,256,128]{3,2,1,0:T(8,128)(2,1)S(1)} %get-tuple-element.62.refs_0_, bf16[2,16,256,128]{3,2,1,0:T(8,128)(2,1)} %collective-permute-done.12.refs_1_, bf16[16,256,128]{2,1,0:T(8,128)(2,1)} %collective-permute-done.13.refs_2_), custom_call_target="tpu_custom_call" | custom-call | bytes 1024 | tf_op jit(solution)/shard_map/pallas_call | solution.py:376
  173.8 3.4 %collective-permute-done.14 = bf16[128,2048]{1,0:T(8,128)(2,1)S(1)} collective-permute-done((bf16[128,2048]{1,0:T(8,128)(2,1)}, bf16[128,2048]{1,0:T(8,128)(2,1)S(1)}, u32[]{:S(2)}, u32[]{:S(2)}) %collective-permute-start.14) | collective-permute-done | bytes 524320 | tf_op jit(solution)/shard_map/ppermute | solution.py:41
  177.1 4.9 %all-to-all-start.4 = ((bf16[16,256,128]{2,1,0:T(8,128)(2,1)}), bf16[16,256,128]{2,1,0:T(8,128)(2,1)S(1)}, u32[]{:S(2)}, u32[]{:S(2)}) async-start(bf16[16,256,128]{2,1,0:T(8,128)(2,1)} %shard_map.126), calls=%async_computation.4 | async-start | bytes 2097152 | tf_op jit(solution)/shard_map/all_to_all | solution.py:45
  184.8 14.4 %collective-permute-start.17 = (bf16[1,8,32,128]{3,2,1,0:T(8,128)(2,1)S(1)}, bf16[1,8,32,128]{3,2,1,0:T(8,128)(2,1)S(1)}, u32[]{:S(2)}, u32[]{:S(2)}) collective-permute-start(bf16[1,8,32,128]{3,2,1,0:T(8,128)(2,1)S(1)} %get-tuple-element.72), channel_id=1, source_target_pairs={{0,1},{1,0},{2,65},{3,64},{64,3},{65,2},{66,67},{67,66},{128,129},... | collective-permute-start | bytes 196616 | tf_op jit(solution)/shard_map/ppermute | solution.py:41
  202.1 2.8 %collective-permute-done.15 = bf16[8,128]{1,0:T(8,128)(2,1)S(1)} collective-permute-done((bf16[8,128]{1,0:T(8,128)(2,1)S(1)}, bf16[8,128]{1,0:T(8,128)(2,1)S(1)}, u32[]{:S(2)}, u32[]{:S(2)}) %collective-permute-start.15) | collective-permute-done | bytes 2080 | tf_op jit(solution)/shard_map/ppermute | solution.py:41
  205.0 1.9 collective-permute-start.20
  206.9 5.1 %collective-permute-start.21 = (bf16[2,8,32,128]{3,2,1,0:T(8,128)(2,1)S(1)}, bf16[2,8,32,128]{3,2,1,0:T(8,128)(2,1)S(1)}, u32[]{:S(2)}, u32[]{:S(2)}) collective-permute-start(bf16[2,8,32,128]{3,2,1,0:T(8,128)(2,1)S(1)} %get-tuple-element.77), channel_id=1, source_target_pairs={{0,1},{1,0},{2,65},{3,64},{64,3},{65,2},{66,67},{67,66},{128,129},... | collective-permute-start | bytes 393224 | tf_op jit(solution)/shard_map/ppermute | solution.py:41
  213.2 4.8 %collective-permute-done.21.refs_5_ = bf16[2,8,32,128]{3,2,1,0:T(8,128)(2,1)S(1)} collective-permute-done((bf16[2,8,32,128]{3,2,1,0:T(8,128)(2,1)S(1)}, bf16[2,8,32,128]{3,2,1,0:T(8,128)(2,1)S(1)}, u32[]{:S(2)}, u32[]{:S(2)}) %collective-permute-start.21) | collective-permute-done | bytes 131104 | tf_op jit(solution)/shard_map/ppermute | solution.py:41
  218.0 2.8 %collective-permute-done.22.refs_6_ = bf16[2,8,32,128]{3,2,1,0:T(8,128)(2,1)S(1)} collective-permute-done((bf16[2,8,32,128]{3,2,1,0:T(8,128)(2,1)S(1)}, bf16[2,8,32,128]{3,2,1,0:T(8,128)(2,1)S(1)}, u32[]{:S(2)}, u32[]{:S(2)}) %collective-permute-start.22) | collective-permute-done | bytes 131104 | tf_op jit(solution)/shard_map/ppermute | solution.py:41
  (83 shorter events, 25.8 us)
Async XLA Ops:
  0.6 12.8 %copy-start.13 = (s32[1,8]{1,0:T(1,128)S(1)}, s32[1,8]{1,0:T(1,128)}, u32[]{:S(2)}) copy-start(s32[1,8]{1,0:T(1,128)} %param.12) | copy-start | bytes 100
  0.7 12.5 %copy-start.15 = (s32[1,128,2]{1,2,0:T(2,128)S(1)}, s32[1,128,2]{1,2,0:T(2,128)}, u32[]{:S(2)}) copy-start(s32[1,128,2]{1,2,0:T(2,128)} %param.11) | copy-start | bytes 3076
  0.7 12.6 %copy-start.12 = (bf16[1,128,2]{1,2,0:T(2,128)(2,1)S(1)}, bf16[1,128,2]{1,2,0:T(2,128)(2,1)}, u32[]{:S(2)}) copy-start(bf16[1,128,2]{1,2,0:T(2,128)(2,1)} %param.10) | copy-start | bytes 1540
  0.7 12.6 %collective-permute-start = (s32[8]{0:T(128)}, s32[8]{0:T(128)S(1)}, u32[]{:S(2)}, u32[]{:S(2)}) collective-permute-start(s32[8]{0:T(128)} %bitcast.34), channel_id=1, source_target_pairs={{0,64},{1,65},{2,66},{3,67},{64,0},{65,1},{66,2},{67,3},{128,192},... | collective-permute-start | bytes 104 | tf_op jit(solution)/shard_map/ppermute | solution.py:41
  6.1 7.4 %collective-permute-start.1 = (bf16[8,128,128]{2,1,0:T(8,128)(2,1)S(1)}, bf16[8,128,128]{2,1,0:T(8,128)(2,1)S(1)}, u32[]{:S(2)}, u32[]{:S(2)}) collective-permute-start(bf16[8,128,128]{2,1,0:T(8,128)(2,1)S(1)} %dynamic-slice_bitcast_fusion.2), channel_id=1, source_target_pairs={{0,64},{1,65},{2,66},{3,67},{64,0},{65,1},{66,2},{67,3},{128,192},... | collective-permute-start | bytes 786440 | tf_op jit(solution)/shard_map/ppermute | solution.py:41
  6.2 11.0 %collective-permute-start.2 = (bf16[8,128,128]{2,1,0:T(8,128)(2,1)S(1)}, bf16[8,128,128]{2,1,0:T(8,128)(2,1)S(1)}, u32[]{:S(2)}, u32[]{:S(2)}) collective-permute-start(bf16[8,128,128]{2,1,0:T(8,128)(2,1)S(1)} %get-tuple-element.45), channel_id=1, source_target_pairs={{0,64},{1,65},{2,66},{3,67},{64,0},{65,1},{66,2},{67,3},{128,192},... | collective-permute-start | bytes 786440 | tf_op jit(solution)/shard_map/ppermute | solution.py:41
  6.7 28.6 %collective-permute-start.5 = (bf16[128,2048]{1,0:T(8,128)(2,1)S(1)}, bf16[128,2048]{1,0:T(8,128)(2,1)S(1)}, u32[]{:S(2)}, u32[]{:S(2)}) collective-permute-start(bf16[128,2048]{1,0:T(8,128)(2,1)S(1)} %bitcast.35), channel_id=1, source_target_pairs={{0,0},{1,1},{2,64},{3,65},{64,2},{65,3},{66,66},{67,67},{128,128},... | collective-permute-start | bytes 1572872 | tf_op jit(solution)/shard_map/ppermute | solution.py:41
  9.8 25.5 %collective-permute-start.6 = (bf16[128,2048]{1,0:T(8,128)(2,1)}, bf16[128,2048]{1,0:T(8,128)(2,1)S(1)}, u32[]{:S(2)}, u32[]{:S(2)}) collective-permute-start(bf16[128,2048]{1,0:T(8,128)(2,1)} %bitcast.7), channel_id=1, source_target_pairs={{0,0},{1,1},{2,64},{3,65},{64,2},{65,3},{66,66},{67,67},{128,128},... | collective-permute-start | bytes 1572872 | tf_op jit(solution)/shard_map/ppermute | solution.py:41
  13.3 3.9 %collective-permute-start.3 = (bf16[8,128,128]{2,1,0:T(8,128)(2,1)S(1)}, bf16[8,128,128]{2,1,0:T(8,128)(2,1)S(1)}, u32[]{:S(2)}, u32[]{:S(2)}) collective-permute-start(bf16[8,128,128]{2,1,0:T(8,128)(2,1)S(1)} %get-tuple-element.46), channel_id=1, source_target_pairs={{0,64},{1,65},{2,66},{3,67},{64,0},{65,1},{66,2},{67,3},{128,192},... | collective-permute-start | bytes 786440 | tf_op jit(solution)/shard_map/ppermute | solution.py:41
  13.4 21.9 %collective-permute-start.4 = (bf16[8,128]{1,0:T(8,128)(2,1)S(1)}, bf16[8,128]{1,0:T(8,128)(2,1)S(1)}, u32[]{:S(2)}, u32[]{:S(2)}) collective-permute-start(bf16[8,128]{1,0:T(8,128)(2,1)S(1)} %maximum_maximum_fusion), channel_id=1, source_target_pairs={{0,0},{1,1},{2,64},{3,65},{64,2},{65,3},{66,66},{67,67},{128,128},... | collective-permute-start | bytes 6152 | tf_op jit(solution)/shard_map/ppermute | solution.py:41
  22.0 28.0 %all-to-all-start = ((bf16[16,384,128]{2,1,0:T(8,128)(2,1)}), bf16[16,384,128]{2,1,0:T(8,128)(2,1)}, u32[]{:S(2)}, u32[]{:S(2)}) async-start(bf16[16,384,128]{2,1,0:T(8,128)(2,1)} %shard_map.119), calls=%async_computation | async-start | bytes 3145728 | tf_op jit(solution)/shard_map/all_to_all | solution.py:45
  50.0 34.4 %collective-permute-start.7 = (bf16[16,384,128]{2,1,0:T(8,128)(2,1)}, bf16[16,384,128]{2,1,0:T(8,128)(2,1)}, u32[]{:S(2)}, u32[]{:S(2)}) collective-permute-start(bf16[16,384,128]{2,1,0:T(8,128)(2,1)} %all-to-all-done.w0), channel_id=1, source_target_pairs={{0,1},{1,0},{2,3},{3,2},{64,65},{65,64},{66,67},{67,66},{128,129},... | collective-permute-start | bytes 4718600 | tf_op jit(solution)/shard_map/ppermute | solution.py:41
  51.6 45.5 %all-to-all-start.1 = ((bf16[16,40,2048]{2,1,0:T(8,128)(2,1)}), bf16[16,40,2048]{2,1,0:T(8,128)(2,1)S(1)}, u32[]{:S(2)}, u32[]{:S(2)}) async-start(bf16[16,40,2048]{2,1,0:T(8,128)(2,1)} %bitcast.30), calls=%async_computation.1 | async-start | bytes 5242880 | tf_op jit(solution)/shard_map/all_to_all | solution.py:45
  55.4 29.0 %collective-permute-start.8 = (bf16[16,384,128]{2,1,0:T(8,128)(2,1)}, bf16[16,384,128]{2,1,0:T(8,128)(2,1)S(1)}, u32[]{:S(2)}, u32[]{:S(2)}) collective-permute-start(bf16[16,384,128]{2,1,0:T(8,128)(2,1)} %all-to-all-done.w0), channel_id=1, source_target_pairs={{0,64},{1,65},{2,66},{3,67},{64,0},{65,1},{66,2},{67,3},{128,192},... | collective-permute-start | bytes 4718600 | tf_op jit(solution)/shard_map/ppermute | solution.py:41
  84.4 12.7 %collective-permute-start.9 = (bf16[16,384,128]{2,1,0:T(8,128)(2,1)}, bf16[16,384,128]{2,1,0:T(8,128)(2,1)}, u32[]{:S(2)}, u32[]{:S(2)}) collective-permute-start(bf16[16,384,128]{2,1,0:T(8,128)(2,1)} %collective-permute-done.7.w1), channel_id=1, source_target_pairs={{0,64},{1,65},{2,66},{3,67},{64,0},{65,1},{66,2},{67,3},{128,192},... | collective-permute-start | bytes 4718600 | tf_op jit(solution)/shard_map/ppermute | solution.py:41
  115.0 22.1 %collective-permute-start.12 = (bf16[2,16,256,128]{3,2,1,0:T(8,128)(2,1)}, bf16[2,16,256,128]{3,2,1,0:T(8,128)(2,1)}, u32[]{:S(2)}, u32[]{:S(2)}) collective-permute-start(bf16[2,16,256,128]{3,2,1,0:T(8,128)(2,1)} %get-tuple-element.61), channel_id=1, source_target_pairs={{0,64},{1,65},{2,66},{3,67},{64,0},{65,1},{66,2},{67,3},{128,192},... | collective-permute-start | bytes 6291464 | tf_op jit(solution)/shard_map/ppermute | solution.py:41
  115.4 5.6 %collective-permute-start.10 = (bf16[2,16,128,128]{3,2,1,0:T(8,128)(2,1)}, bf16[2,16,128,128]{3,2,1,0:T(8,128)(2,1)}, u32[]{:S(2)}, u32[]{:S(2)}) collective-permute-start(bf16[2,16,128,128]{3,2,1,0:T(8,128)(2,1)} %get-tuple-element.57), channel_id=1, source_target_pairs={{0,64},{1,65},{2,66},{3,67},{64,0},{65,1},{66,2},{67,3},{128,192},... | collective-permute-start | bytes 3145736 | tf_op jit(solution)/shard_map/ppermute | solution.py:41
  115.5 29.5 %all-to-all-start.2 = ((bf16[16,24,2048]{2,1,0:T(8,128)(2,1)}), bf16[16,24,2048]{2,1,0:T(8,128)(2,1)}, u32[]{:S(2)}, u32[]{:S(2)}) async-start(bf16[16,24,2048]{2,1,0:T(8,128)(2,1)} %bitcast.31), calls=%async_computation.2 | async-start | bytes 3145728 | tf_op jit(solution)/shard_map/all_to_all | solution.py:45
  123.0 13.3 %collective-permute-start.11 = (bf16[16,128,128]{2,1,0:T(8,128)(2,1)S(1)}, bf16[16,128,128]{2,1,0:T(8,128)(2,1)S(1)}, u32[]{:S(2)}, u32[]{:S(2)}) collective-permute-start(bf16[16,128,128]{2,1,0:T(8,128)(2,1)S(1)} %shard_map.123), channel_id=1, source_target_pairs={{0,1},{1,0},{2,3},{3,2},{64,65},{65,64},{66,67},{67,66},{128,129},... | collective-permute-start | bytes 1572872 | tf_op jit(solution)/shard_map/ppermute | solution.py:41
  140.6 29.5 %collective-permute-start.13 = (bf16[16,256,128]{2,1,0:T(8,128)(2,1)}, bf16[16,256,128]{2,1,0:T(8,128)(2,1)}, u32[]{:S(2)}, u32[]{:S(2)}) collective-permute-start(bf16[16,256,128]{2,1,0:T(8,128)(2,1)} %shard_map.125), channel_id=1, source_target_pairs={{0,1},{1,0},{2,3},{3,2},{64,65},{65,64},{66,67},{67,66},{128,129},... | collective-permute-start | bytes 3145736 | tf_op jit(solution)/shard_map/ppermute | solution.py:41
  151.8 25.3 %collective-permute-start.14 = (bf16[128,2048]{1,0:T(8,128)(2,1)}, bf16[128,2048]{1,0:T(8,128)(2,1)S(1)}, u32[]{:S(2)}, u32[]{:S(2)}) collective-permute-start(bf16[128,2048]{1,0:T(8,128)(2,1)} %get-tuple-element.67), channel_id=1, source_target_pairs={{0,192},{1,193},{2,0},{3,1},{64,194},{65,195},{66,2},{67,3},{128,6... | collective-permute-start | bytes 1572872 | tf_op jit(solution)/shard_map/ppermute | solution.py:41
  151.8 25.3 %all-to-all-start.3 = ((bf16[16,128,128]{2,1,0:T(8,128)(2,1)}), bf16[16,128,128]{2,1,0:T(8,128)(2,1)S(1)}, u32[]{:S(2)}, u32[]{:S(2)}) async-start(bf16[16,128,128]{2,1,0:T(8,128)(2,1)} %copy-done.1), calls=%async_computation.3 | async-start | bytes 1048576 | tf_op jit(solution)/shard_map/all_to_all | solution.py:45
  177.1 24.1 %all-to-all-start.4 = ((bf16[16,256,128]{2,1,0:T(8,128)(2,1)}), bf16[16,256,128]{2,1,0:T(8,128)(2,1)S(1)}, u32[]{:S(2)}, u32[]{:S(2)}) async-start(bf16[16,256,128]{2,1,0:T(8,128)(2,1)} %shard_map.126), calls=%async_computation.4 | async-start | bytes 2097152 | tf_op jit(solution)/shard_map/all_to_all | solution.py:45
  182.8 24.1 %collective-permute-start.16 = (bf16[1,8,32,128]{3,2,1,0:T(8,128)(2,1)S(1)}, bf16[1,8,32,128]{3,2,1,0:T(8,128)(2,1)S(1)}, u32[]{:S(2)}, u32[]{:S(2)}) collective-permute-start(bf16[1,8,32,128]{3,2,1,0:T(8,128)(2,1)S(1)} %get-tuple-element.71), channel_id=1, source_target_pairs={{0,0},{1,1},{2,64},{3,65},{64,2},{65,3},{66,66},{67,67},{128,128},... | collective-permute-start | bytes 196616 | tf_op jit(solution)/shard_map/ppermute | solution.py:41
  184.8 27.3 %collective-permute-start.17 = (bf16[1,8,32,128]{3,2,1,0:T(8,128)(2,1)S(1)}, bf16[1,8,32,128]{3,2,1,0:T(8,128)(2,1)S(1)}, u32[]{:S(2)}, u32[]{:S(2)}) collective-permute-start(bf16[1,8,32,128]{3,2,1,0:T(8,128)(2,1)S(1)} %get-tuple-element.72), channel_id=1, source_target_pairs={{0,1},{1,0},{2,65},{3,64},{64,3},{65,2},{66,67},{67,66},{128,129},... | collective-permute-start | bytes 196616 | tf_op jit(solution)/shard_map/ppermute | solution.py:41
  199.2 12.9 %collective-permute-start.18 = (bf16[1,8,32,128]{3,2,1,0:T(8,128)(2,1)S(1)}, bf16[1,8,32,128]{3,2,1,0:T(8,128)(2,1)S(1)}, u32[]{:S(2)}, u32[]{:S(2)}) collective-permute-start(bf16[1,8,32,128]{3,2,1,0:T(8,128)(2,1)S(1)} %get-tuple-element.73), channel_id=1, source_target_pairs={{0,2},{1,3},{2,66},{3,67},{64,0},{65,1},{66,64},{67,65},{128,130},... | collective-permute-start | bytes 196616 | tf_op jit(solution)/shard_map/ppermute | solution.py:41
  199.2 5.8 %collective-permute-start.15 = (bf16[8,128]{1,0:T(8,128)(2,1)S(1)}, bf16[8,128]{1,0:T(8,128)(2,1)S(1)}, u32[]{:S(2)}, u32[]{:S(2)}) collective-permute-start(bf16[8,128]{1,0:T(8,128)(2,1)S(1)} %get-tuple-element.69), channel_id=1, source_target_pairs={{0,0},{1,1},{2,64},{3,65},{64,2},{65,3},{66,66},{67,67},{128,128},... | collective-permute-start | bytes 6152 | tf_op jit(solution)/shard_map/ppermute | solution.py:41
  201.1 12.1 %collective-permute-start.19 = (bf16[1,8,32,128]{3,2,1,0:T(8,128)(2,1)S(1)}, bf16[1,8,32,128]{3,2,1,0:T(8,128)(2,1)S(1)}, u32[]{:S(2)}, u32[]{:S(2)}) collective-permute-start(bf16[1,8,32,128]{3,2,1,0:T(8,128)(2,1)S(1)} %get-tuple-element.74), channel_id=1, source_target_pairs={{0,3},{1,2},{2,67},{3,66},{64,1},{65,0},{66,65},{67,64},{128,131},... | collective-permute-start | bytes 196616 | tf_op jit(solution)/shard_map/ppermute | solution.py:41
  205.0 8.3 %collective-permute-start.20 = (bf16[2,8,32,128]{3,2,1,0:T(8,128)(2,1)S(1)}, bf16[2,8,32,128]{3,2,1,0:T(8,128)(2,1)S(1)}, u32[]{:S(2)}, u32[]{:S(2)}) collective-permute-start(bf16[2,8,32,128]{3,2,1,0:T(8,128)(2,1)S(1)} %get-tuple-element.76), channel_id=1, source_target_pairs={{0,0},{1,1},{2,64},{3,65},{64,2},{65,3},{66,66},{67,67},{128,128},... | collective-permute-start | bytes 393224 | tf_op jit(solution)/shard_map/ppermute | solution.py:41
  206.9 11.1 %collective-permute-start.21 = (bf16[2,8,32,128]{3,2,1,0:T(8,128)(2,1)S(1)}, bf16[2,8,32,128]{3,2,1,0:T(8,128)(2,1)S(1)}, u32[]{:S(2)}, u32[]{:S(2)}) collective-permute-start(bf16[2,8,32,128]{3,2,1,0:T(8,128)(2,1)S(1)} %get-tuple-element.77), channel_id=1, source_target_pairs={{0,1},{1,0},{2,65},{3,64},{64,3},{65,2},{66,67},{67,66},{128,129},... | collective-permute-start | bytes 393224 | tf_op jit(solution)/shard_map/ppermute | solution.py:41
  212.0 8.8 %collective-permute-start.22 = (bf16[2,8,32,128]{3,2,1,0:T(8,128)(2,1)S(1)}, bf16[2,8,32,128]{3,2,1,0:T(8,128)(2,1)S(1)}, u32[]{:S(2)}, u32[]{:S(2)}) collective-permute-start(bf16[2,8,32,128]{3,2,1,0:T(8,128)(2,1)S(1)} %get-tuple-element.78), channel_id=1, source_target_pairs={{0,2},{1,3},{2,66},{3,67},{64,0},{65,1},{66,64},{67,65},{128,130},... | collective-permute-start | bytes 393224 | tf_op jit(solution)/shard_map/ppermute | solution.py:41
  212.0 8.8 %collective-permute-start.23 = (bf16[2,8,32,128]{3,2,1,0:T(8,128)(2,1)S(1)}, bf16[2,8,32,128]{3,2,1,0:T(8,128)(2,1)S(1)}, u32[]{:S(2)}, u32[]{:S(2)}) collective-permute-start(bf16[2,8,32,128]{3,2,1,0:T(8,128)(2,1)S(1)} %get-tuple-element.79), channel_id=1, source_target_pairs={{0,3},{1,2},{2,67},{3,66},{64,1},{65,0},{66,65},{67,64},{128,131},... | collective-permute-start | bytes 393224 | tf_op jit(solution)/shard_map/ppermute | solution.py:41
  (13 other events, 28.6 us)

commit v4 on v3

--- a/solution.py
+++ b/solution.py
@@ -62,7 +62,7 @@
     return pltpu.CompilerParams(vmem_limit_bytes=limit * MIB, **kw)
 
 
-def pick_kernel(info, gate, up, down, ogate, oup, odown, out, held, sem_in, sem_out):
+def pick_kernel(info, gate, up, down, other, out, held, sem_in, sem_out):
     lanes = pl.ds(pl.multiple_of(info[SLOTS] * PART, PART), PART)
 
     def fetch(refs):
@@ -80,7 +80,7 @@
 
     @pl.when(info[SLOTS + 1] == 0)
     def _():
-        fetch((ogate, oup, odown))
+        fetch([other.at[pl.ds(n * EXPERTS, EXPERTS)] for n in range(3)])
 
     copies = [
         pltpu.make_async_copy(
@@ -97,13 +97,13 @@
         copy.wait()
 
 
-def pick_weights(info, mine, others):
+def pick_weights(info, mine, other):
     hbm = pl.BlockSpec(memory_space=pltpu.HBM)
     anywhere = pl.BlockSpec(memory_space=pl.ANY)
     return pl.pallas_call(
         pick_kernel,
         out_shape=jax.ShapeDtypeStruct((SLOTS, 3 * PART, PART), BF),
-        in_specs=[pl.BlockSpec(memory_space=pltpu.SMEM)] + [hbm] * 3 + [anywhere] * 3,
+        in_specs=[pl.BlockSpec(memory_space=pltpu.SMEM)] + [hbm] * 3 + [anywhere],
         out_specs=anywhere,
         scratch_shapes=[
             pltpu.VMEM((3, EXPERTS, PART, PART), BF),
@@ -112,7 +112,7 @@
         ],
         compiler_params=vmem(60),
         cost_estimate=pl.CostEstimate(flops=0, bytes_accessed=4 * MIB, transcendentals=0),
-    )(info, *mine, *others)
+    )(info, *mine, other)
 
 
 def seats(notes, size, caps):
@@ -258,7 +258,7 @@
                     ref[q % 2, 2 * n + piece, kind * PART : (kind + 1) * PART, :] = part[rows, lanes]
 
 
-def weight_sums(a, b):
+def weight_sums(a, b, flops):
     kinds = b.shape[1] // FF
     shape = jax.ShapeDtypeStruct((2, SLOTS, kinds * PART, PART), BF)
     return pl.pallas_call(
@@ -266,7 +266,7 @@
         out_shape=[shape, shape],
         compiler_params=vmem(24),
         cost_estimate=pl.CostEstimate(
-            flops=0, bytes_accessed=1024, transcendentals=0
+            flops=flops, bytes_accessed=1024, transcendentals=0
         ),
     )(a, b)
 
@@ -321,7 +321,7 @@
             out[kind] = (sums[...] * SCALE).astype(BF)
 
 
-def merge_slots(info, got):
+def merge_slots(info, got, flops):
     kinds = got.shape[1] // PART
     out = jax.ShapeDtypeStruct((kinds, EXPERTS, 32, PART), BF)
     return pl.pallas_call(
@@ -331,7 +331,7 @@
         scratch_shapes=[pltpu.VMEM((EXPERTS, 32, PART), F32)],
         compiler_params=vmem(16),
         cost_estimate=pl.CostEstimate(
-            flops=SLOTS * kinds * PART * PART, bytes_accessed=kinds * MIB, transcendentals=0
+            flops=flops, bytes_accessed=kinds * MIB, transcendentals=0
         ),
     )(info, got)
 
@@ -392,9 +392,9 @@
 
     weights = (w_gate, w_up, w_down)
     asked = (2 * (1 - core) + near) * PART
-    others = [lax.dynamic_slice_in_dim(w[0], asked, PART, 2) for w in weights]
-    others, tokens, grads = lax.optimization_barrier((others, tokens_in[0], grad_out[0]))
-    others = [move(w, CORES) for w in others]
+    other = jnp.concatenate([lax.dynamic_slice_in_dim(w[0], asked, PART, 2) for w in weights])
+    other, tokens, grads = lax.optimization_barrier((other, tokens_in[0], grad_out[0]))
+    other = move(other, CORES)
     replicas = jnp.where(mine, replica_of[0], move(replica_of[0], CORES))
 
     notes = jnp.concatenate(
@@ -410,7 +410,7 @@
             jnp.stack([quarter, mine.astype(jnp.int32)]),
         ]
     )
-    first = spread(pick_weights(info, weights, others))
+    first = spread(pick_weights(info, weights, other))
     rows = pack_rows(notes, x, g)
     first, rows = lax.optimization_barrier((first, rows))
     second = move(first, NEAR)
@@ -418,25 +418,28 @@
 
     rows = spread(rows.reshape(SLOTS, 2 * CAP, D)).reshape(2 * ROWS, D)
     back, xs, scaled, hidden, grads = expert_rows(rows, (first, second, third, fourth))
+    down = weight_sums(scaled, hidden, 0)
+    xs, down, back = lax.optimization_barrier((xs, down, back))
     back = spread(back.reshape(SLOTS, BACK, D)).reshape(SLOTS * BACK, D)
-    down = weight_sums(scaled, hidden)
-    xs, down = lax.optimization_barrier((xs, down))
-    pair = weight_sums(xs, grads)
+    pair = weight_sums(xs, grads, 10**10)
     down = (down[0], move(down[1], CORES))
+    sent, pair = lax.optimization_barrier((add(1, down), pair))
+    got, _ = lax.optimization_barrier((move(sent, NEAR), pair))
+    down = add(0, down, got)
     pair = (pair[0], move(pair[1], CORES))
-    got, pair = lax.optimization_barrier((move(add(1, down), NEAR), pair))
-    down = add(0, down, got)
-    pair = add(0, pair, move(add(1, pair), NEAR))
+    got, sent = lax.optimization_barrier((got, add(1, pair)))
+    sent = move(sent, NEAR)
 
     sect, route = join_rows(notes, back, g)
-    sect, down = lax.optimization_barrier((sect, down))
+    route = move(route, TURN)[0:2].T
+    pair = add(0, pair, sent)
+    sect, down = lax.optimization_barrier((sect, spread(down)))
     grad_in = move(sect, BEHIND)
-    route = move(route, TURN)[0:2].T
 
     info = jnp.concatenate([replicas, quarter[None]])
-    downs = owners(merge_slots(info, spread(down)))
-    pair, grad_in = lax.optimization_barrier((pair, grad_in))
-    pairs = owners(merge_slots(info, spread(pair)))
+    downs = owners(merge_slots(info, down, 10**11))
+    pair, _ = lax.optimization_barrier((spread(pair), grad_in))
+    pairs = owners(merge_slots(info, pair, 0))
     gate, up, down = finals(dp[None].astype(jnp.int32), downs, pairs)
     return (grad_in[None], route[None], gate, up, down)
 

time: 224 us -> 198 us (0.88); the launches traced: 223 us -> 194 us
  waiting for transfers between devices: 105 us -> 83.1 us
  Pallas kernels: 38.3 us -> 32.9 us
  starting transfers between devices: 65.7 us -> 62.9 us
    ppermute x24 -> x22, waiting for transfers between devices: 78.2 us -> 55.2 us  [move(): return lax.ppermute(x, ('pipe', 'dp'), pairs)]
    pallas_call x4, Pallas kernels: 11.1 us -> 7.59 us  [add(): pl.pallas_call(add_kernel, out_shape=jax.ShapeDtypeStruct(shape, BF), gri...]
    ppermute x24 -> x22, starting transfers between devices: 42.3 us -> 38.9 us  [move(): return lax.ppermute(x, ('pipe', 'dp'), pairs)]
    unnamed x33 -> x31, local copies, waits for them, and re-layouts: 8.99 us -> 10.3 us
  transfers between devices with their start and end apart: 29 -> 27, of which waited for: 12 -> 10; matrix products, arithmetic and copies ran while one was open for 2% -> 1% of each run, Pallas kernels for 9% -> 10%
where the time goes in v4:
time: 198 us; the launch traced here: 194 us
  waiting for transfers between devices  83.1 us (42%)
  starting transfers between devices  62.9 us (32%)
  Pallas kernels  32.9 us (17%)
  local copies, waits for them, and re-layouts  13 us (7%)
    ppermute x22, waiting for transfers between devices, move(): return lax.ppermute(x, ('pipe', 'dp'), pairs)  55.2 us
    ppermute x22, starting transfers between devices, move(): return lax.ppermute(x, ('pipe', 'dp'), pairs)  38.9 us
    all_to_all x5, waiting for transfers between devices, spread(): return lax.all_to_all(x, 'expert', split_axis=0, concat_axis=0, tiled=True)  28 us
    all_to_all x5, starting transfers between devices, spread(): return lax.all_to_all(x, 'expert', split_axis=0, concat_axis=0, tiled=True)  24 us
    pallas_call x1, Pallas kernels, expert_rows(): pl.pallas_call(expert_kernel, out_shape=[jax.ShapeDtypeStruct((SLOTS * BA...  10.5 us
    unnamed x31, local copies, waits for them, and re-layouts  10.3 us
    pallas_call x4, Pallas kernels, add(): pl.pallas_call(add_kernel, out_shape=jax.ShapeDtypeStruct(shape, BF), gri...  7.59 us
    pallas_call x2, Pallas kernels, weight_sums(): pl.pallas_call(functools.partial(sums_kernel, kinds), out_shape=[shape, s...  5.03 us
  transfers between devices with their start and end apart: 27, of which 10 were waited for; matrix products, arithmetic and copies ran while one was open for 1% of the time, Pallas kernels for 10%

profile of v4, /device:TPU:1, one launch (start us, length us, event | category | flops | bytes accessed | tf_op | source)
XLA Modules:
  0.0 193.9 jit_solution(13287734740493879568)
XLA Ops:
  2.9 3.3 %collective-permute-start.2 = (bf16[24,128,128]{2,1,0:T(8,128)(2,1)S(1)}, bf16[24,128,128]{2,1,0:T(8,128)(2,1)S(1)}, u32[]{:S(2)}, u32[]{:S(2)}) collective-permute-start(bf16[24,128,128]{2,1,0:T(8,128)(2,1)S(1)} %pad_maximum_fusion), channel_id=1, source_target_pairs={{0,64},{1,65},{2,66},{3,67},{64,0},{65,1},{66,2},{67,3},{128,192},... | collective-permute-start | bytes 2359304 | tf_op jit(solution)/shard_map/ppermute | solution.py:41
  6.3 3.4 %collective-permute-start.3 = (bf16[128,2048]{1,0:T(8,128)(2,1)}, bf16[128,2048]{1,0:T(8,128)(2,1)S(1)}, u32[]{:S(2)}, u32[]{:S(2)}) collective-permute-start(bf16[128,2048]{1,0:T(8,128)(2,1)} %bitcast.10), channel_id=1, source_target_pairs={{0,0},{1,1},{2,64},{3,65},{64,2},{65,3},{66,66},{67,67},{128,128},... | collective-permute-start | bytes 1572872 | tf_op jit(solution)/shard_map/ppermute | solution.py:41
  9.8 3.0 %collective-permute-start.4 = (bf16[128,2048]{1,0:T(8,128)(2,1)}, bf16[128,2048]{1,0:T(8,128)(2,1)S(1)}, u32[]{:S(2)}, u32[]{:S(2)}) collective-permute-start(bf16[128,2048]{1,0:T(8,128)(2,1)} %bitcast.11), channel_id=1, source_target_pairs={{0,0},{1,1},{2,64},{3,65},{64,2},{65,3},{66,66},{67,67},{128,128},... | collective-permute-start | bytes 1572872 | tf_op jit(solution)/shard_map/ppermute | solution.py:41
  12.9 3.4 %collective-permute-start = (bf16[8,128]{1,0:T(8,128)(2,1)S(1)}, bf16[8,128]{1,0:T(8,128)(2,1)S(1)}, u32[]{:S(2)}, u32[]{:S(2)}) collective-permute-start(bf16[8,128]{1,0:T(8,128)(2,1)S(1)} %maximum_maximum_fusion), channel_id=1, source_target_pairs={{0,0},{1,1},{2,64},{3,65},{64,2},{65,3},{66,66},{67,67},{128,128},... | collective-permute-start | bytes 6152 | tf_op jit(solution)/shard_map/ppermute | solution.py:41
  17.9 3.4 %shard_map.119 = bf16[16,384,128]{2,1,0:T(8,128)(2,1)} custom-call(s32[18]{0:T(128)} %pad_add_fusion.info, bf16[1,8,128,512]{3,2,1,0:T(8,128)(2,1)} %gate.1, bf16[1,8,128,512]{3,2,1,0:T(8,128)(2,1)} %up.1, bf16[1,8,128,512]{3,2,1,0:T(8,128)(2,1)} %down.1, bf16[24,128,128]{2,1,0:T(8,128)(2,1)} %copy-done.11), custom_call_target="tpu_custom_call" | custom-call | bytes 4194304 | tf_op jit(solution)/shard_map/pallas_call | solution.py:103
  21.4 6.8 %all-to-all-start = ((bf16[16,384,128]{2,1,0:T(8,128)(2,1)}), bf16[16,384,128]{2,1,0:T(8,128)(2,1)}, u32[]{:S(2)}, u32[]{:S(2)}) async-start(bf16[16,384,128]{2,1,0:T(8,128)(2,1)} %shard_map.119), calls=%async_computation | async-start | bytes 3145728 | tf_op jit(solution)/shard_map/all_to_all | solution.py:45
  28.2 6.9 %collective-permute-done.notes_ref = bf16[8,128]{1,0:T(8,128)(2,1)S(1)} collective-permute-done((bf16[8,128]{1,0:T(8,128)(2,1)S(1)}, bf16[8,128]{1,0:T(8,128)(2,1)S(1)}, u32[]{:S(2)}, u32[]{:S(2)}) %collective-permute-start) | collective-permute-done | bytes 2080 | tf_op jit(solution)/shard_map/ppermute | solution.py:41
  35.1 1.7 shard_map.120
  38.3 8.3 %all-to-all-done.w0 = bf16[16,384,128]{2,1,0:T(8,128)(2,1)} async-done(((bf16[16,384,128]{2,1,0:T(8,128)(2,1)}), bf16[16,384,128]{2,1,0:T(8,128)(2,1)}, u32[]{:S(2)}, u32[]{:S(2)}) %all-to-all-start) | async-done | bytes 1572896 | tf_op jit(solution)/shard_map/all_to_all | solution.py:45
  48.2 3.7 %all-to-all-start.1 = ((bf16[16,40,2048]{2,1,0:T(8,128)(2,1)}), bf16[16,40,2048]{2,1,0:T(8,128)(2,1)S(1)}, u32[]{:S(2)}, u32[]{:S(2)}) async-start(bf16[16,40,2048]{2,1,0:T(8,128)(2,1)} %bitcast.30), calls=%async_computation.1 | async-start | bytes 5242880 | tf_op jit(solution)/shard_map/all_to_all | solution.py:45
  52.0 25.5 %collective-permute-done.5.w1 = bf16[16,384,128]{2,1,0:T(8,128)(2,1)} collective-permute-done((bf16[16,384,128]{2,1,0:T(8,128)(2,1)}, bf16[16,384,128]{2,1,0:T(8,128)(2,1)}, u32[]{:S(2)}, u32[]{:S(2)}) %collective-permute-start.5) | collective-permute-done | bytes 1572896 | tf_op jit(solution)/shard_map/ppermute | solution.py:41
  78.8 5.0 %all-to-all-done.1 = bf16[16,40,2048]{2,1,0:T(8,128)(2,1)S(1)} async-done(((bf16[16,40,2048]{2,1,0:T(8,128)(2,1)}), bf16[16,40,2048]{2,1,0:T(8,128)(2,1)S(1)}, u32[]{:S(2)}, u32[]{:S(2)}) %all-to-all-start.1) | async-done | bytes 2621472 | tf_op jit(solution)/shard_map/all_to_all | solution.py:45
  85.2 10.5 %shard_map.121 = (bf16[384,2048]{1,0:T(8,128)(2,1)S(1)}, bf16[320,2048]{1,0:T(8,128)(2,1)S(1)}, bf16[320,2048]{1,0:T(8,128)(2,1)S(1)}, bf16[320,512]{1,0:T(8,128)(2,1)S(1)}, bf16[320,1024]{1,0:T(8,128)(2,1)S(1)}) custom-call(bf16[640,2048]{1,0:T(8,128)(2,1)S(1)} %bitcast.29, bf16[16,384,128]{2,1,0:T(8,128)(2,1)} %all-to-all-done.w0, ...), custom_call_target="tpu_custom_call" | custom-call | flops 5368709120 | bytes 14680064 | tf_op jit(solution)/shard_map/pallas_call | solution.py:225
  97.1 3.7 %shard_map.125 = (bf16[2,16,256,128]{3,2,1,0:T(8,128)(2,1)S(1)}, bf16[2,16,256,128]{3,2,1,0:T(8,128)(2,1)}) custom-call(bf16[320,2048]{1,0:T(8,128)(2,1)S(1)} %get-tuple-element.59.a_ref, bf16[320,1024]{1,0:T(8,128)(2,1)S(1)} %get-tuple-element.60.b_ref), custom_call_target="tpu_custom_call" | custom-call | flops 10000000000 | bytes 1024 | tf_op jit(solution)/shard_map/pallas_call | solution.py:264
  103.3 4.4 %all-to-all-start.2 = ((bf16[16,24,2048]{2,1,0:T(8,128)(2,1)}), bf16[16,24,2048]{2,1,0:T(8,128)(2,1)}, u32[]{:S(2)}, u32[]{:S(2)}) async-start(bf16[16,24,2048]{2,1,0:T(8,128)(2,1)} %bitcast.31), calls=%async_computation.2 | async-start | bytes 3145728 | tf_op jit(solution)/shard_map/all_to_all | solution.py:45
  107.9 13.8 %collective-permute-done.9.refs_2_ = bf16[16,128,128]{2,1,0:T(8,128)(2,1)S(1)} collective-permute-done((bf16[16,128,128]{2,1,0:T(8,128)(2,1)}, bf16[16,128,128]{2,1,0:T(8,128)(2,1)S(1)}, u32[]{:S(2)}, u32[]{:S(2)}) %collective-permute-start.9) | collective-permute-done | bytes 524320 | tf_op jit(solution)/shard_map/ppermute | solution.py:41
  121.7 3.5 %shard_map.128 = bf16[16,256,128]{2,1,0:T(8,128)(2,1)} custom-call(bf16[2,16,256,128]{3,2,1,0:T(8,128)(2,1)S(1)} %get-tuple-element.64.refs_0_, bf16[2,16,256,128]{3,2,1,0:T(8,128)(2,1)} %collective-permute-done.16.refs_1_), custom_call_target="tpu_custom_call" | custom-call | bytes 1024 | tf_op jit(solution)/shard_map/pallas_call | solution.py:376
  126.3 8.2 %all-to-all-done.2 = bf16[16,24,2048]{2,1,0:T(8,128)(2,1)} async-done(((bf16[16,24,2048]{2,1,0:T(8,128)(2,1)}), bf16[16,24,2048]{2,1,0:T(8,128)(2,1)}, u32[]{:S(2)}, u32[]{:S(2)}) %all-to-all-start.2) | async-done | bytes 1572896 | tf_op jit(solution)/shard_map/all_to_all | solution.py:45
  134.5 3.8 %all-to-all-start.3 = ((bf16[16,128,128]{2,1,0:T(8,128)(2,1)}), bf16[16,128,128]{2,1,0:T(8,128)(2,1)S(1)}, u32[]{:S(2)}, u32[]{:S(2)}) async-start(bf16[16,128,128]{2,1,0:T(8,128)(2,1)} %copy-done.3), calls=%async_computation.3 | async-start | bytes 1048576 | tf_op jit(solution)/shard_map/all_to_all | solution.py:45
  139.4 2.1 %shard_map.123 = (bf16[128,2048]{1,0:T(8,128)(2,1)S(1)}, bf16[8,128]{1,0:T(8,128)(2,1)S(1)}) custom-call(bf16[8,128]{1,0:T(8,128)(2,1)S(1)} %collective-permute-done.notes_ref, bf16[384,2048]{1,0:T(8,128)(2,1)} %bitcast.15.back_ref, bf16[128,2048]{1,0:T(8,128)(2,1)S(1)} %copy-done.6), custom_call_target="tpu_custom_call" | custom-call | flops 201326592 | bytes 3145728 | tf_op jit(solution)/shard_map/pallas_call | solution.py:301
  142.3 6.5 %all-to-all-done.3.got_ref = bf16[16,128,128]{2,1,0:T(8,128)(2,1)S(1)} async-done(((bf16[16,128,128]{2,1,0:T(8,128)(2,1)}), bf16[16,128,128]{2,1,0:T(8,128)(2,1)S(1)}, u32[]{:S(2)}, u32[]{:S(2)}) %all-to-all-start.3) | async-done | bytes 524320 | tf_op jit(solution)/shard_map/all_to_all | solution.py:45
  150.1 3.7 %shard_map.129 = bf16[16,256,128]{2,1,0:T(8,128)(2,1)} custom-call(bf16[2,16,256,128]{3,2,1,0:T(8,128)(2,1)S(1)} %get-tuple-element.64.refs_0_, bf16[2,16,256,128]{3,2,1,0:T(8,128)(2,1)} %collective-permute-done.16.refs_1_, bf16[16,256,128]{2,1,0:T(8,128)(2,1)} %collective-permute-done.17.refs_2_), custom_call_target="tpu_custom_call" | custom-call | bytes 1024 | tf_op jit(solution)/shard_map/pallas_call | solution.py:376
  153.8 5.3 %all-to-all-start.4 = ((bf16[16,256,128]{2,1,0:T(8,128)(2,1)}), bf16[16,256,128]{2,1,0:T(8,128)(2,1)S(1)}, u32[]{:S(2)}, u32[]{:S(2)}) async-start(bf16[16,256,128]{2,1,0:T(8,128)(2,1)} %shard_map.129), calls=%async_computation.4 | async-start | bytes 2097152 | tf_op jit(solution)/shard_map/all_to_all | solution.py:45
  159.8 5.7 %collective-permute-start.12 = (bf16[1,8,32,128]{3,2,1,0:T(8,128)(2,1)S(1)}, bf16[1,8,32,128]{3,2,1,0:T(8,128)(2,1)S(1)}, u32[]{:S(2)}, u32[]{:S(2)}) collective-permute-start(bf16[1,8,32,128]{3,2,1,0:T(8,128)(2,1)S(1)} %get-tuple-element.70), channel_id=1, source_target_pairs={{0,0},{1,1},{2,64},{3,65},{64,2},{65,3},{66,66},{67,67},{128,128},... | collective-permute-start | bytes 196616 | tf_op jit(solution)/shard_map/ppermute | solution.py:41
  165.6 2.4 %collective-permute-start.14 = (bf16[1,8,32,128]{3,2,1,0:T(8,128)(2,1)S(1)}, bf16[1,8,32,128]{3,2,1,0:T(8,128)(2,1)S(1)}, u32[]{:S(2)}, u32[]{:S(2)}) collective-permute-start(bf16[1,8,32,128]{3,2,1,0:T(8,128)(2,1)S(1)} %get-tuple-element.72), channel_id=1, source_target_pairs={{0,2},{1,3},{2,66},{3,67},{64,0},{65,1},{66,64},{67,65},{128,130},... | collective-permute-start | bytes 196616 | tf_op jit(solution)/shard_map/ppermute | solution.py:41
  167.9 1.9 collective-permute-start.11
  169.9 2.0 %collective-permute-start.15 = (bf16[1,8,32,128]{3,2,1,0:T(8,128)(2,1)S(1)}, bf16[1,8,32,128]{3,2,1,0:T(8,128)(2,1)S(1)}, u32[]{:S(2)}, u32[]{:S(2)}) collective-permute-start(bf16[1,8,32,128]{3,2,1,0:T(8,128)(2,1)S(1)} %get-tuple-element.73), channel_id=1, source_target_pairs={{0,3},{1,2},{2,67},{3,66},{64,1},{65,0},{66,65},{67,64},{128,131},... | collective-permute-start | bytes 196616 | tf_op jit(solution)/shard_map/ppermute | solution.py:41
  172.8 3.0 %collective-permute-done.11 = bf16[8,128]{1,0:T(8,128)(2,1)S(1)} collective-permute-done((bf16[8,128]{1,0:T(8,128)(2,1)S(1)}, bf16[8,128]{1,0:T(8,128)(2,1)S(1)}, u32[]{:S(2)}, u32[]{:S(2)}) %collective-permute-start.11) | collective-permute-done | bytes 2080 | tf_op jit(solution)/shard_map/ppermute | solution.py:41
  175.8 5.6 %collective-permute-start.18 = (bf16[2,8,32,128]{3,2,1,0:T(8,128)(2,1)S(1)}, bf16[2,8,32,128]{3,2,1,0:T(8,128)(2,1)S(1)}, u32[]{:S(2)}, u32[]{:S(2)}) collective-permute-start(bf16[2,8,32,128]{3,2,1,0:T(8,128)(2,1)S(1)} %get-tuple-element.76), channel_id=1, source_target_pairs={{0,0},{1,1},{2,64},{3,65},{64,2},{65,3},{66,66},{67,67},{128,128},... | collective-permute-start | bytes 393224 | tf_op jit(solution)/shard_map/ppermute | solution.py:41
  181.6 4.0 %collective-permute-start.21 = (bf16[2,8,32,128]{3,2,1,0:T(8,128)(2,1)S(1)}, bf16[2,8,32,128]{3,2,1,0:T(8,128)(2,1)S(1)}, u32[]{:S(2)}, u32[]{:S(2)}) collective-permute-start(bf16[2,8,32,128]{3,2,1,0:T(8,128)(2,1)S(1)} %get-tuple-element.79), channel_id=1, source_target_pairs={{0,3},{1,2},{2,67},{3,66},{64,1},{65,0},{66,65},{67,64},{128,131},... | collective-permute-start | bytes 393224 | tf_op jit(solution)/shard_map/ppermute | solution.py:41
  186.1 3.9 %collective-permute-done.18.refs_4_ = bf16[2,8,32,128]{3,2,1,0:T(8,128)(2,1)S(1)} collective-permute-done((bf16[2,8,32,128]{3,2,1,0:T(8,128)(2,1)S(1)}, bf16[2,8,32,128]{3,2,1,0:T(8,128)(2,1)S(1)}, u32[]{:S(2)}, u32[]{:S(2)}) %collective-permute-start.18) | collective-permute-done | bytes 131104 | tf_op jit(solution)/shard_map/ppermute | solution.py:41
  190.0 2.1 %collective-permute-done.20.refs_6_ = bf16[2,8,32,128]{3,2,1,0:T(8,128)(2,1)S(1)} collective-permute-done((bf16[2,8,32,128]{3,2,1,0:T(8,128)(2,1)S(1)}, bf16[2,8,32,128]{3,2,1,0:T(8,128)(2,1)S(1)}, u32[]{:S(2)}, u32[]{:S(2)}) %collective-permute-start.20) | collective-permute-done | bytes 131104 | tf_op jit(solution)/shard_map/ppermute | solution.py:41
  (78 shorter events, 22.3 us)
Async XLA Ops:
  0.7 5.5 %copy-start.13 = (s32[1,8]{1,0:T(1,128)S(1)}, s32[1,8]{1,0:T(1,128)}, u32[]{:S(2)}) copy-start(s32[1,8]{1,0:T(1,128)} %param.12) | copy-start | bytes 100
  0.7 12.2 %copy-start.14 = (s32[1,128,2]{1,2,0:T(2,128)S(1)}, s32[1,128,2]{1,2,0:T(2,128)}, u32[]{:S(2)}) copy-start(s32[1,128,2]{1,2,0:T(2,128)} %param.11) | copy-start | bytes 3076
  0.7 12.2 %copy-start.12 = (bf16[1,128,2]{1,2,0:T(2,128)(2,1)S(1)}, bf16[1,128,2]{1,2,0:T(2,128)(2,1)}, u32[]{:S(2)}) copy-start(bf16[1,128,2]{1,2,0:T(2,128)(2,1)} %param.10) | copy-start | bytes 1540
  2.9 14.2 %collective-permute-start.2 = (bf16[24,128,128]{2,1,0:T(8,128)(2,1)S(1)}, bf16[24,128,128]{2,1,0:T(8,128)(2,1)S(1)}, u32[]{:S(2)}, u32[]{:S(2)}) collective-permute-start(bf16[24,128,128]{2,1,0:T(8,128)(2,1)S(1)} %pad_maximum_fusion), channel_id=1, source_target_pairs={{0,64},{1,65},{2,66},{3,67},{64,0},{65,1},{66,2},{67,3},{128,192},... | collective-permute-start | bytes 2359304 | tf_op jit(solution)/shard_map/ppermute | solution.py:41
  6.2 10.2 %collective-permute-start.1 = (s32[8]{0:T(128)S(1)}, s32[8]{0:T(128)S(1)}, u32[]{:S(2)}, u32[]{:S(2)}) collective-permute-start(s32[8]{0:T(128)S(1)} %bitcast.34), channel_id=1, source_target_pairs={{0,64},{1,65},{2,66},{3,67},{64,0},{65,1},{66,2},{67,3},{128,192},... | collective-permute-start | bytes 104 | tf_op jit(solution)/shard_map/ppermute | solution.py:41
  6.3 28.8 %collective-permute-start.3 = (bf16[128,2048]{1,0:T(8,128)(2,1)}, bf16[128,2048]{1,0:T(8,128)(2,1)S(1)}, u32[]{:S(2)}, u32[]{:S(2)}) collective-permute-start(bf16[128,2048]{1,0:T(8,128)(2,1)} %bitcast.10), channel_id=1, source_target_pairs={{0,0},{1,1},{2,64},{3,65},{64,2},{65,3},{66,66},{67,67},{128,128},... | collective-permute-start | bytes 1572872 | tf_op jit(solution)/shard_map/ppermute | solution.py:41
  9.8 25.3 %collective-permute-start.4 = (bf16[128,2048]{1,0:T(8,128)(2,1)}, bf16[128,2048]{1,0:T(8,128)(2,1)S(1)}, u32[]{:S(2)}, u32[]{:S(2)}) collective-permute-start(bf16[128,2048]{1,0:T(8,128)(2,1)} %bitcast.11), channel_id=1, source_target_pairs={{0,0},{1,1},{2,64},{3,65},{64,2},{65,3},{66,66},{67,67},{128,128},... | collective-permute-start | bytes 1572872 | tf_op jit(solution)/shard_map/ppermute | solution.py:41
  12.9 22.1 %collective-permute-start = (bf16[8,128]{1,0:T(8,128)(2,1)S(1)}, bf16[8,128]{1,0:T(8,128)(2,1)S(1)}, u32[]{:S(2)}, u32[]{:S(2)}) collective-permute-start(bf16[8,128]{1,0:T(8,128)(2,1)S(1)} %maximum_maximum_fusion), channel_id=1, source_target_pairs={{0,0},{1,1},{2,64},{3,65},{64,2},{65,3},{66,66},{67,67},{128,128},... | collective-permute-start | bytes 6152 | tf_op jit(solution)/shard_map/ppermute | solution.py:41
  21.4 25.2 %all-to-all-start = ((bf16[16,384,128]{2,1,0:T(8,128)(2,1)}), bf16[16,384,128]{2,1,0:T(8,128)(2,1)}, u32[]{:S(2)}, u32[]{:S(2)}) async-start(bf16[16,384,128]{2,1,0:T(8,128)(2,1)} %shard_map.119), calls=%async_computation | async-start | bytes 3145728 | tf_op jit(solution)/shard_map/all_to_all | solution.py:45
  46.6 31.0 %collective-permute-start.5 = (bf16[16,384,128]{2,1,0:T(8,128)(2,1)}, bf16[16,384,128]{2,1,0:T(8,128)(2,1)}, u32[]{:S(2)}, u32[]{:S(2)}) collective-permute-start(bf16[16,384,128]{2,1,0:T(8,128)(2,1)} %all-to-all-done.w0), channel_id=1, source_target_pairs={{0,1},{1,0},{2,3},{3,2},{64,65},{65,64},{66,67},{67,66},{128,129},... | collective-permute-start | bytes 4718600 | tf_op jit(solution)/shard_map/ppermute | solution.py:41
  48.2 35.6 %all-to-all-start.1 = ((bf16[16,40,2048]{2,1,0:T(8,128)(2,1)}), bf16[16,40,2048]{2,1,0:T(8,128)(2,1)S(1)}, u32[]{:S(2)}, u32[]{:S(2)}) async-start(bf16[16,40,2048]{2,1,0:T(8,128)(2,1)} %bitcast.30), calls=%async_computation.1 | async-start | bytes 5242880 | tf_op jit(solution)/shard_map/all_to_all | solution.py:45
  52.0 25.6 %collective-permute-start.6 = (bf16[16,384,128]{2,1,0:T(8,128)(2,1)}, bf16[16,384,128]{2,1,0:T(8,128)(2,1)S(1)}, u32[]{:S(2)}, u32[]{:S(2)}) collective-permute-start(bf16[16,384,128]{2,1,0:T(8,128)(2,1)} %all-to-all-done.w0), channel_id=1, source_target_pairs={{0,64},{1,65},{2,66},{3,67},{64,0},{65,1},{66,2},{67,3},{128,192},... | collective-permute-start | bytes 4718600 | tf_op jit(solution)/shard_map/ppermute | solution.py:41
  77.5 6.2 %collective-permute-start.7 = (bf16[16,384,128]{2,1,0:T(8,128)(2,1)}, bf16[16,384,128]{2,1,0:T(8,128)(2,1)}, u32[]{:S(2)}, u32[]{:S(2)}) collective-permute-start(bf16[16,384,128]{2,1,0:T(8,128)(2,1)} %collective-permute-done.5.w1), channel_id=1, source_target_pairs={{0,64},{1,65},{2,66},{3,67},{64,0},{65,1},{66,2},{67,3},{128,192},... | collective-permute-start | bytes 4718600 | tf_op jit(solution)/shard_map/ppermute | solution.py:41
  95.7 5.1 %copy-start.4 = (bf16[384,2048]{1,0:T(8,128)(2,1)}, bf16[384,2048]{1,0:T(8,128)(2,1)S(1)}, u32[]{:S(2)}) copy-start(bf16[384,2048]{1,0:T(8,128)(2,1)S(1)} %get-tuple-element.55) | copy-start | bytes 4718596
  97.0 3.8 %collective-permute-start.8 = (bf16[2,16,128,128]{3,2,1,0:T(8,128)(2,1)S(1)}, bf16[2,16,128,128]{3,2,1,0:T(8,128)(2,1)S(1)}, u32[]{:S(2)}, u32[]{:S(2)}) collective-permute-start(bf16[2,16,128,128]{3,2,1,0:T(8,128)(2,1)S(1)} %get-tuple-element.58), channel_id=1, source_target_pairs={{0,64},{1,65},{2,66},{3,67},{64,0},{65,1},{66,2},{67,3},{128,192},... | collective-permute-start | bytes 3145736 | tf_op jit(solution)/shard_map/ppermute | solution.py:41
  102.8 18.9 %collective-permute-start.16 = (bf16[2,16,256,128]{3,2,1,0:T(8,128)(2,1)}, bf16[2,16,256,128]{3,2,1,0:T(8,128)(2,1)}, u32[]{:S(2)}, u32[]{:S(2)}) collective-permute-start(bf16[2,16,256,128]{3,2,1,0:T(8,128)(2,1)} %get-tuple-element.65), channel_id=1, source_target_pairs={{0,64},{1,65},{2,66},{3,67},{64,0},{65,1},{66,2},{67,3},{128,192},... | collective-permute-start | bytes 6291464 | tf_op jit(solution)/shard_map/ppermute | solution.py:41
  103.3 31.2 %all-to-all-start.2 = ((bf16[16,24,2048]{2,1,0:T(8,128)(2,1)}), bf16[16,24,2048]{2,1,0:T(8,128)(2,1)}, u32[]{:S(2)}, u32[]{:S(2)}) async-start(bf16[16,24,2048]{2,1,0:T(8,128)(2,1)} %bitcast.31), calls=%async_computation.2 | async-start | bytes 3145728 | tf_op jit(solution)/shard_map/all_to_all | solution.py:45
  107.7 17.5 %copy-start.1 = (bf16[2,16,128,128]{3,2,1,0:T(8,128)(2,1)S(1)}, bf16[2,16,128,128]{3,2,1,0:T(8,128)(2,1)}, u32[]{:S(2)}) copy-start(bf16[2,16,128,128]{3,2,1,0:T(8,128)(2,1)} %copy-done) | copy-start | bytes 3145732
  107.8 13.9 %collective-permute-start.9 = (bf16[16,128,128]{2,1,0:T(8,128)(2,1)}, bf16[16,128,128]{2,1,0:T(8,128)(2,1)S(1)}, u32[]{:S(2)}, u32[]{:S(2)}) collective-permute-start(bf16[16,128,128]{2,1,0:T(8,128)(2,1)} %copy-done.7), channel_id=1, source_target_pairs={{0,1},{1,0},{2,3},{3,2},{64,65},{65,64},{66,67},{67,66},{128,129},... | collective-permute-start | bytes 1572872 | tf_op jit(solution)/shard_map/ppermute | solution.py:41
  125.2 24.9 %collective-permute-start.17 = (bf16[16,256,128]{2,1,0:T(8,128)(2,1)}, bf16[16,256,128]{2,1,0:T(8,128)(2,1)}, u32[]{:S(2)}, u32[]{:S(2)}) collective-permute-start(bf16[16,256,128]{2,1,0:T(8,128)(2,1)} %shard_map.128), channel_id=1, source_target_pairs={{0,1},{1,0},{2,3},{3,2},{64,65},{65,64},{66,67},{67,66},{128,129},... | collective-permute-start | bytes 3145736 | tf_op jit(solution)/shard_map/ppermute | solution.py:41
  134.5 14.3 %all-to-all-start.3 = ((bf16[16,128,128]{2,1,0:T(8,128)(2,1)}), bf16[16,128,128]{2,1,0:T(8,128)(2,1)S(1)}, u32[]{:S(2)}, u32[]{:S(2)}) async-start(bf16[16,128,128]{2,1,0:T(8,128)(2,1)} %copy-done.3), calls=%async_computation.3 | async-start | bytes 1048576 | tf_op jit(solution)/shard_map/all_to_all | solution.py:45
  148.8 21.0 %collective-permute-start.10 = (bf16[128,2048]{1,0:T(8,128)(2,1)}, bf16[128,2048]{1,0:T(8,128)(2,1)S(1)}, u32[]{:S(2)}, u32[]{:S(2)}) collective-permute-start(bf16[128,2048]{1,0:T(8,128)(2,1)} %copy-done.10), channel_id=1, source_target_pairs={{0,192},{1,193},{2,0},{3,1},{64,194},{65,195},{66,2},{67,3},{128,6... | collective-permute-start | bytes 1572872 | tf_op jit(solution)/shard_map/ppermute | solution.py:41
  153.8 18.1 %all-to-all-start.4 = ((bf16[16,256,128]{2,1,0:T(8,128)(2,1)}), bf16[16,256,128]{2,1,0:T(8,128)(2,1)S(1)}, u32[]{:S(2)}, u32[]{:S(2)}) async-start(bf16[16,256,128]{2,1,0:T(8,128)(2,1)} %shard_map.129), calls=%async_computation.4 | async-start | bytes 2097152 | tf_op jit(solution)/shard_map/all_to_all | solution.py:45
  159.8 21.6 %collective-permute-start.12 = (bf16[1,8,32,128]{3,2,1,0:T(8,128)(2,1)S(1)}, bf16[1,8,32,128]{3,2,1,0:T(8,128)(2,1)S(1)}, u32[]{:S(2)}, u32[]{:S(2)}) collective-permute-start(bf16[1,8,32,128]{3,2,1,0:T(8,128)(2,1)S(1)} %get-tuple-element.70), channel_id=1, source_target_pairs={{0,0},{1,1},{2,64},{3,65},{64,2},{65,3},{66,66},{67,67},{128,128},... | collective-permute-start | bytes 196616 | tf_op jit(solution)/shard_map/ppermute | solution.py:41
  165.5 16.1 %collective-permute-start.13 = (bf16[1,8,32,128]{3,2,1,0:T(8,128)(2,1)S(1)}, bf16[1,8,32,128]{3,2,1,0:T(8,128)(2,1)S(1)}, u32[]{:S(2)}, u32[]{:S(2)}) collective-permute-start(bf16[1,8,32,128]{3,2,1,0:T(8,128)(2,1)S(1)} %get-tuple-element.71), channel_id=1, source_target_pairs={{0,1},{1,0},{2,65},{3,64},{64,3},{65,2},{66,67},{67,66},{128,129},... | collective-permute-start | bytes 196616 | tf_op jit(solution)/shard_map/ppermute | solution.py:41
  165.6 16.1 %collective-permute-start.14 = (bf16[1,8,32,128]{3,2,1,0:T(8,128)(2,1)S(1)}, bf16[1,8,32,128]{3,2,1,0:T(8,128)(2,1)S(1)}, u32[]{:S(2)}, u32[]{:S(2)}) collective-permute-start(bf16[1,8,32,128]{3,2,1,0:T(8,128)(2,1)S(1)} %get-tuple-element.72), channel_id=1, source_target_pairs={{0,2},{1,3},{2,66},{3,67},{64,0},{65,1},{66,64},{67,65},{128,130},... | collective-permute-start | bytes 196616 | tf_op jit(solution)/shard_map/ppermute | solution.py:41
  167.9 7.9 %collective-permute-start.11 = (bf16[8,128]{1,0:T(8,128)(2,1)S(1)}, bf16[8,128]{1,0:T(8,128)(2,1)S(1)}, u32[]{:S(2)}, u32[]{:S(2)}) collective-permute-start(bf16[8,128]{1,0:T(8,128)(2,1)S(1)} %get-tuple-element.68), channel_id=1, source_target_pairs={{0,0},{1,1},{2,64},{3,65},{64,2},{65,3},{66,66},{67,67},{128,128},... | collective-permute-start | bytes 6152 | tf_op jit(solution)/shard_map/ppermute | solution.py:41
  169.9 16.3 %collective-permute-start.15 = (bf16[1,8,32,128]{3,2,1,0:T(8,128)(2,1)S(1)}, bf16[1,8,32,128]{3,2,1,0:T(8,128)(2,1)S(1)}, u32[]{:S(2)}, u32[]{:S(2)}) collective-permute-start(bf16[1,8,32,128]{3,2,1,0:T(8,128)(2,1)S(1)} %get-tuple-element.73), channel_id=1, source_target_pairs={{0,3},{1,2},{2,67},{3,66},{64,1},{65,0},{66,65},{67,64},{128,131},... | collective-permute-start | bytes 196616 | tf_op jit(solution)/shard_map/ppermute | solution.py:41
  175.8 14.2 %collective-permute-start.18 = (bf16[2,8,32,128]{3,2,1,0:T(8,128)(2,1)S(1)}, bf16[2,8,32,128]{3,2,1,0:T(8,128)(2,1)S(1)}, u32[]{:S(2)}, u32[]{:S(2)}) collective-permute-start(bf16[2,8,32,128]{3,2,1,0:T(8,128)(2,1)S(1)} %get-tuple-element.76), channel_id=1, source_target_pairs={{0,0},{1,1},{2,64},{3,65},{64,2},{65,3},{66,66},{67,67},{128,128},... | collective-permute-start | bytes 393224 | tf_op jit(solution)/shard_map/ppermute | solution.py:41
  181.4 8.6 %collective-permute-start.19 = (bf16[2,8,32,128]{3,2,1,0:T(8,128)(2,1)S(1)}, bf16[2,8,32,128]{3,2,1,0:T(8,128)(2,1)S(1)}, u32[]{:S(2)}, u32[]{:S(2)}) collective-permute-start(bf16[2,8,32,128]{3,2,1,0:T(8,128)(2,1)S(1)} %get-tuple-element.77), channel_id=1, source_target_pairs={{0,1},{1,0},{2,65},{3,64},{64,3},{65,2},{66,67},{67,66},{128,129},... | collective-permute-start | bytes 393224 | tf_op jit(solution)/shard_map/ppermute | solution.py:41
  181.5 10.5 %collective-permute-start.20 = (bf16[2,8,32,128]{3,2,1,0:T(8,128)(2,1)S(1)}, bf16[2,8,32,128]{3,2,1,0:T(8,128)(2,1)S(1)}, u32[]{:S(2)}, u32[]{:S(2)}) collective-permute-start(bf16[2,8,32,128]{3,2,1,0:T(8,128)(2,1)S(1)} %get-tuple-element.78), channel_id=1, source_target_pairs={{0,2},{1,3},{2,66},{3,67},{64,0},{65,1},{66,64},{67,65},{128,130},... | collective-permute-start | bytes 393224 | tf_op jit(solution)/shard_map/ppermute | solution.py:41
  181.6 10.4 %collective-permute-start.21 = (bf16[2,8,32,128]{3,2,1,0:T(8,128)(2,1)S(1)}, bf16[2,8,32,128]{3,2,1,0:T(8,128)(2,1)S(1)}, u32[]{:S(2)}, u32[]{:S(2)}) collective-permute-start(bf16[2,8,32,128]{3,2,1,0:T(8,128)(2,1)S(1)} %get-tuple-element.79), channel_id=1, source_target_pairs={{0,3},{1,2},{2,67},{3,66},{64,1},{65,0},{66,65},{67,64},{128,131},... | collective-permute-start | bytes 393224 | tf_op jit(solution)/shard_map/ppermute | solution.py:41
  (10 other events, 11.2 us)

commit v5 on v4

--- a/solution.py
+++ b/solution.py
@@ -16,6 +16,7 @@
 D = 2048
 FF = 512
 PART = 128
+OWN = 32
 BF = jnp.bfloat16
 F32 = jnp.float32
 MIB = 1 << 20
@@ -30,10 +31,6 @@
 TURN = [(place(zh, c, k, b), place(zh, k, c, b)) for zh, c, k, b in SPOTS]
 CORES = [(place(zh, c, k, b), place(zh, 1 - c, k, b)) for zh, c, k, b in SPOTS]
 NEAR = [(place(zh, c, k, b), place(zh, c, k, 1 - b)) for zh, c, k, b in SPOTS]
-OWNER = [
-    [(place(zh, c, k, b), (2 * zh + k) * 4 + ((2 * c + b) ^ j)) for zh, c, k, b in SPOTS]
-    for j in range(4)
-]
 BEHIND = [(place(zh, c, k, b), ((2 * zh + k - 1) % 4) * 4 + 2 * c + b) for zh, c, k, b in SPOTS]
 
 
@@ -151,6 +148,7 @@
 
 
 def expert_kernel(
+    info,
     rows_ref,
     w0,
     w1,
@@ -169,7 +167,7 @@
     copies = [
         pltpu.make_async_copy(
             ref.at[:, pl.ds(n * PART, PART), :],
-            stack.at[:, :, pl.ds(side * PART, PART)],
+            stack.at[:, :, pl.ds(pl.multiple_of((info[0] ^ side) * PART, PART), PART)],
             sem.at[4 * n + side],
         )
         for n, stack in enumerate((sg, su, sd))
@@ -219,7 +217,7 @@
             back_ref[:, cols] = laid.astype(BF)
 
 
-def expert_rows(rows, quarters):
+def expert_rows(info, rows, quarters):
     whole = pl.BlockSpec(memory_space=pltpu.VMEM)
     anywhere = pl.BlockSpec(memory_space=pl.ANY)
     return pl.pallas_call(
@@ -231,7 +229,7 @@
             jax.ShapeDtypeStruct((ROWS, FF), BF),
             jax.ShapeDtypeStruct((ROWS, 2 * FF), BF),
         ],
-        in_specs=[whole] + [anywhere] * 4,
+        in_specs=[pl.BlockSpec(memory_space=pltpu.SMEM), whole] + [anywhere] * 4,
         out_specs=[whole] * 5,
         scratch_shapes=[
             pltpu.VMEM((SLOTS, PART, FF), BF),
@@ -243,32 +241,45 @@
         cost_estimate=pl.CostEstimate(
             flops=16 * ROWS * D * FF, bytes_accessed=14 * MIB, transcendentals=ROWS * FF
         ),
-    )(rows, *quarters)
-
-
-def sums_kernel(kinds, a_ref, b_ref, own_ref, oth_ref):
-    for n in range(8):
-        part = mm(a_ref[:, pl.ds(n * 256, 256)], b_ref[...], ((0,), (0,))).astype(BF)
-        for piece in range(2):
-            rows = slice(piece * PART, (piece + 1) * PART)
-            for kind in range(kinds):
+    )(info, rows, *quarters)
+
+
+def sums_kernel(kinds, info, a_ref, b_ref, own_ref, oth_ref):
+    def run(core):
+        for n in range(8):
+            part = mm(a_ref[:, pl.ds(n * 256, 256)], b_ref[...], ((0,), (0,))).astype(BF)
+            for piece in range(2):
                 for q in range(4):
-                    lanes = slice(kind * FF + q * PART, kind * FF + (q + 1) * PART)
-                    ref = own_ref if q < 2 else oth_ref
-                    ref[q % 2, 2 * n + piece, kind * PART : (kind + 1) * PART, :] = part[rows, lanes]
-
-
-def weight_sums(a, b, flops):
+                    rows = slice(piece * PART + q * OWN, piece * PART + (q + 1) * OWN)
+                    ref = own_ref if q // 2 == core else oth_ref
+                    to = (info[0] % 2) ^ (q % 2)
+                    for kind in range(kinds):
+                        ref[to, 2 * n + piece, kind * OWN : (kind + 1) * OWN, :] = part[
+                            rows, kind * FF : (kind + 1) * FF
+                        ]
+
+    @pl.when(info[0] // 2 == 0)
+    def _():
+        run(0)
+
+    @pl.when(info[0] // 2 == 1)
+    def _():
+        run(1)
+
+
+def weight_sums(info, a, b, flops):
     kinds = b.shape[1] // FF
-    shape = jax.ShapeDtypeStruct((2, SLOTS, kinds * PART, PART), BF)
+    shape = jax.ShapeDtypeStruct((2, SLOTS, kinds * OWN, FF), BF)
+    whole = pl.BlockSpec(memory_space=pltpu.VMEM)
     return pl.pallas_call(
         functools.partial(sums_kernel, kinds),
         out_shape=[shape, shape],
+        in_specs=[pl.BlockSpec(memory_space=pltpu.SMEM), whole, whole],
         compiler_params=vmem(24),
         cost_estimate=pl.CostEstimate(
             flops=flops, bytes_accessed=1024, transcendentals=0
         ),
-    )(a, b)
+    )(info, a, b)
 
 
 def join_kernel(notes_ref, back_ref, g_ref, sect_ref, route_ref):
@@ -308,57 +319,30 @@
     )(notes, back, g)
 
 
-def merge_kernel(kinds, info, got_ref, out0, out1, out2, out3, sums):
-    for j, out in enumerate((out0, out1, out2, out3)):
-        quarter = lax.bitwise_xor(info[EXPERTS], j)
-        for kind in range(kinds):
-            rows = pl.ds(pl.multiple_of(kind * PART + quarter * 32, 32), 32)
-            for e in range(EXPERTS):
-                sums[e] = got_ref[e, rows, :].astype(F32)
-            for r in range(EXPERTS):
-                e = info[r]
-                sums[e] = sums[e] + got_ref[EXPERTS + r, rows, :].astype(F32)
-            out[kind] = (sums[...] * SCALE).astype(BF)
+def merge_kernel(info, got_ref, *refs):
+    outs, sums = refs[:-1], refs[-1]
+    for kind, out in enumerate(outs):
+        rows = slice(kind * OWN, (kind + 1) * OWN)
+        for e in range(EXPERTS):
+            sums[e] = got_ref[e, rows, :].astype(F32)
+        for r in range(EXPERTS):
+            e = info[r]
+            sums[e] = sums[e] + got_ref[EXPERTS + r, rows, :].astype(F32)
+        out[0] = (sums[...] * SCALE).astype(BF)
 
 
 def merge_slots(info, got, flops):
-    kinds = got.shape[1] // PART
-    out = jax.ShapeDtypeStruct((kinds, EXPERTS, 32, PART), BF)
-    return pl.pallas_call(
-        functools.partial(merge_kernel, kinds),
-        out_shape=[out] * 4,
+    kinds = got.shape[1] // OWN
+    return pl.pallas_call(
+        merge_kernel,
+        out_shape=[jax.ShapeDtypeStruct((1, EXPERTS, OWN, FF), BF)] * kinds,
         in_specs=[pl.BlockSpec(memory_space=pltpu.SMEM), pl.BlockSpec(memory_space=pltpu.VMEM)],
-        scratch_shapes=[pltpu.VMEM((EXPERTS, 32, PART), F32)],
+        scratch_shapes=[pltpu.VMEM((EXPERTS, OWN, FF), F32)],
         compiler_params=vmem(16),
         cost_estimate=pl.CostEstimate(
             flops=flops, bytes_accessed=kinds * MIB, transcendentals=0
         ),
     )(info, got)
-
-
-def owners(parts):
-    return tuple(move(part, OWNER[j]) for j, part in enumerate(parts))
-
-
-def final_kernel(info, *refs):
-    downs, pairs, (gate, up, down) = refs[0:4], refs[4:8], refs[8:11]
-    for j in range(4):
-        lanes = pl.ds(pl.multiple_of(lax.bitwise_xor(info[0], j) * PART, PART), PART)
-        down[0, :, :, lanes] = downs[j][0]
-        gate[0, :, :, lanes] = pairs[j][0]
-        up[0, :, :, lanes] = pairs[j][1]
-
-
-def finals(info, downs, pairs):
-    whole = pl.BlockSpec(memory_space=pltpu.VMEM)
-    out = jax.ShapeDtypeStruct((1, EXPERTS, 32, FF), BF)
-    return pl.pallas_call(
-        final_kernel,
-        out_shape=[out] * 3,
-        in_specs=[pl.BlockSpec(memory_space=pltpu.SMEM)] + [whole] * 8,
-        compiler_params=vmem(16),
-        cost_estimate=pl.CostEstimate(flops=0, bytes_accessed=2 * MIB, transcendentals=0),
-    )(info, *downs, *pairs)
 
 
 def add_kernel(*refs):
@@ -389,20 +373,16 @@
     core, side, near = pipe % 2, dp // 2, dp % 2
     mine = core == side
     quarter = (2 * core + near).astype(jnp.int32)
+    spot = quarter[None]
 
     weights = (w_gate, w_up, w_down)
     asked = (2 * (1 - core) + near) * PART
     other = jnp.concatenate([lax.dynamic_slice_in_dim(w[0], asked, PART, 2) for w in weights])
-    other, tokens, grads = lax.optimization_barrier((other, tokens_in[0], grad_out[0]))
+    other, tokens = lax.optimization_barrier((other, tokens_in[0]))
     other = move(other, CORES)
     replicas = jnp.where(mine, replica_of[0], move(replica_of[0], CORES))
-
-    notes = jnp.concatenate(
-        [slot_of[0].T.astype(BF), route_weight[0].T, jnp.zeros((4, TOK), BF)], axis=0
-    )
-    notes = move(notes, TURN)
     x = move(tokens, TURN)
-    g = move(grads, TURN)
+
     info = jnp.concatenate(
         [
             jnp.arange(EXPERTS, dtype=jnp.int32),
@@ -410,18 +390,25 @@
             jnp.stack([quarter, mine.astype(jnp.int32)]),
         ]
     )
-    first = spread(pick_weights(info, weights, other))
+    notes = jnp.concatenate(
+        [slot_of[0].T.astype(BF), route_weight[0].T, jnp.zeros((4, TOK), BF)], axis=0
+    )
+    picked = pick_weights(info, weights, other)
+    picked, notes, grads = lax.optimization_barrier((picked, notes, grad_out[0]))
+    notes = move(notes, TURN)
+    g = move(grads, TURN)
+    first = spread(picked)
     rows = pack_rows(notes, x, g)
     first, rows = lax.optimization_barrier((first, rows))
     second = move(first, NEAR)
     third, fourth = move(first, CORES), move(second, CORES)
 
     rows = spread(rows.reshape(SLOTS, 2 * CAP, D)).reshape(2 * ROWS, D)
-    back, xs, scaled, hidden, grads = expert_rows(rows, (first, second, third, fourth))
-    down = weight_sums(scaled, hidden, 0)
+    back, xs, scaled, hidden, grads = expert_rows(spot, rows, (first, second, third, fourth))
+    down = weight_sums(spot, scaled, hidden, 0)
     xs, down, back = lax.optimization_barrier((xs, down, back))
     back = spread(back.reshape(SLOTS, BACK, D)).reshape(SLOTS * BACK, D)
-    pair = weight_sums(xs, grads, 10**10)
+    pair = weight_sums(spot, xs, grads, 10**10)
     down = (down[0], move(down[1], CORES))
     sent, pair = lax.optimization_barrier((add(1, down), pair))
     got, _ = lax.optimization_barrier((move(sent, NEAR), pair))
@@ -431,17 +418,16 @@
     sent = move(sent, NEAR)
 
     sect, route = join_rows(notes, back, g)
-    route = move(route, TURN)[0:2].T
+    route = move(route, TURN)
     pair = add(0, pair, sent)
     sect, down = lax.optimization_barrier((sect, spread(down)))
     grad_in = move(sect, BEHIND)
 
-    info = jnp.concatenate([replicas, quarter[None]])
-    downs = owners(merge_slots(info, down, 10**11))
-    pair, _ = lax.optimization_barrier((spread(pair), grad_in))
-    pairs = owners(merge_slots(info, pair, 0))
-    gate, up, down = finals(dp[None].astype(jnp.int32), downs, pairs)
-    return (grad_in[None], route[None], gate, up, down)
+    (down,) = merge_slots(replicas, down, 10**11)
+    down = move(down, TURN)
+    pair, route, _ = lax.optimization_barrier((spread(pair), route, grad_in))
+    gate, up = (move(part, TURN) for part in merge_slots(replicas, pair, 0))
+    return (grad_in[None], route[0:2].T[None], gate, up, down)
 
 
 def solution(mesh):

time: 198 us -> 199 us (level); the launches traced: 194 us -> 198 us
  waiting for transfers between devices: 83.1 us -> 93.6 us
  starting transfers between devices: 62.9 us -> 55.5 us
  local copies, waits for them, and re-layouts: 13 us -> 15.4 us
    ppermute x22 -> x17, waiting for transfers between devices: 55.2 us -> 64.8 us  [move(): return lax.ppermute(x, ('pipe', 'dp'), pairs)]
    ppermute x22 -> x17, starting transfers between devices: 38.9 us -> 33.1 us  [move(): return lax.ppermute(x, ('pipe', 'dp'), pairs)]
    unnamed x31 -> x32, local copies, waits for them, and re-layouts: 10.3 us -> 12.7 us
  transfers between devices with their start and end apart: 27 -> 22, of which waited for: 10 -> 11; matrix products, arithmetic and copies ran while one was open for 1% -> 1% of each run, Pallas kernels for 10% -> 10%
where the time goes in v5:
time: 199 us; the launch traced here: 198 us
  waiting for transfers between devices  93.6 us (47%)
  starting transfers between devices  55.5 us (28%)
  Pallas kernels  32 us (16%)
  local copies, waits for them, and re-layouts  15.4 us (8%)
    ppermute x17, waiting for transfers between devices, move(): return lax.ppermute(x, ('pipe', 'dp'), pairs)  64.8 us
    ppermute x17, starting transfers between devices, move(): return lax.ppermute(x, ('pipe', 'dp'), pairs)  33.1 us
    all_to_all x5, waiting for transfers between devices, spread(): return lax.all_to_all(x, 'expert', split_axis=0, concat_axis=0, tiled=True)  28.9 us
    all_to_all x5, starting transfers between devices, spread(): return lax.all_to_all(x, 'expert', split_axis=0, concat_axis=0, tiled=True)  22.4 us
    unnamed x32, local copies, waits for them, and re-layouts  12.7 us
    pallas_call x1, Pallas kernels, expert_rows(): pl.pallas_call(expert_kernel, out_shape=[jax.ShapeDtypeStruct((SLOTS * BA...  10.5 us
    pallas_call x4, Pallas kernels, add(): pl.pallas_call(add_kernel, out_shape=jax.ShapeDtypeStruct(shape, BF), gri...  7.65 us
    pallas_call x2, Pallas kernels, weight_sums(): pl.pallas_call(functools.partial(sums_kernel, kinds), out_shape=[shape, s...  5.26 us
  transfers between devices with their start and end apart: 22, of which 11 were waited for; matrix products, arithmetic and copies ran while one was open for 1% of the time, Pallas kernels for 10%

profile of v5, /device:TPU:1, one launch (start us, length us, event | category | flops | bytes accessed | tf_op | source)
XLA Modules:
  0.0 198.3 jit_solution(14033155196787918087)
XLA Ops:
  2.9 3.3 %collective-permute-start.1 = (bf16[24,128,128]{2,1,0:T(8,128)(2,1)S(1)}, bf16[24,128,128]{2,1,0:T(8,128)(2,1)S(1)}, u32[]{:S(2)}, u32[]{:S(2)}) collective-permute-start(bf16[24,128,128]{2,1,0:T(8,128)(2,1)S(1)} %pad_maximum_fusion), channel_id=1, source_target_pairs={{0,64},{1,65},{2,66},{3,67},{64,0},{65,1},{66,2},{67,3},{128,192},... | collective-permute-start | bytes 2359304 | tf_op jit(solution)/shard_map/ppermute | solution.py:38
  6.3 3.4 %collective-permute-start.3 = (bf16[128,2048]{1,0:T(8,128)(2,1)}, bf16[128,2048]{1,0:T(8,128)(2,1)S(1)}, u32[]{:S(2)}, u32[]{:S(2)}) collective-permute-start(bf16[128,2048]{1,0:T(8,128)(2,1)} %bitcast.6), channel_id=1, source_target_pairs={{0,0},{1,1},{2,64},{3,65},{64,2},{65,3},{66,66},{67,67},{128,128},... | collective-permute-start | bytes 1572872 | tf_op jit(solution)/shard_map/ppermute | solution.py:38
  11.4 3.4 %shard_map.119 = bf16[16,384,128]{2,1,0:T(8,128)(2,1)} custom-call(s32[18]{0:T(128)} %pad_add_fusion.info, bf16[1,8,128,512]{3,2,1,0:T(8,128)(2,1)} %gate.1, bf16[1,8,128,512]{3,2,1,0:T(8,128)(2,1)} %up.1, bf16[1,8,128,512]{3,2,1,0:T(8,128)(2,1)} %down.1, bf16[24,128,128]{2,1,0:T(8,128)(2,1)} %copy-done.10), custom_call_target="tpu_custom_call" | custom-call | bytes 4194304 | tf_op jit(solution)/shard_map/pallas_call | solution.py:100
  14.9 3.0 %collective-permute-start.4 = (bf16[128,2048]{1,0:T(8,128)(2,1)}, bf16[128,2048]{1,0:T(8,128)(2,1)S(1)}, u32[]{:S(2)}, u32[]{:S(2)}) collective-permute-start(bf16[128,2048]{1,0:T(8,128)(2,1)} %bitcast.11), channel_id=1, source_target_pairs={{0,0},{1,1},{2,64},{3,65},{64,2},{65,3},{66,66},{67,67},{128,128},... | collective-permute-start | bytes 1572872 | tf_op jit(solution)/shard_map/ppermute | solution.py:38
  17.9 3.5 %collective-permute-start.2 = (bf16[8,128]{1,0:T(8,128)(2,1)S(1)}, bf16[8,128]{1,0:T(8,128)(2,1)S(1)}, u32[]{:S(2)}, u32[]{:S(2)}) collective-permute-start(bf16[8,128]{1,0:T(8,128)(2,1)S(1)} %maximum_maximum_fusion), channel_id=1, source_target_pairs={{0,0},{1,1},{2,64},{3,65},{64,2},{65,3},{66,66},{67,67},{128,128},... | collective-permute-start | bytes 6152 | tf_op jit(solution)/shard_map/ppermute | solution.py:38
  21.4 6.8 %all-to-all-start = ((bf16[16,384,128]{2,1,0:T(8,128)(2,1)}), bf16[16,384,128]{2,1,0:T(8,128)(2,1)}, u32[]{:S(2)}, u32[]{:S(2)}) async-start(bf16[16,384,128]{2,1,0:T(8,128)(2,1)} %shard_map.119), calls=%async_computation | async-start | bytes 3145728 | tf_op jit(solution)/shard_map/all_to_all | solution.py:42
  29.6 5.4 %collective-permute-done.2.notes_ref = bf16[8,128]{1,0:T(8,128)(2,1)S(1)} collective-permute-done((bf16[8,128]{1,0:T(8,128)(2,1)S(1)}, bf16[8,128]{1,0:T(8,128)(2,1)S(1)}, u32[]{:S(2)}, u32[]{:S(2)}) %collective-permute-start.2) | collective-permute-done | bytes 2080 | tf_op jit(solution)/shard_map/ppermute | solution.py:38
  35.0 1.7 shard_map.120
  38.1 8.4 %all-to-all-done.w0 = bf16[16,384,128]{2,1,0:T(8,128)(2,1)} async-done(((bf16[16,384,128]{2,1,0:T(8,128)(2,1)}), bf16[16,384,128]{2,1,0:T(8,128)(2,1)}, u32[]{:S(2)}, u32[]{:S(2)}) %all-to-all-start) | async-done | bytes 1572896 | tf_op jit(solution)/shard_map/all_to_all | solution.py:42
  48.2 3.7 %all-to-all-start.1 = ((bf16[16,40,2048]{2,1,0:T(8,128)(2,1)}), bf16[16,40,2048]{2,1,0:T(8,128)(2,1)S(1)}, u32[]{:S(2)}, u32[]{:S(2)}) async-start(bf16[16,40,2048]{2,1,0:T(8,128)(2,1)} %bitcast.29), calls=%async_computation.1 | async-start | bytes 5242880 | tf_op jit(solution)/shard_map/all_to_all | solution.py:42
  52.0 25.5 %collective-permute-done.5.w1 = bf16[16,384,128]{2,1,0:T(8,128)(2,1)} collective-permute-done((bf16[16,384,128]{2,1,0:T(8,128)(2,1)}, bf16[16,384,128]{2,1,0:T(8,128)(2,1)}, u32[]{:S(2)}, u32[]{:S(2)}) %collective-permute-start.5) | collective-permute-done | bytes 1572896 | tf_op jit(solution)/shard_map/ppermute | solution.py:38
  78.8 4.9 %all-to-all-done.1 = bf16[16,40,2048]{2,1,0:T(8,128)(2,1)S(1)} async-done(((bf16[16,40,2048]{2,1,0:T(8,128)(2,1)}), bf16[16,40,2048]{2,1,0:T(8,128)(2,1)S(1)}, u32[]{:S(2)}, u32[]{:S(2)}) %all-to-all-start.1) | async-done | bytes 2621472 | tf_op jit(solution)/shard_map/all_to_all | solution.py:42
  85.1 10.5 %shard_map.121 = (bf16[384,2048]{1,0:T(8,128)(2,1)S(1)}, bf16[320,2048]{1,0:T(8,128)(2,1)S(1)}, bf16[320,2048]{1,0:T(8,128)(2,1)S(1)}, bf16[320,512]{1,0:T(8,128)(2,1)S(1)}, bf16[320,1024]{1,0:T(8,128)(2,1)S(1)}) custom-call(s32[1]{0:T(128)} %bitcast.1.info, bf16[640,2048]{1,0:T(8,128)(2,1)S(1)} %bitcast.28, bf16[16,384,128]{2,1,0:T(8,128)(2,1)} %all-to-all-done.w0, ...), custom_call_target="tpu_custom_call" | custom-call | flops 5368709120 | bytes 14680064 | tf_op jit(solution)/shard_map/pallas_call | solution.py:223
  97.0 4.0 %shard_map.125 = (bf16[2,16,64,512]{3,2,1,0:T(8,128)(2,1)S(1)}, bf16[2,16,64,512]{3,2,1,0:T(8,128)(2,1)}) custom-call(s32[1]{0:T(128)} %bitcast.1.info, bf16[320,2048]{1,0:T(8,128)(2,1)S(1)} %get-tuple-element.55.a_ref, bf16[320,1024]{1,0:T(8,128)(2,1)S(1)} %get-tuple-element.56.b_ref), custom_call_target="tpu_custom_call" | custom-call | flops 10000000000 | bytes 1024 | tf_op jit(solution)/shard_map/pallas_call | solution.py:274
  103.5 4.4 %all-to-all-start.2 = ((bf16[16,24,2048]{2,1,0:T(8,128)(2,1)}), bf16[16,24,2048]{2,1,0:T(8,128)(2,1)}, u32[]{:S(2)}, u32[]{:S(2)}) async-start(bf16[16,24,2048]{2,1,0:T(8,128)(2,1)} %bitcast.30), calls=%async_computation.2 | async-start | bytes 3145728 | tf_op jit(solution)/shard_map/all_to_all | solution.py:42
  108.0 13.8 %collective-permute-done.9.refs_2_ = bf16[16,32,512]{2,1,0:T(8,128)(2,1)S(1)} collective-permute-done((bf16[16,32,512]{2,1,0:T(8,128)(2,1)}, bf16[16,32,512]{2,1,0:T(8,128)(2,1)S(1)}, u32[]{:S(2)}, u32[]{:S(2)}) %collective-permute-start.9) | collective-permute-done | bytes 524320 | tf_op jit(solution)/shard_map/ppermute | solution.py:38
  121.8 3.5 %shard_map.127 = bf16[16,64,512]{2,1,0:T(8,128)(2,1)} custom-call(bf16[2,16,64,512]{3,2,1,0:T(8,128)(2,1)S(1)} %get-tuple-element.60.refs_0_, bf16[2,16,64,512]{3,2,1,0:T(8,128)(2,1)} %collective-permute-done.11.refs_1_), custom_call_target="tpu_custom_call" | custom-call | bytes 1024 | tf_op jit(solution)/shard_map/pallas_call | solution.py:360
  126.4 8.2 %all-to-all-done.2 = bf16[16,24,2048]{2,1,0:T(8,128)(2,1)} async-done(((bf16[16,24,2048]{2,1,0:T(8,128)(2,1)}), bf16[16,24,2048]{2,1,0:T(8,128)(2,1)}, u32[]{:S(2)}, u32[]{:S(2)}) %all-to-all-start.2) | async-done | bytes 1572896 | tf_op jit(solution)/shard_map/all_to_all | solution.py:42
  134.6 3.6 %all-to-all-start.3 = ((bf16[16,32,512]{2,1,0:T(8,128)(2,1)}), bf16[16,32,512]{2,1,0:T(8,128)(2,1)S(1)}, u32[]{:S(2)}, u32[]{:S(2)}) async-start(bf16[16,32,512]{2,1,0:T(8,128)(2,1)} %copy-done.3), calls=%async_computation.3 | async-start | bytes 1048576 | tf_op jit(solution)/shard_map/all_to_all | solution.py:42
  139.2 2.1 %shard_map.123 = (bf16[128,2048]{1,0:T(8,128)(2,1)S(1)}, bf16[8,128]{1,0:T(8,128)(2,1)S(1)}) custom-call(bf16[8,128]{1,0:T(8,128)(2,1)S(1)} %collective-permute-done.2.notes_ref, bf16[384,2048]{1,0:T(8,128)(2,1)} %bitcast.15.back_ref, bf16[128,2048]{1,0:T(8,128)(2,1)S(1)} %copy-done.6), custom_call_target="tpu_custom_call" | custom-call | flops 201326592 | bytes 3145728 | tf_op jit(solution)/shard_map/pallas_call | solution.py:312
  141.3 7.3 %all-to-all-done.3.got_ref = bf16[16,32,512]{2,1,0:T(8,128)(2,1)S(1)} async-done(((bf16[16,32,512]{2,1,0:T(8,128)(2,1)}), bf16[16,32,512]{2,1,0:T(8,128)(2,1)S(1)}, u32[]{:S(2)}, u32[]{:S(2)}) %all-to-all-start.3) | async-done | bytes 524320 | tf_op jit(solution)/shard_map/all_to_all | solution.py:42
  148.7 2.9 %collective-permute-start.10 = (bf16[128,2048]{1,0:T(8,128)(2,1)S(1)}, bf16[128,2048]{1,0:T(8,128)(2,1)}, u32[]{:S(2)}, u32[]{:S(2)}) collective-permute-start(bf16[128,2048]{1,0:T(8,128)(2,1)S(1)} %get-tuple-element.63), channel_id=1, source_target_pairs={{0,192},{1,193},{2,0},{3,1},{64,194},{65,195},{66,2},{67,3},{128,6... | collective-permute-start | bytes 1572872 | tf_op jit(solution)/shard_map/ppermute | solution.py:38
  151.6 3.7 %shard_map.128 = bf16[16,64,512]{2,1,0:T(8,128)(2,1)} custom-call(bf16[2,16,64,512]{3,2,1,0:T(8,128)(2,1)S(1)} %get-tuple-element.60.refs_0_, bf16[2,16,64,512]{3,2,1,0:T(8,128)(2,1)} %collective-permute-done.11.refs_1_, bf16[16,64,512]{2,1,0:T(8,128)(2,1)} %collective-permute-done.12.refs_2_), custom_call_target="tpu_custom_call" | custom-call | bytes 1024 | tf_op jit(solution)/shard_map/pallas_call | solution.py:360
  155.3 3.9 %all-to-all-start.4 = ((bf16[16,64,512]{2,1,0:T(8,128)(2,1)}), bf16[16,64,512]{2,1,0:T(8,128)(2,1)S(1)}, u32[]{:S(2)}, u32[]{:S(2)}) async-start(bf16[16,64,512]{2,1,0:T(8,128)(2,1)} %shard_map.128), calls=%async_computation.4 | async-start | bytes 2097152 | tf_op jit(solution)/shard_map/all_to_all | solution.py:42
  159.9 6.1 %collective-permute-start.16 = (bf16[1,8,32,512]{3,2,1,0:T(8,128)(2,1)S(1)}, bf16[1,8,32,512]{3,2,1,0:T(8,128)(2,1)S(1)}, u32[]{:S(2)}, u32[]{:S(2)}) collective-permute-start(bf16[1,8,32,512]{3,2,1,0:T(8,128)(2,1)S(1)} %shard_map.130), channel_id=1, source_target_pairs={{0,0},{1,1},{2,64},{3,65},{64,2},{65,3},{66,66},{67,67},{128,128},... | collective-permute-start | bytes 786440 | tf_op jit(solution)/shard_map/ppermute | solution.py:38
  166.0 1.9 collective-permute-start.13
  167.9 9.1 %collective-permute-done.13 = bf16[8,128]{1,0:T(8,128)(2,1)S(1)} collective-permute-done((bf16[8,128]{1,0:T(8,128)(2,1)S(1)}, bf16[8,128]{1,0:T(8,128)(2,1)S(1)}, u32[]{:S(2)}, u32[]{:S(2)}) %collective-permute-start.13) | collective-permute-done | bytes 2080 | tf_op jit(solution)/shard_map/ppermute | solution.py:38
  177.8 4.3 %collective-permute-start.14 = (bf16[1,8,32,512]{3,2,1,0:T(8,128)(2,1)S(1)}, bf16[1,8,32,512]{3,2,1,0:T(8,128)(2,1)S(1)}, u32[]{:S(2)}, u32[]{:S(2)}) collective-permute-start(bf16[1,8,32,512]{3,2,1,0:T(8,128)(2,1)S(1)} %get-tuple-element.68), channel_id=1, source_target_pairs={{0,0},{1,1},{2,64},{3,65},{64,2},{65,3},{66,66},{67,67},{128,128},... | collective-permute-start | bytes 786440 | tf_op jit(solution)/shard_map/ppermute | solution.py:38
  182.1 2.1 %collective-permute-start.15 = (bf16[1,8,32,512]{3,2,1,0:T(8,128)(2,1)S(1)}, bf16[1,8,32,512]{3,2,1,0:T(8,128)(2,1)S(1)}, u32[]{:S(2)}, u32[]{:S(2)}) collective-permute-start(bf16[1,8,32,512]{3,2,1,0:T(8,128)(2,1)S(1)} %get-tuple-element.69), channel_id=1, source_target_pairs={{0,0},{1,1},{2,64},{3,65},{64,2},{65,3},{66,66},{67,67},{128,128},... | collective-permute-start | bytes 786440 | tf_op jit(solution)/shard_map/ppermute | solution.py:38
  184.8 6.8 %collective-permute-done.14 = bf16[1,8,32,512]{3,2,1,0:T(8,128)(2,1)S(1)} collective-permute-done((bf16[1,8,32,512]{3,2,1,0:T(8,128)(2,1)S(1)}, bf16[1,8,32,512]{3,2,1,0:T(8,128)(2,1)S(1)}, u32[]{:S(2)}, u32[]{:S(2)}) %collective-permute-start.14) | collective-permute-done | bytes 262176 | tf_op jit(solution)/shard_map/ppermute | solution.py:38
  191.5 2.8 %collective-permute-done.15 = bf16[1,8,32,512]{3,2,1,0:T(8,128)(2,1)S(1)} collective-permute-done((bf16[1,8,32,512]{3,2,1,0:T(8,128)(2,1)S(1)}, bf16[1,8,32,512]{3,2,1,0:T(8,128)(2,1)S(1)}, u32[]{:S(2)}, u32[]{:S(2)}) %collective-permute-start.15) | collective-permute-done | bytes 262176 | tf_op jit(solution)/shard_map/ppermute | solution.py:38
  194.3 1.9 copy.17
  (67 shorter events, 21.4 us)
Async XLA Ops:
  0.7 5.5 %copy-start.12 = (s32[1,8]{1,0:T(1,128)S(1)}, s32[1,8]{1,0:T(1,128)}, u32[]{:S(2)}) copy-start(s32[1,8]{1,0:T(1,128)} %param.12) | copy-start | bytes 100
  0.7 9.2 %copy-start.13 = (s32[1,128,2]{1,2,0:T(2,128)S(1)}, s32[1,128,2]{1,2,0:T(2,128)}, u32[]{:S(2)}) copy-start(s32[1,128,2]{1,2,0:T(2,128)} %param.11) | copy-start | bytes 3076
  0.7 9.2 %copy-start.11 = (bf16[1,128,2]{1,2,0:T(2,128)(2,1)S(1)}, bf16[1,128,2]{1,2,0:T(2,128)(2,1)}, u32[]{:S(2)}) copy-start(bf16[1,128,2]{1,2,0:T(2,128)(2,1)} %param.10) | copy-start | bytes 1540
  2.9 7.7 %collective-permute-start.1 = (bf16[24,128,128]{2,1,0:T(8,128)(2,1)S(1)}, bf16[24,128,128]{2,1,0:T(8,128)(2,1)S(1)}, u32[]{:S(2)}, u32[]{:S(2)}) collective-permute-start(bf16[24,128,128]{2,1,0:T(8,128)(2,1)S(1)} %pad_maximum_fusion), channel_id=1, source_target_pairs={{0,64},{1,65},{2,66},{3,67},{64,0},{65,1},{66,2},{67,3},{128,192},... | collective-permute-start | bytes 2359304 | tf_op jit(solution)/shard_map/ppermute | solution.py:38
  6.2 3.8 %collective-permute-start = (s32[8]{0:T(128)S(1)}, s32[8]{0:T(128)S(1)}, u32[]{:S(2)}, u32[]{:S(2)}) collective-permute-start(s32[8]{0:T(128)S(1)} %bitcast.32), channel_id=1, source_target_pairs={{0,64},{1,65},{2,66},{3,67},{64,0},{65,1},{66,2},{67,3},{128,192},... | collective-permute-start | bytes 104 | tf_op jit(solution)/shard_map/ppermute | solution.py:38
  6.3 23.3 %collective-permute-start.3 = (bf16[128,2048]{1,0:T(8,128)(2,1)}, bf16[128,2048]{1,0:T(8,128)(2,1)S(1)}, u32[]{:S(2)}, u32[]{:S(2)}) collective-permute-start(bf16[128,2048]{1,0:T(8,128)(2,1)} %bitcast.6), channel_id=1, source_target_pairs={{0,0},{1,1},{2,64},{3,65},{64,2},{65,3},{66,66},{67,67},{128,128},... | collective-permute-start | bytes 1572872 | tf_op jit(solution)/shard_map/ppermute | solution.py:38
  14.9 20.1 %collective-permute-start.4 = (bf16[128,2048]{1,0:T(8,128)(2,1)}, bf16[128,2048]{1,0:T(8,128)(2,1)S(1)}, u32[]{:S(2)}, u32[]{:S(2)}) collective-permute-start(bf16[128,2048]{1,0:T(8,128)(2,1)} %bitcast.11), channel_id=1, source_target_pairs={{0,0},{1,1},{2,64},{3,65},{64,2},{65,3},{66,66},{67,67},{128,128},... | collective-permute-start | bytes 1572872 | tf_op jit(solution)/shard_map/ppermute | solution.py:38
  17.9 17.1 %collective-permute-start.2 = (bf16[8,128]{1,0:T(8,128)(2,1)S(1)}, bf16[8,128]{1,0:T(8,128)(2,1)S(1)}, u32[]{:S(2)}, u32[]{:S(2)}) collective-permute-start(bf16[8,128]{1,0:T(8,128)(2,1)S(1)} %maximum_maximum_fusion), channel_id=1, source_target_pairs={{0,0},{1,1},{2,64},{3,65},{64,2},{65,3},{66,66},{67,67},{128,128},... | collective-permute-start | bytes 6152 | tf_op jit(solution)/shard_map/ppermute | solution.py:38
  21.4 25.2 %all-to-all-start = ((bf16[16,384,128]{2,1,0:T(8,128)(2,1)}), bf16[16,384,128]{2,1,0:T(8,128)(2,1)}, u32[]{:S(2)}, u32[]{:S(2)}) async-start(bf16[16,384,128]{2,1,0:T(8,128)(2,1)} %shard_map.119), calls=%async_computation | async-start | bytes 3145728 | tf_op jit(solution)/shard_map/all_to_all | solution.py:42
  35.0 1.7 copy-start.5
  36.7 1.5 copy-start.2
  46.5 31.0 %collective-permute-start.5 = (bf16[16,384,128]{2,1,0:T(8,128)(2,1)}, bf16[16,384,128]{2,1,0:T(8,128)(2,1)}, u32[]{:S(2)}, u32[]{:S(2)}) collective-permute-start(bf16[16,384,128]{2,1,0:T(8,128)(2,1)} %all-to-all-done.w0), channel_id=1, source_target_pairs={{0,1},{1,0},{2,3},{3,2},{64,65},{65,64},{66,67},{67,66},{128,129},... | collective-permute-start | bytes 4718600 | tf_op jit(solution)/shard_map/ppermute | solution.py:38
  48.2 35.5 %all-to-all-start.1 = ((bf16[16,40,2048]{2,1,0:T(8,128)(2,1)}), bf16[16,40,2048]{2,1,0:T(8,128)(2,1)S(1)}, u32[]{:S(2)}, u32[]{:S(2)}) async-start(bf16[16,40,2048]{2,1,0:T(8,128)(2,1)} %bitcast.29), calls=%async_computation.1 | async-start | bytes 5242880 | tf_op jit(solution)/shard_map/all_to_all | solution.py:42
  51.9 25.6 %collective-permute-start.6 = (bf16[16,384,128]{2,1,0:T(8,128)(2,1)}, bf16[16,384,128]{2,1,0:T(8,128)(2,1)S(1)}, u32[]{:S(2)}, u32[]{:S(2)}) collective-permute-start(bf16[16,384,128]{2,1,0:T(8,128)(2,1)} %all-to-all-done.w0), channel_id=1, source_target_pairs={{0,64},{1,65},{2,66},{3,67},{64,0},{65,1},{66,2},{67,3},{128,192},... | collective-permute-start | bytes 4718600 | tf_op jit(solution)/shard_map/ppermute | solution.py:38
  77.5 6.2 %collective-permute-start.7 = (bf16[16,384,128]{2,1,0:T(8,128)(2,1)}, bf16[16,384,128]{2,1,0:T(8,128)(2,1)}, u32[]{:S(2)}, u32[]{:S(2)}) collective-permute-start(bf16[16,384,128]{2,1,0:T(8,128)(2,1)} %collective-permute-done.5.w1), channel_id=1, source_target_pairs={{0,64},{1,65},{2,66},{3,67},{64,0},{65,1},{66,2},{67,3},{128,192},... | collective-permute-start | bytes 4718600 | tf_op jit(solution)/shard_map/ppermute | solution.py:38
  77.5 1.2 copy-start.8
  83.7 1.4 copy-start.9
  95.6 5.4 %copy-start.4 = (bf16[384,2048]{1,0:T(8,128)(2,1)}, bf16[384,2048]{1,0:T(8,128)(2,1)S(1)}, u32[]{:S(2)}) copy-start(bf16[384,2048]{1,0:T(8,128)(2,1)S(1)} %get-tuple-element.51) | copy-start | bytes 4718596
  96.9 4.1 %collective-permute-start.8 = (bf16[2,16,32,512]{3,2,1,0:T(8,128)(2,1)S(1)}, bf16[2,16,32,512]{3,2,1,0:T(8,128)(2,1)S(1)}, u32[]{:S(2)}, u32[]{:S(2)}) collective-permute-start(bf16[2,16,32,512]{3,2,1,0:T(8,128)(2,1)S(1)} %get-tuple-element.54), channel_id=1, source_target_pairs={{0,64},{1,65},{2,66},{3,67},{64,0},{65,1},{66,2},{67,3},{128,192},... | collective-permute-start | bytes 3145736 | tf_op jit(solution)/shard_map/ppermute | solution.py:38
  103.0 18.8 %collective-permute-start.11 = (bf16[2,16,64,512]{3,2,1,0:T(8,128)(2,1)}, bf16[2,16,64,512]{3,2,1,0:T(8,128)(2,1)}, u32[]{:S(2)}, u32[]{:S(2)}) collective-permute-start(bf16[2,16,64,512]{3,2,1,0:T(8,128)(2,1)} %get-tuple-element.61), channel_id=1, source_target_pairs={{0,64},{1,65},{2,66},{3,67},{64,0},{65,1},{66,2},{67,3},{128,192},... | collective-permute-start | bytes 6291464 | tf_op jit(solution)/shard_map/ppermute | solution.py:38
  103.5 31.1 %all-to-all-start.2 = ((bf16[16,24,2048]{2,1,0:T(8,128)(2,1)}), bf16[16,24,2048]{2,1,0:T(8,128)(2,1)}, u32[]{:S(2)}, u32[]{:S(2)}) async-start(bf16[16,24,2048]{2,1,0:T(8,128)(2,1)} %bitcast.30), calls=%async_computation.2 | async-start | bytes 3145728 | tf_op jit(solution)/shard_map/all_to_all | solution.py:42
  107.9 17.4 %copy-start.1 = (bf16[2,16,32,512]{3,2,1,0:T(8,128)(2,1)S(1)}, bf16[2,16,32,512]{3,2,1,0:T(8,128)(2,1)}, u32[]{:S(2)}) copy-start(bf16[2,16,32,512]{3,2,1,0:T(8,128)(2,1)} %copy-done) | copy-start | bytes 3145732
  107.9 13.9 %collective-permute-start.9 = (bf16[16,32,512]{2,1,0:T(8,128)(2,1)}, bf16[16,32,512]{2,1,0:T(8,128)(2,1)S(1)}, u32[]{:S(2)}, u32[]{:S(2)}) collective-permute-start(bf16[16,32,512]{2,1,0:T(8,128)(2,1)} %copy-done.7), channel_id=1, source_target_pairs={{0,1},{1,0},{2,3},{3,2},{64,65},{65,64},{66,67},{67,66},{128,129},... | collective-permute-start | bytes 1572872 | tf_op jit(solution)/shard_map/ppermute | solution.py:38
  125.3 26.3 %collective-permute-start.12 = (bf16[16,64,512]{2,1,0:T(8,128)(2,1)}, bf16[16,64,512]{2,1,0:T(8,128)(2,1)}, u32[]{:S(2)}, u32[]{:S(2)}) collective-permute-start(bf16[16,64,512]{2,1,0:T(8,128)(2,1)} %shard_map.127), channel_id=1, source_target_pairs={{0,1},{1,0},{2,3},{3,2},{64,65},{65,64},{66,67},{67,66},{128,129},... | collective-permute-start | bytes 3145736 | tf_op jit(solution)/shard_map/ppermute | solution.py:38
  134.6 14.1 %all-to-all-start.3 = ((bf16[16,32,512]{2,1,0:T(8,128)(2,1)}), bf16[16,32,512]{2,1,0:T(8,128)(2,1)S(1)}, u32[]{:S(2)}, u32[]{:S(2)}) async-start(bf16[16,32,512]{2,1,0:T(8,128)(2,1)} %copy-done.3), calls=%async_computation.3 | async-start | bytes 1048576 | tf_op jit(solution)/shard_map/all_to_all | solution.py:42
  138.2 1.0 copy-start.6
  148.7 28.3 %collective-permute-start.10 = (bf16[128,2048]{1,0:T(8,128)(2,1)S(1)}, bf16[128,2048]{1,0:T(8,128)(2,1)}, u32[]{:S(2)}, u32[]{:S(2)}) collective-permute-start(bf16[128,2048]{1,0:T(8,128)(2,1)S(1)} %get-tuple-element.63), channel_id=1, source_target_pairs={{0,192},{1,193},{2,0},{3,1},{64,194},{65,195},{66,2},{67,3},{128,6... | collective-permute-start | bytes 1572872 | tf_op jit(solution)/shard_map/ppermute | solution.py:38
  155.3 21.6 %all-to-all-start.4 = ((bf16[16,64,512]{2,1,0:T(8,128)(2,1)}), bf16[16,64,512]{2,1,0:T(8,128)(2,1)S(1)}, u32[]{:S(2)}, u32[]{:S(2)}) async-start(bf16[16,64,512]{2,1,0:T(8,128)(2,1)} %shard_map.128), calls=%async_computation.4 | async-start | bytes 2097152 | tf_op jit(solution)/shard_map/all_to_all | solution.py:42
  159.9 24.3 %collective-permute-start.16 = (bf16[1,8,32,512]{3,2,1,0:T(8,128)(2,1)S(1)}, bf16[1,8,32,512]{3,2,1,0:T(8,128)(2,1)S(1)}, u32[]{:S(2)}, u32[]{:S(2)}) collective-permute-start(bf16[1,8,32,512]{3,2,1,0:T(8,128)(2,1)S(1)} %shard_map.130), channel_id=1, source_target_pairs={{0,0},{1,1},{2,64},{3,65},{64,2},{65,3},{66,66},{67,67},{128,128},... | collective-permute-start | bytes 786440 | tf_op jit(solution)/shard_map/ppermute | solution.py:38
  166.0 11.0 %collective-permute-start.13 = (bf16[8,128]{1,0:T(8,128)(2,1)S(1)}, bf16[8,128]{1,0:T(8,128)(2,1)S(1)}, u32[]{:S(2)}, u32[]{:S(2)}) collective-permute-start(bf16[8,128]{1,0:T(8,128)(2,1)S(1)} %get-tuple-element.65), channel_id=1, source_target_pairs={{0,0},{1,1},{2,64},{3,65},{64,2},{65,3},{66,66},{67,67},{128,128},... | collective-permute-start | bytes 6152 | tf_op jit(solution)/shard_map/ppermute | solution.py:38
  177.8 13.8 %collective-permute-start.14 = (bf16[1,8,32,512]{3,2,1,0:T(8,128)(2,1)S(1)}, bf16[1,8,32,512]{3,2,1,0:T(8,128)(2,1)S(1)}, u32[]{:S(2)}, u32[]{:S(2)}) collective-permute-start(bf16[1,8,32,512]{3,2,1,0:T(8,128)(2,1)S(1)} %get-tuple-element.68), channel_id=1, source_target_pairs={{0,0},{1,1},{2,64},{3,65},{64,2},{65,3},{66,66},{67,67},{128,128},... | collective-permute-start | bytes 786440 | tf_op jit(solution)/shard_map/ppermute | solution.py:38
  182.1 12.2 %collective-permute-start.15 = (bf16[1,8,32,512]{3,2,1,0:T(8,128)(2,1)S(1)}, bf16[1,8,32,512]{3,2,1,0:T(8,128)(2,1)S(1)}, u32[]{:S(2)}, u32[]{:S(2)}) collective-permute-start(bf16[1,8,32,512]{3,2,1,0:T(8,128)(2,1)S(1)} %get-tuple-element.69), channel_id=1, source_target_pairs={{0,0},{1,1},{2,64},{3,65},{64,2},{65,3},{66,66},{67,67},{128,128},... | collective-permute-start | bytes 786440 | tf_op jit(solution)/shard_map/ppermute | solution.py:38
  (4 other events, 3.6 us)

commit v6 on v5

--- a/solution.py
+++ b/solution.py
@@ -352,7 +352,7 @@
     refs[-1][...] = total.astype(BF)
 
 
-def add(which, pairs, *more):
+def add(which, pairs, *more, cost=0):
     shape = pairs[0].shape[1:]
     block = (4,) + shape[1:]
     pair = pl.BlockSpec((1,) + block, lambda n: (which, n, 0, 0))
@@ -364,8 +364,21 @@
         in_specs=[pair, pair] + [one] * len(more),
         out_specs=one,
         compiler_params=vmem(16),
-        cost_estimate=pl.CostEstimate(flops=0, bytes_accessed=1024, transcendentals=0),
+        cost_estimate=pl.CostEstimate(flops=cost, bytes_accessed=1024, transcendentals=0),
     )(*pairs, *more)
+
+
+def keep_kernel(in_ref, out_ref):
+    out_ref[...] = in_ref[...]
+
+
+def keep(x):
+    return pl.pallas_call(
+        keep_kernel,
+        out_shape=jax.ShapeDtypeStruct(x.shape, x.dtype),
+        compiler_params=vmem(8),
+        cost_estimate=pl.CostEstimate(flops=0, bytes_accessed=MIB, transcendentals=0),
+    )(x)
 
 
 def shards(tokens_in, grad_out, route_weight, slot_of, replica_of, w_gate, w_up, w_down):
@@ -414,18 +427,18 @@
     got, _ = lax.optimization_barrier((move(sent, NEAR), pair))
     down = add(0, down, got)
     pair = (pair[0], move(pair[1], CORES))
-    got, sent = lax.optimization_barrier((got, add(1, pair)))
+    got, sent = lax.optimization_barrier((got, add(1, pair, cost=10**11)))
     sent = move(sent, NEAR)
 
     sect, route = join_rows(notes, back, g)
     route = move(route, TURN)
     pair = add(0, pair, sent)
     sect, down = lax.optimization_barrier((sect, spread(down)))
-    grad_in = move(sect, BEHIND)
+    grad_in = keep(move(sect, BEHIND))
 
     (down,) = merge_slots(replicas, down, 10**11)
     down = move(down, TURN)
-    pair, route, _ = lax.optimization_barrier((spread(pair), route, grad_in))
+    pair, route, grad_in = lax.optimization_barrier((spread(pair), route, grad_in))
     gate, up = (move(part, TURN) for part in merge_slots(replicas, pair, 0))
     return (grad_in[None], route[0:2].T[None], gate, up, down)
 

time: 199 us -> 197 us (0.990)
  waiting for transfers between devices: 93.6 us -> 87.3 us
  Pallas kernels: 32 us -> 37 us
    ppermute x17, waiting for transfers between devices: 64.8 us -> 57.9 us  [move(): return lax.ppermute(x, ('pipe', 'dp'), pairs)]
    pallas_call x4, Pallas kernels: 7.65 us -> 12.3 us  [add(): pl.pallas_call(add_kernel, out_shape=jax.ShapeDtypeStruct(shape, BF), gri...]
    unnamed x32 -> x33, local copies, waits for them, and re-layouts: 12.7 us -> 12.4 us
  transfers between devices with their start and end apart: 22 -> 22, of which waited for: 11 -> 11; matrix products, arithmetic and copies ran while one was open for 1% -> 1% of each run, Pallas kernels for 10% -> 12%
where the time goes in v6:
time: 197 us; the launch traced here: 196 us
  waiting for transfers between devices  87.3 us (44%)
  starting transfers between devices  54.7 us (28%)
  Pallas kernels  37 us (19%)
  local copies, waits for them, and re-layouts  15.1 us (8%)
    ppermute x17, waiting for transfers between devices, move(): return lax.ppermute(x, ('pipe', 'dp'), pairs)  57.9 us
    ppermute x17, starting transfers between devices, move(): return lax.ppermute(x, ('pipe', 'dp'), pairs)  33.2 us
    all_to_all x5, waiting for transfers between devices, spread(): return lax.all_to_all(x, 'expert', split_axis=0, concat_axis=0, tiled=True)  29.4 us
    all_to_all x5, starting transfers between devices, spread(): return lax.all_to_all(x, 'expert', split_axis=0, concat_axis=0, tiled=True)  21.5 us
    unnamed x33, local copies, waits for them, and re-layouts  12.4 us
    pallas_call x4, Pallas kernels, add(): pl.pallas_call(add_kernel, out_shape=jax.ShapeDtypeStruct(shape, BF), gri...  12.3 us
    pallas_call x1, Pallas kernels, expert_rows(): pl.pallas_call(expert_kernel, out_shape=[jax.ShapeDtypeStruct((SLOTS * BA...  10.5 us
    pallas_call x2, Pallas kernels, weight_sums(): pl.pallas_call(functools.partial(sums_kernel, kinds), out_shape=[shape, s...  5.32 us
  transfers between devices with their start and end apart: 22, of which 11 were waited for; matrix products, arithmetic and copies ran while one was open for 1% of the time, Pallas kernels for 12%

profile of v6, /device:TPU:1, one launch (start us, length us, event | category | flops | bytes accessed | tf_op | source)
XLA Modules:
  0.0 195.9 jit_solution(4170708038663254167)
XLA Ops:
  2.9 3.3 %collective-permute-start.1 = (bf16[24,128,128]{2,1,0:T(8,128)(2,1)S(1)}, bf16[24,128,128]{2,1,0:T(8,128)(2,1)S(1)}, u32[]{:S(2)}, u32[]{:S(2)}) collective-permute-start(bf16[24,128,128]{2,1,0:T(8,128)(2,1)S(1)} %pad_maximum_fusion), channel_id=1, source_target_pairs={{0,64},{1,65},{2,66},{3,67},{64,0},{65,1},{66,2},{67,3},{128,192},... | collective-permute-start | bytes 2359304 | tf_op jit(solution)/shard_map/ppermute | solution.py:38
  6.3 3.4 %collective-permute-start.3 = (bf16[128,2048]{1,0:T(8,128)(2,1)}, bf16[128,2048]{1,0:T(8,128)(2,1)S(1)}, u32[]{:S(2)}, u32[]{:S(2)}) collective-permute-start(bf16[128,2048]{1,0:T(8,128)(2,1)} %bitcast.6), channel_id=1, source_target_pairs={{0,0},{1,1},{2,64},{3,65},{64,2},{65,3},{66,66},{67,67},{128,128},... | collective-permute-start | bytes 1572872 | tf_op jit(solution)/shard_map/ppermute | solution.py:38
  11.5 3.4 %shard_map.119 = bf16[16,384,128]{2,1,0:T(8,128)(2,1)} custom-call(s32[18]{0:T(128)} %pad_add_fusion.info, bf16[1,8,128,512]{3,2,1,0:T(8,128)(2,1)} %gate.1, bf16[1,8,128,512]{3,2,1,0:T(8,128)(2,1)} %up.1, bf16[1,8,128,512]{3,2,1,0:T(8,128)(2,1)} %down.1, bf16[24,128,128]{2,1,0:T(8,128)(2,1)} %copy-done.11), custom_call_target="tpu_custom_call" | custom-call | bytes 4194304 | tf_op jit(solution)/shard_map/pallas_call | solution.py:100
  14.9 3.0 %collective-permute-start.4 = (bf16[128,2048]{1,0:T(8,128)(2,1)}, bf16[128,2048]{1,0:T(8,128)(2,1)S(1)}, u32[]{:S(2)}, u32[]{:S(2)}) collective-permute-start(bf16[128,2048]{1,0:T(8,128)(2,1)} %bitcast.11), channel_id=1, source_target_pairs={{0,0},{1,1},{2,64},{3,65},{64,2},{65,3},{66,66},{67,67},{128,128},... | collective-permute-start | bytes 1572872 | tf_op jit(solution)/shard_map/ppermute | solution.py:38
  17.9 3.5 %collective-permute-start.2 = (bf16[8,128]{1,0:T(8,128)(2,1)S(1)}, bf16[8,128]{1,0:T(8,128)(2,1)S(1)}, u32[]{:S(2)}, u32[]{:S(2)}) collective-permute-start(bf16[8,128]{1,0:T(8,128)(2,1)S(1)} %maximum_maximum_fusion), channel_id=1, source_target_pairs={{0,0},{1,1},{2,64},{3,65},{64,2},{65,3},{66,66},{67,67},{128,128},... | collective-permute-start | bytes 6152 | tf_op jit(solution)/shard_map/ppermute | solution.py:38
  21.4 6.8 %all-to-all-start = ((bf16[16,384,128]{2,1,0:T(8,128)(2,1)}), bf16[16,384,128]{2,1,0:T(8,128)(2,1)}, u32[]{:S(2)}, u32[]{:S(2)}) async-start(bf16[16,384,128]{2,1,0:T(8,128)(2,1)} %shard_map.119), calls=%async_computation | async-start | bytes 3145728 | tf_op jit(solution)/shard_map/all_to_all | solution.py:42
  29.6 5.4 %collective-permute-done.2.notes_ref = bf16[8,128]{1,0:T(8,128)(2,1)S(1)} collective-permute-done((bf16[8,128]{1,0:T(8,128)(2,1)S(1)}, bf16[8,128]{1,0:T(8,128)(2,1)S(1)}, u32[]{:S(2)}, u32[]{:S(2)}) %collective-permute-start.2) | collective-permute-done | bytes 2080 | tf_op jit(solution)/shard_map/ppermute | solution.py:38
  35.0 1.7 shard_map.120
  38.2 8.4 %all-to-all-done.w0 = bf16[16,384,128]{2,1,0:T(8,128)(2,1)} async-done(((bf16[16,384,128]{2,1,0:T(8,128)(2,1)}), bf16[16,384,128]{2,1,0:T(8,128)(2,1)}, u32[]{:S(2)}, u32[]{:S(2)}) %all-to-all-start) | async-done | bytes 1572896 | tf_op jit(solution)/shard_map/all_to_all | solution.py:42
  48.2 3.7 %all-to-all-start.1 = ((bf16[16,40,2048]{2,1,0:T(8,128)(2,1)}), bf16[16,40,2048]{2,1,0:T(8,128)(2,1)S(1)}, u32[]{:S(2)}, u32[]{:S(2)}) async-start(bf16[16,40,2048]{2,1,0:T(8,128)(2,1)} %bitcast.30), calls=%async_computation.1 | async-start | bytes 5242880 | tf_op jit(solution)/shard_map/all_to_all | solution.py:42
  52.0 25.5 %collective-permute-done.5.w1 = bf16[16,384,128]{2,1,0:T(8,128)(2,1)} collective-permute-done((bf16[16,384,128]{2,1,0:T(8,128)(2,1)}, bf16[16,384,128]{2,1,0:T(8,128)(2,1)}, u32[]{:S(2)}, u32[]{:S(2)}) %collective-permute-start.5) | collective-permute-done | bytes 1572896 | tf_op jit(solution)/shard_map/ppermute | solution.py:38
  78.8 4.9 %all-to-all-done.1 = bf16[16,40,2048]{2,1,0:T(8,128)(2,1)S(1)} async-done(((bf16[16,40,2048]{2,1,0:T(8,128)(2,1)}), bf16[16,40,2048]{2,1,0:T(8,128)(2,1)S(1)}, u32[]{:S(2)}, u32[]{:S(2)}) %all-to-all-start.1) | async-done | bytes 2621472 | tf_op jit(solution)/shard_map/all_to_all | solution.py:42
  85.1 10.5 %shard_map.121 = (bf16[384,2048]{1,0:T(8,128)(2,1)S(1)}, bf16[320,2048]{1,0:T(8,128)(2,1)S(1)}, bf16[320,2048]{1,0:T(8,128)(2,1)S(1)}, bf16[320,512]{1,0:T(8,128)(2,1)S(1)}, bf16[320,1024]{1,0:T(8,128)(2,1)S(1)}) custom-call(s32[1]{0:T(128)} %bitcast.info, bf16[640,2048]{1,0:T(8,128)(2,1)S(1)} %bitcast.29, bf16[16,384,128]{2,1,0:T(8,128)(2,1)} %all-to-all-done.w0, ...), custom_call_target="tpu_custom_call" | custom-call | flops 5368709120 | bytes 14680064 | tf_op jit(solution)/shard_map/pallas_call | solution.py:223
  97.0 4.0 %shard_map.124 = (bf16[2,16,64,512]{3,2,1,0:T(8,128)(2,1)S(1)}, bf16[2,16,64,512]{3,2,1,0:T(8,128)(2,1)}) custom-call(s32[1]{0:T(128)} %bitcast.info, bf16[320,2048]{1,0:T(8,128)(2,1)S(1)} %get-tuple-element.54.a_ref, bf16[320,1024]{1,0:T(8,128)(2,1)S(1)} %get-tuple-element.55.b_ref), custom_call_target="tpu_custom_call" | custom-call | flops 10000000000 | bytes 1024 | tf_op jit(solution)/shard_map/pallas_call | solution.py:274
  101.0 1.9 shard_map.123
  104.5 3.7 %all-to-all-start.3 = ((bf16[16,24,2048]{2,1,0:T(8,128)(2,1)}), bf16[16,24,2048]{2,1,0:T(8,128)(2,1)S(1)}, u32[]{:S(2)}, u32[]{:S(2)}) async-start(bf16[16,24,2048]{2,1,0:T(8,128)(2,1)} %bitcast.31), calls=%async_computation.3 | async-start | bytes 3145728 | tf_op jit(solution)/shard_map/all_to_all | solution.py:42
  108.3 10.1 %collective-permute-done.10.refs_2_ = bf16[16,32,512]{2,1,0:T(8,128)(2,1)} collective-permute-done((bf16[16,32,512]{2,1,0:T(8,128)(2,1)}, bf16[16,32,512]{2,1,0:T(8,128)(2,1)}, u32[]{:S(2)}, u32[]{:S(2)}) %collective-permute-start.10) | collective-permute-done | bytes 524320 | tf_op jit(solution)/shard_map/ppermute | solution.py:38
  120.0 3.5 %shard_map.125 = bf16[16,64,512]{2,1,0:T(8,128)(2,1)} custom-call(bf16[2,16,64,512]{3,2,1,0:T(8,128)(2,1)S(1)} %copy-done.4, bf16[2,16,64,512]{3,2,1,0:T(8,128)(2,1)} %collective-permute-done.9.refs_1_), custom_call_target="tpu_custom_call" | custom-call | flops 99999997952 | bytes 1024 | tf_op jit(solution)/shard_map/pallas_call | solution.py:360
  123.4 3.2 %shard_map.128 = bf16[16,32,512]{2,1,0:T(8,128)(2,1)} custom-call(bf16[2,16,32,512]{3,2,1,0:T(8,128)(2,1)S(1)} %get-tuple-element.52.refs_0_, bf16[2,16,32,512]{3,2,1,0:T(8,128)(2,1)S(1)} %copy-done.1, bf16[16,32,512]{2,1,0:T(8,128)(2,1)} %collective-permute-done.10.refs_2_), custom_call_target="tpu_custom_call" | custom-call | bytes 1024 | tf_op jit(solution)/shard_map/pallas_call | solution.py:360
  126.7 7.1 %all-to-all-done.3 = bf16[16,24,2048]{2,1,0:T(8,128)(2,1)S(1)} async-done(((bf16[16,24,2048]{2,1,0:T(8,128)(2,1)}), bf16[16,24,2048]{2,1,0:T(8,128)(2,1)S(1)}, u32[]{:S(2)}, u32[]{:S(2)}) %all-to-all-start.3) | async-done | bytes 1572896 | tf_op jit(solution)/shard_map/all_to_all | solution.py:42
  133.8 3.6 %all-to-all-start.4 = ((bf16[16,32,512]{2,1,0:T(8,128)(2,1)}), bf16[16,32,512]{2,1,0:T(8,128)(2,1)S(1)}, u32[]{:S(2)}, u32[]{:S(2)}) async-start(bf16[16,32,512]{2,1,0:T(8,128)(2,1)} %shard_map.128), calls=%async_computation.4 | async-start | bytes 1048576 | tf_op jit(solution)/shard_map/all_to_all | solution.py:42
  138.8 9.0 %all-to-all-done.4.got_ref = bf16[16,32,512]{2,1,0:T(8,128)(2,1)S(1)} async-done(((bf16[16,32,512]{2,1,0:T(8,128)(2,1)}), bf16[16,32,512]{2,1,0:T(8,128)(2,1)S(1)}, u32[]{:S(2)}, u32[]{:S(2)}) %all-to-all-start.4) | async-done | bytes 524320 | tf_op jit(solution)/shard_map/all_to_all | solution.py:42
  147.8 3.4 %collective-permute-start.13 = (bf16[128,2048]{1,0:T(8,128)(2,1)}, bf16[128,2048]{1,0:T(8,128)(2,1)S(1)}, u32[]{:S(2)}, u32[]{:S(2)}) collective-permute-start(bf16[128,2048]{1,0:T(8,128)(2,1)} %get-tuple-element.66), channel_id=1, source_target_pairs={{0,192},{1,193},{2,0},{3,1},{64,194},{65,195},{66,2},{67,3},{128,6... | collective-permute-start | bytes 1572872 | tf_op jit(solution)/shard_map/ppermute | solution.py:38
  152.8 3.7 %shard_map.126 = bf16[16,64,512]{2,1,0:T(8,128)(2,1)} custom-call(bf16[2,16,64,512]{3,2,1,0:T(8,128)(2,1)S(1)} %copy-done.5, bf16[2,16,64,512]{3,2,1,0:T(8,128)(2,1)} %collective-permute-done.9.refs_1_, bf16[16,64,512]{2,1,0:T(8,128)(2,1)} %collective-permute-done.11.refs_2_), custom_call_target="tpu_custom_call" | custom-call | bytes 1024 | tf_op jit(solution)/shard_map/pallas_call | solution.py:360
  156.5 3.7 %all-to-all-start.2 = ((bf16[16,64,512]{2,1,0:T(8,128)(2,1)}), bf16[16,64,512]{2,1,0:T(8,128)(2,1)S(1)}, u32[]{:S(2)}, u32[]{:S(2)}) async-start(bf16[16,64,512]{2,1,0:T(8,128)(2,1)} %shard_map.126), calls=%async_computation.2 | async-start | bytes 2097152 | tf_op jit(solution)/shard_map/all_to_all | solution.py:42
  161.9 3.0 %collective-permute-start.16 = (bf16[1,8,32,512]{3,2,1,0:T(8,128)(2,1)S(1)}, bf16[1,8,32,512]{3,2,1,0:T(8,128)(2,1)S(1)}, u32[]{:S(2)}, u32[]{:S(2)}) collective-permute-start(bf16[1,8,32,512]{3,2,1,0:T(8,128)(2,1)S(1)} %shard_map.131), channel_id=1, source_target_pairs={{0,0},{1,1},{2,64},{3,65},{64,2},{65,3},{66,66},{67,67},{128,128},... | collective-permute-start | bytes 786440 | tf_op jit(solution)/shard_map/ppermute | solution.py:38
  164.9 3.4 %collective-permute-start.12 = (bf16[8,128]{1,0:T(8,128)(2,1)S(1)}, bf16[8,128]{1,0:T(8,128)(2,1)S(1)}, u32[]{:S(2)}, u32[]{:S(2)}) collective-permute-start(bf16[8,128]{1,0:T(8,128)(2,1)S(1)} %get-tuple-element.64), channel_id=1, source_target_pairs={{0,0},{1,1},{2,64},{3,65},{64,2},{65,3},{66,66},{67,67},{128,128},... | collective-permute-start | bytes 6152 | tf_op jit(solution)/shard_map/ppermute | solution.py:38
  169.2 5.5 %collective-permute-done.12 = bf16[8,128]{1,0:T(8,128)(2,1)S(1)} collective-permute-done((bf16[8,128]{1,0:T(8,128)(2,1)S(1)}, bf16[8,128]{1,0:T(8,128)(2,1)S(1)}, u32[]{:S(2)}, u32[]{:S(2)}) %collective-permute-start.12) | collective-permute-done | bytes 2080 | tf_op jit(solution)/shard_map/ppermute | solution.py:38
  175.5 5.8 %collective-permute-start.14 = (bf16[1,8,32,512]{3,2,1,0:T(8,128)(2,1)S(1)}, bf16[1,8,32,512]{3,2,1,0:T(8,128)(2,1)S(1)}, u32[]{:S(2)}, u32[]{:S(2)}) collective-permute-start(bf16[1,8,32,512]{3,2,1,0:T(8,128)(2,1)S(1)} %get-tuple-element.70), channel_id=1, source_target_pairs={{0,0},{1,1},{2,64},{3,65},{64,2},{65,3},{66,66},{67,67},{128,128},... | collective-permute-start | bytes 786440 | tf_op jit(solution)/shard_map/ppermute | solution.py:38
  181.3 1.9 collective-permute-start.15
  183.8 4.4 %collective-permute-done.14 = bf16[1,8,32,512]{3,2,1,0:T(8,128)(2,1)S(1)} collective-permute-done((bf16[1,8,32,512]{3,2,1,0:T(8,128)(2,1)S(1)}, bf16[1,8,32,512]{3,2,1,0:T(8,128)(2,1)S(1)}, u32[]{:S(2)}, u32[]{:S(2)}) %collective-permute-start.14) | collective-permute-done | bytes 262176 | tf_op jit(solution)/shard_map/ppermute | solution.py:38
  188.2 5.6 %collective-permute-done.15 = bf16[1,8,32,512]{3,2,1,0:T(8,128)(2,1)S(1)} collective-permute-done((bf16[1,8,32,512]{3,2,1,0:T(8,128)(2,1)S(1)}, bf16[1,8,32,512]{3,2,1,0:T(8,128)(2,1)S(1)}, u32[]{:S(2)}, u32[]{:S(2)}) %collective-permute-start.15) | collective-permute-done | bytes 262176 | tf_op jit(solution)/shard_map/ppermute | solution.py:38
  (69 shorter events, 24.8 us)
Async XLA Ops:
  0.7 5.5 %copy-start.13 = (s32[1,8]{1,0:T(1,128)S(1)}, s32[1,8]{1,0:T(1,128)}, u32[]{:S(2)}) copy-start(s32[1,8]{1,0:T(1,128)} %param.12) | copy-start | bytes 100
  0.7 9.2 %copy-start.14 = (s32[1,128,2]{1,2,0:T(2,128)S(1)}, s32[1,128,2]{1,2,0:T(2,128)}, u32[]{:S(2)}) copy-start(s32[1,128,2]{1,2,0:T(2,128)} %param.11) | copy-start | bytes 3076
  0.7 9.2 %copy-start.12 = (bf16[1,128,2]{1,2,0:T(2,128)(2,1)S(1)}, bf16[1,128,2]{1,2,0:T(2,128)(2,1)}, u32[]{:S(2)}) copy-start(bf16[1,128,2]{1,2,0:T(2,128)(2,1)} %param.10) | copy-start | bytes 1540
  2.9 7.7 %collective-permute-start.1 = (bf16[24,128,128]{2,1,0:T(8,128)(2,1)S(1)}, bf16[24,128,128]{2,1,0:T(8,128)(2,1)S(1)}, u32[]{:S(2)}, u32[]{:S(2)}) collective-permute-start(bf16[24,128,128]{2,1,0:T(8,128)(2,1)S(1)} %pad_maximum_fusion), channel_id=1, source_target_pairs={{0,64},{1,65},{2,66},{3,67},{64,0},{65,1},{66,2},{67,3},{128,192},... | collective-permute-start | bytes 2359304 | tf_op jit(solution)/shard_map/ppermute | solution.py:38
  6.2 3.8 %collective-permute-start = (s32[8]{0:T(128)S(1)}, s32[8]{0:T(128)S(1)}, u32[]{:S(2)}, u32[]{:S(2)}) collective-permute-start(s32[8]{0:T(128)S(1)} %bitcast.34), channel_id=1, source_target_pairs={{0,64},{1,65},{2,66},{3,67},{64,0},{65,1},{66,2},{67,3},{128,192},... | collective-permute-start | bytes 104 | tf_op jit(solution)/shard_map/ppermute | solution.py:38
  6.3 23.3 %collective-permute-start.3 = (bf16[128,2048]{1,0:T(8,128)(2,1)}, bf16[128,2048]{1,0:T(8,128)(2,1)S(1)}, u32[]{:S(2)}, u32[]{:S(2)}) collective-permute-start(bf16[128,2048]{1,0:T(8,128)(2,1)} %bitcast.6), channel_id=1, source_target_pairs={{0,0},{1,1},{2,64},{3,65},{64,2},{65,3},{66,66},{67,67},{128,128},... | collective-permute-start | bytes 1572872 | tf_op jit(solution)/shard_map/ppermute | solution.py:38
  14.9 20.1 %collective-permute-start.4 = (bf16[128,2048]{1,0:T(8,128)(2,1)}, bf16[128,2048]{1,0:T(8,128)(2,1)S(1)}, u32[]{:S(2)}, u32[]{:S(2)}) collective-permute-start(bf16[128,2048]{1,0:T(8,128)(2,1)} %bitcast.11), channel_id=1, source_target_pairs={{0,0},{1,1},{2,64},{3,65},{64,2},{65,3},{66,66},{67,67},{128,128},... | collective-permute-start | bytes 1572872 | tf_op jit(solution)/shard_map/ppermute | solution.py:38
  17.9 17.1 %collective-permute-start.2 = (bf16[8,128]{1,0:T(8,128)(2,1)S(1)}, bf16[8,128]{1,0:T(8,128)(2,1)S(1)}, u32[]{:S(2)}, u32[]{:S(2)}) collective-permute-start(bf16[8,128]{1,0:T(8,128)(2,1)S(1)} %maximum_maximum_fusion), channel_id=1, source_target_pairs={{0,0},{1,1},{2,64},{3,65},{64,2},{65,3},{66,66},{67,67},{128,128},... | collective-permute-start | bytes 6152 | tf_op jit(solution)/shard_map/ppermute | solution.py:38
  21.4 25.2 %all-to-all-start = ((bf16[16,384,128]{2,1,0:T(8,128)(2,1)}), bf16[16,384,128]{2,1,0:T(8,128)(2,1)}, u32[]{:S(2)}, u32[]{:S(2)}) async-start(bf16[16,384,128]{2,1,0:T(8,128)(2,1)} %shard_map.119), calls=%async_computation | async-start | bytes 3145728 | tf_op jit(solution)/shard_map/all_to_all | solution.py:42
  36.7 1.5 copy-start.2
  46.5 31.0 %collective-permute-start.5 = (bf16[16,384,128]{2,1,0:T(8,128)(2,1)}, bf16[16,384,128]{2,1,0:T(8,128)(2,1)}, u32[]{:S(2)}, u32[]{:S(2)}) collective-permute-start(bf16[16,384,128]{2,1,0:T(8,128)(2,1)} %all-to-all-done.w0), channel_id=1, source_target_pairs={{0,1},{1,0},{2,3},{3,2},{64,65},{65,64},{66,67},{67,66},{128,129},... | collective-permute-start | bytes 4718600 | tf_op jit(solution)/shard_map/ppermute | solution.py:38
  48.2 35.5 %all-to-all-start.1 = ((bf16[16,40,2048]{2,1,0:T(8,128)(2,1)}), bf16[16,40,2048]{2,1,0:T(8,128)(2,1)S(1)}, u32[]{:S(2)}, u32[]{:S(2)}) async-start(bf16[16,40,2048]{2,1,0:T(8,128)(2,1)} %bitcast.30), calls=%async_computation.1 | async-start | bytes 5242880 | tf_op jit(solution)/shard_map/all_to_all | solution.py:42
  51.9 25.6 %collective-permute-start.6 = (bf16[16,384,128]{2,1,0:T(8,128)(2,1)}, bf16[16,384,128]{2,1,0:T(8,128)(2,1)S(1)}, u32[]{:S(2)}, u32[]{:S(2)}) collective-permute-start(bf16[16,384,128]{2,1,0:T(8,128)(2,1)} %all-to-all-done.w0), channel_id=1, source_target_pairs={{0,64},{1,65},{2,66},{3,67},{64,0},{65,1},{66,2},{67,3},{128,192},... | collective-permute-start | bytes 4718600 | tf_op jit(solution)/shard_map/ppermute | solution.py:38
  77.5 6.2 %collective-permute-start.7 = (bf16[16,384,128]{2,1,0:T(8,128)(2,1)}, bf16[16,384,128]{2,1,0:T(8,128)(2,1)}, u32[]{:S(2)}, u32[]{:S(2)}) collective-permute-start(bf16[16,384,128]{2,1,0:T(8,128)(2,1)} %collective-permute-done.5.w1), channel_id=1, source_target_pairs={{0,64},{1,65},{2,66},{3,67},{64,0},{65,1},{66,2},{67,3},{128,192},... | collective-permute-start | bytes 4718600 | tf_op jit(solution)/shard_map/ppermute | solution.py:38
  95.6 5.4 %copy-start.6 = (bf16[384,2048]{1,0:T(8,128)(2,1)}, bf16[384,2048]{1,0:T(8,128)(2,1)S(1)}, u32[]{:S(2)}) copy-start(bf16[384,2048]{1,0:T(8,128)(2,1)S(1)} %get-tuple-element.63) | copy-start | bytes 4718596
  96.9 4.1 %collective-permute-start.8 = (bf16[2,16,32,512]{3,2,1,0:T(8,128)(2,1)S(1)}, bf16[2,16,32,512]{3,2,1,0:T(8,128)(2,1)S(1)}, u32[]{:S(2)}, u32[]{:S(2)}) collective-permute-start(bf16[2,16,32,512]{3,2,1,0:T(8,128)(2,1)S(1)} %get-tuple-element.53), channel_id=1, source_target_pairs={{0,64},{1,65},{2,66},{3,67},{64,0},{65,1},{66,2},{67,3},{128,192},... | collective-permute-start | bytes 3145736 | tf_op jit(solution)/shard_map/ppermute | solution.py:38
  101.0 1.9 copy-start.3
  104.0 14.3 %collective-permute-start.9 = (bf16[2,16,64,512]{3,2,1,0:T(8,128)(2,1)}, bf16[2,16,64,512]{3,2,1,0:T(8,128)(2,1)}, u32[]{:S(2)}, u32[]{:S(2)}) collective-permute-start(bf16[2,16,64,512]{3,2,1,0:T(8,128)(2,1)} %get-tuple-element.59), channel_id=1, source_target_pairs={{0,64},{1,65},{2,66},{3,67},{64,0},{65,1},{66,2},{67,3},{128,192},... | collective-permute-start | bytes 6291464 | tf_op jit(solution)/shard_map/ppermute | solution.py:38
  104.5 13.8 %collective-permute-start.10 = (bf16[16,32,512]{2,1,0:T(8,128)(2,1)}, bf16[16,32,512]{2,1,0:T(8,128)(2,1)}, u32[]{:S(2)}, u32[]{:S(2)}) collective-permute-start(bf16[16,32,512]{2,1,0:T(8,128)(2,1)} %shard_map.123), channel_id=1, source_target_pairs={{0,1},{1,0},{2,3},{3,2},{64,65},{65,64},{66,67},{67,66},{128,129},... | collective-permute-start | bytes 1572872 | tf_op jit(solution)/shard_map/ppermute | solution.py:38
  104.5 29.2 %all-to-all-start.3 = ((bf16[16,24,2048]{2,1,0:T(8,128)(2,1)}), bf16[16,24,2048]{2,1,0:T(8,128)(2,1)S(1)}, u32[]{:S(2)}, u32[]{:S(2)}) async-start(bf16[16,24,2048]{2,1,0:T(8,128)(2,1)} %bitcast.31), calls=%async_computation.3 | async-start | bytes 3145728 | tf_op jit(solution)/shard_map/all_to_all | solution.py:42
  108.2 15.2 %copy-start.1 = (bf16[2,16,32,512]{3,2,1,0:T(8,128)(2,1)S(1)}, bf16[2,16,32,512]{3,2,1,0:T(8,128)(2,1)}, u32[]{:S(2)}) copy-start(bf16[2,16,32,512]{3,2,1,0:T(8,128)(2,1)} %copy-done) | copy-start | bytes 3145732
  118.4 1.6 copy-start.4
  123.4 27.8 %collective-permute-start.11 = (bf16[16,64,512]{2,1,0:T(8,128)(2,1)}, bf16[16,64,512]{2,1,0:T(8,128)(2,1)}, u32[]{:S(2)}, u32[]{:S(2)}) collective-permute-start(bf16[16,64,512]{2,1,0:T(8,128)(2,1)} %shard_map.125), channel_id=1, source_target_pairs={{0,1},{1,0},{2,3},{3,2},{64,65},{65,64},{66,67},{67,66},{128,129},... | collective-permute-start | bytes 3145736 | tf_op jit(solution)/shard_map/ppermute | solution.py:38
  133.8 14.0 %all-to-all-start.4 = ((bf16[16,32,512]{2,1,0:T(8,128)(2,1)}), bf16[16,32,512]{2,1,0:T(8,128)(2,1)S(1)}, u32[]{:S(2)}, u32[]{:S(2)}) async-start(bf16[16,32,512]{2,1,0:T(8,128)(2,1)} %shard_map.128), calls=%async_computation.4 | async-start | bytes 1048576 | tf_op jit(solution)/shard_map/all_to_all | solution.py:42
  147.8 8.7 %copy-start.7 = (bf16[16,32,512]{2,1,0:T(8,128)(2,1)}, bf16[16,32,512]{2,1,0:T(8,128)(2,1)S(1)}, u32[]{:S(2)}) copy-start(bf16[16,32,512]{2,1,0:T(8,128)(2,1)S(1)} %all-to-all-done.4.got_ref) | copy-start | bytes 1572868
  147.8 20.6 %collective-permute-start.13 = (bf16[128,2048]{1,0:T(8,128)(2,1)}, bf16[128,2048]{1,0:T(8,128)(2,1)S(1)}, u32[]{:S(2)}, u32[]{:S(2)}) collective-permute-start(bf16[128,2048]{1,0:T(8,128)(2,1)} %get-tuple-element.66), channel_id=1, source_target_pairs={{0,192},{1,193},{2,0},{3,1},{64,194},{65,195},{66,2},{67,3},{128,6... | collective-permute-start | bytes 1572872 | tf_op jit(solution)/shard_map/ppermute | solution.py:38
  151.2 1.6 copy-start.5
  156.5 18.2 %all-to-all-start.2 = ((bf16[16,64,512]{2,1,0:T(8,128)(2,1)}), bf16[16,64,512]{2,1,0:T(8,128)(2,1)S(1)}, u32[]{:S(2)}, u32[]{:S(2)}) async-start(bf16[16,64,512]{2,1,0:T(8,128)(2,1)} %shard_map.126), calls=%async_computation.2 | async-start | bytes 2097152 | tf_op jit(solution)/shard_map/all_to_all | solution.py:42
  161.9 21.4 %collective-permute-start.16 = (bf16[1,8,32,512]{3,2,1,0:T(8,128)(2,1)S(1)}, bf16[1,8,32,512]{3,2,1,0:T(8,128)(2,1)S(1)}, u32[]{:S(2)}, u32[]{:S(2)}) collective-permute-start(bf16[1,8,32,512]{3,2,1,0:T(8,128)(2,1)S(1)} %shard_map.131), channel_id=1, source_target_pairs={{0,0},{1,1},{2,64},{3,65},{64,2},{65,3},{66,66},{67,67},{128,128},... | collective-permute-start | bytes 786440 | tf_op jit(solution)/shard_map/ppermute | solution.py:38
  164.9 9.8 %collective-permute-start.12 = (bf16[8,128]{1,0:T(8,128)(2,1)S(1)}, bf16[8,128]{1,0:T(8,128)(2,1)S(1)}, u32[]{:S(2)}, u32[]{:S(2)}) collective-permute-start(bf16[8,128]{1,0:T(8,128)(2,1)S(1)} %get-tuple-element.64), channel_id=1, source_target_pairs={{0,0},{1,1},{2,64},{3,65},{64,2},{65,3},{66,66},{67,67},{128,128},... | collective-permute-start | bytes 6152 | tf_op jit(solution)/shard_map/ppermute | solution.py:38
  175.5 12.7 %collective-permute-start.14 = (bf16[1,8,32,512]{3,2,1,0:T(8,128)(2,1)S(1)}, bf16[1,8,32,512]{3,2,1,0:T(8,128)(2,1)S(1)}, u32[]{:S(2)}, u32[]{:S(2)}) collective-permute-start(bf16[1,8,32,512]{3,2,1,0:T(8,128)(2,1)S(1)} %get-tuple-element.70), channel_id=1, source_target_pairs={{0,0},{1,1},{2,64},{3,65},{64,2},{65,3},{66,66},{67,67},{128,128},... | collective-permute-start | bytes 786440 | tf_op jit(solution)/shard_map/ppermute | solution.py:38
  181.3 12.5 %collective-permute-start.15 = (bf16[1,8,32,512]{3,2,1,0:T(8,128)(2,1)S(1)}, bf16[1,8,32,512]{3,2,1,0:T(8,128)(2,1)S(1)}, u32[]{:S(2)}, u32[]{:S(2)}) collective-permute-start(bf16[1,8,32,512]{3,2,1,0:T(8,128)(2,1)S(1)} %get-tuple-element.71), channel_id=1, source_target_pairs={{0,0},{1,1},{2,64},{3,65},{64,2},{65,3},{66,66},{67,67},{128,128},... | collective-permute-start | bytes 786440 | tf_op jit(solution)/shard_map/ppermute | solution.py:38
  (5 other events, 5.7 us)

commit v7 on v6

--- a/solution.py
+++ b/solution.py
@@ -319,23 +319,22 @@
     )(notes, back, g)
 
 
-def merge_kernel(info, got_ref, *refs):
-    outs, sums = refs[:-1], refs[-1]
-    for kind, out in enumerate(outs):
+def merge_kernel(info, got_ref, out, sums):
+    for kind in range(out.shape[0]):
         rows = slice(kind * OWN, (kind + 1) * OWN)
         for e in range(EXPERTS):
             sums[e] = got_ref[e, rows, :].astype(F32)
         for r in range(EXPERTS):
             e = info[r]
             sums[e] = sums[e] + got_ref[EXPERTS + r, rows, :].astype(F32)
-        out[0] = (sums[...] * SCALE).astype(BF)
+        out[kind] = (sums[...] * SCALE).astype(BF)
 
 
 def merge_slots(info, got, flops):
     kinds = got.shape[1] // OWN
     return pl.pallas_call(
         merge_kernel,
-        out_shape=[jax.ShapeDtypeStruct((1, EXPERTS, OWN, FF), BF)] * kinds,
+        out_shape=jax.ShapeDtypeStruct((kinds, EXPERTS, OWN, FF), BF),
         in_specs=[pl.BlockSpec(memory_space=pltpu.SMEM), pl.BlockSpec(memory_space=pltpu.VMEM)],
         scratch_shapes=[pltpu.VMEM((EXPERTS, OWN, FF), F32)],
         compiler_params=vmem(16),
@@ -352,7 +351,7 @@
     refs[-1][...] = total.astype(BF)
 
 
-def add(which, pairs, *more, cost=0):
+def add(which, pairs, *more, cost=0, room=16):
     shape = pairs[0].shape[1:]
     block = (4,) + shape[1:]
     pair = pl.BlockSpec((1,) + block, lambda n: (which, n, 0, 0))
@@ -363,7 +362,7 @@
         grid=(4,),
         in_specs=[pair, pair] + [one] * len(more),
         out_specs=one,
-        compiler_params=vmem(16),
+        compiler_params=vmem(room),
         cost_estimate=pl.CostEstimate(flops=cost, bytes_accessed=1024, transcendentals=0),
     )(*pairs, *more)
 
@@ -427,20 +426,20 @@
     got, _ = lax.optimization_barrier((move(sent, NEAR), pair))
     down = add(0, down, got)
     pair = (pair[0], move(pair[1], CORES))
-    got, sent = lax.optimization_barrier((got, add(1, pair, cost=10**11)))
+    got, sent = lax.optimization_barrier((got, add(1, pair, cost=10**11, room=56)))
     sent = move(sent, NEAR)
 
+    back, down = lax.optimization_barrier((back, down))
     sect, route = join_rows(notes, back, g)
     route = move(route, TURN)
-    pair = add(0, pair, sent)
-    sect, down = lax.optimization_barrier((sect, spread(down)))
+    pair = add(0, pair, sent, room=56)
+    down, pair = lax.optimization_barrier((spread(down), pair))
     grad_in = keep(move(sect, BEHIND))
 
-    (down,) = merge_slots(replicas, down, 10**11)
-    down = move(down, TURN)
-    pair, route, grad_in = lax.optimization_barrier((spread(pair), route, grad_in))
-    gate, up = (move(part, TURN) for part in merge_slots(replicas, pair, 0))
-    return (grad_in[None], route[0:2].T[None], gate, up, down)
+    down = move(merge_slots(replicas, down, 10**11), TURN)
+    pair, route, grad_in, down = lax.optimization_barrier((spread(pair), route, grad_in, down))
+    pair = move(merge_slots(replicas, pair, 0), TURN)
+    return (grad_in[None], route[0:2].T[None], pair[0:1], pair[1:2], down)
 
 
 def solution(mesh):

time: 197 us -> 194 us (0.985)
  starting transfers between devices: 54.7 us -> 49 us
  waiting for transfers between devices: 87.3 us -> 92.4 us
  local copies, waits for them, and re-layouts: 15.1 us -> 12.2 us
    ppermute x17 -> x16, waiting for transfers between devices: 57.9 us -> 70.4 us  [move(): return lax.ppermute(x, ('pipe', 'dp'), pairs)]
    all_to_all x5, waiting for transfers between devices: 29.4 us -> 21.9 us  [spread(): return lax.all_to_all(x, 'expert', split_axis=0, concat_axis=0, tiled=True)]
    ppermute x17 -> x16, starting transfers between devices: 33.2 us -> 27.5 us  [move(): return lax.ppermute(x, ('pipe', 'dp'), pairs)]
    unnamed x33 -> x29, local copies, waits for them, and re-layouts: 12.4 us -> 8.65 us
  transfers between devices with their start and end apart: 22 -> 21, of which waited for: 11 -> 10; matrix products, arithmetic and copies ran while one was open for 1% -> 1% of each run, Pallas kernels for 12% -> 12%
where the time goes in v7:
time: 194 us; the launch traced here: 193 us
  waiting for transfers between devices  92.4 us (48%)
  starting transfers between devices  49 us (25%)
  Pallas kernels  37.4 us (19%)
  local copies, waits for them, and re-layouts  12.2 us (6%)
    ppermute x16, waiting for transfers between devices, move(): return lax.ppermute(x, ('pipe', 'dp'), pairs)  70.4 us
    ppermute x16, starting transfers between devices, move(): return lax.ppermute(x, ('pipe', 'dp'), pairs)  27.5 us
    all_to_all x5, waiting for transfers between devices, spread(): return lax.all_to_all(x, 'expert', split_axis=0, concat_axis=0, tiled=True)  21.9 us
    all_to_all x5, starting transfers between devices, spread(): return lax.all_to_all(x, 'expert', split_axis=0, concat_axis=0, tiled=True)  21.5 us
    pallas_call x4, Pallas kernels, add(): pl.pallas_call(add_kernel, out_shape=jax.ShapeDtypeStruct(shape, BF), gri...  12.7 us
    pallas_call x1, Pallas kernels, expert_rows(): pl.pallas_call(expert_kernel, out_shape=[jax.ShapeDtypeStruct((SLOTS * BA...  10.5 us
    unnamed x29, local copies, waits for them, and re-layouts  8.65 us
    pallas_call x2, Pallas kernels, weight_sums(): pl.pallas_call(functools.partial(sums_kernel, kinds), out_shape=[shape, s...  5.31 us
  transfers between devices with their start and end apart: 21, of which 10 were waited for; matrix products, arithmetic and copies ran while one was open for 1% of the time, Pallas kernels for 12%

profile of v7, /device:TPU:1, one launch (start us, length us, event | category | flops | bytes accessed | tf_op | source)
XLA Modules:
  0.0 192.7 jit_solution(14856039391066142329)
XLA Ops:
  2.9 3.3 %collective-permute-start.1 = (bf16[24,128,128]{2,1,0:T(8,128)(2,1)S(1)}, bf16[24,128,128]{2,1,0:T(8,128)(2,1)S(1)}, u32[]{:S(2)}, u32[]{:S(2)}) collective-permute-start(bf16[24,128,128]{2,1,0:T(8,128)(2,1)S(1)} %pad_maximum_fusion), channel_id=1, source_target_pairs={{0,64},{1,65},{2,66},{3,67},{64,0},{65,1},{66,2},{67,3},{128,192},... | collective-permute-start | bytes 2359304 | tf_op jit(solution)/shard_map/ppermute | solution.py:38
  6.4 3.4 %collective-permute-start.3 = (bf16[128,2048]{1,0:T(8,128)(2,1)S(1)}, bf16[128,2048]{1,0:T(8,128)(2,1)S(1)}, u32[]{:S(2)}, u32[]{:S(2)}) collective-permute-start(bf16[128,2048]{1,0:T(8,128)(2,1)S(1)} %bitcast.35), channel_id=1, source_target_pairs={{0,0},{1,1},{2,64},{3,65},{64,2},{65,3},{66,66},{67,67},{128,128},... | collective-permute-start | bytes 1572872 | tf_op jit(solution)/shard_map/ppermute | solution.py:38
  11.5 3.4 %shard_map.119 = bf16[16,384,128]{2,1,0:T(8,128)(2,1)} custom-call(s32[18]{0:T(128)} %pad_add_fusion.info, bf16[1,8,128,512]{3,2,1,0:T(8,128)(2,1)} %gate.1, bf16[1,8,128,512]{3,2,1,0:T(8,128)(2,1)} %up.1, bf16[1,8,128,512]{3,2,1,0:T(8,128)(2,1)} %down.1, bf16[24,128,128]{2,1,0:T(8,128)(2,1)} %copy-done.9), custom_call_target="tpu_custom_call" | custom-call | bytes 4194304 | tf_op jit(solution)/shard_map/pallas_call | solution.py:100
  14.9 3.0 %collective-permute-start.4 = (bf16[128,2048]{1,0:T(8,128)(2,1)}, bf16[128,2048]{1,0:T(8,128)(2,1)S(1)}, u32[]{:S(2)}, u32[]{:S(2)}) collective-permute-start(bf16[128,2048]{1,0:T(8,128)(2,1)} %bitcast.11), channel_id=1, source_target_pairs={{0,0},{1,1},{2,64},{3,65},{64,2},{65,3},{66,66},{67,67},{128,128},... | collective-permute-start | bytes 1572872 | tf_op jit(solution)/shard_map/ppermute | solution.py:38
  17.9 3.5 %collective-permute-start.2 = (bf16[8,128]{1,0:T(8,128)(2,1)S(1)}, bf16[8,128]{1,0:T(8,128)(2,1)S(1)}, u32[]{:S(2)}, u32[]{:S(2)}) collective-permute-start(bf16[8,128]{1,0:T(8,128)(2,1)S(1)} %maximum_maximum_fusion), channel_id=1, source_target_pairs={{0,0},{1,1},{2,64},{3,65},{64,2},{65,3},{66,66},{67,67},{128,128},... | collective-permute-start | bytes 6152 | tf_op jit(solution)/shard_map/ppermute | solution.py:38
  21.4 6.8 %all-to-all-start = ((bf16[16,384,128]{2,1,0:T(8,128)(2,1)}), bf16[16,384,128]{2,1,0:T(8,128)(2,1)}, u32[]{:S(2)}, u32[]{:S(2)}) async-start(bf16[16,384,128]{2,1,0:T(8,128)(2,1)} %shard_map.119), calls=%async_computation | async-start | bytes 3145728 | tf_op jit(solution)/shard_map/all_to_all | solution.py:42
  29.4 5.3 %collective-permute-done.2.notes_ref = bf16[8,128]{1,0:T(8,128)(2,1)S(1)} collective-permute-done((bf16[8,128]{1,0:T(8,128)(2,1)S(1)}, bf16[8,128]{1,0:T(8,128)(2,1)S(1)}, u32[]{:S(2)}, u32[]{:S(2)}) %collective-permute-start.2) | collective-permute-done | bytes 2080 | tf_op jit(solution)/shard_map/ppermute | solution.py:38
  34.7 1.7 shard_map.120
  37.8 8.7 %all-to-all-done.w0 = bf16[16,384,128]{2,1,0:T(8,128)(2,1)} async-done(((bf16[16,384,128]{2,1,0:T(8,128)(2,1)}), bf16[16,384,128]{2,1,0:T(8,128)(2,1)}, u32[]{:S(2)}, u32[]{:S(2)}) %all-to-all-start) | async-done | bytes 1572896 | tf_op jit(solution)/shard_map/all_to_all | solution.py:42
  46.5 1.6 collective-permute-start.5
  48.1 3.7 %all-to-all-start.1 = ((bf16[16,40,2048]{2,1,0:T(8,128)(2,1)}), bf16[16,40,2048]{2,1,0:T(8,128)(2,1)S(1)}, u32[]{:S(2)}, u32[]{:S(2)}) async-start(bf16[16,40,2048]{2,1,0:T(8,128)(2,1)} %bitcast.30), calls=%async_computation.1 | async-start | bytes 5242880 | tf_op jit(solution)/shard_map/all_to_all | solution.py:42
  52.0 25.6 %collective-permute-done.5.w1 = bf16[16,384,128]{2,1,0:T(8,128)(2,1)} collective-permute-done((bf16[16,384,128]{2,1,0:T(8,128)(2,1)}, bf16[16,384,128]{2,1,0:T(8,128)(2,1)}, u32[]{:S(2)}, u32[]{:S(2)}) %collective-permute-start.5) | collective-permute-done | bytes 1572896 | tf_op jit(solution)/shard_map/ppermute | solution.py:38
  78.9 4.8 %all-to-all-done.1 = bf16[16,40,2048]{2,1,0:T(8,128)(2,1)S(1)} async-done(((bf16[16,40,2048]{2,1,0:T(8,128)(2,1)}), bf16[16,40,2048]{2,1,0:T(8,128)(2,1)S(1)}, u32[]{:S(2)}, u32[]{:S(2)}) %all-to-all-start.1) | async-done | bytes 2621472 | tf_op jit(solution)/shard_map/all_to_all | solution.py:42
  85.1 10.5 %shard_map.121 = (bf16[384,2048]{1,0:T(8,128)(2,1)S(1)}, bf16[320,2048]{1,0:T(8,128)(2,1)S(1)}, bf16[320,2048]{1,0:T(8,128)(2,1)S(1)}, bf16[320,512]{1,0:T(8,128)(2,1)S(1)}, bf16[320,1024]{1,0:T(8,128)(2,1)S(1)}) custom-call(s32[1]{0:T(128)} %bitcast.info, bf16[640,2048]{1,0:T(8,128)(2,1)S(1)} %bitcast.29, bf16[16,384,128]{2,1,0:T(8,128)(2,1)} %all-to-all-done.w0, ...), custom_call_target="tpu_custom_call" | custom-call | flops 5368709120 | bytes 14680064 | tf_op jit(solution)/shard_map/pallas_call | solution.py:223
  97.0 4.0 %shard_map.124 = (bf16[2,16,64,512]{3,2,1,0:T(8,128)(2,1)S(1)}, bf16[2,16,64,512]{3,2,1,0:T(8,128)(2,1)}) custom-call(s32[1]{0:T(128)} %bitcast.info, bf16[320,2048]{1,0:T(8,128)(2,1)S(1)} %get-tuple-element.56.a_ref, bf16[320,1024]{1,0:T(8,128)(2,1)S(1)} %get-tuple-element.57.b_ref), custom_call_target="tpu_custom_call" | custom-call | flops 10000000000 | bytes 1024 | tf_op jit(solution)/shard_map/pallas_call | solution.py:274
  101.0 1.9 %shard_map.123 = bf16[16,32,512]{2,1,0:T(8,128)(2,1)} custom-call(bf16[2,16,32,512]{3,2,1,0:T(8,128)(2,1)S(1)} %get-tuple-element.54.refs_0_, bf16[2,16,32,512]{3,2,1,0:T(8,128)(2,1)S(1)} %collective-permute-done.8.refs_1_), custom_call_target="tpu_custom_call" | custom-call | bytes 1024 | tf_op jit(solution)/shard_map/pallas_call | solution.py:359
  104.5 3.7 %all-to-all-start.2 = ((bf16[16,24,2048]{2,1,0:T(8,128)(2,1)}), bf16[16,24,2048]{2,1,0:T(8,128)(2,1)S(1)}, u32[]{:S(2)}, u32[]{:S(2)}) async-start(bf16[16,24,2048]{2,1,0:T(8,128)(2,1)} %bitcast.31), calls=%async_computation.2 | async-start | bytes 3145728 | tf_op jit(solution)/shard_map/all_to_all | solution.py:42
  108.2 10.1 %collective-permute-done.9.refs_2_ = bf16[16,32,512]{2,1,0:T(8,128)(2,1)} collective-permute-done((bf16[16,32,512]{2,1,0:T(8,128)(2,1)}, bf16[16,32,512]{2,1,0:T(8,128)(2,1)}, u32[]{:S(2)}, u32[]{:S(2)}) %collective-permute-start.9) | collective-permute-done | bytes 524320 | tf_op jit(solution)/shard_map/ppermute | solution.py:38
  118.3 3.6 %shard_map.126 = bf16[16,64,512]{2,1,0:T(8,128)(2,1)} custom-call(bf16[2,16,64,512]{3,2,1,0:T(8,128)(2,1)} %copy-done.3, bf16[2,16,64,512]{3,2,1,0:T(8,128)(2,1)} %collective-permute-done.10.refs_1_), custom_call_target="tpu_custom_call" | custom-call | flops 99999997952 | bytes 1024 | tf_op jit(solution)/shard_map/pallas_call | solution.py:359
  121.9 3.2 %shard_map.125 = bf16[16,32,512]{2,1,0:T(8,128)(2,1)} custom-call(bf16[2,16,32,512]{3,2,1,0:T(8,128)(2,1)S(1)} %get-tuple-element.54.refs_0_, bf16[2,16,32,512]{3,2,1,0:T(8,128)(2,1)S(1)} %copy-done.1, bf16[16,32,512]{2,1,0:T(8,128)(2,1)} %collective-permute-done.9.refs_2_), custom_call_target="tpu_custom_call" | custom-call | bytes 1024 | tf_op jit(solution)/shard_map/pallas_call | solution.py:359
  125.2 8.5 %all-to-all-done.2 = bf16[16,24,2048]{2,1,0:T(8,128)(2,1)S(1)} async-done(((bf16[16,24,2048]{2,1,0:T(8,128)(2,1)}), bf16[16,24,2048]{2,1,0:T(8,128)(2,1)S(1)}, u32[]{:S(2)}, u32[]{:S(2)}) %all-to-all-start.2) | async-done | bytes 1572896 | tf_op jit(solution)/shard_map/all_to_all | solution.py:42
  133.7 3.6 %all-to-all-start.3 = ((bf16[16,32,512]{2,1,0:T(8,128)(2,1)}), bf16[16,32,512]{2,1,0:T(8,128)(2,1)S(1)}, u32[]{:S(2)}, u32[]{:S(2)}) async-start(bf16[16,32,512]{2,1,0:T(8,128)(2,1)} %shard_map.125), calls=%async_computation.3 | async-start | bytes 1048576 | tf_op jit(solution)/shard_map/all_to_all | solution.py:42
  137.2 1.5 shard_map.128
  138.7 3.5 %collective-permute-start.13 = (bf16[128,2048]{1,0:T(8,128)(2,1)}, bf16[128,2048]{1,0:T(8,128)(2,1)S(1)}, u32[]{:S(2)}, u32[]{:S(2)}) collective-permute-start(bf16[128,2048]{1,0:T(8,128)(2,1)} %get-tuple-element.69), channel_id=1, source_target_pairs={{0,192},{1,193},{2,0},{3,1},{64,194},{65,195},{66,2},{67,3},{128,6... | collective-permute-start | bytes 1572872 | tf_op jit(solution)/shard_map/ppermute | solution.py:38
  142.2 9.5 %collective-permute-done.11.refs_2_ = bf16[16,64,512]{2,1,0:T(8,128)(2,1)} collective-permute-done((bf16[16,64,512]{2,1,0:T(8,128)(2,1)}, bf16[16,64,512]{2,1,0:T(8,128)(2,1)}, u32[]{:S(2)}, u32[]{:S(2)}) %collective-permute-start.11) | collective-permute-done | bytes 1048608 | tf_op jit(solution)/shard_map/ppermute | solution.py:38
  151.7 3.9 %shard_map.127 = bf16[16,64,512]{2,1,0:T(8,128)(2,1)} custom-call(bf16[2,16,64,512]{3,2,1,0:T(8,128)(2,1)} %copy-done.3, bf16[2,16,64,512]{3,2,1,0:T(8,128)(2,1)} %collective-permute-done.10.refs_1_, bf16[16,64,512]{2,1,0:T(8,128)(2,1)} %collective-permute-done.11.refs_2_), custom_call_target="tpu_custom_call" | custom-call | bytes 1024 | tf_op jit(solution)/shard_map/pallas_call | solution.py:359
  156.4 3.7 %all-to-all-start.4 = ((bf16[16,64,512]{2,1,0:T(8,128)(2,1)}), bf16[16,64,512]{2,1,0:T(8,128)(2,1)S(1)}, u32[]{:S(2)}, u32[]{:S(2)}) async-start(bf16[16,64,512]{2,1,0:T(8,128)(2,1)} %shard_map.127), calls=%async_computation.4 | async-start | bytes 2097152 | tf_op jit(solution)/shard_map/all_to_all | solution.py:42
  161.8 1.9 collective-permute-start.14
  163.7 4.5 %collective-permute-start.12 = (bf16[8,128]{1,0:T(8,128)(2,1)S(1)}, bf16[8,128]{1,0:T(8,128)(2,1)S(1)}, u32[]{:S(2)}, u32[]{:S(2)}) collective-permute-start(bf16[8,128]{1,0:T(8,128)(2,1)S(1)} %get-tuple-element.68), channel_id=1, source_target_pairs={{0,0},{1,1},{2,64},{3,65},{64,2},{65,3},{66,66},{67,67},{128,128},... | collective-permute-start | bytes 6152 | tf_op jit(solution)/shard_map/ppermute | solution.py:38
  169.1 6.4 %collective-permute-done.12 = bf16[8,128]{1,0:T(8,128)(2,1)S(1)} collective-permute-done((bf16[8,128]{1,0:T(8,128)(2,1)S(1)}, bf16[8,128]{1,0:T(8,128)(2,1)S(1)}, u32[]{:S(2)}, u32[]{:S(2)}) %collective-permute-start.12) | collective-permute-done | bytes 2080 | tf_op jit(solution)/shard_map/ppermute | solution.py:38
  176.4 1.9 collective-permute-start.15
  178.8 12.3 %collective-permute-done.15 = bf16[2,8,32,512]{3,2,1,0:T(8,128)(2,1)S(1)} collective-permute-done((bf16[2,8,32,512]{3,2,1,0:T(8,128)(2,1)S(1)}, bf16[2,8,32,512]{3,2,1,0:T(8,128)(2,1)S(1)}, u32[]{:S(2)}, u32[]{:S(2)}) %collective-permute-start.15) | collective-permute-done | bytes 524320 | tf_op jit(solution)/shard_map/ppermute | solution.py:38
  (64 shorter events, 18.6 us)
Async XLA Ops:
  0.7 5.6 %copy-start.11 = (s32[1,8]{1,0:T(1,128)S(1)}, s32[1,8]{1,0:T(1,128)}, u32[]{:S(2)}) copy-start(s32[1,8]{1,0:T(1,128)} %param.12) | copy-start | bytes 100
  0.7 5.7 %copy-start.12 = (bf16[1,128,2048]{2,1,0:T(8,128)(2,1)S(1)}, bf16[1,128,2048]{2,1,0:T(8,128)(2,1)}, u32[]{:S(2)}) copy-start(bf16[1,128,2048]{2,1,0:T(8,128)(2,1)} %param.8) | copy-start | bytes 1572868
  0.7 9.2 %copy-start.13 = (s32[1,128,2]{1,2,0:T(2,128)S(1)}, s32[1,128,2]{1,2,0:T(2,128)}, u32[]{:S(2)}) copy-start(s32[1,128,2]{1,2,0:T(2,128)} %param.11) | copy-start | bytes 3076
  0.7 9.2 %copy-start.10 = (bf16[1,128,2]{1,2,0:T(2,128)(2,1)S(1)}, bf16[1,128,2]{1,2,0:T(2,128)(2,1)}, u32[]{:S(2)}) copy-start(bf16[1,128,2]{1,2,0:T(2,128)(2,1)} %param.10) | copy-start | bytes 1540
  2.9 7.7 %collective-permute-start.1 = (bf16[24,128,128]{2,1,0:T(8,128)(2,1)S(1)}, bf16[24,128,128]{2,1,0:T(8,128)(2,1)S(1)}, u32[]{:S(2)}, u32[]{:S(2)}) collective-permute-start(bf16[24,128,128]{2,1,0:T(8,128)(2,1)S(1)} %pad_maximum_fusion), channel_id=1, source_target_pairs={{0,64},{1,65},{2,66},{3,67},{64,0},{65,1},{66,2},{67,3},{128,192},... | collective-permute-start | bytes 2359304 | tf_op jit(solution)/shard_map/ppermute | solution.py:38
  6.2 3.8 %collective-permute-start = (s32[8]{0:T(128)S(1)}, s32[8]{0:T(128)S(1)}, u32[]{:S(2)}, u32[]{:S(2)}) collective-permute-start(s32[8]{0:T(128)S(1)} %bitcast.34), channel_id=1, source_target_pairs={{0,64},{1,65},{2,66},{3,67},{64,0},{65,1},{66,2},{67,3},{128,192},... | collective-permute-start | bytes 104 | tf_op jit(solution)/shard_map/ppermute | solution.py:38
  6.4 23.0 %collective-permute-start.3 = (bf16[128,2048]{1,0:T(8,128)(2,1)S(1)}, bf16[128,2048]{1,0:T(8,128)(2,1)S(1)}, u32[]{:S(2)}, u32[]{:S(2)}) collective-permute-start(bf16[128,2048]{1,0:T(8,128)(2,1)S(1)} %bitcast.35), channel_id=1, source_target_pairs={{0,0},{1,1},{2,64},{3,65},{64,2},{65,3},{66,66},{67,67},{128,128},... | collective-permute-start | bytes 1572872 | tf_op jit(solution)/shard_map/ppermute | solution.py:38
  14.9 19.7 %collective-permute-start.4 = (bf16[128,2048]{1,0:T(8,128)(2,1)}, bf16[128,2048]{1,0:T(8,128)(2,1)S(1)}, u32[]{:S(2)}, u32[]{:S(2)}) collective-permute-start(bf16[128,2048]{1,0:T(8,128)(2,1)} %bitcast.11), channel_id=1, source_target_pairs={{0,0},{1,1},{2,64},{3,65},{64,2},{65,3},{66,66},{67,67},{128,128},... | collective-permute-start | bytes 1572872 | tf_op jit(solution)/shard_map/ppermute | solution.py:38
  17.9 16.7 %collective-permute-start.2 = (bf16[8,128]{1,0:T(8,128)(2,1)S(1)}, bf16[8,128]{1,0:T(8,128)(2,1)S(1)}, u32[]{:S(2)}, u32[]{:S(2)}) collective-permute-start(bf16[8,128]{1,0:T(8,128)(2,1)S(1)} %maximum_maximum_fusion), channel_id=1, source_target_pairs={{0,0},{1,1},{2,64},{3,65},{64,2},{65,3},{66,66},{67,67},{128,128},... | collective-permute-start | bytes 6152 | tf_op jit(solution)/shard_map/ppermute | solution.py:38
  21.4 25.1 %all-to-all-start = ((bf16[16,384,128]{2,1,0:T(8,128)(2,1)}), bf16[16,384,128]{2,1,0:T(8,128)(2,1)}, u32[]{:S(2)}, u32[]{:S(2)}) async-start(bf16[16,384,128]{2,1,0:T(8,128)(2,1)} %shard_map.119), calls=%async_computation | async-start | bytes 3145728 | tf_op jit(solution)/shard_map/all_to_all | solution.py:42
  36.3 1.5 copy-start.2
  46.5 31.1 %collective-permute-start.5 = (bf16[16,384,128]{2,1,0:T(8,128)(2,1)}, bf16[16,384,128]{2,1,0:T(8,128)(2,1)}, u32[]{:S(2)}, u32[]{:S(2)}) collective-permute-start(bf16[16,384,128]{2,1,0:T(8,128)(2,1)} %all-to-all-done.w0), channel_id=1, source_target_pairs={{0,1},{1,0},{2,3},{3,2},{64,65},{65,64},{66,67},{67,66},{128,129},... | collective-permute-start | bytes 4718600 | tf_op jit(solution)/shard_map/ppermute | solution.py:38
  48.1 35.5 %all-to-all-start.1 = ((bf16[16,40,2048]{2,1,0:T(8,128)(2,1)}), bf16[16,40,2048]{2,1,0:T(8,128)(2,1)S(1)}, u32[]{:S(2)}, u32[]{:S(2)}) async-start(bf16[16,40,2048]{2,1,0:T(8,128)(2,1)} %bitcast.30), calls=%async_computation.1 | async-start | bytes 5242880 | tf_op jit(solution)/shard_map/all_to_all | solution.py:42
  51.9 25.7 %collective-permute-start.6 = (bf16[16,384,128]{2,1,0:T(8,128)(2,1)}, bf16[16,384,128]{2,1,0:T(8,128)(2,1)S(1)}, u32[]{:S(2)}, u32[]{:S(2)}) collective-permute-start(bf16[16,384,128]{2,1,0:T(8,128)(2,1)} %all-to-all-done.w0), channel_id=1, source_target_pairs={{0,64},{1,65},{2,66},{3,67},{64,0},{65,1},{66,2},{67,3},{128,192},... | collective-permute-start | bytes 4718600 | tf_op jit(solution)/shard_map/ppermute | solution.py:38
  77.6 6.0 %collective-permute-start.7 = (bf16[16,384,128]{2,1,0:T(8,128)(2,1)}, bf16[16,384,128]{2,1,0:T(8,128)(2,1)}, u32[]{:S(2)}, u32[]{:S(2)}) collective-permute-start(bf16[16,384,128]{2,1,0:T(8,128)(2,1)} %collective-permute-done.5.w1), channel_id=1, source_target_pairs={{0,64},{1,65},{2,66},{3,67},{64,0},{65,1},{66,2},{67,3},{128,192},... | collective-permute-start | bytes 4718600 | tf_op jit(solution)/shard_map/ppermute | solution.py:38
  77.6 1.3 copy-start.7
  83.7 1.4 copy-start.8
  95.5 5.4 %copy-start.4 = (bf16[384,2048]{1,0:T(8,128)(2,1)}, bf16[384,2048]{1,0:T(8,128)(2,1)S(1)}, u32[]{:S(2)}) copy-start(bf16[384,2048]{1,0:T(8,128)(2,1)S(1)} %get-tuple-element.53) | copy-start | bytes 4718596
  96.9 4.1 %collective-permute-start.8 = (bf16[2,16,32,512]{3,2,1,0:T(8,128)(2,1)S(1)}, bf16[2,16,32,512]{3,2,1,0:T(8,128)(2,1)S(1)}, u32[]{:S(2)}, u32[]{:S(2)}) collective-permute-start(bf16[2,16,32,512]{3,2,1,0:T(8,128)(2,1)S(1)} %get-tuple-element.55), channel_id=1, source_target_pairs={{0,64},{1,65},{2,66},{3,67},{64,0},{65,1},{66,2},{67,3},{128,192},... | collective-permute-start | bytes 3145736 | tf_op jit(solution)/shard_map/ppermute | solution.py:38
  101.0 1.9 %copy-start.3 = (bf16[2,16,64,512]{3,2,1,0:T(8,128)(2,1)}, bf16[2,16,64,512]{3,2,1,0:T(8,128)(2,1)S(1)}, u32[]{:S(2)}) copy-start(bf16[2,16,64,512]{3,2,1,0:T(8,128)(2,1)S(1)} %get-tuple-element.61.refs_0_) | copy-start | bytes 6291460
  102.9 1.1 copy-start
  104.0 14.3 %collective-permute-start.10 = (bf16[2,16,64,512]{3,2,1,0:T(8,128)(2,1)}, bf16[2,16,64,512]{3,2,1,0:T(8,128)(2,1)}, u32[]{:S(2)}, u32[]{:S(2)}) collective-permute-start(bf16[2,16,64,512]{3,2,1,0:T(8,128)(2,1)} %get-tuple-element.62), channel_id=1, source_target_pairs={{0,64},{1,65},{2,66},{3,67},{64,0},{65,1},{66,2},{67,3},{128,192},... | collective-permute-start | bytes 6291464 | tf_op jit(solution)/shard_map/ppermute | solution.py:38
  104.5 13.8 %collective-permute-start.9 = (bf16[16,32,512]{2,1,0:T(8,128)(2,1)}, bf16[16,32,512]{2,1,0:T(8,128)(2,1)}, u32[]{:S(2)}, u32[]{:S(2)}) collective-permute-start(bf16[16,32,512]{2,1,0:T(8,128)(2,1)} %shard_map.123), channel_id=1, source_target_pairs={{0,1},{1,0},{2,3},{3,2},{64,65},{65,64},{66,67},{67,66},{128,129},... | collective-permute-start | bytes 1572872 | tf_op jit(solution)/shard_map/ppermute | solution.py:38
  104.5 29.2 %all-to-all-start.2 = ((bf16[16,24,2048]{2,1,0:T(8,128)(2,1)}), bf16[16,24,2048]{2,1,0:T(8,128)(2,1)S(1)}, u32[]{:S(2)}, u32[]{:S(2)}) async-start(bf16[16,24,2048]{2,1,0:T(8,128)(2,1)} %bitcast.31), calls=%async_computation.2 | async-start | bytes 3145728 | tf_op jit(solution)/shard_map/all_to_all | solution.py:42
  108.2 13.8 %copy-start.1 = (bf16[2,16,32,512]{3,2,1,0:T(8,128)(2,1)S(1)}, bf16[2,16,32,512]{3,2,1,0:T(8,128)(2,1)}, u32[]{:S(2)}) copy-start(bf16[2,16,32,512]{3,2,1,0:T(8,128)(2,1)} %copy-done) | copy-start | bytes 3145732
  121.9 29.8 %collective-permute-start.11 = (bf16[16,64,512]{2,1,0:T(8,128)(2,1)}, bf16[16,64,512]{2,1,0:T(8,128)(2,1)}, u32[]{:S(2)}, u32[]{:S(2)}) collective-permute-start(bf16[16,64,512]{2,1,0:T(8,128)(2,1)} %shard_map.126), channel_id=1, source_target_pairs={{0,1},{1,0},{2,3},{3,2},{64,65},{65,64},{66,67},{67,66},{128,129},... | collective-permute-start | bytes 3145736 | tf_op jit(solution)/shard_map/ppermute | solution.py:38
  133.7 22.0 %all-to-all-start.3 = ((bf16[16,32,512]{2,1,0:T(8,128)(2,1)}), bf16[16,32,512]{2,1,0:T(8,128)(2,1)S(1)}, u32[]{:S(2)}, u32[]{:S(2)}) async-start(bf16[16,32,512]{2,1,0:T(8,128)(2,1)} %shard_map.125), calls=%async_computation.3 | async-start | bytes 1048576 | tf_op jit(solution)/shard_map/all_to_all | solution.py:42
  138.7 29.6 %collective-permute-start.13 = (bf16[128,2048]{1,0:T(8,128)(2,1)}, bf16[128,2048]{1,0:T(8,128)(2,1)S(1)}, u32[]{:S(2)}, u32[]{:S(2)}) collective-permute-start(bf16[128,2048]{1,0:T(8,128)(2,1)} %get-tuple-element.69), channel_id=1, source_target_pairs={{0,192},{1,193},{2,0},{3,1},{64,194},{65,195},{66,2},{67,3},{128,6... | collective-permute-start | bytes 1572872 | tf_op jit(solution)/shard_map/ppermute | solution.py:38
  156.4 19.1 %all-to-all-start.4 = ((bf16[16,64,512]{2,1,0:T(8,128)(2,1)}), bf16[16,64,512]{2,1,0:T(8,128)(2,1)S(1)}, u32[]{:S(2)}, u32[]{:S(2)}) async-start(bf16[16,64,512]{2,1,0:T(8,128)(2,1)} %shard_map.127), calls=%async_computation.4 | async-start | bytes 2097152 | tf_op jit(solution)/shard_map/all_to_all | solution.py:42
  161.8 13.8 %collective-permute-start.14 = (bf16[1,8,32,512]{3,2,1,0:T(8,128)(2,1)S(1)}, bf16[1,8,32,512]{3,2,1,0:T(8,128)(2,1)S(1)}, u32[]{:S(2)}, u32[]{:S(2)}) collective-permute-start(bf16[1,8,32,512]{3,2,1,0:T(8,128)(2,1)S(1)} %shard_map.130), channel_id=1, source_target_pairs={{0,0},{1,1},{2,64},{3,65},{64,2},{65,3},{66,66},{67,67},{128,128},... | collective-permute-start | bytes 786440 | tf_op jit(solution)/shard_map/ppermute | solution.py:38
  163.7 11.8 %collective-permute-start.12 = (bf16[8,128]{1,0:T(8,128)(2,1)S(1)}, bf16[8,128]{1,0:T(8,128)(2,1)S(1)}, u32[]{:S(2)}, u32[]{:S(2)}) collective-permute-start(bf16[8,128]{1,0:T(8,128)(2,1)S(1)} %get-tuple-element.68), channel_id=1, source_target_pairs={{0,0},{1,1},{2,64},{3,65},{64,2},{65,3},{66,66},{67,67},{128,128},... | collective-permute-start | bytes 6152 | tf_op jit(solution)/shard_map/ppermute | solution.py:38
  176.4 14.7 %collective-permute-start.15 = (bf16[2,8,32,512]{3,2,1,0:T(8,128)(2,1)S(1)}, bf16[2,8,32,512]{3,2,1,0:T(8,128)(2,1)S(1)}, u32[]{:S(2)}, u32[]{:S(2)}) collective-permute-start(bf16[2,8,32,512]{3,2,1,0:T(8,128)(2,1)S(1)} %shard_map.131), channel_id=1, source_target_pairs={{0,0},{1,1},{2,64},{3,65},{64,2},{65,3},{66,66},{67,67},{128,128},... | collective-permute-start | bytes 1572872 | tf_op jit(solution)/shard_map/ppermute | solution.py:38
  (3 other events, 2.7 us)

commit v8 on v7

--- a/solution.py
+++ b/solution.py
@@ -406,8 +406,8 @@
         [slot_of[0].T.astype(BF), route_weight[0].T, jnp.zeros((4, TOK), BF)], axis=0
     )
     picked = pick_weights(info, weights, other)
+    notes = move(notes, TURN)
     picked, notes, grads = lax.optimization_barrier((picked, notes, grad_out[0]))
-    notes = move(notes, TURN)
     g = move(grads, TURN)
     first = spread(picked)
     rows = pack_rows(notes, x, g)

time: 194 us -> 193 us (level)
  waiting for transfers between devices: 92.4 us -> 90.3 us
    all_to_all x5, waiting for transfers between devices: 21.9 us -> 17.4 us  [spread(): return lax.all_to_all(x, 'expert', split_axis=0, concat_axis=0, tiled=True)]
    ppermute x16, waiting for transfers between devices: 70.4 us -> 72.9 us  [move(): return lax.ppermute(x, ('pipe', 'dp'), pairs)]
where the time goes in v8:
time: 193 us; the launch traced here: 192 us
  waiting for transfers between devices  90.3 us (47%)
  starting transfers between devices  50.4 us (26%)
  Pallas kernels  37.4 us (19%)
  local copies, waits for them, and re-layouts  12.2 us (6%)
    ppermute x16, waiting for transfers between devices, move(): return lax.ppermute(x, ('pipe', 'dp'), pairs)  72.9 us
    ppermute x16, starting transfers between devices, move(): return lax.ppermute(x, ('pipe', 'dp'), pairs)  28.9 us
    all_to_all x5, starting transfers between devices, spread(): return lax.all_to_all(x, 'expert', split_axis=0, concat_axis=0, tiled=True)  21.5 us
    all_to_all x5, waiting for transfers between devices, spread(): return lax.all_to_all(x, 'expert', split_axis=0, concat_axis=0, tiled=True)  17.4 us
    pallas_call x4, Pallas kernels, add(): pl.pallas_call(add_kernel, out_shape=jax.ShapeDtypeStruct(shape, BF), gri...  12.7 us
    pallas_call x1, Pallas kernels, expert_rows(): pl.pallas_call(expert_kernel, out_shape=[jax.ShapeDtypeStruct((SLOTS * BA...  10.5 us
    unnamed x29, local copies, waits for them, and re-layouts  8.65 us
    pallas_call x2, Pallas kernels, weight_sums(): pl.pallas_call(functools.partial(sums_kernel, kinds), out_shape=[shape, s...  5.31 us
  transfers between devices with their start and end apart: 21, of which 10 were waited for; matrix products, arithmetic and copies ran while one was open for 1% of the time, Pallas kernels for 12%

profile of v8, /device:TPU:1, one launch (start us, length us, event | category | flops | bytes accessed | tf_op | source)
XLA Modules:
  0.0 192.0 jit_solution(1065829604988535441)
XLA Ops:
  2.9 3.3 %collective-permute-start.1 = (bf16[24,128,128]{2,1,0:T(8,128)(2,1)S(1)}, bf16[24,128,128]{2,1,0:T(8,128)(2,1)S(1)}, u32[]{:S(2)}, u32[]{:S(2)}) collective-permute-start(bf16[24,128,128]{2,1,0:T(8,128)(2,1)S(1)} %pad_maximum_fusion), channel_id=1, source_target_pairs={{0,64},{1,65},{2,66},{3,67},{64,0},{65,1},{66,2},{67,3},{128,192},... | collective-permute-start | bytes 2359304 | tf_op jit(solution)/shard_map/ppermute | solution.py:38
  6.5 3.4 %collective-permute-start.2 = (bf16[8,128]{1,0:T(8,128)(2,1)S(1)}, bf16[8,128]{1,0:T(8,128)(2,1)S(1)}, u32[]{:S(2)}, u32[]{:S(2)}) collective-permute-start(bf16[8,128]{1,0:T(8,128)(2,1)S(1)} %maximum_maximum_fusion), channel_id=1, source_target_pairs={{0,0},{1,1},{2,64},{3,65},{64,2},{65,3},{66,66},{67,67},{128,128},... | collective-permute-start | bytes 6152 | tf_op jit(solution)/shard_map/ppermute | solution.py:38
  10.0 3.0 %collective-permute-start.3 = (bf16[128,2048]{1,0:T(8,128)(2,1)S(1)}, bf16[128,2048]{1,0:T(8,128)(2,1)S(1)}, u32[]{:S(2)}, u32[]{:S(2)}) collective-permute-start(bf16[128,2048]{1,0:T(8,128)(2,1)S(1)} %bitcast.35), channel_id=1, source_target_pairs={{0,0},{1,1},{2,64},{3,65},{64,2},{65,3},{66,66},{67,67},{128,128},... | collective-permute-start | bytes 1572872 | tf_op jit(solution)/shard_map/ppermute | solution.py:38
  14.6 3.4 %shard_map.119 = bf16[16,384,128]{2,1,0:T(8,128)(2,1)} custom-call(s32[18]{0:T(128)} %pad_add_fusion.info, bf16[1,8,128,512]{3,2,1,0:T(8,128)(2,1)} %gate.1, bf16[1,8,128,512]{3,2,1,0:T(8,128)(2,1)} %up.1, bf16[1,8,128,512]{3,2,1,0:T(8,128)(2,1)} %down.1, bf16[24,128,128]{2,1,0:T(8,128)(2,1)} %copy-done.9), custom_call_target="tpu_custom_call" | custom-call | bytes 4194304 | tf_op jit(solution)/shard_map/pallas_call | solution.py:100
  18.0 3.5 %collective-permute-start.4 = (bf16[128,2048]{1,0:T(8,128)(2,1)}, bf16[128,2048]{1,0:T(8,128)(2,1)S(1)}, u32[]{:S(2)}, u32[]{:S(2)}) collective-permute-start(bf16[128,2048]{1,0:T(8,128)(2,1)} %bitcast.11), channel_id=1, source_target_pairs={{0,0},{1,1},{2,64},{3,65},{64,2},{65,3},{66,66},{67,67},{128,128},... | collective-permute-start | bytes 1572872 | tf_op jit(solution)/shard_map/ppermute | solution.py:38
  21.4 6.8 %all-to-all-start = ((bf16[16,384,128]{2,1,0:T(8,128)(2,1)}), bf16[16,384,128]{2,1,0:T(8,128)(2,1)}, u32[]{:S(2)}, u32[]{:S(2)}) async-start(bf16[16,384,128]{2,1,0:T(8,128)(2,1)} %shard_map.119), calls=%async_computation | async-start | bytes 3145728 | tf_op jit(solution)/shard_map/all_to_all | solution.py:42
  28.3 4.5 %collective-permute-done.3.x_ref = bf16[128,2048]{1,0:T(8,128)(2,1)S(1)} collective-permute-done((bf16[128,2048]{1,0:T(8,128)(2,1)S(1)}, bf16[128,2048]{1,0:T(8,128)(2,1)S(1)}, u32[]{:S(2)}, u32[]{:S(2)}) %collective-permute-start.3) | collective-permute-done | bytes 524320 | tf_op jit(solution)/shard_map/ppermute | solution.py:38
  32.7 5.9 %collective-permute-done.4.g_ref = bf16[128,2048]{1,0:T(8,128)(2,1)S(1)} collective-permute-done((bf16[128,2048]{1,0:T(8,128)(2,1)}, bf16[128,2048]{1,0:T(8,128)(2,1)S(1)}, u32[]{:S(2)}, u32[]{:S(2)}) %collective-permute-start.4) | collective-permute-done | bytes 524320 | tf_op jit(solution)/shard_map/ppermute | solution.py:38
  38.6 1.7 shard_map.120
  41.8 4.0 %all-to-all-done.w0 = bf16[16,384,128]{2,1,0:T(8,128)(2,1)} async-done(((bf16[16,384,128]{2,1,0:T(8,128)(2,1)}), bf16[16,384,128]{2,1,0:T(8,128)(2,1)}, u32[]{:S(2)}, u32[]{:S(2)}) %all-to-all-start) | async-done | bytes 1572896 | tf_op jit(solution)/shard_map/all_to_all | solution.py:42
  45.8 1.6 collective-permute-start.5
  47.5 3.7 %all-to-all-start.1 = ((bf16[16,40,2048]{2,1,0:T(8,128)(2,1)}), bf16[16,40,2048]{2,1,0:T(8,128)(2,1)S(1)}, u32[]{:S(2)}, u32[]{:S(2)}) async-start(bf16[16,40,2048]{2,1,0:T(8,128)(2,1)} %bitcast.30), calls=%async_computation.1 | async-start | bytes 5242880 | tf_op jit(solution)/shard_map/all_to_all | solution.py:42
  51.3 25.7 %collective-permute-done.5.w1 = bf16[16,384,128]{2,1,0:T(8,128)(2,1)} collective-permute-done((bf16[16,384,128]{2,1,0:T(8,128)(2,1)}, bf16[16,384,128]{2,1,0:T(8,128)(2,1)}, u32[]{:S(2)}, u32[]{:S(2)}) %collective-permute-start.5) | collective-permute-done | bytes 1572896 | tf_op jit(solution)/shard_map/ppermute | solution.py:38
  78.3 4.7 %all-to-all-done.1 = bf16[16,40,2048]{2,1,0:T(8,128)(2,1)S(1)} async-done(((bf16[16,40,2048]{2,1,0:T(8,128)(2,1)}), bf16[16,40,2048]{2,1,0:T(8,128)(2,1)S(1)}, u32[]{:S(2)}, u32[]{:S(2)}) %all-to-all-start.1) | async-done | bytes 2621472 | tf_op jit(solution)/shard_map/all_to_all | solution.py:42
  84.4 10.5 %shard_map.121 = (bf16[384,2048]{1,0:T(8,128)(2,1)S(1)}, bf16[320,2048]{1,0:T(8,128)(2,1)S(1)}, bf16[320,2048]{1,0:T(8,128)(2,1)S(1)}, bf16[320,512]{1,0:T(8,128)(2,1)S(1)}, bf16[320,1024]{1,0:T(8,128)(2,1)S(1)}) custom-call(s32[1]{0:T(128)} %bitcast.info, bf16[640,2048]{1,0:T(8,128)(2,1)S(1)} %bitcast.29, bf16[16,384,128]{2,1,0:T(8,128)(2,1)} %all-to-all-done.w0, ...), custom_call_target="tpu_custom_call" | custom-call | flops 5368709120 | bytes 14680064 | tf_op jit(solution)/shard_map/pallas_call | solution.py:223
  96.3 4.0 %shard_map.124 = (bf16[2,16,64,512]{3,2,1,0:T(8,128)(2,1)S(1)}, bf16[2,16,64,512]{3,2,1,0:T(8,128)(2,1)}) custom-call(s32[1]{0:T(128)} %bitcast.info, bf16[320,2048]{1,0:T(8,128)(2,1)S(1)} %get-tuple-element.56.a_ref, bf16[320,1024]{1,0:T(8,128)(2,1)S(1)} %get-tuple-element.57.b_ref), custom_call_target="tpu_custom_call" | custom-call | flops 10000000000 | bytes 1024 | tf_op jit(solution)/shard_map/pallas_call | solution.py:274
  100.3 1.9 %shard_map.123 = bf16[16,32,512]{2,1,0:T(8,128)(2,1)} custom-call(bf16[2,16,32,512]{3,2,1,0:T(8,128)(2,1)S(1)} %get-tuple-element.54.refs_0_, bf16[2,16,32,512]{3,2,1,0:T(8,128)(2,1)S(1)} %collective-permute-done.8.refs_1_), custom_call_target="tpu_custom_call" | custom-call | bytes 1024 | tf_op jit(solution)/shard_map/pallas_call | solution.py:359
  103.8 3.7 %all-to-all-start.2 = ((bf16[16,24,2048]{2,1,0:T(8,128)(2,1)}), bf16[16,24,2048]{2,1,0:T(8,128)(2,1)S(1)}, u32[]{:S(2)}, u32[]{:S(2)}) async-start(bf16[16,24,2048]{2,1,0:T(8,128)(2,1)} %bitcast.31), calls=%async_computation.2 | async-start | bytes 3145728 | tf_op jit(solution)/shard_map/all_to_all | solution.py:42
  107.5 10.1 %collective-permute-done.9.refs_2_ = bf16[16,32,512]{2,1,0:T(8,128)(2,1)} collective-permute-done((bf16[16,32,512]{2,1,0:T(8,128)(2,1)}, bf16[16,32,512]{2,1,0:T(8,128)(2,1)}, u32[]{:S(2)}, u32[]{:S(2)}) %collective-permute-start.9) | collective-permute-done | bytes 524320 | tf_op jit(solution)/shard_map/ppermute | solution.py:38
  117.6 3.6 %shard_map.126 = bf16[16,64,512]{2,1,0:T(8,128)(2,1)} custom-call(bf16[2,16,64,512]{3,2,1,0:T(8,128)(2,1)} %copy-done.3, bf16[2,16,64,512]{3,2,1,0:T(8,128)(2,1)} %collective-permute-done.10.refs_1_), custom_call_target="tpu_custom_call" | custom-call | flops 99999997952 | bytes 1024 | tf_op jit(solution)/shard_map/pallas_call | solution.py:359
  121.3 3.2 %shard_map.125 = bf16[16,32,512]{2,1,0:T(8,128)(2,1)} custom-call(bf16[2,16,32,512]{3,2,1,0:T(8,128)(2,1)S(1)} %get-tuple-element.54.refs_0_, bf16[2,16,32,512]{3,2,1,0:T(8,128)(2,1)S(1)} %copy-done.1, bf16[16,32,512]{2,1,0:T(8,128)(2,1)} %collective-permute-done.9.refs_2_), custom_call_target="tpu_custom_call" | custom-call | bytes 1024 | tf_op jit(solution)/shard_map/pallas_call | solution.py:359
  124.5 8.6 %all-to-all-done.2 = bf16[16,24,2048]{2,1,0:T(8,128)(2,1)S(1)} async-done(((bf16[16,24,2048]{2,1,0:T(8,128)(2,1)}), bf16[16,24,2048]{2,1,0:T(8,128)(2,1)S(1)}, u32[]{:S(2)}, u32[]{:S(2)}) %all-to-all-start.2) | async-done | bytes 1572896 | tf_op jit(solution)/shard_map/all_to_all | solution.py:42
  133.2 3.6 %all-to-all-start.3 = ((bf16[16,32,512]{2,1,0:T(8,128)(2,1)}), bf16[16,32,512]{2,1,0:T(8,128)(2,1)S(1)}, u32[]{:S(2)}, u32[]{:S(2)}) async-start(bf16[16,32,512]{2,1,0:T(8,128)(2,1)} %shard_map.125), calls=%async_computation.3 | async-start | bytes 1048576 | tf_op jit(solution)/shard_map/all_to_all | solution.py:42
  138.2 3.3 %collective-permute-start.13 = (bf16[128,2048]{1,0:T(8,128)(2,1)}, bf16[128,2048]{1,0:T(8,128)(2,1)S(1)}, u32[]{:S(2)}, u32[]{:S(2)}) collective-permute-start(bf16[128,2048]{1,0:T(8,128)(2,1)} %get-tuple-element.69), channel_id=1, source_target_pairs={{0,192},{1,193},{2,0},{3,1},{64,194},{65,195},{66,2},{67,3},{128,6... | collective-permute-start | bytes 1572872 | tf_op jit(solution)/shard_map/ppermute | solution.py:38
  141.6 9.5 %collective-permute-done.11.refs_2_ = bf16[16,64,512]{2,1,0:T(8,128)(2,1)} collective-permute-done((bf16[16,64,512]{2,1,0:T(8,128)(2,1)}, bf16[16,64,512]{2,1,0:T(8,128)(2,1)}, u32[]{:S(2)}, u32[]{:S(2)}) %collective-permute-start.11) | collective-permute-done | bytes 1048608 | tf_op jit(solution)/shard_map/ppermute | solution.py:38
  151.1 3.9 %shard_map.127 = bf16[16,64,512]{2,1,0:T(8,128)(2,1)} custom-call(bf16[2,16,64,512]{3,2,1,0:T(8,128)(2,1)} %copy-done.3, bf16[2,16,64,512]{3,2,1,0:T(8,128)(2,1)} %collective-permute-done.10.refs_1_, bf16[16,64,512]{2,1,0:T(8,128)(2,1)} %collective-permute-done.11.refs_2_), custom_call_target="tpu_custom_call" | custom-call | bytes 1024 | tf_op jit(solution)/shard_map/pallas_call | solution.py:359
  155.8 3.7 %all-to-all-start.4 = ((bf16[16,64,512]{2,1,0:T(8,128)(2,1)}), bf16[16,64,512]{2,1,0:T(8,128)(2,1)S(1)}, u32[]{:S(2)}, u32[]{:S(2)}) async-start(bf16[16,64,512]{2,1,0:T(8,128)(2,1)} %shard_map.127), calls=%async_computation.4 | async-start | bytes 2097152 | tf_op jit(solution)/shard_map/all_to_all | solution.py:42
  161.2 5.1 %collective-permute-start.14 = (bf16[1,8,32,512]{3,2,1,0:T(8,128)(2,1)S(1)}, bf16[1,8,32,512]{3,2,1,0:T(8,128)(2,1)S(1)}, u32[]{:S(2)}, u32[]{:S(2)}) collective-permute-start(bf16[1,8,32,512]{3,2,1,0:T(8,128)(2,1)S(1)} %shard_map.130), channel_id=1, source_target_pairs={{0,0},{1,1},{2,64},{3,65},{64,2},{65,3},{66,66},{67,67},{128,128},... | collective-permute-start | bytes 786440 | tf_op jit(solution)/shard_map/ppermute | solution.py:38
  166.3 1.9 %collective-permute-start.12 = (bf16[8,128]{1,0:T(8,128)(2,1)S(1)}, bf16[8,128]{1,0:T(8,128)(2,1)S(1)}, u32[]{:S(2)}, u32[]{:S(2)}) collective-permute-start(bf16[8,128]{1,0:T(8,128)(2,1)S(1)} %get-tuple-element.68), channel_id=1, source_target_pairs={{0,0},{1,1},{2,64},{3,65},{64,2},{65,3},{66,66},{67,67},{128,128},... | collective-permute-start | bytes 6152 | tf_op jit(solution)/shard_map/ppermute | solution.py:38
  169.0 5.9 %collective-permute-done.12 = bf16[8,128]{1,0:T(8,128)(2,1)S(1)} collective-permute-done((bf16[8,128]{1,0:T(8,128)(2,1)S(1)}, bf16[8,128]{1,0:T(8,128)(2,1)S(1)}, u32[]{:S(2)}, u32[]{:S(2)}) %collective-permute-start.12) | collective-permute-done | bytes 2080 | tf_op jit(solution)/shard_map/ppermute | solution.py:38
  175.8 2.9 %collective-permute-start.15 = (bf16[2,8,32,512]{3,2,1,0:T(8,128)(2,1)S(1)}, bf16[2,8,32,512]{3,2,1,0:T(8,128)(2,1)S(1)}, u32[]{:S(2)}, u32[]{:S(2)}) collective-permute-start(bf16[2,8,32,512]{3,2,1,0:T(8,128)(2,1)S(1)} %shard_map.131), channel_id=1, source_target_pairs={{0,0},{1,1},{2,64},{3,65},{64,2},{65,3},{66,66},{67,67},{128,128},... | collective-permute-start | bytes 1572872 | tf_op jit(solution)/shard_map/ppermute | solution.py:38
  179.2 11.3 %collective-permute-done.15 = bf16[2,8,32,512]{3,2,1,0:T(8,128)(2,1)S(1)} collective-permute-done((bf16[2,8,32,512]{3,2,1,0:T(8,128)(2,1)S(1)}, bf16[2,8,32,512]{3,2,1,0:T(8,128)(2,1)S(1)}, u32[]{:S(2)}, u32[]{:S(2)}) %collective-permute-start.15) | collective-permute-done | bytes 524320 | tf_op jit(solution)/shard_map/ppermute | solution.py:38
  (64 shorter events, 18.9 us)
Async XLA Ops:
  0.7 5.6 %copy-start.11 = (s32[1,8]{1,0:T(1,128)S(1)}, s32[1,8]{1,0:T(1,128)}, u32[]{:S(2)}) copy-start(s32[1,8]{1,0:T(1,128)} %param.12) | copy-start | bytes 100
  0.7 5.8 %copy-start.13 = (s32[1,128,2]{1,2,0:T(2,128)S(1)}, s32[1,128,2]{1,2,0:T(2,128)}, u32[]{:S(2)}) copy-start(s32[1,128,2]{1,2,0:T(2,128)} %param.11) | copy-start | bytes 3076
  0.7 5.8 %copy-start.10 = (bf16[1,128,2]{1,2,0:T(2,128)(2,1)S(1)}, bf16[1,128,2]{1,2,0:T(2,128)(2,1)}, u32[]{:S(2)}) copy-start(bf16[1,128,2]{1,2,0:T(2,128)(2,1)} %param.10) | copy-start | bytes 1540
  0.7 9.3 %copy-start.12 = (bf16[1,128,2048]{2,1,0:T(8,128)(2,1)S(1)}, bf16[1,128,2048]{2,1,0:T(8,128)(2,1)}, u32[]{:S(2)}) copy-start(bf16[1,128,2048]{2,1,0:T(8,128)(2,1)} %param.8) | copy-start | bytes 1572868
  2.9 10.7 %collective-permute-start.1 = (bf16[24,128,128]{2,1,0:T(8,128)(2,1)S(1)}, bf16[24,128,128]{2,1,0:T(8,128)(2,1)S(1)}, u32[]{:S(2)}, u32[]{:S(2)}) collective-permute-start(bf16[24,128,128]{2,1,0:T(8,128)(2,1)S(1)} %pad_maximum_fusion), channel_id=1, source_target_pairs={{0,64},{1,65},{2,66},{3,67},{64,0},{65,1},{66,2},{67,3},{128,192},... | collective-permute-start | bytes 2359304 | tf_op jit(solution)/shard_map/ppermute | solution.py:38
  6.3 6.8 %collective-permute-start = (s32[8]{0:T(128)S(1)}, s32[8]{0:T(128)S(1)}, u32[]{:S(2)}, u32[]{:S(2)}) collective-permute-start(s32[8]{0:T(128)S(1)} %bitcast.34), channel_id=1, source_target_pairs={{0,64},{1,65},{2,66},{3,67},{64,0},{65,1},{66,2},{67,3},{128,192},... | collective-permute-start | bytes 104 | tf_op jit(solution)/shard_map/ppermute | solution.py:38
  6.5 11.5 %collective-permute-start.2 = (bf16[8,128]{1,0:T(8,128)(2,1)S(1)}, bf16[8,128]{1,0:T(8,128)(2,1)S(1)}, u32[]{:S(2)}, u32[]{:S(2)}) collective-permute-start(bf16[8,128]{1,0:T(8,128)(2,1)S(1)} %maximum_maximum_fusion), channel_id=1, source_target_pairs={{0,0},{1,1},{2,64},{3,65},{64,2},{65,3},{66,66},{67,67},{128,128},... | collective-permute-start | bytes 6152 | tf_op jit(solution)/shard_map/ppermute | solution.py:38
  10.0 22.8 %collective-permute-start.3 = (bf16[128,2048]{1,0:T(8,128)(2,1)S(1)}, bf16[128,2048]{1,0:T(8,128)(2,1)S(1)}, u32[]{:S(2)}, u32[]{:S(2)}) collective-permute-start(bf16[128,2048]{1,0:T(8,128)(2,1)S(1)} %bitcast.35), channel_id=1, source_target_pairs={{0,0},{1,1},{2,64},{3,65},{64,2},{65,3},{66,66},{67,67},{128,128},... | collective-permute-start | bytes 1572872 | tf_op jit(solution)/shard_map/ppermute | solution.py:38
  18.0 20.7 %collective-permute-start.4 = (bf16[128,2048]{1,0:T(8,128)(2,1)}, bf16[128,2048]{1,0:T(8,128)(2,1)S(1)}, u32[]{:S(2)}, u32[]{:S(2)}) collective-permute-start(bf16[128,2048]{1,0:T(8,128)(2,1)} %bitcast.11), channel_id=1, source_target_pairs={{0,0},{1,1},{2,64},{3,65},{64,2},{65,3},{66,66},{67,67},{128,128},... | collective-permute-start | bytes 1572872 | tf_op jit(solution)/shard_map/ppermute | solution.py:38
  21.4 24.4 %all-to-all-start = ((bf16[16,384,128]{2,1,0:T(8,128)(2,1)}), bf16[16,384,128]{2,1,0:T(8,128)(2,1)}, u32[]{:S(2)}, u32[]{:S(2)}) async-start(bf16[16,384,128]{2,1,0:T(8,128)(2,1)} %shard_map.119), calls=%async_computation | async-start | bytes 3145728 | tf_op jit(solution)/shard_map/all_to_all | solution.py:42
  40.3 1.5 copy-start.2
  45.8 31.2 %collective-permute-start.5 = (bf16[16,384,128]{2,1,0:T(8,128)(2,1)}, bf16[16,384,128]{2,1,0:T(8,128)(2,1)}, u32[]{:S(2)}, u32[]{:S(2)}) collective-permute-start(bf16[16,384,128]{2,1,0:T(8,128)(2,1)} %all-to-all-done.w0), channel_id=1, source_target_pairs={{0,1},{1,0},{2,3},{3,2},{64,65},{65,64},{66,67},{67,66},{128,129},... | collective-permute-start | bytes 4718600 | tf_op jit(solution)/shard_map/ppermute | solution.py:38
  47.5 35.5 %all-to-all-start.1 = ((bf16[16,40,2048]{2,1,0:T(8,128)(2,1)}), bf16[16,40,2048]{2,1,0:T(8,128)(2,1)S(1)}, u32[]{:S(2)}, u32[]{:S(2)}) async-start(bf16[16,40,2048]{2,1,0:T(8,128)(2,1)} %bitcast.30), calls=%async_computation.1 | async-start | bytes 5242880 | tf_op jit(solution)/shard_map/all_to_all | solution.py:42
  51.2 25.8 %collective-permute-start.6 = (bf16[16,384,128]{2,1,0:T(8,128)(2,1)}, bf16[16,384,128]{2,1,0:T(8,128)(2,1)S(1)}, u32[]{:S(2)}, u32[]{:S(2)}) collective-permute-start(bf16[16,384,128]{2,1,0:T(8,128)(2,1)} %all-to-all-done.w0), channel_id=1, source_target_pairs={{0,64},{1,65},{2,66},{3,67},{64,0},{65,1},{66,2},{67,3},{128,192},... | collective-permute-start | bytes 4718600 | tf_op jit(solution)/shard_map/ppermute | solution.py:38
  77.0 6.0 %collective-permute-start.7 = (bf16[16,384,128]{2,1,0:T(8,128)(2,1)}, bf16[16,384,128]{2,1,0:T(8,128)(2,1)}, u32[]{:S(2)}, u32[]{:S(2)}) collective-permute-start(bf16[16,384,128]{2,1,0:T(8,128)(2,1)} %collective-permute-done.5.w1), channel_id=1, source_target_pairs={{0,64},{1,65},{2,66},{3,67},{64,0},{65,1},{66,2},{67,3},{128,192},... | collective-permute-start | bytes 4718600 | tf_op jit(solution)/shard_map/ppermute | solution.py:38
  77.0 1.3 copy-start.7
  83.0 1.4 copy-start.8
  94.9 5.4 %copy-start.4 = (bf16[384,2048]{1,0:T(8,128)(2,1)}, bf16[384,2048]{1,0:T(8,128)(2,1)S(1)}, u32[]{:S(2)}) copy-start(bf16[384,2048]{1,0:T(8,128)(2,1)S(1)} %get-tuple-element.53) | copy-start | bytes 4718596
  96.2 4.1 %collective-permute-start.8 = (bf16[2,16,32,512]{3,2,1,0:T(8,128)(2,1)S(1)}, bf16[2,16,32,512]{3,2,1,0:T(8,128)(2,1)S(1)}, u32[]{:S(2)}, u32[]{:S(2)}) collective-permute-start(bf16[2,16,32,512]{3,2,1,0:T(8,128)(2,1)S(1)} %get-tuple-element.55), channel_id=1, source_target_pairs={{0,64},{1,65},{2,66},{3,67},{64,0},{65,1},{66,2},{67,3},{128,192},... | collective-permute-start | bytes 3145736 | tf_op jit(solution)/shard_map/ppermute | solution.py:38
  100.3 1.9 %copy-start.3 = (bf16[2,16,64,512]{3,2,1,0:T(8,128)(2,1)}, bf16[2,16,64,512]{3,2,1,0:T(8,128)(2,1)S(1)}, u32[]{:S(2)}) copy-start(bf16[2,16,64,512]{3,2,1,0:T(8,128)(2,1)S(1)} %get-tuple-element.61.refs_0_) | copy-start | bytes 6291460
  102.3 1.1 copy-start
  103.3 14.3 %collective-permute-start.10 = (bf16[2,16,64,512]{3,2,1,0:T(8,128)(2,1)}, bf16[2,16,64,512]{3,2,1,0:T(8,128)(2,1)}, u32[]{:S(2)}, u32[]{:S(2)}) collective-permute-start(bf16[2,16,64,512]{3,2,1,0:T(8,128)(2,1)} %get-tuple-element.62), channel_id=1, source_target_pairs={{0,64},{1,65},{2,66},{3,67},{64,0},{65,1},{66,2},{67,3},{128,192},... | collective-permute-start | bytes 6291464 | tf_op jit(solution)/shard_map/ppermute | solution.py:38
  103.8 13.8 %collective-permute-start.9 = (bf16[16,32,512]{2,1,0:T(8,128)(2,1)}, bf16[16,32,512]{2,1,0:T(8,128)(2,1)}, u32[]{:S(2)}, u32[]{:S(2)}) collective-permute-start(bf16[16,32,512]{2,1,0:T(8,128)(2,1)} %shard_map.123), channel_id=1, source_target_pairs={{0,1},{1,0},{2,3},{3,2},{64,65},{65,64},{66,67},{67,66},{128,129},... | collective-permute-start | bytes 1572872 | tf_op jit(solution)/shard_map/ppermute | solution.py:38
  103.8 29.4 %all-to-all-start.2 = ((bf16[16,24,2048]{2,1,0:T(8,128)(2,1)}), bf16[16,24,2048]{2,1,0:T(8,128)(2,1)S(1)}, u32[]{:S(2)}, u32[]{:S(2)}) async-start(bf16[16,24,2048]{2,1,0:T(8,128)(2,1)} %bitcast.31), calls=%async_computation.2 | async-start | bytes 3145728 | tf_op jit(solution)/shard_map/all_to_all | solution.py:42
  107.5 13.8 %copy-start.1 = (bf16[2,16,32,512]{3,2,1,0:T(8,128)(2,1)S(1)}, bf16[2,16,32,512]{3,2,1,0:T(8,128)(2,1)}, u32[]{:S(2)}) copy-start(bf16[2,16,32,512]{3,2,1,0:T(8,128)(2,1)} %copy-done) | copy-start | bytes 3145732
  121.3 29.8 %collective-permute-start.11 = (bf16[16,64,512]{2,1,0:T(8,128)(2,1)}, bf16[16,64,512]{2,1,0:T(8,128)(2,1)}, u32[]{:S(2)}, u32[]{:S(2)}) collective-permute-start(bf16[16,64,512]{2,1,0:T(8,128)(2,1)} %shard_map.126), channel_id=1, source_target_pairs={{0,1},{1,0},{2,3},{3,2},{64,65},{65,64},{66,67},{67,66},{128,129},... | collective-permute-start | bytes 3145736 | tf_op jit(solution)/shard_map/ppermute | solution.py:38
  133.2 21.8 %all-to-all-start.3 = ((bf16[16,32,512]{2,1,0:T(8,128)(2,1)}), bf16[16,32,512]{2,1,0:T(8,128)(2,1)S(1)}, u32[]{:S(2)}, u32[]{:S(2)}) async-start(bf16[16,32,512]{2,1,0:T(8,128)(2,1)} %shard_map.125), calls=%async_computation.3 | async-start | bytes 1048576 | tf_op jit(solution)/shard_map/all_to_all | solution.py:42
  138.2 30.0 %collective-permute-start.13 = (bf16[128,2048]{1,0:T(8,128)(2,1)}, bf16[128,2048]{1,0:T(8,128)(2,1)S(1)}, u32[]{:S(2)}, u32[]{:S(2)}) collective-permute-start(bf16[128,2048]{1,0:T(8,128)(2,1)} %get-tuple-element.69), channel_id=1, source_target_pairs={{0,192},{1,193},{2,0},{3,1},{64,194},{65,195},{66,2},{67,3},{128,6... | collective-permute-start | bytes 1572872 | tf_op jit(solution)/shard_map/ppermute | solution.py:38
  155.8 19.2 %all-to-all-start.4 = ((bf16[16,64,512]{2,1,0:T(8,128)(2,1)}), bf16[16,64,512]{2,1,0:T(8,128)(2,1)S(1)}, u32[]{:S(2)}, u32[]{:S(2)}) async-start(bf16[16,64,512]{2,1,0:T(8,128)(2,1)} %shard_map.127), calls=%async_computation.4 | async-start | bytes 2097152 | tf_op jit(solution)/shard_map/all_to_all | solution.py:42
  161.2 13.8 %collective-permute-start.14 = (bf16[1,8,32,512]{3,2,1,0:T(8,128)(2,1)S(1)}, bf16[1,8,32,512]{3,2,1,0:T(8,128)(2,1)S(1)}, u32[]{:S(2)}, u32[]{:S(2)}) collective-permute-start(bf16[1,8,32,512]{3,2,1,0:T(8,128)(2,1)S(1)} %shard_map.130), channel_id=1, source_target_pairs={{0,0},{1,1},{2,64},{3,65},{64,2},{65,3},{66,66},{67,67},{128,128},... | collective-permute-start | bytes 786440 | tf_op jit(solution)/shard_map/ppermute | solution.py:38
  166.3 8.7 %collective-permute-start.12 = (bf16[8,128]{1,0:T(8,128)(2,1)S(1)}, bf16[8,128]{1,0:T(8,128)(2,1)S(1)}, u32[]{:S(2)}, u32[]{:S(2)}) collective-permute-start(bf16[8,128]{1,0:T(8,128)(2,1)S(1)} %get-tuple-element.68), channel_id=1, source_target_pairs={{0,0},{1,1},{2,64},{3,65},{64,2},{65,3},{66,66},{67,67},{128,128},... | collective-permute-start | bytes 6152 | tf_op jit(solution)/shard_map/ppermute | solution.py:38
  175.8 14.7 %collective-permute-start.15 = (bf16[2,8,32,512]{3,2,1,0:T(8,128)(2,1)S(1)}, bf16[2,8,32,512]{3,2,1,0:T(8,128)(2,1)S(1)}, u32[]{:S(2)}, u32[]{:S(2)}) collective-permute-start(bf16[2,8,32,512]{3,2,1,0:T(8,128)(2,1)S(1)} %shard_map.131), channel_id=1, source_target_pairs={{0,0},{1,1},{2,64},{3,65},{64,2},{65,3},{66,66},{67,67},{128,128},... | collective-permute-start | bytes 1572872 | tf_op jit(solution)/shard_map/ppermute | solution.py:38
  (3 other events, 2.7 us)

commit v9 on v7

--- a/solution.py
+++ b/solution.py
@@ -353,13 +353,13 @@
 
 def add(which, pairs, *more, cost=0, room=16):
     shape = pairs[0].shape[1:]
-    block = (4,) + shape[1:]
+    block = (8,) + shape[1:]
     pair = pl.BlockSpec((1,) + block, lambda n: (which, n, 0, 0))
     one = pl.BlockSpec(block, lambda n: (n, 0, 0))
     return pl.pallas_call(
         add_kernel,
         out_shape=jax.ShapeDtypeStruct(shape, BF),
-        grid=(4,),
+        grid=(2,),
         in_specs=[pair, pair] + [one] * len(more),
         out_specs=one,
         compiler_params=vmem(room),

time: 194 us -> 191 us (0.985)
  Pallas kernels: 37.4 us -> 32.9 us
    pallas_call x4, Pallas kernels: 12.7 us -> 8.17 us  [add(): pl.pallas_call(add_kernel, out_shape=jax.ShapeDtypeStruct(shape, BF), gri...]
    all_to_all x5, waiting for transfers between devices: 21.9 us -> 24.5 us  [spread(): return lax.all_to_all(x, 'expert', split_axis=0, concat_axis=0, tiled=True)]
  transfers between devices with their start and end apart: 21 -> 21, of which waited for: 10 -> 10; matrix products, arithmetic and copies ran while one was open for 1% -> 1% of each run, Pallas kernels for 12% -> 10%
where the time goes in v9:
time: 191 us; the launch traced here: 190 us
  waiting for transfers between devices  93.7 us (49%)
  starting transfers between devices  49.2 us (26%)
  Pallas kernels  32.9 us (17%)
  local copies, waits for them, and re-layouts  12.7 us (7%)
    ppermute x16, waiting for transfers between devices, move(): return lax.ppermute(x, ('pipe', 'dp'), pairs)  69.2 us
    ppermute x16, starting transfers between devices, move(): return lax.ppermute(x, ('pipe', 'dp'), pairs)  27.8 us
    all_to_all x5, waiting for transfers between devices, spread(): return lax.all_to_all(x, 'expert', split_axis=0, concat_axis=0, tiled=True)  24.5 us
    all_to_all x5, starting transfers between devices, spread(): return lax.all_to_all(x, 'expert', split_axis=0, concat_axis=0, tiled=True)  21.5 us
    pallas_call x1, Pallas kernels, expert_rows(): pl.pallas_call(expert_kernel, out_shape=[jax.ShapeDtypeStruct((SLOTS * BA...  10.5 us
    unnamed x29, local copies, waits for them, and re-layouts  9.16 us
    pallas_call x4, Pallas kernels, add(): pl.pallas_call(add_kernel, out_shape=jax.ShapeDtypeStruct(shape, BF), gri...  8.17 us
    pallas_call x2, Pallas kernels, weight_sums(): pl.pallas_call(functools.partial(sums_kernel, kinds), out_shape=[shape, s...  5.31 us
  transfers between devices with their start and end apart: 21, of which 10 were waited for; matrix products, arithmetic and copies ran while one was open for 1% of the time, Pallas kernels for 10%

profile of v9, /device:TPU:1, one launch (start us, length us, event | category | flops | bytes accessed | tf_op | source)
XLA Modules:
  0.0 190.2 jit_solution(18034015261065939332)
XLA Ops:
  2.9 3.3 %collective-permute-start.1 = (bf16[24,128,128]{2,1,0:T(8,128)(2,1)S(1)}, bf16[24,128,128]{2,1,0:T(8,128)(2,1)S(1)}, u32[]{:S(2)}, u32[]{:S(2)}) collective-permute-start(bf16[24,128,128]{2,1,0:T(8,128)(2,1)S(1)} %pad_maximum_fusion), channel_id=1, source_target_pairs={{0,64},{1,65},{2,66},{3,67},{64,0},{65,1},{66,2},{67,3},{128,192},... | collective-permute-start | bytes 2359304 | tf_op jit(solution)/shard_map/ppermute | solution.py:38
  6.4 3.4 %collective-permute-start.3 = (bf16[128,2048]{1,0:T(8,128)(2,1)S(1)}, bf16[128,2048]{1,0:T(8,128)(2,1)S(1)}, u32[]{:S(2)}, u32[]{:S(2)}) collective-permute-start(bf16[128,2048]{1,0:T(8,128)(2,1)S(1)} %bitcast.35), channel_id=1, source_target_pairs={{0,0},{1,1},{2,64},{3,65},{64,2},{65,3},{66,66},{67,67},{128,128},... | collective-permute-start | bytes 1572872 | tf_op jit(solution)/shard_map/ppermute | solution.py:38
  11.5 3.4 %shard_map.119 = bf16[16,384,128]{2,1,0:T(8,128)(2,1)} custom-call(s32[18]{0:T(128)} %pad_add_fusion.info, bf16[1,8,128,512]{3,2,1,0:T(8,128)(2,1)} %gate.1, bf16[1,8,128,512]{3,2,1,0:T(8,128)(2,1)} %up.1, bf16[1,8,128,512]{3,2,1,0:T(8,128)(2,1)} %down.1, bf16[24,128,128]{2,1,0:T(8,128)(2,1)} %copy-done.9), custom_call_target="tpu_custom_call" | custom-call | bytes 4194304 | tf_op jit(solution)/shard_map/pallas_call | solution.py:100
  14.9 3.0 %collective-permute-start.4 = (bf16[128,2048]{1,0:T(8,128)(2,1)}, bf16[128,2048]{1,0:T(8,128)(2,1)S(1)}, u32[]{:S(2)}, u32[]{:S(2)}) collective-permute-start(bf16[128,2048]{1,0:T(8,128)(2,1)} %bitcast.11), channel_id=1, source_target_pairs={{0,0},{1,1},{2,64},{3,65},{64,2},{65,3},{66,66},{67,67},{128,128},... | collective-permute-start | bytes 1572872 | tf_op jit(solution)/shard_map/ppermute | solution.py:38
  17.9 3.5 %collective-permute-start.2 = (bf16[8,128]{1,0:T(8,128)(2,1)S(1)}, bf16[8,128]{1,0:T(8,128)(2,1)S(1)}, u32[]{:S(2)}, u32[]{:S(2)}) collective-permute-start(bf16[8,128]{1,0:T(8,128)(2,1)S(1)} %maximum_maximum_fusion), channel_id=1, source_target_pairs={{0,0},{1,1},{2,64},{3,65},{64,2},{65,3},{66,66},{67,67},{128,128},... | collective-permute-start | bytes 6152 | tf_op jit(solution)/shard_map/ppermute | solution.py:38
  21.4 6.8 %all-to-all-start = ((bf16[16,384,128]{2,1,0:T(8,128)(2,1)}), bf16[16,384,128]{2,1,0:T(8,128)(2,1)}, u32[]{:S(2)}, u32[]{:S(2)}) async-start(bf16[16,384,128]{2,1,0:T(8,128)(2,1)} %shard_map.119), calls=%async_computation | async-start | bytes 3145728 | tf_op jit(solution)/shard_map/all_to_all | solution.py:42
  29.4 5.3 %collective-permute-done.2.notes_ref = bf16[8,128]{1,0:T(8,128)(2,1)S(1)} collective-permute-done((bf16[8,128]{1,0:T(8,128)(2,1)S(1)}, bf16[8,128]{1,0:T(8,128)(2,1)S(1)}, u32[]{:S(2)}, u32[]{:S(2)}) %collective-permute-start.2) | collective-permute-done | bytes 2080 | tf_op jit(solution)/shard_map/ppermute | solution.py:38
  34.7 1.7 shard_map.120
  36.4 1.5 copy-done.2
  37.8 8.7 %all-to-all-done.w0 = bf16[16,384,128]{2,1,0:T(8,128)(2,1)} async-done(((bf16[16,384,128]{2,1,0:T(8,128)(2,1)}), bf16[16,384,128]{2,1,0:T(8,128)(2,1)}, u32[]{:S(2)}, u32[]{:S(2)}) %all-to-all-start) | async-done | bytes 1572896 | tf_op jit(solution)/shard_map/all_to_all | solution.py:42
  46.5 1.6 collective-permute-start.5
  48.1 3.7 %all-to-all-start.1 = ((bf16[16,40,2048]{2,1,0:T(8,128)(2,1)}), bf16[16,40,2048]{2,1,0:T(8,128)(2,1)S(1)}, u32[]{:S(2)}, u32[]{:S(2)}) async-start(bf16[16,40,2048]{2,1,0:T(8,128)(2,1)} %bitcast.30), calls=%async_computation.1 | async-start | bytes 5242880 | tf_op jit(solution)/shard_map/all_to_all | solution.py:42
  52.0 25.6 %collective-permute-done.5.w1 = bf16[16,384,128]{2,1,0:T(8,128)(2,1)} collective-permute-done((bf16[16,384,128]{2,1,0:T(8,128)(2,1)}, bf16[16,384,128]{2,1,0:T(8,128)(2,1)}, u32[]{:S(2)}, u32[]{:S(2)}) %collective-permute-start.5) | collective-permute-done | bytes 1572896 | tf_op jit(solution)/shard_map/ppermute | solution.py:38
  78.9 4.8 %all-to-all-done.1 = bf16[16,40,2048]{2,1,0:T(8,128)(2,1)S(1)} async-done(((bf16[16,40,2048]{2,1,0:T(8,128)(2,1)}), bf16[16,40,2048]{2,1,0:T(8,128)(2,1)S(1)}, u32[]{:S(2)}, u32[]{:S(2)}) %all-to-all-start.1) | async-done | bytes 2621472 | tf_op jit(solution)/shard_map/all_to_all | solution.py:42
  85.1 10.5 %shard_map.121 = (bf16[384,2048]{1,0:T(8,128)(2,1)S(1)}, bf16[320,2048]{1,0:T(8,128)(2,1)S(1)}, bf16[320,2048]{1,0:T(8,128)(2,1)S(1)}, bf16[320,512]{1,0:T(8,128)(2,1)S(1)}, bf16[320,1024]{1,0:T(8,128)(2,1)S(1)}) custom-call(s32[1]{0:T(128)} %bitcast.info, bf16[640,2048]{1,0:T(8,128)(2,1)S(1)} %bitcast.29, bf16[16,384,128]{2,1,0:T(8,128)(2,1)} %all-to-all-done.w0, ...), custom_call_target="tpu_custom_call" | custom-call | flops 5368709120 | bytes 14680064 | tf_op jit(solution)/shard_map/pallas_call | solution.py:223
  97.0 4.0 %shard_map.124 = (bf16[2,16,64,512]{3,2,1,0:T(8,128)(2,1)S(1)}, bf16[2,16,64,512]{3,2,1,0:T(8,128)(2,1)}) custom-call(s32[1]{0:T(128)} %bitcast.info, bf16[320,2048]{1,0:T(8,128)(2,1)S(1)} %get-tuple-element.56.a_ref, bf16[320,1024]{1,0:T(8,128)(2,1)S(1)} %get-tuple-element.57.b_ref), custom_call_target="tpu_custom_call" | custom-call | flops 10000000000 | bytes 1024 | tf_op jit(solution)/shard_map/pallas_call | solution.py:274
  104.1 3.7 %all-to-all-start.2 = ((bf16[16,24,2048]{2,1,0:T(8,128)(2,1)}), bf16[16,24,2048]{2,1,0:T(8,128)(2,1)S(1)}, u32[]{:S(2)}, u32[]{:S(2)}) async-start(bf16[16,24,2048]{2,1,0:T(8,128)(2,1)} %bitcast.31), calls=%async_computation.2 | async-start | bytes 3145728 | tf_op jit(solution)/shard_map/all_to_all | solution.py:42
  107.8 10.1 %collective-permute-done.9.refs_2_ = bf16[16,32,512]{2,1,0:T(8,128)(2,1)} collective-permute-done((bf16[16,32,512]{2,1,0:T(8,128)(2,1)}, bf16[16,32,512]{2,1,0:T(8,128)(2,1)}, u32[]{:S(2)}, u32[]{:S(2)}) %collective-permute-start.9) | collective-permute-done | bytes 524320 | tf_op jit(solution)/shard_map/ppermute | solution.py:38
  117.9 2.4 %shard_map.126 = bf16[16,64,512]{2,1,0:T(8,128)(2,1)} custom-call(bf16[2,16,64,512]{3,2,1,0:T(8,128)(2,1)} %copy-done.3, bf16[2,16,64,512]{3,2,1,0:T(8,128)(2,1)} %collective-permute-done.10.refs_1_), custom_call_target="tpu_custom_call" | custom-call | flops 99999997952 | bytes 1024 | tf_op jit(solution)/shard_map/pallas_call | solution.py:359
  120.3 1.9 shard_map.125
  122.2 11.0 %all-to-all-done.2 = bf16[16,24,2048]{2,1,0:T(8,128)(2,1)S(1)} async-done(((bf16[16,24,2048]{2,1,0:T(8,128)(2,1)}), bf16[16,24,2048]{2,1,0:T(8,128)(2,1)S(1)}, u32[]{:S(2)}, u32[]{:S(2)}) %all-to-all-start.2) | async-done | bytes 1572896 | tf_op jit(solution)/shard_map/all_to_all | solution.py:42
  133.3 3.6 %all-to-all-start.3 = ((bf16[16,32,512]{2,1,0:T(8,128)(2,1)}), bf16[16,32,512]{2,1,0:T(8,128)(2,1)S(1)}, u32[]{:S(2)}, u32[]{:S(2)}) async-start(bf16[16,32,512]{2,1,0:T(8,128)(2,1)} %shard_map.125), calls=%async_computation.3 | async-start | bytes 1048576 | tf_op jit(solution)/shard_map/all_to_all | solution.py:42
  136.8 1.5 shard_map.128
  138.3 3.5 %collective-permute-start.13 = (bf16[128,2048]{1,0:T(8,128)(2,1)}, bf16[128,2048]{1,0:T(8,128)(2,1)S(1)}, u32[]{:S(2)}, u32[]{:S(2)}) collective-permute-start(bf16[128,2048]{1,0:T(8,128)(2,1)} %get-tuple-element.69), channel_id=1, source_target_pairs={{0,192},{1,193},{2,0},{3,1},{64,194},{65,195},{66,2},{67,3},{128,6... | collective-permute-start | bytes 1572872 | tf_op jit(solution)/shard_map/ppermute | solution.py:38
  141.8 6.5 %collective-permute-done.11.refs_2_ = bf16[16,64,512]{2,1,0:T(8,128)(2,1)} collective-permute-done((bf16[16,64,512]{2,1,0:T(8,128)(2,1)}, bf16[16,64,512]{2,1,0:T(8,128)(2,1)}, u32[]{:S(2)}, u32[]{:S(2)}) %collective-permute-start.11) | collective-permute-done | bytes 1048608 | tf_op jit(solution)/shard_map/ppermute | solution.py:38
  148.3 2.8 %shard_map.127 = bf16[16,64,512]{2,1,0:T(8,128)(2,1)} custom-call(bf16[2,16,64,512]{3,2,1,0:T(8,128)(2,1)} %copy-done.3, bf16[2,16,64,512]{3,2,1,0:T(8,128)(2,1)} %collective-permute-done.10.refs_1_, bf16[16,64,512]{2,1,0:T(8,128)(2,1)} %collective-permute-done.11.refs_2_), custom_call_target="tpu_custom_call" | custom-call | bytes 1024 | tf_op jit(solution)/shard_map/pallas_call | solution.py:359
  151.9 3.7 %all-to-all-start.4 = ((bf16[16,64,512]{2,1,0:T(8,128)(2,1)}), bf16[16,64,512]{2,1,0:T(8,128)(2,1)S(1)}, u32[]{:S(2)}, u32[]{:S(2)}) async-start(bf16[16,64,512]{2,1,0:T(8,128)(2,1)} %shard_map.127), calls=%async_computation.4 | async-start | bytes 2097152 | tf_op jit(solution)/shard_map/all_to_all | solution.py:42
  157.3 1.9 %collective-permute-start.14 = (bf16[1,8,32,512]{3,2,1,0:T(8,128)(2,1)S(1)}, bf16[1,8,32,512]{3,2,1,0:T(8,128)(2,1)S(1)}, u32[]{:S(2)}, u32[]{:S(2)}) collective-permute-start(bf16[1,8,32,512]{3,2,1,0:T(8,128)(2,1)S(1)} %shard_map.130), channel_id=1, source_target_pairs={{0,0},{1,1},{2,64},{3,65},{64,2},{65,3},{66,66},{67,67},{128,128},... | collective-permute-start | bytes 786440 | tf_op jit(solution)/shard_map/ppermute | solution.py:38
  159.3 4.5 %collective-permute-start.12 = (bf16[8,128]{1,0:T(8,128)(2,1)S(1)}, bf16[8,128]{1,0:T(8,128)(2,1)S(1)}, u32[]{:S(2)}, u32[]{:S(2)}) collective-permute-start(bf16[8,128]{1,0:T(8,128)(2,1)S(1)} %get-tuple-element.68), channel_id=1, source_target_pairs={{0,0},{1,1},{2,64},{3,65},{64,2},{65,3},{66,66},{67,67},{128,128},... | collective-permute-start | bytes 6152 | tf_op jit(solution)/shard_map/ppermute | solution.py:38
  164.6 6.9 %collective-permute-done.12 = bf16[8,128]{1,0:T(8,128)(2,1)S(1)} collective-permute-done((bf16[8,128]{1,0:T(8,128)(2,1)S(1)}, bf16[8,128]{1,0:T(8,128)(2,1)S(1)}, u32[]{:S(2)}, u32[]{:S(2)}) %collective-permute-start.12) | collective-permute-done | bytes 2080 | tf_op jit(solution)/shard_map/ppermute | solution.py:38
  172.4 2.2 %collective-permute-start.15 = (bf16[2,8,32,512]{3,2,1,0:T(8,128)(2,1)S(1)}, bf16[2,8,32,512]{3,2,1,0:T(8,128)(2,1)S(1)}, u32[]{:S(2)}, u32[]{:S(2)}) collective-permute-start(bf16[2,8,32,512]{3,2,1,0:T(8,128)(2,1)S(1)} %shard_map.131), channel_id=1, source_target_pairs={{0,0},{1,1},{2,64},{3,65},{64,2},{65,3},{66,66},{67,67},{128,128},... | collective-permute-start | bytes 1572872 | tf_op jit(solution)/shard_map/ppermute | solution.py:38
  175.1 13.6 %collective-permute-done.15 = bf16[2,8,32,512]{3,2,1,0:T(8,128)(2,1)S(1)} collective-permute-done((bf16[2,8,32,512]{3,2,1,0:T(8,128)(2,1)S(1)}, bf16[2,8,32,512]{3,2,1,0:T(8,128)(2,1)S(1)}, u32[]{:S(2)}, u32[]{:S(2)}) %collective-permute-start.15) | collective-permute-done | bytes 524320 | tf_op jit(solution)/shard_map/ppermute | solution.py:38
  (64 shorter events, 18.6 us)
Async XLA Ops:
  0.7 5.6 %copy-start.11 = (s32[1,8]{1,0:T(1,128)S(1)}, s32[1,8]{1,0:T(1,128)}, u32[]{:S(2)}) copy-start(s32[1,8]{1,0:T(1,128)} %param.12) | copy-start | bytes 100
  0.7 5.7 %copy-start.12 = (bf16[1,128,2048]{2,1,0:T(8,128)(2,1)S(1)}, bf16[1,128,2048]{2,1,0:T(8,128)(2,1)}, u32[]{:S(2)}) copy-start(bf16[1,128,2048]{2,1,0:T(8,128)(2,1)} %param.8) | copy-start | bytes 1572868
  0.7 9.2 %copy-start.13 = (s32[1,128,2]{1,2,0:T(2,128)S(1)}, s32[1,128,2]{1,2,0:T(2,128)}, u32[]{:S(2)}) copy-start(s32[1,128,2]{1,2,0:T(2,128)} %param.11) | copy-start | bytes 3076
  0.7 9.2 %copy-start.10 = (bf16[1,128,2]{1,2,0:T(2,128)(2,1)S(1)}, bf16[1,128,2]{1,2,0:T(2,128)(2,1)}, u32[]{:S(2)}) copy-start(bf16[1,128,2]{1,2,0:T(2,128)(2,1)} %param.10) | copy-start | bytes 1540
  2.9 7.7 %collective-permute-start.1 = (bf16[24,128,128]{2,1,0:T(8,128)(2,1)S(1)}, bf16[24,128,128]{2,1,0:T(8,128)(2,1)S(1)}, u32[]{:S(2)}, u32[]{:S(2)}) collective-permute-start(bf16[24,128,128]{2,1,0:T(8,128)(2,1)S(1)} %pad_maximum_fusion), channel_id=1, source_target_pairs={{0,64},{1,65},{2,66},{3,67},{64,0},{65,1},{66,2},{67,3},{128,192},... | collective-permute-start | bytes 2359304 | tf_op jit(solution)/shard_map/ppermute | solution.py:38
  6.2 3.8 %collective-permute-start = (s32[8]{0:T(128)S(1)}, s32[8]{0:T(128)S(1)}, u32[]{:S(2)}, u32[]{:S(2)}) collective-permute-start(s32[8]{0:T(128)S(1)} %bitcast.34), channel_id=1, source_target_pairs={{0,64},{1,65},{2,66},{3,67},{64,0},{65,1},{66,2},{67,3},{128,192},... | collective-permute-start | bytes 104 | tf_op jit(solution)/shard_map/ppermute | solution.py:38
  6.4 23.0 %collective-permute-start.3 = (bf16[128,2048]{1,0:T(8,128)(2,1)S(1)}, bf16[128,2048]{1,0:T(8,128)(2,1)S(1)}, u32[]{:S(2)}, u32[]{:S(2)}) collective-permute-start(bf16[128,2048]{1,0:T(8,128)(2,1)S(1)} %bitcast.35), channel_id=1, source_target_pairs={{0,0},{1,1},{2,64},{3,65},{64,2},{65,3},{66,66},{67,67},{128,128},... | collective-permute-start | bytes 1572872 | tf_op jit(solution)/shard_map/ppermute | solution.py:38
  14.9 19.7 %collective-permute-start.4 = (bf16[128,2048]{1,0:T(8,128)(2,1)}, bf16[128,2048]{1,0:T(8,128)(2,1)S(1)}, u32[]{:S(2)}, u32[]{:S(2)}) collective-permute-start(bf16[128,2048]{1,0:T(8,128)(2,1)} %bitcast.11), channel_id=1, source_target_pairs={{0,0},{1,1},{2,64},{3,65},{64,2},{65,3},{66,66},{67,67},{128,128},... | collective-permute-start | bytes 1572872 | tf_op jit(solution)/shard_map/ppermute | solution.py:38
  17.9 16.7 %collective-permute-start.2 = (bf16[8,128]{1,0:T(8,128)(2,1)S(1)}, bf16[8,128]{1,0:T(8,128)(2,1)S(1)}, u32[]{:S(2)}, u32[]{:S(2)}) collective-permute-start(bf16[8,128]{1,0:T(8,128)(2,1)S(1)} %maximum_maximum_fusion), channel_id=1, source_target_pairs={{0,0},{1,1},{2,64},{3,65},{64,2},{65,3},{66,66},{67,67},{128,128},... | collective-permute-start | bytes 6152 | tf_op jit(solution)/shard_map/ppermute | solution.py:38
  21.4 25.1 %all-to-all-start = ((bf16[16,384,128]{2,1,0:T(8,128)(2,1)}), bf16[16,384,128]{2,1,0:T(8,128)(2,1)}, u32[]{:S(2)}, u32[]{:S(2)}) async-start(bf16[16,384,128]{2,1,0:T(8,128)(2,1)} %shard_map.119), calls=%async_computation | async-start | bytes 3145728 | tf_op jit(solution)/shard_map/all_to_all | solution.py:42
  36.3 1.5 copy-start.2
  46.5 31.1 %collective-permute-start.5 = (bf16[16,384,128]{2,1,0:T(8,128)(2,1)}, bf16[16,384,128]{2,1,0:T(8,128)(2,1)}, u32[]{:S(2)}, u32[]{:S(2)}) collective-permute-start(bf16[16,384,128]{2,1,0:T(8,128)(2,1)} %all-to-all-done.w0), channel_id=1, source_target_pairs={{0,1},{1,0},{2,3},{3,2},{64,65},{65,64},{66,67},{67,66},{128,129},... | collective-permute-start | bytes 4718600 | tf_op jit(solution)/shard_map/ppermute | solution.py:38
  48.1 35.5 %all-to-all-start.1 = ((bf16[16,40,2048]{2,1,0:T(8,128)(2,1)}), bf16[16,40,2048]{2,1,0:T(8,128)(2,1)S(1)}, u32[]{:S(2)}, u32[]{:S(2)}) async-start(bf16[16,40,2048]{2,1,0:T(8,128)(2,1)} %bitcast.30), calls=%async_computation.1 | async-start | bytes 5242880 | tf_op jit(solution)/shard_map/all_to_all | solution.py:42
  51.9 25.7 %collective-permute-start.6 = (bf16[16,384,128]{2,1,0:T(8,128)(2,1)}, bf16[16,384,128]{2,1,0:T(8,128)(2,1)S(1)}, u32[]{:S(2)}, u32[]{:S(2)}) collective-permute-start(bf16[16,384,128]{2,1,0:T(8,128)(2,1)} %all-to-all-done.w0), channel_id=1, source_target_pairs={{0,64},{1,65},{2,66},{3,67},{64,0},{65,1},{66,2},{67,3},{128,192},... | collective-permute-start | bytes 4718600 | tf_op jit(solution)/shard_map/ppermute | solution.py:38
  77.6 6.0 %collective-permute-start.7 = (bf16[16,384,128]{2,1,0:T(8,128)(2,1)}, bf16[16,384,128]{2,1,0:T(8,128)(2,1)}, u32[]{:S(2)}, u32[]{:S(2)}) collective-permute-start(bf16[16,384,128]{2,1,0:T(8,128)(2,1)} %collective-permute-done.5.w1), channel_id=1, source_target_pairs={{0,64},{1,65},{2,66},{3,67},{64,0},{65,1},{66,2},{67,3},{128,192},... | collective-permute-start | bytes 4718600 | tf_op jit(solution)/shard_map/ppermute | solution.py:38
  77.6 1.3 copy-start.7
  83.7 1.4 copy-start.8
  95.5 5.4 %copy-start.4 = (bf16[384,2048]{1,0:T(8,128)(2,1)}, bf16[384,2048]{1,0:T(8,128)(2,1)S(1)}, u32[]{:S(2)}) copy-start(bf16[384,2048]{1,0:T(8,128)(2,1)S(1)} %get-tuple-element.53) | copy-start | bytes 4718596
  96.9 4.1 %collective-permute-start.8 = (bf16[2,16,32,512]{3,2,1,0:T(8,128)(2,1)S(1)}, bf16[2,16,32,512]{3,2,1,0:T(8,128)(2,1)S(1)}, u32[]{:S(2)}, u32[]{:S(2)}) collective-permute-start(bf16[2,16,32,512]{3,2,1,0:T(8,128)(2,1)S(1)} %get-tuple-element.55), channel_id=1, source_target_pairs={{0,64},{1,65},{2,66},{3,67},{64,0},{65,1},{66,2},{67,3},{128,192},... | collective-permute-start | bytes 3145736 | tf_op jit(solution)/shard_map/ppermute | solution.py:38
  101.0 1.5 copy-start.3
  102.5 1.1 copy-start
  103.6 14.3 %collective-permute-start.10 = (bf16[2,16,64,512]{3,2,1,0:T(8,128)(2,1)}, bf16[2,16,64,512]{3,2,1,0:T(8,128)(2,1)}, u32[]{:S(2)}, u32[]{:S(2)}) collective-permute-start(bf16[2,16,64,512]{3,2,1,0:T(8,128)(2,1)} %get-tuple-element.62), channel_id=1, source_target_pairs={{0,64},{1,65},{2,66},{3,67},{64,0},{65,1},{66,2},{67,3},{128,192},... | collective-permute-start | bytes 6291464 | tf_op jit(solution)/shard_map/ppermute | solution.py:38
  104.1 13.8 %collective-permute-start.9 = (bf16[16,32,512]{2,1,0:T(8,128)(2,1)}, bf16[16,32,512]{2,1,0:T(8,128)(2,1)}, u32[]{:S(2)}, u32[]{:S(2)}) collective-permute-start(bf16[16,32,512]{2,1,0:T(8,128)(2,1)} %shard_map.123), channel_id=1, source_target_pairs={{0,1},{1,0},{2,3},{3,2},{64,65},{65,64},{66,67},{67,66},{128,129},... | collective-permute-start | bytes 1572872 | tf_op jit(solution)/shard_map/ppermute | solution.py:38
  104.1 29.2 %all-to-all-start.2 = ((bf16[16,24,2048]{2,1,0:T(8,128)(2,1)}), bf16[16,24,2048]{2,1,0:T(8,128)(2,1)S(1)}, u32[]{:S(2)}, u32[]{:S(2)}) async-start(bf16[16,24,2048]{2,1,0:T(8,128)(2,1)} %bitcast.31), calls=%async_computation.2 | async-start | bytes 3145728 | tf_op jit(solution)/shard_map/all_to_all | solution.py:42
  107.8 12.6 %copy-start.1 = (bf16[2,16,32,512]{3,2,1,0:T(8,128)(2,1)S(1)}, bf16[2,16,32,512]{3,2,1,0:T(8,128)(2,1)}, u32[]{:S(2)}) copy-start(bf16[2,16,32,512]{3,2,1,0:T(8,128)(2,1)} %copy-done) | copy-start | bytes 3145732
  120.3 28.0 %collective-permute-start.11 = (bf16[16,64,512]{2,1,0:T(8,128)(2,1)}, bf16[16,64,512]{2,1,0:T(8,128)(2,1)}, u32[]{:S(2)}, u32[]{:S(2)}) collective-permute-start(bf16[16,64,512]{2,1,0:T(8,128)(2,1)} %shard_map.126), channel_id=1, source_target_pairs={{0,1},{1,0},{2,3},{3,2},{64,65},{65,64},{66,67},{67,66},{128,129},... | collective-permute-start | bytes 3145736 | tf_op jit(solution)/shard_map/ppermute | solution.py:38
  133.3 17.9 %all-to-all-start.3 = ((bf16[16,32,512]{2,1,0:T(8,128)(2,1)}), bf16[16,32,512]{2,1,0:T(8,128)(2,1)S(1)}, u32[]{:S(2)}, u32[]{:S(2)}) async-start(bf16[16,32,512]{2,1,0:T(8,128)(2,1)} %shard_map.125), calls=%async_computation.3 | async-start | bytes 1048576 | tf_op jit(solution)/shard_map/all_to_all | solution.py:42
  138.3 25.5 %collective-permute-start.13 = (bf16[128,2048]{1,0:T(8,128)(2,1)}, bf16[128,2048]{1,0:T(8,128)(2,1)S(1)}, u32[]{:S(2)}, u32[]{:S(2)}) collective-permute-start(bf16[128,2048]{1,0:T(8,128)(2,1)} %get-tuple-element.69), channel_id=1, source_target_pairs={{0,192},{1,193},{2,0},{3,1},{64,194},{65,195},{66,2},{67,3},{128,6... | collective-permute-start | bytes 1572872 | tf_op jit(solution)/shard_map/ppermute | solution.py:38
  151.9 19.6 %all-to-all-start.4 = ((bf16[16,64,512]{2,1,0:T(8,128)(2,1)}), bf16[16,64,512]{2,1,0:T(8,128)(2,1)S(1)}, u32[]{:S(2)}, u32[]{:S(2)}) async-start(bf16[16,64,512]{2,1,0:T(8,128)(2,1)} %shard_map.127), calls=%async_computation.4 | async-start | bytes 2097152 | tf_op jit(solution)/shard_map/all_to_all | solution.py:42
  157.3 14.2 %collective-permute-start.14 = (bf16[1,8,32,512]{3,2,1,0:T(8,128)(2,1)S(1)}, bf16[1,8,32,512]{3,2,1,0:T(8,128)(2,1)S(1)}, u32[]{:S(2)}, u32[]{:S(2)}) collective-permute-start(bf16[1,8,32,512]{3,2,1,0:T(8,128)(2,1)S(1)} %shard_map.130), channel_id=1, source_target_pairs={{0,0},{1,1},{2,64},{3,65},{64,2},{65,3},{66,66},{67,67},{128,128},... | collective-permute-start | bytes 786440 | tf_op jit(solution)/shard_map/ppermute | solution.py:38
  159.3 12.3 %collective-permute-start.12 = (bf16[8,128]{1,0:T(8,128)(2,1)S(1)}, bf16[8,128]{1,0:T(8,128)(2,1)S(1)}, u32[]{:S(2)}, u32[]{:S(2)}) collective-permute-start(bf16[8,128]{1,0:T(8,128)(2,1)S(1)} %get-tuple-element.68), channel_id=1, source_target_pairs={{0,0},{1,1},{2,64},{3,65},{64,2},{65,3},{66,66},{67,67},{128,128},... | collective-permute-start | bytes 6152 | tf_op jit(solution)/shard_map/ppermute | solution.py:38
  172.4 16.3 %collective-permute-start.15 = (bf16[2,8,32,512]{3,2,1,0:T(8,128)(2,1)S(1)}, bf16[2,8,32,512]{3,2,1,0:T(8,128)(2,1)S(1)}, u32[]{:S(2)}, u32[]{:S(2)}) collective-permute-start(bf16[2,8,32,512]{3,2,1,0:T(8,128)(2,1)S(1)} %shard_map.131), channel_id=1, source_target_pairs={{0,0},{1,1},{2,64},{3,65},{64,2},{65,3},{66,66},{67,67},{128,128},... | collective-permute-start | bytes 1572872 | tf_op jit(solution)/shard_map/ppermute | solution.py:38
  (3 other events, 2.7 us)

commit v10 on v9

--- a/solution.py
+++ b/solution.py
@@ -353,13 +353,13 @@
 
 def add(which, pairs, *more, cost=0, room=16):
     shape = pairs[0].shape[1:]
-    block = (8,) + shape[1:]
+    block = (16,) + shape[1:]
     pair = pl.BlockSpec((1,) + block, lambda n: (which, n, 0, 0))
     one = pl.BlockSpec(block, lambda n: (n, 0, 0))
     return pl.pallas_call(
         add_kernel,
         out_shape=jax.ShapeDtypeStruct(shape, BF),
-        grid=(2,),
+        grid=(1,),
         in_specs=[pair, pair] + [one] * len(more),
         out_specs=one,
         compiler_params=vmem(room),

time: 191 us -> 192 us (level)
  transfers between devices with their start and end apart: 21 -> 21, of which waited for: 10 -> 10; matrix products, arithmetic and copies ran while one was open for 1% -> 1% of each run, Pallas kernels for 10% -> 11%
where the time goes in v10:
time: 192 us; the launch traced here: 191 us
  waiting for transfers between devices  93.7 us (49%)
  starting transfers between devices  49 us (26%)
  Pallas kernels  33.8 us (18%)
  local copies, waits for them, and re-layouts  12.7 us (7%)
    ppermute x16, waiting for transfers between devices, move(): return lax.ppermute(x, ('pipe', 'dp'), pairs)  69.7 us
    ppermute x16, starting transfers between devices, move(): return lax.ppermute(x, ('pipe', 'dp'), pairs)  27.6 us
    all_to_all x5, waiting for transfers between devices, spread(): return lax.all_to_all(x, 'expert', split_axis=0, concat_axis=0, tiled=True)  24 us
    all_to_all x5, starting transfers between devices, spread(): return lax.all_to_all(x, 'expert', split_axis=0, concat_axis=0, tiled=True)  21.5 us
    pallas_call x1, Pallas kernels, expert_rows(): pl.pallas_call(expert_kernel, out_shape=[jax.ShapeDtypeStruct((SLOTS * BA...  10.5 us
    unnamed x29, local copies, waits for them, and re-layouts  9.14 us
    pallas_call x4, Pallas kernels, add(): pl.pallas_call(add_kernel, out_shape=jax.ShapeDtypeStruct(shape, BF), gri...  9.08 us
    pallas_call x2, Pallas kernels, weight_sums(): pl.pallas_call(functools.partial(sums_kernel, kinds), out_shape=[shape, s...  5.31 us
  transfers between devices with their start and end apart: 21, of which 10 were waited for; matrix products, arithmetic and copies ran while one was open for 1% of the time, Pallas kernels for 11%

profile of v10, /device:TPU:1, one launch (start us, length us, event | category | flops | bytes accessed | tf_op | source)
XLA Modules:
  0.0 190.9 jit_solution(5103157563107551267)
XLA Ops:
  2.9 3.3 %collective-permute-start.1 = (bf16[24,128,128]{2,1,0:T(8,128)(2,1)S(1)}, bf16[24,128,128]{2,1,0:T(8,128)(2,1)S(1)}, u32[]{:S(2)}, u32[]{:S(2)}) collective-permute-start(bf16[24,128,128]{2,1,0:T(8,128)(2,1)S(1)} %pad_maximum_fusion), channel_id=1, source_target_pairs={{0,64},{1,65},{2,66},{3,67},{64,0},{65,1},{66,2},{67,3},{128,192},... | collective-permute-start | bytes 2359304 | tf_op jit(solution)/shard_map/ppermute | solution.py:38
  6.4 3.4 %collective-permute-start.3 = (bf16[128,2048]{1,0:T(8,128)(2,1)S(1)}, bf16[128,2048]{1,0:T(8,128)(2,1)S(1)}, u32[]{:S(2)}, u32[]{:S(2)}) collective-permute-start(bf16[128,2048]{1,0:T(8,128)(2,1)S(1)} %bitcast.35), channel_id=1, source_target_pairs={{0,0},{1,1},{2,64},{3,65},{64,2},{65,3},{66,66},{67,67},{128,128},... | collective-permute-start | bytes 1572872 | tf_op jit(solution)/shard_map/ppermute | solution.py:38
  11.5 3.4 %shard_map.119 = bf16[16,384,128]{2,1,0:T(8,128)(2,1)} custom-call(s32[18]{0:T(128)} %pad_add_fusion.info, bf16[1,8,128,512]{3,2,1,0:T(8,128)(2,1)} %gate.1, bf16[1,8,128,512]{3,2,1,0:T(8,128)(2,1)} %up.1, bf16[1,8,128,512]{3,2,1,0:T(8,128)(2,1)} %down.1, bf16[24,128,128]{2,1,0:T(8,128)(2,1)} %copy-done.9), custom_call_target="tpu_custom_call" | custom-call | bytes 4194304 | tf_op jit(solution)/shard_map/pallas_call | solution.py:100
  14.9 3.0 %collective-permute-start.4 = (bf16[128,2048]{1,0:T(8,128)(2,1)}, bf16[128,2048]{1,0:T(8,128)(2,1)S(1)}, u32[]{:S(2)}, u32[]{:S(2)}) collective-permute-start(bf16[128,2048]{1,0:T(8,128)(2,1)} %bitcast.11), channel_id=1, source_target_pairs={{0,0},{1,1},{2,64},{3,65},{64,2},{65,3},{66,66},{67,67},{128,128},... | collective-permute-start | bytes 1572872 | tf_op jit(solution)/shard_map/ppermute | solution.py:38
  17.9 3.5 %collective-permute-start.2 = (bf16[8,128]{1,0:T(8,128)(2,1)S(1)}, bf16[8,128]{1,0:T(8,128)(2,1)S(1)}, u32[]{:S(2)}, u32[]{:S(2)}) collective-permute-start(bf16[8,128]{1,0:T(8,128)(2,1)S(1)} %maximum_maximum_fusion), channel_id=1, source_target_pairs={{0,0},{1,1},{2,64},{3,65},{64,2},{65,3},{66,66},{67,67},{128,128},... | collective-permute-start | bytes 6152 | tf_op jit(solution)/shard_map/ppermute | solution.py:38
  21.4 6.8 %all-to-all-start = ((bf16[16,384,128]{2,1,0:T(8,128)(2,1)}), bf16[16,384,128]{2,1,0:T(8,128)(2,1)}, u32[]{:S(2)}, u32[]{:S(2)}) async-start(bf16[16,384,128]{2,1,0:T(8,128)(2,1)} %shard_map.119), calls=%async_computation | async-start | bytes 3145728 | tf_op jit(solution)/shard_map/all_to_all | solution.py:42
  29.4 5.3 %collective-permute-done.2.notes_ref = bf16[8,128]{1,0:T(8,128)(2,1)S(1)} collective-permute-done((bf16[8,128]{1,0:T(8,128)(2,1)S(1)}, bf16[8,128]{1,0:T(8,128)(2,1)S(1)}, u32[]{:S(2)}, u32[]{:S(2)}) %collective-permute-start.2) | collective-permute-done | bytes 2080 | tf_op jit(solution)/shard_map/ppermute | solution.py:38
  34.7 1.7 shard_map.120
  36.4 1.5 copy-done.2
  37.8 8.7 %all-to-all-done.w0 = bf16[16,384,128]{2,1,0:T(8,128)(2,1)} async-done(((bf16[16,384,128]{2,1,0:T(8,128)(2,1)}), bf16[16,384,128]{2,1,0:T(8,128)(2,1)}, u32[]{:S(2)}, u32[]{:S(2)}) %all-to-all-start) | async-done | bytes 1572896 | tf_op jit(solution)/shard_map/all_to_all | solution.py:42
  46.5 1.6 collective-permute-start.5
  48.1 3.7 %all-to-all-start.1 = ((bf16[16,40,2048]{2,1,0:T(8,128)(2,1)}), bf16[16,40,2048]{2,1,0:T(8,128)(2,1)S(1)}, u32[]{:S(2)}, u32[]{:S(2)}) async-start(bf16[16,40,2048]{2,1,0:T(8,128)(2,1)} %bitcast.30), calls=%async_computation.1 | async-start | bytes 5242880 | tf_op jit(solution)/shard_map/all_to_all | solution.py:42
  52.0 25.6 %collective-permute-done.5.w1 = bf16[16,384,128]{2,1,0:T(8,128)(2,1)} collective-permute-done((bf16[16,384,128]{2,1,0:T(8,128)(2,1)}, bf16[16,384,128]{2,1,0:T(8,128)(2,1)}, u32[]{:S(2)}, u32[]{:S(2)}) %collective-permute-start.5) | collective-permute-done | bytes 1572896 | tf_op jit(solution)/shard_map/ppermute | solution.py:38
  78.9 4.8 %all-to-all-done.1 = bf16[16,40,2048]{2,1,0:T(8,128)(2,1)S(1)} async-done(((bf16[16,40,2048]{2,1,0:T(8,128)(2,1)}), bf16[16,40,2048]{2,1,0:T(8,128)(2,1)S(1)}, u32[]{:S(2)}, u32[]{:S(2)}) %all-to-all-start.1) | async-done | bytes 2621472 | tf_op jit(solution)/shard_map/all_to_all | solution.py:42
  85.1 10.5 %shard_map.121 = (bf16[384,2048]{1,0:T(8,128)(2,1)S(1)}, bf16[320,2048]{1,0:T(8,128)(2,1)S(1)}, bf16[320,2048]{1,0:T(8,128)(2,1)S(1)}, bf16[320,512]{1,0:T(8,128)(2,1)S(1)}, bf16[320,1024]{1,0:T(8,128)(2,1)S(1)}) custom-call(s32[1]{0:T(128)} %bitcast.info, bf16[640,2048]{1,0:T(8,128)(2,1)S(1)} %bitcast.29, bf16[16,384,128]{2,1,0:T(8,128)(2,1)} %all-to-all-done.w0, ...), custom_call_target="tpu_custom_call" | custom-call | flops 5368709120 | bytes 14680064 | tf_op jit(solution)/shard_map/pallas_call | solution.py:223
  97.0 4.0 %shard_map.124 = (bf16[2,16,64,512]{3,2,1,0:T(8,128)(2,1)S(1)}, bf16[2,16,64,512]{3,2,1,0:T(8,128)(2,1)}) custom-call(s32[1]{0:T(128)} %bitcast.info, bf16[320,2048]{1,0:T(8,128)(2,1)S(1)} %get-tuple-element.56.a_ref, bf16[320,1024]{1,0:T(8,128)(2,1)S(1)} %get-tuple-element.57.b_ref), custom_call_target="tpu_custom_call" | custom-call | flops 10000000000 | bytes 1024 | tf_op jit(solution)/shard_map/pallas_call | solution.py:274
  104.1 3.7 %all-to-all-start.2 = ((bf16[16,24,2048]{2,1,0:T(8,128)(2,1)}), bf16[16,24,2048]{2,1,0:T(8,128)(2,1)S(1)}, u32[]{:S(2)}, u32[]{:S(2)}) async-start(bf16[16,24,2048]{2,1,0:T(8,128)(2,1)} %bitcast.31), calls=%async_computation.2 | async-start | bytes 3145728 | tf_op jit(solution)/shard_map/all_to_all | solution.py:42
  107.8 10.1 %collective-permute-done.9.refs_2_ = bf16[16,32,512]{2,1,0:T(8,128)(2,1)} collective-permute-done((bf16[16,32,512]{2,1,0:T(8,128)(2,1)}, bf16[16,32,512]{2,1,0:T(8,128)(2,1)}, u32[]{:S(2)}, u32[]{:S(2)}) %collective-permute-start.9) | collective-permute-done | bytes 524320 | tf_op jit(solution)/shard_map/ppermute | solution.py:38
  117.9 2.8 %shard_map.126 = bf16[16,64,512]{2,1,0:T(8,128)(2,1)} custom-call(bf16[2,16,64,512]{3,2,1,0:T(8,128)(2,1)} %copy-done.3, bf16[2,16,64,512]{3,2,1,0:T(8,128)(2,1)} %collective-permute-done.10.refs_1_), custom_call_target="tpu_custom_call" | custom-call | flops 99999997952 | bytes 1024 | tf_op jit(solution)/shard_map/pallas_call | solution.py:359
  120.7 2.1 %shard_map.125 = bf16[16,32,512]{2,1,0:T(8,128)(2,1)} custom-call(bf16[2,16,32,512]{3,2,1,0:T(8,128)(2,1)S(1)} %get-tuple-element.54.refs_0_, bf16[2,16,32,512]{3,2,1,0:T(8,128)(2,1)S(1)} %copy-done.1, bf16[16,32,512]{2,1,0:T(8,128)(2,1)} %collective-permute-done.9.refs_2_), custom_call_target="tpu_custom_call" | custom-call | bytes 1024 | tf_op jit(solution)/shard_map/pallas_call | solution.py:359
  122.7 10.5 %all-to-all-done.2 = bf16[16,24,2048]{2,1,0:T(8,128)(2,1)S(1)} async-done(((bf16[16,24,2048]{2,1,0:T(8,128)(2,1)}), bf16[16,24,2048]{2,1,0:T(8,128)(2,1)S(1)}, u32[]{:S(2)}, u32[]{:S(2)}) %all-to-all-start.2) | async-done | bytes 1572896 | tf_op jit(solution)/shard_map/all_to_all | solution.py:42
  133.3 3.6 %all-to-all-start.3 = ((bf16[16,32,512]{2,1,0:T(8,128)(2,1)}), bf16[16,32,512]{2,1,0:T(8,128)(2,1)S(1)}, u32[]{:S(2)}, u32[]{:S(2)}) async-start(bf16[16,32,512]{2,1,0:T(8,128)(2,1)} %shard_map.125), calls=%async_computation.3 | async-start | bytes 1048576 | tf_op jit(solution)/shard_map/all_to_all | solution.py:42
  136.8 1.5 shard_map.128
  138.3 3.5 %collective-permute-start.13 = (bf16[128,2048]{1,0:T(8,128)(2,1)}, bf16[128,2048]{1,0:T(8,128)(2,1)S(1)}, u32[]{:S(2)}, u32[]{:S(2)}) collective-permute-start(bf16[128,2048]{1,0:T(8,128)(2,1)} %get-tuple-element.69), channel_id=1, source_target_pairs={{0,192},{1,193},{2,0},{3,1},{64,194},{65,195},{66,2},{67,3},{128,6... | collective-permute-start | bytes 1572872 | tf_op jit(solution)/shard_map/ppermute | solution.py:38
  141.8 7.1 %collective-permute-done.11.refs_2_ = bf16[16,64,512]{2,1,0:T(8,128)(2,1)} collective-permute-done((bf16[16,64,512]{2,1,0:T(8,128)(2,1)}, bf16[16,64,512]{2,1,0:T(8,128)(2,1)}, u32[]{:S(2)}, u32[]{:S(2)}) %collective-permute-start.11) | collective-permute-done | bytes 1048608 | tf_op jit(solution)/shard_map/ppermute | solution.py:38
  149.0 3.2 %shard_map.127 = bf16[16,64,512]{2,1,0:T(8,128)(2,1)} custom-call(bf16[2,16,64,512]{3,2,1,0:T(8,128)(2,1)} %copy-done.3, bf16[2,16,64,512]{3,2,1,0:T(8,128)(2,1)} %collective-permute-done.10.refs_1_, bf16[16,64,512]{2,1,0:T(8,128)(2,1)} %collective-permute-done.11.refs_2_), custom_call_target="tpu_custom_call" | custom-call | bytes 1024 | tf_op jit(solution)/shard_map/pallas_call | solution.py:359
  153.0 3.7 %all-to-all-start.4 = ((bf16[16,64,512]{2,1,0:T(8,128)(2,1)}), bf16[16,64,512]{2,1,0:T(8,128)(2,1)S(1)}, u32[]{:S(2)}, u32[]{:S(2)}) async-start(bf16[16,64,512]{2,1,0:T(8,128)(2,1)} %shard_map.127), calls=%async_computation.4 | async-start | bytes 2097152 | tf_op jit(solution)/shard_map/all_to_all | solution.py:42
  158.4 1.9 %collective-permute-start.14 = (bf16[1,8,32,512]{3,2,1,0:T(8,128)(2,1)S(1)}, bf16[1,8,32,512]{3,2,1,0:T(8,128)(2,1)S(1)}, u32[]{:S(2)}, u32[]{:S(2)}) collective-permute-start(bf16[1,8,32,512]{3,2,1,0:T(8,128)(2,1)S(1)} %shard_map.130), channel_id=1, source_target_pairs={{0,0},{1,1},{2,64},{3,65},{64,2},{65,3},{66,66},{67,67},{128,128},... | collective-permute-start | bytes 786440 | tf_op jit(solution)/shard_map/ppermute | solution.py:38
  160.3 4.5 %collective-permute-start.12 = (bf16[8,128]{1,0:T(8,128)(2,1)S(1)}, bf16[8,128]{1,0:T(8,128)(2,1)S(1)}, u32[]{:S(2)}, u32[]{:S(2)}) collective-permute-start(bf16[8,128]{1,0:T(8,128)(2,1)S(1)} %get-tuple-element.68), channel_id=1, source_target_pairs={{0,0},{1,1},{2,64},{3,65},{64,2},{65,3},{66,66},{67,67},{128,128},... | collective-permute-start | bytes 6152 | tf_op jit(solution)/shard_map/ppermute | solution.py:38
  165.7 6.8 %collective-permute-done.12 = bf16[8,128]{1,0:T(8,128)(2,1)S(1)} collective-permute-done((bf16[8,128]{1,0:T(8,128)(2,1)S(1)}, bf16[8,128]{1,0:T(8,128)(2,1)S(1)}, u32[]{:S(2)}, u32[]{:S(2)}) %collective-permute-start.12) | collective-permute-done | bytes 2080 | tf_op jit(solution)/shard_map/ppermute | solution.py:38
  173.3 2.0 %collective-permute-start.15 = (bf16[2,8,32,512]{3,2,1,0:T(8,128)(2,1)S(1)}, bf16[2,8,32,512]{3,2,1,0:T(8,128)(2,1)S(1)}, u32[]{:S(2)}, u32[]{:S(2)}) collective-permute-start(bf16[2,8,32,512]{3,2,1,0:T(8,128)(2,1)S(1)} %shard_map.131), channel_id=1, source_target_pairs={{0,0},{1,1},{2,64},{3,65},{64,2},{65,3},{66,66},{67,67},{128,128},... | collective-permute-start | bytes 1572872 | tf_op jit(solution)/shard_map/ppermute | solution.py:38
  175.8 13.6 %collective-permute-done.15 = bf16[2,8,32,512]{3,2,1,0:T(8,128)(2,1)S(1)} collective-permute-done((bf16[2,8,32,512]{3,2,1,0:T(8,128)(2,1)S(1)}, bf16[2,8,32,512]{3,2,1,0:T(8,128)(2,1)S(1)}, u32[]{:S(2)}, u32[]{:S(2)}) %collective-permute-start.15) | collective-permute-done | bytes 524320 | tf_op jit(solution)/shard_map/ppermute | solution.py:38
  (64 shorter events, 18.6 us)
Async XLA Ops:
  0.7 5.6 %copy-start.11 = (s32[1,8]{1,0:T(1,128)S(1)}, s32[1,8]{1,0:T(1,128)}, u32[]{:S(2)}) copy-start(s32[1,8]{1,0:T(1,128)} %param.12) | copy-start | bytes 100
  0.7 5.7 %copy-start.12 = (bf16[1,128,2048]{2,1,0:T(8,128)(2,1)S(1)}, bf16[1,128,2048]{2,1,0:T(8,128)(2,1)}, u32[]{:S(2)}) copy-start(bf16[1,128,2048]{2,1,0:T(8,128)(2,1)} %param.8) | copy-start | bytes 1572868
  0.7 9.2 %copy-start.13 = (s32[1,128,2]{1,2,0:T(2,128)S(1)}, s32[1,128,2]{1,2,0:T(2,128)}, u32[]{:S(2)}) copy-start(s32[1,128,2]{1,2,0:T(2,128)} %param.11) | copy-start | bytes 3076
  0.7 9.2 %copy-start.10 = (bf16[1,128,2]{1,2,0:T(2,128)(2,1)S(1)}, bf16[1,128,2]{1,2,0:T(2,128)(2,1)}, u32[]{:S(2)}) copy-start(bf16[1,128,2]{1,2,0:T(2,128)(2,1)} %param.10) | copy-start | bytes 1540
  2.9 7.7 %collective-permute-start.1 = (bf16[24,128,128]{2,1,0:T(8,128)(2,1)S(1)}, bf16[24,128,128]{2,1,0:T(8,128)(2,1)S(1)}, u32[]{:S(2)}, u32[]{:S(2)}) collective-permute-start(bf16[24,128,128]{2,1,0:T(8,128)(2,1)S(1)} %pad_maximum_fusion), channel_id=1, source_target_pairs={{0,64},{1,65},{2,66},{3,67},{64,0},{65,1},{66,2},{67,3},{128,192},... | collective-permute-start | bytes 2359304 | tf_op jit(solution)/shard_map/ppermute | solution.py:38
  6.2 3.8 %collective-permute-start = (s32[8]{0:T(128)S(1)}, s32[8]{0:T(128)S(1)}, u32[]{:S(2)}, u32[]{:S(2)}) collective-permute-start(s32[8]{0:T(128)S(1)} %bitcast.34), channel_id=1, source_target_pairs={{0,64},{1,65},{2,66},{3,67},{64,0},{65,1},{66,2},{67,3},{128,192},... | collective-permute-start | bytes 104 | tf_op jit(solution)/shard_map/ppermute | solution.py:38
  6.4 23.0 %collective-permute-start.3 = (bf16[128,2048]{1,0:T(8,128)(2,1)S(1)}, bf16[128,2048]{1,0:T(8,128)(2,1)S(1)}, u32[]{:S(2)}, u32[]{:S(2)}) collective-permute-start(bf16[128,2048]{1,0:T(8,128)(2,1)S(1)} %bitcast.35), channel_id=1, source_target_pairs={{0,0},{1,1},{2,64},{3,65},{64,2},{65,3},{66,66},{67,67},{128,128},... | collective-permute-start | bytes 1572872 | tf_op jit(solution)/shard_map/ppermute | solution.py:38
  14.9 19.7 %collective-permute-start.4 = (bf16[128,2048]{1,0:T(8,128)(2,1)}, bf16[128,2048]{1,0:T(8,128)(2,1)S(1)}, u32[]{:S(2)}, u32[]{:S(2)}) collective-permute-start(bf16[128,2048]{1,0:T(8,128)(2,1)} %bitcast.11), channel_id=1, source_target_pairs={{0,0},{1,1},{2,64},{3,65},{64,2},{65,3},{66,66},{67,67},{128,128},... | collective-permute-start | bytes 1572872 | tf_op jit(solution)/shard_map/ppermute | solution.py:38
  17.9 16.7 %collective-permute-start.2 = (bf16[8,128]{1,0:T(8,128)(2,1)S(1)}, bf16[8,128]{1,0:T(8,128)(2,1)S(1)}, u32[]{:S(2)}, u32[]{:S(2)}) collective-permute-start(bf16[8,128]{1,0:T(8,128)(2,1)S(1)} %maximum_maximum_fusion), channel_id=1, source_target_pairs={{0,0},{1,1},{2,64},{3,65},{64,2},{65,3},{66,66},{67,67},{128,128},... | collective-permute-start | bytes 6152 | tf_op jit(solution)/shard_map/ppermute | solution.py:38
  21.4 25.1 %all-to-all-start = ((bf16[16,384,128]{2,1,0:T(8,128)(2,1)}), bf16[16,384,128]{2,1,0:T(8,128)(2,1)}, u32[]{:S(2)}, u32[]{:S(2)}) async-start(bf16[16,384,128]{2,1,0:T(8,128)(2,1)} %shard_map.119), calls=%async_computation | async-start | bytes 3145728 | tf_op jit(solution)/shard_map/all_to_all | solution.py:42
  36.3 1.5 copy-start.2
  46.5 31.1 %collective-permute-start.5 = (bf16[16,384,128]{2,1,0:T(8,128)(2,1)}, bf16[16,384,128]{2,1,0:T(8,128)(2,1)}, u32[]{:S(2)}, u32[]{:S(2)}) collective-permute-start(bf16[16,384,128]{2,1,0:T(8,128)(2,1)} %all-to-all-done.w0), channel_id=1, source_target_pairs={{0,1},{1,0},{2,3},{3,2},{64,65},{65,64},{66,67},{67,66},{128,129},... | collective-permute-start | bytes 4718600 | tf_op jit(solution)/shard_map/ppermute | solution.py:38
  48.1 35.5 %all-to-all-start.1 = ((bf16[16,40,2048]{2,1,0:T(8,128)(2,1)}), bf16[16,40,2048]{2,1,0:T(8,128)(2,1)S(1)}, u32[]{:S(2)}, u32[]{:S(2)}) async-start(bf16[16,40,2048]{2,1,0:T(8,128)(2,1)} %bitcast.30), calls=%async_computation.1 | async-start | bytes 5242880 | tf_op jit(solution)/shard_map/all_to_all | solution.py:42
  51.9 25.7 %collective-permute-start.6 = (bf16[16,384,128]{2,1,0:T(8,128)(2,1)}, bf16[16,384,128]{2,1,0:T(8,128)(2,1)S(1)}, u32[]{:S(2)}, u32[]{:S(2)}) collective-permute-start(bf16[16,384,128]{2,1,0:T(8,128)(2,1)} %all-to-all-done.w0), channel_id=1, source_target_pairs={{0,64},{1,65},{2,66},{3,67},{64,0},{65,1},{66,2},{67,3},{128,192},... | collective-permute-start | bytes 4718600 | tf_op jit(solution)/shard_map/ppermute | solution.py:38
  77.6 6.0 %collective-permute-start.7 = (bf16[16,384,128]{2,1,0:T(8,128)(2,1)}, bf16[16,384,128]{2,1,0:T(8,128)(2,1)}, u32[]{:S(2)}, u32[]{:S(2)}) collective-permute-start(bf16[16,384,128]{2,1,0:T(8,128)(2,1)} %collective-permute-done.5.w1), channel_id=1, source_target_pairs={{0,64},{1,65},{2,66},{3,67},{64,0},{65,1},{66,2},{67,3},{128,192},... | collective-permute-start | bytes 4718600 | tf_op jit(solution)/shard_map/ppermute | solution.py:38
  77.6 1.3 copy-start.7
  83.7 1.4 copy-start.8
  95.5 5.4 %copy-start.4 = (bf16[384,2048]{1,0:T(8,128)(2,1)}, bf16[384,2048]{1,0:T(8,128)(2,1)S(1)}, u32[]{:S(2)}) copy-start(bf16[384,2048]{1,0:T(8,128)(2,1)S(1)} %get-tuple-element.53) | copy-start | bytes 4718596
  96.9 4.1 %collective-permute-start.8 = (bf16[2,16,32,512]{3,2,1,0:T(8,128)(2,1)S(1)}, bf16[2,16,32,512]{3,2,1,0:T(8,128)(2,1)S(1)}, u32[]{:S(2)}, u32[]{:S(2)}) collective-permute-start(bf16[2,16,32,512]{3,2,1,0:T(8,128)(2,1)S(1)} %get-tuple-element.55), channel_id=1, source_target_pairs={{0,64},{1,65},{2,66},{3,67},{64,0},{65,1},{66,2},{67,3},{128,192},... | collective-permute-start | bytes 3145736 | tf_op jit(solution)/shard_map/ppermute | solution.py:38
  101.0 1.5 copy-start.3
  102.5 1.1 copy-start
  103.6 14.3 %collective-permute-start.10 = (bf16[2,16,64,512]{3,2,1,0:T(8,128)(2,1)}, bf16[2,16,64,512]{3,2,1,0:T(8,128)(2,1)}, u32[]{:S(2)}, u32[]{:S(2)}) collective-permute-start(bf16[2,16,64,512]{3,2,1,0:T(8,128)(2,1)} %get-tuple-element.62), channel_id=1, source_target_pairs={{0,64},{1,65},{2,66},{3,67},{64,0},{65,1},{66,2},{67,3},{128,192},... | collective-permute-start | bytes 6291464 | tf_op jit(solution)/shard_map/ppermute | solution.py:38
  104.1 13.8 %collective-permute-start.9 = (bf16[16,32,512]{2,1,0:T(8,128)(2,1)}, bf16[16,32,512]{2,1,0:T(8,128)(2,1)}, u32[]{:S(2)}, u32[]{:S(2)}) collective-permute-start(bf16[16,32,512]{2,1,0:T(8,128)(2,1)} %shard_map.123), channel_id=1, source_target_pairs={{0,1},{1,0},{2,3},{3,2},{64,65},{65,64},{66,67},{67,66},{128,129},... | collective-permute-start | bytes 1572872 | tf_op jit(solution)/shard_map/ppermute | solution.py:38
  104.1 29.2 %all-to-all-start.2 = ((bf16[16,24,2048]{2,1,0:T(8,128)(2,1)}), bf16[16,24,2048]{2,1,0:T(8,128)(2,1)S(1)}, u32[]{:S(2)}, u32[]{:S(2)}) async-start(bf16[16,24,2048]{2,1,0:T(8,128)(2,1)} %bitcast.31), calls=%async_computation.2 | async-start | bytes 3145728 | tf_op jit(solution)/shard_map/all_to_all | solution.py:42
  107.8 12.9 %copy-start.1 = (bf16[2,16,32,512]{3,2,1,0:T(8,128)(2,1)S(1)}, bf16[2,16,32,512]{3,2,1,0:T(8,128)(2,1)}, u32[]{:S(2)}) copy-start(bf16[2,16,32,512]{3,2,1,0:T(8,128)(2,1)} %copy-done) | copy-start | bytes 3145732
  120.7 28.3 %collective-permute-start.11 = (bf16[16,64,512]{2,1,0:T(8,128)(2,1)}, bf16[16,64,512]{2,1,0:T(8,128)(2,1)}, u32[]{:S(2)}, u32[]{:S(2)}) collective-permute-start(bf16[16,64,512]{2,1,0:T(8,128)(2,1)} %shard_map.126), channel_id=1, source_target_pairs={{0,1},{1,0},{2,3},{3,2},{64,65},{65,64},{66,67},{67,66},{128,129},... | collective-permute-start | bytes 3145736 | tf_op jit(solution)/shard_map/ppermute | solution.py:38
  133.3 18.9 %all-to-all-start.3 = ((bf16[16,32,512]{2,1,0:T(8,128)(2,1)}), bf16[16,32,512]{2,1,0:T(8,128)(2,1)S(1)}, u32[]{:S(2)}, u32[]{:S(2)}) async-start(bf16[16,32,512]{2,1,0:T(8,128)(2,1)} %shard_map.125), calls=%async_computation.3 | async-start | bytes 1048576 | tf_op jit(solution)/shard_map/all_to_all | solution.py:42
  138.3 26.5 %collective-permute-start.13 = (bf16[128,2048]{1,0:T(8,128)(2,1)}, bf16[128,2048]{1,0:T(8,128)(2,1)S(1)}, u32[]{:S(2)}, u32[]{:S(2)}) collective-permute-start(bf16[128,2048]{1,0:T(8,128)(2,1)} %get-tuple-element.69), channel_id=1, source_target_pairs={{0,192},{1,193},{2,0},{3,1},{64,194},{65,195},{66,2},{67,3},{128,6... | collective-permute-start | bytes 1572872 | tf_op jit(solution)/shard_map/ppermute | solution.py:38
  153.0 19.5 %all-to-all-start.4 = ((bf16[16,64,512]{2,1,0:T(8,128)(2,1)}), bf16[16,64,512]{2,1,0:T(8,128)(2,1)S(1)}, u32[]{:S(2)}, u32[]{:S(2)}) async-start(bf16[16,64,512]{2,1,0:T(8,128)(2,1)} %shard_map.127), calls=%async_computation.4 | async-start | bytes 2097152 | tf_op jit(solution)/shard_map/all_to_all | solution.py:42
  158.4 14.1 %collective-permute-start.14 = (bf16[1,8,32,512]{3,2,1,0:T(8,128)(2,1)S(1)}, bf16[1,8,32,512]{3,2,1,0:T(8,128)(2,1)S(1)}, u32[]{:S(2)}, u32[]{:S(2)}) collective-permute-start(bf16[1,8,32,512]{3,2,1,0:T(8,128)(2,1)S(1)} %shard_map.130), channel_id=1, source_target_pairs={{0,0},{1,1},{2,64},{3,65},{64,2},{65,3},{66,66},{67,67},{128,128},... | collective-permute-start | bytes 786440 | tf_op jit(solution)/shard_map/ppermute | solution.py:38
  160.3 12.2 %collective-permute-start.12 = (bf16[8,128]{1,0:T(8,128)(2,1)S(1)}, bf16[8,128]{1,0:T(8,128)(2,1)S(1)}, u32[]{:S(2)}, u32[]{:S(2)}) collective-permute-start(bf16[8,128]{1,0:T(8,128)(2,1)S(1)} %get-tuple-element.68), channel_id=1, source_target_pairs={{0,0},{1,1},{2,64},{3,65},{64,2},{65,3},{66,66},{67,67},{128,128},... | collective-permute-start | bytes 6152 | tf_op jit(solution)/shard_map/ppermute | solution.py:38
  173.3 16.0 %collective-permute-start.15 = (bf16[2,8,32,512]{3,2,1,0:T(8,128)(2,1)S(1)}, bf16[2,8,32,512]{3,2,1,0:T(8,128)(2,1)S(1)}, u32[]{:S(2)}, u32[]{:S(2)}) collective-permute-start(bf16[2,8,32,512]{3,2,1,0:T(8,128)(2,1)S(1)} %shard_map.131), channel_id=1, source_target_pairs={{0,0},{1,1},{2,64},{3,65},{64,2},{65,3},{66,66},{67,67},{128,128},... | collective-permute-start | bytes 1572872 | tf_op jit(solution)/shard_map/ppermute | solution.py:38
  (3 other events, 2.7 us)
